TPU v7x, 32 devices: a whole 2x2x4 slice. The times are simulated.
32 devices in a mesh: row: 8 (over y, x, core), col: 4 (over z).
Axes of the slice: x: 2, y: 2, z: 4, core: 2. Of those that a mesh axis runs over, the one named last changes fastest.
Arguments:
- query_tokens: bfloat16 [128, 128, 768], P(('row', 'col')), may hold values from -5 to 5
- passage_tokens: bfloat16 [64, 512, 768], P(('row', 'col')), may hold values from -5 to 5
- query_lengths: int32 [128], P(('row', 'col')), may hold values from 102 to 128, as said below
- passage_lengths: int32 [64], P(('row', 'col')), may hold values from 409 to 512, as said below
- positives: int32 [128], P(('row', 'col')), may hold values from 0 to 63
- w_query: bfloat16 [768, 768], replicated, may hold values from -0.21875 to 0.21875
- w_key: bfloat16 [768, 768], replicated, may hold values from -0.21875 to 0.21875
- w_value: bfloat16 [768, 768], replicated, may hold values from -0.21875 to 0.21875
- w_attn_out: bfloat16 [768, 768], replicated, may hold values from -0.21875 to 0.21875
- w_inner: bfloat16 [768, 3072], replicated, may hold values from -0.21875 to 0.21875
- w_outer: bfloat16 [3072, 768], replicated, may hold values from -0.109375 to 0.109375
- bias_query: float32 [768], replicated, may hold values from -3 to 3
- bias_value: float32 [768], replicated, may hold values from -0.3 to 0.3
- bias_attn_out: float32 [768], replicated, may hold values from -0.6 to 0.6
- bias_inner: float32 [3072], replicated, may hold values from -0.6 to 0.6
- bias_outer: float32 [768], replicated, may hold values from -0.6 to 0.6
- gain_one: float32 [768], replicated, may hold values from 0.5 to 1.5
- shift_one: float32 [768], replicated, may hold values from -0.6 to 0.6
- gain_two: float32 [768], replicated, may hold values from 0.5 to 1.5
- shift_two: float32 [768], replicated, may hold values from -0.3 to 0.3
Outputs:
- loss: float32 [], replicated
- query_out: bfloat16 [128, 128, 768], P(('row', 'col'))
- passage_out: bfloat16 [64, 512, 768], P(('row', 'col'))
- query_grad: bfloat16 [128, 128, 768], P(('row', 'col'))
- passage_grad: bfloat16 [64, 512, 768], P(('row', 'col'))
- grad_w_query: float32 [768, 768], P('row')
- grad_w_key: float32 [768, 768], P('row')
- grad_w_value: float32 [768, 768], P('row')
- grad_w_attn_out: float32 [768, 768], P('row')
- grad_w_inner: float32 [768, 3072], P('row')
- grad_w_outer: float32 [3072, 768], P('row')
- grad_bias_query: float32 [768], P('row')
- grad_bias_value: float32 [768], P('row')
- grad_bias_attn_out: float32 [768], P('row')
- grad_bias_inner: float32 [3072], P('row')
- grad_bias_outer: float32 [768], P('row')
- grad_gain_one: float32 [768], P('row')
- grad_shift_one: float32 [768], P('row')
- grad_gain_two: float32 [768], P('row')
- grad_shift_two: float32 [768], P('row')
Inputs may be any that keep to these rules, and one draw needn't show every extreme that they name: `query_lengths`: each query has 102 to 128 live tokens, the first ones of its slots; some query has exactly 128. `passage_lengths`: each passage has 409 to 512 live tokens, the first ones of its slots; some passage has exactly 512.
All inputs are finite; a program needn't handle non-finite values.
Results may differ from a plain program's by a relative error of at most 0.029.
Values may be sent and summed in bfloat16 or wider, within the bound.
No kernel may reach another device: no remote copies, remote signals or barrier semaphores. Data moves between devices by JAX's collectives and lax.ppermute only.
A program may use at most 256 MiB of HBM per device.

v0:
```python
from functools import partial

import jax
import jax.numpy as jnp
from jax import lax
from jax.sharding import PartitionSpec as P

HEADS = 12


EPS_NORM = 1e-12
EPS_POOL = 1e-06
SCALE_LOSS = 128.0
INV_TEMP = 100.0


def to_low(value):
    return value.astype(jnp.bfloat16)


def outer_sum(left, right):
    return lax.dot_general(
        left, right, (((0,), (0,)), ((), ())), preferred_element_type=jnp.float32
    )


def with_trans(left, right):
    return lax.dot_general(
        left, right, (((1,), (1,)), ((), ())), preferred_element_type=jnp.float32
    )


def normalize(hidden, gain, shift):
    center = hidden - jnp.mean(hidden, -1, keepdims=True)
    spread = jnp.mean(center * center, -1, keepdims=True)
    return center * lax.rsqrt(spread + EPS_NORM) * gain + shift


def gelu_exact(inner_pre):
    return jax.nn.gelu(inner_pre, approximate=False)


def pool_embed(states, lengths, seq_len):
    total_rows, model_width = states.shape
    grouped = states.reshape(total_rows // seq_len, seq_len, model_width)
    live_rows = (
        lax.broadcasted_iota(jnp.int32, (grouped.shape[0], seq_len), 1) < lengths[:, None]
    ).astype(jnp.float32)
    pooled = jnp.sum(grouped * live_rows[:, :, None], 1) / lengths.astype(jnp.float32)[:, None]
    return pooled * lax.rsqrt(jnp.sum(pooled * pooled, -1, keepdims=True) + EPS_POOL)


def layer_forward(tokens, lengths, weights):
    (
        w_query,
        w_key,
        w_value,
        w_attn_out,
        w_inner,
        w_outer,
        bias_query,
        bias_value,
        bias_attn_out,
        bias_inner,
        bias_outer,
        gain_one,
        shift_one,
        gain_two,
        shift_two,
    ) = weights
    seq_count, seq_len, model_width = tokens.shape
    head_dim = model_width // HEADS
    shape_heads = (seq_count, seq_len, HEADS, head_dim)
    flat_rows = tokens.reshape(seq_count * seq_len, model_width)
    query_rows = to_low(
        jnp.dot(flat_rows, w_query, preferred_element_type=jnp.float32) + bias_query
    )
    key_rows = to_low(jnp.dot(flat_rows, w_key, preferred_element_type=jnp.float32))
    value_rows = to_low(
        jnp.dot(flat_rows, w_value, preferred_element_type=jnp.float32) + bias_value
    )
    raw_scores = jnp.einsum(
        "bqhd,bkhd->bhqk",
        query_rows.reshape(shape_heads),
        key_rows.reshape(shape_heads),
        preferred_element_type=jnp.float32,
    )
    scores = raw_scores * head_dim ** (-0.5)
    live_keys = lax.broadcasted_iota(jnp.int32, (seq_count, seq_len), 1) < lengths[:, None]
    masked = jnp.where(live_keys[:, None, None, :], scores, -1e30)
    probs = jax.nn.softmax(masked, axis=-1)
    probs_low = to_low(probs)
    context = jnp.einsum(
        "bhqk,bkhd->bqhd",
        probs_low,
        value_rows.reshape(shape_heads),
        preferred_element_type=jnp.float32,
    )
    context = to_low(context.reshape(flat_rows.shape))
    attn_out = jnp.dot(context, w_attn_out, preferred_element_type=jnp.float32) + bias_attn_out
    hidden_one = flat_rows.astype(jnp.float32) + attn_out
    normed_one = normalize(hidden_one, gain_one, shift_one)
    normed_low = to_low(normed_one)
    inner_pre = jnp.dot(normed_low, w_inner, preferred_element_type=jnp.float32) + bias_inner
    active = to_low(gelu_exact(inner_pre))
    hidden_two = (
        normed_one + jnp.dot(active, w_outer, preferred_element_type=jnp.float32) + bias_outer
    )
    normed_two = normalize(hidden_two, gain_two, shift_two)
    saved = (
        flat_rows,
        query_rows,
        key_rows,
        value_rows,
        probs,
        probs_low,
        context,
        hidden_one,
        normed_low,
        inner_pre,
        active,
        hidden_two,
    )
    return (normed_two, saved)


def layer_backward(saved, grad_two, weights, shape_heads):
    (
        w_query,
        w_key,
        w_value,
        w_attn_out,
        w_inner,
        w_outer,
        bias_query,
        bias_value,
        bias_attn_out,
        bias_inner,
        bias_outer,
        gain_one,
        shift_one,
        gain_two,
        shift_two,
    ) = weights
    (
        flat_rows,
        query_rows,
        key_rows,
        value_rows,
        probs,
        probs_low,
        context,
        hidden_one,
        normed_low,
        inner_pre,
        active,
        hidden_two,
    ) = saved
    head_dim = shape_heads[3]
    flat_shape = flat_rows.shape
    _, back_two = jax.vjp(normalize, hidden_two, gain_two, shift_two)
    grad_hidden_two, grad_gain_two, grad_shift_two = back_two(grad_two)
    grad_outer_low = to_low(grad_hidden_two)
    grad_w_outer = outer_sum(active, grad_outer_low)
    grad_bias_outer = jnp.sum(grad_outer_low.astype(jnp.float32), 0)
    grad_active = with_trans(grad_outer_low, w_outer)
    _, back_gelu = jax.vjp(gelu_exact, inner_pre)
    grad_inner_low = to_low(back_gelu(grad_active)[0])
    grad_w_inner = outer_sum(normed_low, grad_inner_low)
    grad_bias_inner = jnp.sum(grad_inner_low.astype(jnp.float32), 0)
    grad_normed = grad_hidden_two + with_trans(grad_inner_low, w_inner)
    _, back_one = jax.vjp(normalize, hidden_one, gain_one, shift_one)
    grad_hidden_one, grad_gain_one, grad_shift_one = back_one(grad_normed)
    grad_attn_low = to_low(grad_hidden_one)
    grad_w_attn_out = outer_sum(context, grad_attn_low)
    grad_bias_attn_out = jnp.sum(grad_attn_low.astype(jnp.float32), 0)
    grad_context = to_low(with_trans(grad_attn_low, w_attn_out)).reshape(shape_heads)
    grad_value = jnp.einsum(
        "bhqk,bqhd->bkhd", probs_low, grad_context, preferred_element_type=jnp.float32
    )
    grad_probs = jnp.einsum(
        "bqhd,bkhd->bhqk",
        grad_context,
        value_rows.reshape(shape_heads),
        preferred_element_type=jnp.float32,
    )
    grad_scores = to_low(probs * (grad_probs - jnp.sum(probs * grad_probs, -1, keepdims=True)))
    head_scale = head_dim ** (-0.5)
    grad_query = (
        jnp.einsum(
            "bhqk,bkhd->bqhd",
            grad_scores,
            key_rows.reshape(shape_heads),
            preferred_element_type=jnp.float32,
        )
        * head_scale
    )
    grad_key = (
        jnp.einsum(
            "bhqk,bqhd->bkhd",
            grad_scores,
            query_rows.reshape(shape_heads),
            preferred_element_type=jnp.float32,
        )
        * head_scale
    )
    query_low = to_low(grad_query.reshape(flat_shape))
    key_low = to_low(grad_key.reshape(flat_shape))
    value_low = to_low(grad_value.reshape(flat_shape))
    grad_w_query = outer_sum(flat_rows, query_low)
    grad_w_key = outer_sum(flat_rows, key_low)
    grad_w_value = outer_sum(flat_rows, value_low)
    grad_bias_query = jnp.sum(query_low.astype(jnp.float32), 0)
    grad_bias_value = jnp.sum(value_low.astype(jnp.float32), 0)
    grad_input = (
        grad_hidden_one
        + with_trans(query_low, w_query)
        + with_trans(key_low, w_key)
        + with_trans(value_low, w_value)
    )
    grads = (
        grad_w_query,
        grad_w_key,
        grad_w_value,
        grad_w_attn_out,
        grad_w_inner,
        grad_w_outer,
        grad_bias_query,
        grad_bias_value,
        grad_bias_attn_out,
        grad_bias_inner,
        grad_bias_outer,
        grad_gain_one,
        grad_shift_one,
        grad_gain_two,
        grad_shift_two,
    )
    return (grad_input, grads)


def per_device(
    query_tokens,
    passage_tokens,
    query_lengths,
    passage_lengths,
    positives,
    w_query,
    w_key,
    w_value,
    w_attn_out,
    w_inner,
    w_outer,
    bias_query,
    bias_value,
    bias_attn_out,
    bias_inner,
    bias_outer,
    gain_one,
    shift_one,
    gain_two,
    shift_two,
):
    weights = (
        w_query,
        w_key,
        w_value,
        w_attn_out,
        w_inner,
        w_outer,
        bias_query,
        bias_value,
        bias_attn_out,
        bias_inner,
        bias_outer,
        gain_one,
        shift_one,
        gain_two,
        shift_two,
    )
    q_dev, q_len, model_width = query_tokens.shape
    p_dev, p_len, _ = passage_tokens.shape
    head_dim = model_width // HEADS
    row_count = lax.axis_size("row")
    col_count = lax.axis_size("col")
    col_here = lax.axis_index("col")
    query_states, query_saved = layer_forward(query_tokens, query_lengths, weights)
    passage_states, passage_saved = layer_forward(passage_tokens, passage_lengths, weights)
    query_embed, query_pull = jax.vjp(
        partial(pool_embed, lengths=query_lengths, seq_len=q_len), query_states
    )
    passage_embed, passage_pull = jax.vjp(
        partial(pool_embed, lengths=passage_lengths, seq_len=p_len), passage_states
    )
    query_block, positive_block = (
        lax.all_gather(to_low(query_embed), "col", axis=0, tiled=True),
        lax.all_gather(positives, "col", axis=0, tiled=True),
    )
    passage_block = lax.all_gather(to_low(passage_embed), "row", axis=0, tiled=True)
    scores = with_trans(query_block, passage_block) * INV_TEMP
    columns = lax.broadcasted_iota(jnp.int32, scores.shape, 1)
    owner_col = positive_block // p_dev % col_count
    place = positive_block // (p_dev * col_count) * p_dev + positive_block % p_dev
    target = ((columns == place[:, None]) & (owner_col == col_here)[:, None]).astype(jnp.float32)
    local_top = jnp.max(scores, 1)
    picked_local = jnp.sum(scores * target, 1)
    top_all = lax.pmax(local_top, "col")
    sums_all, picked = lax.psum(
        (jnp.sum(jnp.exp(scores - top_all[:, None]), 1), picked_local), "col"
    )
    totals = top_all + jnp.log(sums_all)
    losses = totals - picked
    own_losses = lax.dynamic_slice_in_dim(losses, col_here * q_dev, q_dev)
    loss = lax.psum(jnp.sum(own_losses), ("row", "col")) / (q_dev * row_count * col_count)
    probs_all = jnp.exp(scores - totals[:, None])
    grad_raw = to_low(INV_TEMP * (SCALE_LOSS * (probs_all - target)))
    query_back = lax.psum_scatter(
        jnp.dot(grad_raw, passage_block, preferred_element_type=jnp.float32).astype(jnp.bfloat16),
        "col",
        scatter_dimension=0,
        tiled=True,
    ).astype(jnp.float32)
    passage_back = lax.psum_scatter(
        outer_sum(grad_raw, query_block).astype(jnp.bfloat16),
        "row",
        scatter_dimension=0,
        tiled=True,
    ).astype(jnp.float32)
    query_grad_two = query_pull(query_back)[0]
    passage_grad_two = passage_pull(passage_back)[0]
    query_input_grad, query_grads = layer_backward(
        query_saved, query_grad_two, weights, (q_dev, q_len, HEADS, head_dim)
    )
    passage_input_grad, passage_grads = layer_backward(
        passage_saved, passage_grad_two, weights, (p_dev, p_len, HEADS, head_dim)
    )
    grads = tuple(
        (first_grad + second_grad for first_grad, second_grad in zip(query_grads, passage_grads))
    )
    pieces = [item.reshape(row_count, -1) for item in grads]
    piece_widths = [item.shape[1] for item in pieces]
    stacked = jnp.concatenate(pieces, 1)
    summed = lax.psum_scatter(
        stacked.astype(jnp.bfloat16), "row", scatter_dimension=0, tiled=True
    ).astype(jnp.float32)
    summed = lax.psum(summed.astype(jnp.bfloat16), "col").astype(jnp.float32)
    outputs = []
    offset = 0
    for item, piece_width in zip(grads, piece_widths):
        shard_shape = (item.shape[0] // row_count,) + item.shape[1:]
        outputs.append(summed[0, offset : offset + piece_width].reshape(shard_shape))
        offset = offset + piece_width
    query_out = to_low(query_states).reshape(query_tokens.shape)
    passage_out = to_low(passage_states).reshape(passage_tokens.shape)
    query_grad = to_low(query_input_grad).reshape(query_tokens.shape)
    passage_grad = to_low(passage_input_grad).reshape(passage_tokens.shape)
    return (
        loss,
        query_out,
        passage_out,
        query_grad,
        passage_grad,
        outputs[0],
        outputs[1],
        outputs[2],
        outputs[3],
        outputs[4],
        outputs[5],
        outputs[6],
        outputs[7],
        outputs[8],
        outputs[9],
        outputs[10],
        outputs[11],
        outputs[12],
        outputs[13],
        outputs[14],
    )


def solution(mesh):
    in_specs = (
        P(("row", "col"), None, None),
        P(("row", "col"), None, None),
        P(("row", "col")),
        P(("row", "col")),
        P(("row", "col")),
        P(),
        P(),
        P(),
        P(),
        P(),
        P(),
        P(),
        P(),
        P(),
        P(),
        P(),
        P(),
        P(),
        P(),
        P(),
    )
    out_specs = (
        P(),
        P(("row", "col"), None, None),
        P(("row", "col"), None, None),
        P(("row", "col"), None, None),
        P(("row", "col"), None, None),
        P("row", None),
        P("row", None),
        P("row", None),
        P("row", None),
        P("row", None),
        P("row", None),
        P("row"),
        P("row"),
        P("row"),
        P("row"),
        P("row"),
        P("row"),
        P("row"),
        P("row"),
        P("row"),
    )
    return jax.shard_map(
        per_device, mesh=mesh, in_specs=in_specs, out_specs=out_specs, check_vma=False
    )
```

profile of v0, /device:TPU:0, one launch (start us, length us, event | category | flops | bytes accessed | tf_op | source)
XLA Modules:
  0.0 918.6 jit_solution(9402236613288231362)
XLA Ops:
  27.4 10.0 %all-reduce = s32[16]{0:T(128)S(1)} all-reduce(s32[16]{0:T(128)S(1)} %dynamic-update-slice), channel_id=1, replica_groups=mesh['row'=8,'col'=4] {'col'}, use_global_device_ids=true, to_apply=%add | all-reduce | flops 16 | bytes 128
  70.9 18.5 %multiply_convert_fusion.2 = (bf16[512,3072]{1,0:T(8,128)(2,1)S(1)}, f32[512,3072]{1,0:T(8,128)}, f32[512,3072]{1,0:T(8,128)}) fusion(f32[3072]{0:T(1024)S(1)} %copy-done.123, bf16[768,3072]{1,0:T(8,128)(2,1)S(1)} %bitcast.276, f32[512,768]{1,0:T(8,128)S(1)} %get-tuple-element.91, f32[768]{0:T(1024)S(1)} %copy-done.65, f32[768]{0:T(1024)S(1)} %copy-done.59, ...), kind=kOutput, calls=%fused_computation.39 | convolution fusion | flops 2521694208 | bytes 22042624 | tf_op jit(solution)/shard_map/dot_general | solution.py:104
  95.0 13.1 %all-gather = bf16[4,4,768]{2,1,0:T(4,128)(2,1)S(1)} all-gather(bf16[1,4,768]{2,1,0:T(4,128)(2,1)S(1)} %fusion.116), channel_id=1, replica_groups=mesh['row'=8,'col'=4] {'col'}, dimensions={0}, use_global_device_ids=true | all-gather | bytes 30720 | tf_op jit(solution)/shard_map/all_gather | solution.py:295
  108.2 15.1 %fusion.151 = (f32[2,12,512]{2,1,0:T(8,128)S(1)}, f32[2,12,512,512]{2,3,1,0:T(8,128)}) fusion(pred[2,512]{1,0:T(4,128)(4,1)S(1)} %copy-done.109, bf16[2,512,12,64]{1,0,3,2:T(2,128)(2,1)S(1)} %reshape.462, bf16[2,512,12,64]{1,0,3,2:T(2,128)(2,1)} %reshape.461), kind=kOutput, calls=%fused_computation.314 | convolution fusion | flops 830472704 | bytes 28361728 | tf_op jit(solution)/shard_map/sub | solution.py:91
  123.3 11.0 %fusion.50 = bf16[2,512,12,64]{1,3,2,0:T(8,128)(2,1)S(1)} fusion(bf16[2,512,12,64]{1,0,3,2:T(2,128)(2,1)} %reshape.460, f32[2,12,512,512]{2,3,1,0:T(8,128)} %get-tuple-element.96, f32[2,12,512]{2,1,0:T(8,128)S(1)} %get-tuple-element.95), kind=kOutput, calls=%fused_computation.132 | convolution fusion | flops 818675712 | bytes 28360704 | tf_op jit(solution)/shard_map/bhqk,bkhd->bqhd/dot_general | solution.py:93
  140.8 35.5 %multiply_convert_fusion.1 = (bf16[1024,3072]{1,0:T(8,128)(2,1)S(1)}, f32[1024,3072]{1,0:T(8,128)}, f32[1024,3072]{1,0:T(8,128)}) fusion(f32[3072]{0:T(1024)S(1)} %copy-done.124, bf16[768,3072]{1,0:T(8,128)(2,1)S(1)} %bitcast.278, f32[1024,768]{1,0:T(8,128)S(1)} %get-tuple-element.98, f32[768]{0:T(1024)S(1)} %copy-done.65, f32[768]{0:T(1024)S(1)} %copy-done.59, ...), kind=kOutput, calls=%fused_computation.11 | convolution fusion | flops 5043388416 | bytes 39348224 | tf_op jit(solution)/shard_map/dot_general | solution.py:104
  185.0 9.0 all-gather.1
  194.2 10.0 %pmax.7 = f32[16]{0:T(128)S(1)} all-reduce(f32[16]{0:T(128)S(1)} %get-tuple-element.102), channel_id=1, replica_groups=mesh['row'=8,'col'=4] {'col'}, use_global_device_ids=true, to_apply=%region_17.18 | all-reduce | flops 16 | bytes 128 | tf_op jit(solution)/shard_map/pmax | solution.py:306
  204.2 8.8 all-reduce.4
  214.4 22.6 %all-reduce.2 = bf16[16,768]{1,0:T(8,128)(2,1)S(1)} all-reduce(bf16[16,768]{1,0:T(8,128)(2,1)S(1)} %convolution_convert_fusion.6), channel_id=3, replica_groups=mesh['row'=8,'col'=4] {'row'}, use_global_device_ids=true, to_apply=%region_31.32.clone | all-reduce | flops 12288 | bytes 49152
  245.6 17.5 %convert_reduce_fusion = (f32[3072]{0:T(1024)}, bf16[1024,3072]{1,0:T(8,128)(2,1)}) fusion(f32[1024,3072]{1,0:T(8,128)} %get-tuple-element.67, bf16[1024,768]{1,0:T(8,128)(2,1)S(1)} %get-tuple-element.41, bf16[3072,768]{1,0:T(8,128)(2,1)} %param.30, f32[1024,3072]{1,0:T(8,128)} %get-tuple-element.99, f32[3072]{0:T(1024)S(1)} %copy-done.124), kind=kOutput, calls=%fused_computation.9 | convolution fusion | flops 4885312512 | bytes 37773312 | tf_op jit(solution)/shard_map/dot_general | solution.py:28
  263.0 10.7 %multiply_reduce_fusion.2 = (f32[768]{0:T(1024)}, f32[1024]{0:T(1024)S(1)}, f32[768]{0:T(1024)}, f32[1024,768]{1,0:T(8,128)S(1)}) fusion(f32[1024,768]{1,0:T(8,128)S(1)} %copy-done.4, f32[1024]{0:T(1024)S(1)} %fusion.117, f32[1024]{0:T(1024)S(1)} %broadcast_multiply_fusion.1, f32[768]{0:T(1024)S(1)} %copy-done.59, ...), kind=kOutput, calls=%fused_computation.64 | convolution fusion | flops 4839699456 | bytes 20472832 | tf_op jit(solution)/shard_map/dot_general | solution.py:28
  273.8 8.5 fusion.134
  291.9 17.5 %all-reduce.1 = bf16[16,768]{1,0:T(8,128)(2,1)S(1)} all-reduce(bf16[16,768]{1,0:T(8,128)(2,1)S(1)} %convolution_convert_fusion.7), channel_id=2, replica_groups=mesh['row'=8,'col'=4] {'col'}, use_global_device_ids=true, to_apply=%region_24.25.clone | all-reduce | flops 12288 | bytes 49152
  313.8 9.5 %convert_reduce_fusion.1 = (f32[3072]{0:T(1024)}, bf16[512,3072]{1,0:T(8,128)(2,1)S(1)}) fusion(f32[512,3072]{1,0:T(8,128)} %get-tuple-element.71, f32[512,3072]{1,0:T(8,128)} %get-tuple-element.92, f32[3072]{0:T(1024)S(1)} %copy-done.124, bf16[512,768]{1,0:T(8,128)(2,1)S(1)} %get-tuple-element.43, bf16[3072,768]{1,0:T(8,128)(2,1)} %param.30), kind=kOutput, calls=%fused_computation.33 | convolution fusion | flops 2442654720 | bytes 21258240 | tf_op jit(solution)/shard_map/dot_general | solution.py:28
  341.8 8.3 fusion.169
  354.1 14.3 %convert_reduce_fusion.4 = (f32[12,64]{1,0:T(8,128)}, bf16[2,512,12,64]{1,3,2,0:T(8,128)(2,1)}) fusion(f32[2,12,512,512]{2,3,1,0:T(8,128)} %get-tuple-element.96, f32[2,12,512]{2,1,0:T(8,128)} %copy-done.60, bf16[2,512,12,64]{1,0,3,2:T(2,128)(2,1)} %reshape.468), kind=kOutput, calls=%fused_computation.67 | convolution fusion | flops 820247808 | bytes 28363776 | tf_op jit(solution)/shard_map/bhqk,bqhd->bkhd/dot_general | solution.py:178
  368.5 17.4 %multiply_reduce_fusion = (f32[2,12,512]{2,1,0:T(8,128)}, f32[2,12,512,512]{2,3,1,0:T(8,128)}) fusion(f32[2,12,512,512]{2,3,1,0:T(8,128)} %get-tuple-element.96, f32[2,12,512]{2,1,0:T(8,128)} %copy-done.60, bf16[2,512,12,64]{1,0,3,2:T(2,128)(2,1)S(1)} %copy-done.44, bf16[2,512,12,64]{1,0,3,2:T(2,128)(2,1)} %reshape.468), kind=kOutput, calls=%fused_computation.3 | convolution fusion | flops 824168448 | bytes 53575680 | tf_op jit(solution)/shard_map/bqhd,bkhd->bhqk/dot_general | solution.py:181
  385.9 21.6 %multiply_convert_fusion = bf16[2,12,512,512]{2,3,1,0:T(8,128)(2,1)} fusion(f32[2,12,512,512]{2,3,1,0:T(8,128)} %get-tuple-element.109, f32[2,12,512]{2,1,0:T(8,128)} %get-tuple-element.108, f32[2,12,512,512]{2,3,1,0:T(8,128)} %get-tuple-element.96, f32[2,12,512]{2,1,0:T(8,128)} %copy-done.60), kind=kLoop, calls=%fused_computation.2 | loop fusion | flops 25165824 | bytes 63012864 | tf_op jit(solution)/shard_map/convert_element_type | solution.py:18
  407.4 9.7 %fusion.54 = bf16[2,512,12,64]{1,3,2,0:T(8,128)(2,1)} fusion(bf16[2,12,512,512]{2,3,1,0:T(8,128)(2,1)} %multiply_convert_fusion, bf16[2,512,12,64]{1,0,3,2:T(2,128)(2,1)S(1)} %copy-done.25), kind=kOutput, calls=%fused_computation.134 | convolution fusion | flops 806879232 | bytes 15728640 | tf_op jit(solution)/shard_map/bhqk,bqhd->bkhd/dot_general | solution.py:199
  417.2 7.4 convert_reduce_fusion.5
  435.3 10.2 %add_convert_fusion.2 = bf16[768,3072]{1,0:T(8,128)(2,1)} fusion(f32[768,3072]{1,0:T(8,128)} %fusion.134, bf16[512,3072]{1,0:T(8,128)(2,1)} %copy-done.133, f32[512,768]{1,0:T(8,128)} %copy-done.23, f32[768]{0:T(1024)S(1)} %copy-done.65, f32[768]{0:T(1024)S(1)} %copy-done.59, f32[512]{0:T(512)} %copy-done.92, f32[512]{0:T(512)} %copy-done.75), kind=kOutput, calls=%fused_computation.31 | convolution fusion | flops 2422603776 | bytes 18884608 | tf_op jit(solution)/shard_map/dot_general | solution.py:22
  445.5 6.7 reshape.474
  478.8 9.8 %add_convert_fusion.1 = bf16[3072,768]{1,0:T(8,128)(2,1)} fusion(f32[3072,768]{1,0:T(8,128)} %fusion.169, bf16[512,3072]{1,0:T(8,128)(2,1)} %copy-done.132, bf16[512,768]{1,0:T(8,128)(2,1)} %copy-done.55), kind=kOutput, calls=%fused_computation.30 | convolution fusion | flops 2420637696 | bytes 18087936 | tf_op jit(solution)/shard_map/dot_general | solution.py:22
  488.6 6.6 reshape.475
  523.8 6.0 constant_dynamic-update-slice_fusion.1
  546.0 38.5 %psum.30 = f32[]{:T(128)} all-reduce(f32[]{:T(128)} %dynamic-slice_reduce_fusion), channel_id=1, replica_groups=mesh['row'=8,'col'=4] {'row','col'}, use_global_device_ids=true, to_apply=%region_23.24 | all-reduce | flops 1 | bytes 8 | tf_op jit(solution)/shard_map/psum | solution.py:313
  591.8 142.1 %all-reduce.10.cloned.1.call-done = bf16[8,885888]{1,0:T(8,128)(2,1)} async-done(((bf16[8,885888]{1,0:T(8,128)(2,1)}), bf16[8,885888]{1,0:T(8,128)(2,1)}) %all-reduce.10.cloned.1.call-update) | async-done | bytes 14174224
  733.8 8.8 constant_dynamic-slice_fusion
  755.0 122.0 %all-reduce.8.cloned.1.call-done = bf16[1,885888]{1,0:T(2,128)(2,1)} async-done(((bf16[1,885888]{1,0:T(2,128)(2,1)}), bf16[1,885888]{1,0:T(2,128)(2,1)}) %all-reduce.8.cloned.1.call-update) | async-done | bytes 1771792 | tf_op jit(solution)/shard_map/psum | solution.py:345
  877.1 6.5 convert_element_type.346
  888.7 12.3 %slice_reduce_fusion = (f32[294912]{0:T(1024)S(1)}, f32[294912]{0:T(1024)S(1)}) fusion(f32[1,885888]{1,0:T(1,128)S(1)} %convert_element_type.346), kind=kLoop, calls=%fused_computation.162 | loop fusion | bytes 4718592 | tf_op jit(solution)/shard_map/slice | solution.py:350
  (486 shorter events, 233.3 us)
Async XLA Ops:
  7.2 62.3 %copy-start = (bf16[768,768]{1,0:T(8,128)(2,1)S(1)}, bf16[768,768]{1,0:T(8,128)(2,1)}, u32[]{:S(2)}) copy-start(bf16[768,768]{1,0:T(8,128)(2,1)} %param.28) | copy-start | bytes 3538948
  7.2 726.6 %all-reduce.10.cloned.1.call-start = ((), (), s32[]{:S(2)}) async-start(), calls=%async_computation.1 | async-start | bytes 28348416
  8.1 86.1 %copy-start.104 = (f32[4]{0:T(128)}, f32[4]{0:T(128)S(1)}, u32[]{:S(2)}) copy-start(f32[4]{0:T(128)S(1)} %convert_element_type.279) | copy-start | bytes 52
  9.4 84.5 %copy-start.77 = (f32[4,128]{1,0:T(4,128)}, f32[4,128]{1,0:T(4,128)S(1)}, u32[]{:S(2)}) copy-start(f32[4,128]{1,0:T(4,128)S(1)} %get-tuple-element.86) | copy-start | bytes 6148
  50.2 57.9 %copy-start.12 = (bf16[2,512,12,64]{1,0,3,2:T(2,128)(2,1)}, bf16[2,512,12,64]{1,0,3,2:T(2,128)(2,1)S(1)}, u32[]{:S(2)}) copy-start(bf16[2,512,12,64]{1,0,3,2:T(2,128)(2,1)S(1)} %reshape.462) | copy-start | bytes 4718596
  69.5 20.0 %slice-start.2 = ((s8[4718592]{0:T(1024)(128)(4,1)}), s8[4194304]{0:T(1024)(128)(4,1)S(1)}, s32[]{:S(2)}) async-start(s8[4718592]{0:T(1024)(128)(4,1)} %bitcast.271), calls=%async_computation.4 | async-start | bytes 8388608
  70.5 19.0 %copy-start.23 = (f32[512,768]{1,0:T(8,128)}, f32[512,768]{1,0:T(8,128)S(1)}, u32[]{:S(2)}) copy-start(f32[512,768]{1,0:T(8,128)S(1)} %get-tuple-element.91) | copy-start | bytes 4718596
  70.5 19.0 %copy-start.75 = (f32[512]{0:T(512)}, f32[512]{0:T(512)S(1)}, u32[]{:S(2)}) copy-start(f32[512]{0:T(512)S(1)} %broadcast_multiply_fusion.3) | copy-start | bytes 6148
  70.8 18.6 %copy-start.79 = (f32[512]{0:T(512)}, f32[512]{0:T(512)S(1)}, u32[]{:S(2)}) copy-start(f32[512]{0:T(512)S(1)} %multiply_reduce_fusion.13) | copy-start | bytes 6148
  94.4 28.9 %copy-start.112 = (f32[4]{0:T(128)}, f32[4]{0:T(128)S(1)}, u32[]{:S(2)}) copy-start(f32[4]{0:T(128)S(1)} %get-tuple-element.68) | copy-start | bytes 52
  136.4 39.9 %slice-start.4 = ((s8[4718592]{0:T(1024)(128)(4,1)}), s8[4194304]{0:T(1024)(128)(4,1)S(1)}, s32[]{:S(2)}) async-start(s8[4718592]{0:T(1024)(128)(4,1)} %bitcast.273), calls=%async_computation.6 | async-start | bytes 8388608
  138.1 38.1 %copy-start.3 = (f32[1024,768]{1,0:T(8,128)}, f32[1024,768]{1,0:T(8,128)S(1)}, u32[]{:S(2)}) copy-start(f32[1024,768]{1,0:T(8,128)S(1)} %get-tuple-element.98) | copy-start | bytes 9437188
  138.7 37.6 %copy-start.67 = (f32[1024]{0:T(1024)}, f32[1024]{0:T(1024)S(1)}, u32[]{:S(2)}) copy-start(f32[1024]{0:T(1024)S(1)} %multiply_reduce_fusion.7) | copy-start | bytes 12292
  140.8 35.5 %slice-start.5 = ((s8[4718592]{0:T(1024)(128)(4,1)}), s8[524288]{0:T(1024)(128)(4,1)S(1)}, s32[]{:S(2)}) async-start(s8[4718592]{0:T(1024)(128)(4,1)} %bitcast.273), calls=%async_computation.7 | async-start | bytes 1048576
  184.1 20.1 %copy-start.102 = (s32[16]{0:T(128)S(1)}, s32[16]{0:T(128)}, u32[]{:S(2)}) copy-start(s32[16]{0:T(128)} %fusion.122) | copy-start | bytes 196
  184.1 20.1 %copy-start.103 = (pred[16]{0:T(512)(128)(4,1)S(1)}, pred[16]{0:T(512)(128)(4,1)}, u32[]{:S(2)}) copy-start(pred[16]{0:T(512)(128)(4,1)} %fusion.123) | copy-start | bytes 52
  184.1 29.7 %copy-start.131 = (u32[32]{0:T(128)S(1)}, u32[32]{0:T(128)}, u32[]{:S(2)}) copy-start(u32[32]{0:T(128)} %constant.216) | copy-start | bytes 388
  184.1 30.3 %copy-start.90 = (f32[1,4,2,128]{3,2,1,0:T(2,128)S(1)}, f32[1,4,2,128]{3,2,1,0:T(2,128)}, u32[]{:S(2)}) copy-start(f32[1,4,2,128]{3,2,1,0:T(2,128)} %get-tuple-element.80) | copy-start | bytes 12292
  289.2 20.9 %copy-start.57 = (f32[4,768]{1,0:T(4,128)S(1)}, f32[4,768]{1,0:T(4,128)}, u32[]{:S(2)}) copy-start(f32[4,768]{1,0:T(4,128)} %copy-done.56) | copy-start | bytes 36868
  289.2 21.1 %copy-start.113 = (f32[4]{0:T(128)S(1)}, f32[4]{0:T(128)}, u32[]{:S(2)}) copy-start(f32[4]{0:T(128)} %copy-done.112) | copy-start | bytes 52
  289.2 21.1 %copy-start.105 = (f32[4]{0:T(128)S(1)}, f32[4]{0:T(128)}, u32[]{:S(2)}) copy-start(f32[4]{0:T(128)} %copy-done.104) | copy-start | bytes 52
  289.2 21.1 %copy-start.107 = (f32[4]{0:T(128)S(1)}, f32[4]{0:T(128)}, u32[]{:S(2)}) copy-start(f32[4]{0:T(128)} %copy-done.106) | copy-start | bytes 52
  289.2 21.2 %copy-start.78 = (f32[4,128]{1,0:T(4,128)S(1)}, f32[4,128]{1,0:T(4,128)}, u32[]{:S(2)}) copy-start(f32[4,128]{1,0:T(4,128)} %copy-done.77) | copy-start | bytes 6148
  289.2 21.9 %copy-start.8 = (f32[512,768]{1,0:T(8,128)S(1)}, f32[512,768]{1,0:T(8,128)}, u32[]{:S(2)}) copy-start(f32[512,768]{1,0:T(8,128)} %copy-done.7) | copy-start | bytes 4718596
  289.2 21.9 %copy-start.62 = (f32[512]{0:T(512)S(1)}, f32[512]{0:T(512)}, u32[]{:S(2)}) copy-start(f32[512]{0:T(512)} %copy-done.61) | copy-start | bytes 6148
  289.2 21.9 %copy-start.73 = (f32[512]{0:T(512)S(1)}, f32[512]{0:T(512)}, u32[]{:S(2)}) copy-start(f32[512]{0:T(512)} %copy-done.72) | copy-start | bytes 6148
  289.3 21.9 %copy-start.83 = (f32[512]{0:T(512)S(1)}, f32[512]{0:T(512)}, u32[]{:S(2)}) copy-start(f32[512]{0:T(512)} %get-tuple-element.85) | copy-start | bytes 6148
  289.3 23.1 %copy-start.82 = (f32[512]{0:T(512)S(1)}, f32[512]{0:T(512)}, u32[]{:S(2)}) copy-start(f32[512]{0:T(512)} %copy-done.81) | copy-start | bytes 6148
  385.9 21.6 %copy-start.25 = (bf16[2,512,12,64]{1,0,3,2:T(2,128)(2,1)S(1)}, bf16[2,512,12,64]{1,0,3,2:T(2,128)(2,1)}, u32[]{:S(2)}) copy-start(bf16[2,512,12,64]{1,0,3,2:T(2,128)(2,1)} %reshape.461) | copy-start | bytes 4718596
  544.7 40.5 %copy-start.37 = (bf16[4,128,12,64]{1,0,3,2:T(4,128)(2,1)S(1)}, bf16[4,128,12,64]{1,0,3,2:T(4,128)(2,1)}, u32[]{:S(2)}) copy-start(bf16[4,128,12,64]{1,0,3,2:T(4,128)(2,1)} %copy.128) | copy-start | bytes 2359300
  544.7 43.8 %copy-start.49 = (bf16[96,8,2,512]{3,1,2,0:T(8,128)(2,1)S(1)}, bf16[96,8,2,512]{3,1,2,0:T(8,128)(2,1)}, u32[]{:S(2)}) copy-start(bf16[96,8,2,512]{3,1,2,0:T(8,128)(2,1)} %copy-done.48) | copy-start | bytes 4718596
  544.8 332.3 %all-reduce.8.cloned.1.call-start = ((), (), s32[]{:S(2)}) async-start(), calls=%async_computation | async-start | bytes 7087104 | tf_op jit(solution)/shard_map/psum | solution.py:345
  (119 other events, 593.6 us)
Sparse Core Ops, SparseCore 0:
  544.9 188.9 all-reduce.9
  742.8 134.2 all-reduce.7
where the time goes:
time: 925 us; the launch traced here: 919 us
  matrix products  277 us (30%)
  waiting for transfers between devices  264 us (29%)
  local copies, waits for them, and re-layouts  163 us (18%)
  blocking collectives  130 us (14%)
  other arithmetic  64.3 us (7%)
  between operations  19.8 us (2%)
    unnamed x3, waiting for transfers between devices  142 us
    psum x1, waiting for transfers between devices, per_device(): summed = lax.psum(summed.astype(jnp.bfloat16), 'col').astype(jnp.float32)  122 us
    dot_general x13, matrix products, with_trans(): lax.dot_general(left, right, (((1,), (1,)), ((), ())), preferred_element_...  60.4 us
    dot_general x2, matrix products, layer_forward(): jnp.dot(normed_low, w_inner, preferred_element_type=jnp.float32)  54 us
    dot_general x13, matrix products, outer_sum(): lax.dot_general(left, right, (((0,), (0,)), ((), ())), preferred_element_...  52.9 us
    unnamed x324, local copies, waits for them, and re-layouts  51.8 us
    unnamed x3, blocking collectives  50.1 us
    psum x1, blocking collectives, per_device(): lax.psum(jnp.sum(own_losses), ('row', 'col'))  38.5 us
  transfers between devices with their start and end apart: 2, of which 2 were waited for; matrix products, arithmetic and copies ran while one was open for 2% of the time, Pallas kernels for 0%

commit v1 on v0

v1 whole, which is shorter than its diff:
```python
from functools import partial

import jax
import jax.numpy as jnp
from jax import lax
from jax.experimental import pallas as pl
from jax.experimental.pallas import tpu as pltpu
from jax.sharding import PartitionSpec as P

HEADS = 12
EPS_NORM = 1e-12
EPS_POOL = 1e-06
SCALE_LOSS = 128.0
INV_TEMP = 100.0
TILE = 256
SLOTS = 8
VMEM = 60 * 1024 * 1024
LOW = jnp.bfloat16
F32 = jnp.float32


def mm(left, right):
    return lax.dot_general(left, right, (((1,), (0,)), ((), ())), preferred_element_type=F32)


def mm_nt(left, right):
    return lax.dot_general(left, right, (((1,), (1,)), ((), ())), preferred_element_type=F32)


def norm_parts(hidden):
    center = hidden - jnp.mean(hidden, -1, keepdims=True)
    spread = jnp.mean(center * center, -1, keepdims=True)
    scale = lax.rsqrt(spread + EPS_NORM)
    return center * scale, scale


def gelu_parts(u):
    square = u * u
    q = 1.4250060785476853e-06
    for factor in (-3.669345091379551e-05, -8.782652731110375e-05, 0.03639228618131223, 0.7978697123041883):
        q = q * square + factor
    share = 0.5 + 0.5 * jnp.tanh(u * q)
    bell = jnp.exp(-0.5 * square)
    return u * share, share + (0.3989422804014327 * u) * bell


def vec(ref, cols=slice(None)):
    return ref[cols].reshape(1, -1)


def rows_of(step, size):
    return pl.ds(pl.multiple_of(step * size, size), size)


def part_owner(part, q_dev, q_len, p_len, qlen_ref, plen_ref):
    per = p_len // q_len
    beyond = jnp.maximum(part - q_dev, 0)
    is_query = part < q_dev
    slot = jnp.where(is_query, part, q_dev + beyond // per)
    length = jnp.where(is_query, qlen_ref[jnp.where(is_query, part, 0)], plen_ref[beyond // per])
    first = jnp.where(is_query, 0, beyond % per * q_len)
    return slot, length, first


def live_rows(first, length, size):
    return (first + lax.broadcasted_iota(jnp.int32, (size, 1), 0)) < length


def sure_rows(size):
    return size * 4 // 5 // 16 * 16


def half_only(pair_t, which):
    half = pair_t.shape[0] // 2
    zeros = jnp.zeros((half, pair_t.shape[1]), pair_t.dtype)
    if which == 0:
        return jnp.concatenate([pair_t[:half], zeros], 0)
    return jnp.concatenate([zeros, pair_t[half:]], 0)


def staged(count, *stages):
    for step in range(count + len(stages) - 1):
        for late, stage in enumerate(stages):
            if 0 <= step - late < count:
                stage(step - late)


def fetch(source, target, sems, index):
    return pltpu.make_async_copy(source, target, sems.at[index])


def attend_kernel(
    dims, qlen_ref, plen_ref, xq_ref, xp_ref, wq_ref, wk_ref, wv_ref, bq_ref, bv_ref,
    q_ref, k_ref, v_ref, ctx_t_ref, lse_ref,
):
    q_dev, q_len, rows_all, width = dims
    block = pl.program_id(0)
    head_dim = width // HEADS
    x = jnp.where(block == 0, xq_ref[...], xp_ref[...])
    q = ((mm(x, wq_ref[...]) + vec(bq_ref)) * head_dim**-0.5).astype(LOW)
    k = mm(x, wk_ref[...]).astype(LOW)
    v = (mm(x, wv_ref[...]) + vec(bv_ref)).astype(LOW)
    q_ref[...] = q
    k_ref[...] = k
    v_ref[...] = v
    q_t, v_t = q.T, v.T

    def attend(size, starts, lengths):
        items = [(start, length, head) for head in range(HEADS) for start, length in zip(starts, lengths)]
        scores, weights = {}, {}

        def compare(i):
            start, length, head = items[i]
            cols = slice(head // 2 * 2 * head_dim, (head // 2 + 1) * 2 * head_dim)
            here = slice(start, start + size)
            scores[i] = mm(k[here, cols], half_only(q_t[cols, here], head % 2))

        def weigh(i):
            start, length, head = items[i]
            edge = sure_rows(size)
            early, late = scores[i][:edge], scores.pop(i)[edge:]
            late = jnp.where(live_rows(edge, length, size - edge), late, -1e30)
            top = jnp.maximum(jnp.max(early, 0, keepdims=True), jnp.max(late, 0, keepdims=True))
            weights[i] = top, jnp.concatenate([jnp.exp(early - top).astype(LOW), jnp.exp(late - top).astype(LOW)], 0)

        def combine(i):
            start, length, head = items[i]
            here, rows = slice(start, start + size), slice(head * head_dim, (head + 1) * head_dim)
            top, weight = weights.pop(i)
            values = jnp.concatenate([v_t[rows, here], jnp.ones((16, size), LOW)], 0)
            result = mm(values, weight)
            total = result[head_dim : head_dim + 1]
            lse_ref[0, head // 2, head % 2 : head % 2 + 1, here] = top + jnp.log(total)
            ctx_t_ref[rows, here] = (result[:head_dim] * (1.0 / total)).astype(LOW)

        staged(len(items), compare, weigh, combine)

    @pl.when(block == 0)
    def _():
        attend(q_len, [s * q_len for s in range(q_dev)], [qlen_ref[s] for s in range(q_dev)])

    @pl.when(block > 0)
    def _():
        attend(rows_all, [0], [plen_ref[jnp.maximum(block - 1, 0)]])


def dense_kernel(
    dims, qlen_ref, plen_ref, pos_ref, xq_ref, xp_ref, ctx_t_ref, wo_hbm, wi_hbm, wf_hbm,
    bo_ref, bi_ref, bf_ref, g1_ref, s1_ref, g2_ref, s2_ref,
    h1_ref, y1_ref, act_ref, dg_ref, h2_ref, yq_ref, yp_ref, pool_ref, pay_ref,
    wo_ref, wi_ref, wf_ref, sems,
):
    q_dev, q_len, p_len, width, inner = dims
    block = pl.program_id(0)
    rows_all = xq_ref.shape[0]
    query_blocks = q_dev * q_len // rows_all
    copies = [
        fetch(source, target, sems, index)
        for index, (source, target) in enumerate([(wo_hbm, wo_ref), (wi_hbm, wi_ref), (wf_hbm, wf_ref)])
    ]

    @pl.when(block == 0)
    def _():
        for copy in copies:
            copy.start()
        pool_ref[...] = jnp.zeros_like(pool_ref)
        copies[0].wait()

    x = jnp.where(block < query_blocks, xq_ref[...], xp_ref[...])
    hidden = x.astype(F32) + (mm(ctx_t_ref[...].T, wo_ref[...]) + vec(bo_ref))
    h1_ref[...] = hidden.astype(LOW)
    y1 = norm_parts(hidden)[0] * vec(g1_ref) + vec(s1_ref)
    y1_low = y1.astype(LOW)
    y1_ref[...] = y1_low

    @pl.when(block == 0)
    def _():
        copies[1].wait()
        copies[2].wait()

    group = width // TILE
    raw, made = {}, {}
    sums = [y1[:, n * TILE : (n + 1) * TILE] + vec(bf_ref, slice(n * TILE, (n + 1) * TILE)) for n in range(group)]

    def expand(i):
        cols = slice(i * TILE, (i + 1) * TILE)
        raw[i] = mm(y1_low, wi_ref[:, cols]) + vec(bi_ref, cols)

    def activate(i):
        cols = slice(i * TILE, (i + 1) * TILE)
        act, slope = gelu_parts(raw.pop(i))
        made[i] = act.astype(LOW)
        act_ref[:, cols] = made[i]
        dg_ref[:, cols] = slope.astype(LOW)

    def contract(i):
        first, n = i // group * group, i % group
        left = jnp.concatenate([made[first + j] for j in range(group)], 1)
        cols = slice(n * TILE, (n + 1) * TILE)
        sums[n] = sums[n] + mm(left, wf_ref[first * TILE : (first + group) * TILE, cols])

    late = [lambda i: None] * (group - 1)
    staged(inner // TILE, expand, activate, *late, contract)

    total = jnp.concatenate(sums, 1)
    h2_ref[...] = total.astype(LOW)
    y2 = norm_parts(total)[0] * vec(g2_ref) + vec(s2_ref)
    for part in range(rows_all // q_len):
        number = block * (rows_all // q_len) + part
        slot, length, first = part_owner(number, q_dev, q_len, p_len, qlen_ref, plen_ref)
        piece = y2[part * q_len : (part + 1) * q_len]
        summed = jnp.sum(jnp.where(live_rows(first, length, q_len), piece, 0.0), 0, keepdims=True)
        in_slot = lax.broadcasted_iota(jnp.int32, (SLOTS, 1), 0) == slot
        pool_ref[...] += jnp.where(in_slot, summed / length.astype(F32), 0.0)

    @pl.when(block < query_blocks)
    def _():
        yq_ref[...] = y2.astype(LOW)

    @pl.when(block >= query_blocks)
    def _():
        yp_ref[...] = y2.astype(LOW)

    @pl.when(block == pl.num_programs(0) - 1)
    def _():
        pooled = pool_ref[...]
        emb = pooled * lax.rsqrt(jnp.sum(pooled * pooled, -1, keepdims=True) + EPS_POOL)
        pay_ref[:, :width] = emb.astype(LOW)
        row = lax.broadcasted_iota(jnp.int32, (SLOTS, 128), 0)
        col = lax.broadcasted_iota(jnp.int32, (SLOTS, 128), 1)
        place = jnp.zeros((SLOTS, 128), jnp.int32)
        for j in range(q_dev):
            high = pos_ref[j] // 128
            low = pos_ref[j] - high * 128
            place = jnp.where(row == j, jnp.where(col == 0, high, jnp.where(col == 1, low, 0)), place)
        pay_ref[:, width:] = place.astype(F32).astype(LOW)


def loss_kernel(
    dims, me_ref, qlen_ref, plen_ref, own_ref, all_ref, pool_ref, loss_ref, gvec_ref
):
    q_dev, p_dev, width, col_count = dims
    count = all_ref.shape[0]
    every = all_ref[:, :width]
    own = own_ref[:, :width]

    def passage_mask(index):
        spot, place = index % SLOTS, index // SLOTS
        per_core = count // SLOTS // 2
        core, rest = place // per_core, place % per_core
        device = (rest // col_count * 2 + core) * col_count + rest % col_count
        return (spot >= q_dev) & (spot < q_dev + p_dev), device * p_dev + spot - q_dev

    scores = mm_nt(own, every) * INV_TEMP
    valid, ident = passage_mask(lax.broadcasted_iota(jnp.int32, (SLOTS, count), 1))
    scores = jnp.where(valid, scores, -1e30)
    top = jnp.max(scores, -1, keepdims=True)
    totals = top + jnp.log(jnp.sum(jnp.exp(scores - top), -1, keepdims=True))
    marks = own_ref[:, width:].astype(F32)
    wanted = marks[:, 0:1] * 128.0 + marks[:, 1:2]
    target = (valid & (ident.astype(F32) == wanted)).astype(F32)
    raw = (INV_TEMP * (SCALE_LOSS * (jnp.exp(scores - totals) - target))).astype(LOW)
    grad_q = mm(raw, every)

    picker_col = lax.broadcasted_iota(jnp.int32, (SLOTS, 128), 1)
    picker = jnp.where(picker_col == 0, 128.0, jnp.where(picker_col == 1, 1.0, 0.0)).astype(LOW)
    own_row = lax.broadcasted_iota(jnp.int32, (SLOTS, TILE), 0)
    own_valid = (own_row >= q_dev) & (own_row < q_dev + p_dev)
    own_ident = (me_ref[0] * p_dev + own_row - q_dev).astype(F32)

    def body(step, carry):
        total_loss, grad_p = carry
        rows = rows_of(step, TILE)
        some = all_ref[rows, :width]
        place = mm_nt(picker, all_ref[rows, width:])[0:1]
        table = mm_nt(every, some) * INV_TEMP
        ok, names = passage_mask(lax.broadcasted_iota(jnp.int32, (count, TILE), 0))
        picked = jnp.sum(jnp.where(ok & (names.astype(F32) == place), table, 0.0), 0, keepdims=True)
        table = jnp.where(ok, table, -1e30)
        high = jnp.max(table, 0, keepdims=True)
        lse = high + jnp.log(jnp.sum(jnp.exp(table - high), 0, keepdims=True))
        is_query = lax.broadcasted_iota(jnp.int32, (1, TILE), 1) % SLOTS < q_dev
        losses = jnp.where(is_query, lse - picked, 0.0)
        mine = mm_nt(own, some) * INV_TEMP
        hit = (own_ident == place).astype(F32)
        grads = INV_TEMP * (SCALE_LOSS * (jnp.exp(mine - lse) - hit))
        grads = jnp.where(own_valid & is_query, grads, 0.0).astype(LOW)
        return total_loss + jnp.sum(losses, 1, keepdims=True), grad_p + mm(grads, some)

    start = (jnp.zeros((1, 1), F32), jnp.zeros((SLOTS, width), F32))
    total_loss, grad_p = lax.fori_loop(0, count // TILE, body, start)
    loss_ref[...] = jnp.broadcast_to(total_loss / float(count // SLOTS * q_dev), loss_ref.shape)

    slot = lax.broadcasted_iota(jnp.int32, (SLOTS, 1), 0)
    grad = jnp.where(slot < q_dev, grad_q, grad_p)
    pooled = pool_ref[...]
    r = lax.rsqrt(jnp.sum(pooled * pooled, -1, keepdims=True) + EPS_POOL)
    inside = jnp.sum(pooled * grad, -1, keepdims=True)
    length = jnp.ones((SLOTS, 1), F32)
    for j in range(q_dev):
        length = jnp.where(slot == j, qlen_ref[j].astype(F32), length)
    for j in range(p_dev):
        length = jnp.where(slot == q_dev + j, plen_ref[j].astype(F32), length)
    gvec_ref[...] = (r * grad - r * r * r * inside * pooled) / length


def norm_two_kernel(dims, qlen_ref, plen_ref, gvec_ref, h2_ref, g2_ref, gf_ref, gf_t_ref, stat_ref):
    q_dev, q_len, rows_all, width = dims
    block = pl.program_id(0)

    @pl.when(block == 0)
    def _():
        stat_ref[...] = jnp.zeros_like(stat_ref)

    def body(part, carry):
        rows = rows_of(part, q_len)
        number = block * (rows_all // q_len) + part
        slot, length, first = part_owner(number, q_dev, q_len, rows_all, qlen_ref, plen_ref)
        in_slot = lax.broadcasted_iota(jnp.int32, (SLOTS, 1), 0) == slot
        grad_y = jnp.sum(jnp.where(in_slot, gvec_ref[...], 0.0), 0, keepdims=True)
        live = live_rows(first, length, q_len)
        n2, r2 = norm_parts(h2_ref[rows, :].astype(F32))
        g = grad_y * vec(g2_ref)
        grad = r2 * (g - jnp.mean(g, -1, keepdims=True) - n2 * jnp.mean(g * n2, -1, keepdims=True))
        grad = jnp.where(live, grad, 0.0)
        low = grad.astype(LOW)
        gf_ref[rows, :] = low
        gf_t_ref[:, rows] = low.T
        stat_ref[0:1, :] += grad_y * jnp.sum(jnp.where(live, n2, 0.0), 0, keepdims=True)
        stat_ref[1:2, :] += grad_y * jnp.sum(live.astype(F32), 0, keepdims=True)
        stat_ref[2:3, :] += jnp.sum(low.astype(F32), 0, keepdims=True)
        return carry

    lax.fori_loop(0, rows_all // q_len, body, 0)


def dense_back_kernel(
    dims, gf_ref, dg_ref, h1_ref, wf_hbm, wi_hbm, wo_hbm, g1_ref,
    gu_ref, gh1_ref, ga_ref, gc_ref, stat_ref, bi_ref,
    wf_ref, wi_ref, wo_ref, sems,
):
    rows_all, width, inner = dims
    block = pl.program_id(0)
    chunk = TILE
    group = width // chunk
    copies = [
        fetch(wf_hbm.at[pl.ds(0, width), :], wf_ref.at[pl.ds(0, width), :], sems, 0),
        fetch(wi_hbm.at[:, pl.ds(0, width)], wi_ref.at[:, pl.ds(0, width)], sems, 1),
        fetch(wf_hbm.at[pl.ds(width, inner - width), :], wf_ref.at[pl.ds(width, inner - width), :], sems, 2),
        fetch(wi_hbm.at[:, pl.ds(width, inner - width)], wi_ref.at[:, pl.ds(width, inner - width)], sems, 3),
        fetch(wo_hbm, wo_ref, sems, 4),
    ]

    @pl.when(block == 0)
    def _():
        for copy in copies:
            copy.start()
        stat_ref[...] = jnp.zeros_like(stat_ref)
        bi_ref[...] = jnp.zeros_like(bi_ref)
        copies[0].wait()
        copies[1].wait()

    gf = gf_ref[...]
    raw, made = {}, {}
    sums = [gf[:, n * chunk : (n + 1) * chunk].astype(F32) for n in range(group)]
    biases = []

    def spread(i):
        raw[i] = mm_nt(gf, wf_ref[i * chunk : (i + 1) * chunk, :])

    def slope(i):
        cols = slice(i * chunk, (i + 1) * chunk)
        made[i] = (raw.pop(i) * dg_ref[:, cols].astype(F32)).astype(LOW)
        gu_ref[:, cols] = made[i]
        biases.append(jnp.sum(made[i].astype(F32), 0, keepdims=True))

    def gather(i):
        first, n = i // group * group, i % group
        left = jnp.concatenate([made[first + j] for j in range(group)], 1)
        cols = slice(n * chunk, (n + 1) * chunk)
        sums[n] = sums[n] + mm_nt(left, wi_ref[cols, first * chunk : (first + group) * chunk])

    staged(group, spread, slope)

    @pl.when(block == 0)
    def _():
        for copy in copies[2:]:
            copy.wait()

    count = inner // chunk
    staged(
        count,
        lambda i: spread(i + group) if i + group < count else None,
        lambda i: slope(i + group) if i + group < count else None,
        gather,
    )
    bi_ref[0:1, :] += jnp.concatenate(biases, 1)
    total = jnp.concatenate(sums, 1)
    n1, r1 = norm_parts(h1_ref[...].astype(F32))
    stat_ref[0:1, :] += jnp.sum(total * n1, 0, keepdims=True)
    stat_ref[1:2, :] += jnp.sum(total, 0, keepdims=True)
    g = total * vec(g1_ref)
    grad = r1 * (g - jnp.mean(g, -1, keepdims=True) - n1 * jnp.mean(g * n1, -1, keepdims=True))
    gh1_ref[...] = grad
    low = grad.astype(LOW)
    ga_ref[...] = low
    stat_ref[2:3, :] += jnp.sum(low.astype(F32), 0, keepdims=True)
    gc_ref[...] = mm_nt(low, wo_ref[...]).astype(LOW)


def attend_back_kernel(
    dims, qlen_ref, plen_ref, q_ref, k_ref, v_ref, ctx_t_ref, lse_ref, gc_ref, out_ref, stat_ref
):
    q_dev, q_len, rows_all, head_dim = dims
    block = pl.program_id(0)
    pair_dim = 2 * head_dim
    width = q_ref.shape[1]
    pairs = width // pair_dim

    @pl.when(block == 0)
    def _():
        stat_ref[...] = jnp.zeros_like(stat_ref)

    def attend(size, starts, lengths):
        lane = lax.broadcasted_iota(jnp.int32, (size, pair_dim), 1)
        items = [(s, p, which) for s in range(len(starts)) for p in range(pairs) for which in range(2)]
        held, raw, made = {}, {}, {}

        def pair_of(s, p):
            if (s, p) not in held:
                here, cols = slice(starts[s], starts[s] + size), slice(p * pair_dim, (p + 1) * pair_dim)
                q, k, v, gc = q_ref[here, cols], k_ref[here, cols], v_ref[here, cols], gc_ref[here, cols]
                held[s, p] = here, cols, q, k, v, gc, q.T, k.T, gc.T
            return held[s, p]

        def compare(i):
            s, p, which = items[i]
            here, cols, q, k, v, gc, q_t, k_t, gc_t = pair_of(s, p)
            raw[i] = mm(k, half_only(q_t, which)), mm(v, half_only(gc_t, which))

        def weigh(i):
            s, p, which = items[i]
            here, cols, q, k, v, gc, q_t, k_t, gc_t = pair_of(s, p)
            head = slice((p * 2 + which) * head_dim, (p * 2 + which + 1) * head_dim)
            scores, grad_p = raw.pop(i)
            lse = lse_ref[0, p, which : which + 1, here]
            edge = sure_rows(size)
            late = jnp.where(live_rows(edge, lengths[s], size - edge), scores[edge:], -1e30)
            probs = jnp.concatenate([jnp.exp(scores[:edge] - lse), jnp.exp(late - lse)], 0)
            half = slice(which * head_dim, (which + 1) * head_dim)
            delta = jnp.sum(gc_t[half].astype(F32) * ctx_t_ref[head, here].astype(F32), 0, keepdims=True)
            made[i] = probs.astype(LOW), (probs * (grad_p - delta)).astype(LOW)

        def combine(i):
            s, p, which = items[i]
            here, cols, q, k, v, gc, q_t, k_t, gc_t = pair_of(s, p)
            mine = (lane >= head_dim) if which else (lane < head_dim)
            zero = jnp.zeros_like(q)
            probs, grad_s = made.pop(i)
            add_v = mm(probs, jnp.where(mine, gc, zero))
            add_k = mm(grad_s, jnp.where(mine, q, zero))
            add_q = mm(k_t[which * head_dim : (which + 1) * head_dim], grad_s)
            if which == 0:
                made[s, p] = add_v, add_k, add_q
                return
            old_v, old_k, old_q = made.pop((s, p))
            grad_q = (jnp.concatenate([old_q, add_q], 0).T * head_dim**-0.5).astype(LOW)
            grad_v = (old_v + add_v).astype(LOW)
            out_ref[here, cols] = grad_q
            out_ref[here, width + cols.start : width + cols.stop] = (old_k + add_k).astype(LOW)
            out_ref[here, 2 * width + cols.start : 2 * width + cols.stop] = grad_v
            stat_ref[0:1, cols] += jnp.sum(grad_q.astype(F32), 0, keepdims=True)
            stat_ref[1:2, cols] += jnp.sum(grad_v.astype(F32), 0, keepdims=True)

        staged(len(items), compare, weigh, combine)

    @pl.when(block == 0)
    def _():
        attend(q_len, [s * q_len for s in range(q_dev)], [qlen_ref[s] for s in range(q_dev)])

    @pl.when(block > 0)
    def _():
        attend(rows_all, [0], [plen_ref[jnp.maximum(block - 1, 0)]])


def input_grad_kernel(groups, *refs):
    grads, (gh1_ref, wq_ref, wk_ref, wv_ref, gq_ref, gp_ref) = refs[: len(groups)], refs[len(groups) :]
    block = pl.program_id(0)
    total = gh1_ref[...]
    for grad_ref, (start, wide) in zip(grads, groups):
        for number, w_ref in enumerate((wq_ref, wk_ref, wv_ref)):
            total = total + mm_nt(grad_ref[:, number * wide : (number + 1) * wide], w_ref[:, start : start + wide])
    low = total.astype(LOW)

    @pl.when(block == 0)
    def _():
        gq_ref[...] = low

    @pl.when(block > 0)
    def _():
        gp_ref[...] = low


def weight_grad_kernel(shards, by_row, tile, core_ref, left_ref, right_ref, *refs):
    *extra, send_ref, keep_ref = refs
    high, wide = left_ref.shape[0], right_ref.shape[1]
    result = [
        [
            mm(left_ref[row : row + tile[0], :], right_ref[:, col : col + tile[1]]).astype(LOW)
            for col in range(0, wide, tile[1])
        ]
        for row in range(0, high, tile[0])
    ]
    result = jnp.concatenate([jnp.concatenate(items, 1) for items in result], 0)
    count = shards if by_row else send_ref.shape[0] * 2
    size = result.shape[0 if by_row else 1] // count
    tail = [None] * count
    if extra:
        tail = small_rows(extra, count, result.shape[1])

    def store(even, odd):
        for shard in range(count):
            spot = slice(shard * size, (shard + 1) * size)
            piece = result[spot, :] if by_row else result[:, spot]
            target = odd if shard % 2 else even
            if tail[shard] is None:
                target[shard // 2] = piece
            else:
                target[shard // 2, :size] = piece
                target[shard // 2, size:] = tail[shard]

    @pl.when(core_ref[0] == 0)
    def _():
        store(keep_ref, send_ref)

    @pl.when(core_ref[0] == 1)
    def _():
        store(send_ref, keep_ref)


def small_rows(refs, count, wide):
    two, one, inner, *attn = [ref[...] for ref in refs]
    eight = jnp.concatenate(
        [jnp.concatenate([item[0:2] for item in attn], 1), one[2:3], two[2:3], one[0:2], two[0:2]], 0
    )
    inner = inner[0:1]
    short, long = eight.shape[1] // count, inner.shape[1] // count
    rows = []
    for shard in range(count):
        top = eight[:, shard * short : (shard + 1) * short]
        low = inner[:, shard * long : (shard + 1) * long]
        top = jnp.concatenate([top, jnp.zeros((8, wide - short), F32)], 1)
        low = jnp.concatenate([low, jnp.zeros((1, wide - long), F32)], 1)
        rows.append(jnp.concatenate([top, low, jnp.zeros((7, wide), F32)], 0).astype(LOW))
    return rows


def turn_kernel(part_ref, out_ref):
    out_ref[...] = part_ref[...].astype(F32).T


def turn_low_kernel(*refs):
    *inputs, out_ref = refs
    if len(inputs) == 1:
        out_ref[...] = inputs[0][...].T
        return

    @pl.when(pl.program_id(0) == 0)
    def _():
        out_ref[...] = inputs[0][...].T

    @pl.when(pl.program_id(0) > 0)
    def _():
        out_ref[...] = inputs[1][...].T


def const_spec(shape):
    return pl.BlockSpec(shape, lambda i: (0,) * len(shape), pipeline_mode=pl.Buffered(1))


def call(body, operands, in_specs, outs, grid, room, deps=(), old=(), name=None, scratch=(), us=10):
    count, extra = len(operands), len(old)
    if deps:
        tied = min(range(count), key=lambda i: operands[i].size)
        operands = list(operands)
        operands[tied] = lax.optimization_barrier((operands[tied], *deps))[0]

    def kernel(*refs):
        body(*refs[:count], *refs[count + extra :])

    return pl.pallas_call(
        kernel,
        grid=grid,
        in_specs=list(in_specs) + [pl.BlockSpec(memory_space=pl.ANY)] * extra,
        out_specs=[spec for spec, _ in outs],
        out_shape=[kind for _, kind in outs],
        scratch_shapes=scratch,
        input_output_aliases={count + i: i for i in range(extra)},
        compiler_params=pltpu.CompilerParams(vmem_limit_bytes=room * 1024 * 1024),
        cost_estimate=pl.CostEstimate(flops=int(us * 1.15e7), bytes_accessed=0, transcendentals=0),
        name=name,
    )(*operands, *old)


def weight_grad(left_t, right, by_row, row_count, core, deps=(), extra=(), old=(), room=None, tile=(256, 256)):
    height, depth = left_t.shape
    wide = right.shape[1]
    cut = (height if by_row else wide) // row_count
    block = 768
    per_block = row_count if by_row else block // cut if block % cut == 0 else 0
    if wide % block or cut % (16 if by_row else 128) or per_block % 2:
        whole = jnp.dot(left_t, right, preferred_element_type=F32).astype(LOW)
        if by_row:
            whole = whole.reshape(row_count // 2, 2, cut, wide)
        else:
            whole = whole.reshape(height, row_count // 2, 2, cut).transpose(1, 2, 0, 3)
        if extra:

            def rows_kernel(*refs):
                for shard, item in enumerate(small_rows(refs[:-1], row_count, wide)):
                    refs[-1][shard] = item

            rows = pl.pallas_call(
                rows_kernel,
                out_shape=jax.ShapeDtypeStruct((row_count, 16, wide), LOW),
                compiler_params=pltpu.CompilerParams(vmem_limit_bytes=VMEM),
            )(*extra)
            whole = jnp.concatenate([whole, rows.reshape(row_count // 2, 2, 16, wide)], 2)
        result = [lax.dynamic_index_in_dim(whole, side, 1, keepdims=False) for side in (1 - core, core)]
        return [jnp.concatenate([a, b], 2) for a, b in zip(old, result)] if old else result
    if by_row:
        rows = cut + (16 if extra else 0)
        shape = (row_count // 2, rows, room or wide)
        after = (room - wide) // block if old else 0
        spec = pl.BlockSpec((row_count // 2, rows, block), lambda i: (0, 0, i + after))
    else:
        shape = (row_count // 2, height, cut)
        spec = pl.BlockSpec((per_block // 2, height, cut), lambda i: (i, 0, 0))
    return call(
        partial(weight_grad_kernel, row_count, by_row, tile),
        (core.reshape(1), left_t, right, *extra),
        [
            pl.BlockSpec(memory_space=pltpu.SMEM),
            const_spec((height, depth)),
            pl.BlockSpec((depth, block), lambda i: (0, i)),
        ]
        + [const_spec(item.shape) for item in extra],
        [(spec, jax.ShapeDtypeStruct(shape, LOW))] * 2,
        (wide // block,),
        56,
        deps,
        old,
        name="weight_grad",
        us=height * depth * wide * 3.3e-9,
    )


class Flow:
    def __init__(self, sent, kept, line=False):
        bits = lax.axis_size("row").bit_length() - 1
        self.order = [(0,)] + [tuple(range(i, min(i + 2, bits))) for i in range(1, bits, 2)]
        self.left = list(range(bits - 1, 0, -1))
        count = lax.axis_size("col")
        self.line = [(None, [(i, i ^ (1 << bit)) for i in range(count)]) for bit in range(count.bit_length() - 1)]
        if line:
            half = count // 2
            self.line = [(None, [(i, i + 1), (count - 1 - i, count - 2 - i)]) for i in range(half - 1)]
            self.line += [(None, [(half - 1, half), (half, half - 1)])]
            self.line += [
                ((i, count - 1 - i), [(i + 1, i), (count - 2 - i, count - 1 - i)])
                for i in range(half - 2, -1, -1)
            ]
        self.sent, self.kept, self.got = [sent], kept, None

    def shard(self, terms, bits, mask):
        here = lax.axis_index("row")
        order = [self.left.index(bit) for bit in bits]
        total = None
        for term in terms:
            starts, sizes = [0] * term.ndim, list(term.shape)
            for axis, bit in zip(order, bits):
                starts[axis], sizes[axis] = ((here ^ mask) >> bit) & 1, 1
            piece = lax.dynamic_slice(term, starts, sizes)
            piece = piece.reshape([size for i, size in enumerate(sizes) if i not in order]).astype(F32)
            total = piece if total is None else total + piece
        return total.astype(LOW)

    def step(self):
        if self.order:
            bits = self.order[0]
            masks = [
                sum(1 << bit for i, bit in enumerate(bits) if other >> i & 1)
                for other in range(1, 1 << len(bits))
            ]
            if bits != (0,):
                terms = [self.kept, *self.got]
                self.sent = [self.shard(terms, bits, mask) for mask in masks]
                self.kept = self.shard(terms, bits, 0)
                self.left = [bit for bit in self.left if bit not in bits]
            size = lax.axis_size("row")
            self.got = [
                lax.ppermute(sent, "row", [(i, i ^ mask) for i in range(size)])
                for sent, mask in zip(self.sent, masks)
            ]
        else:
            self.sent = [self.kept]
            self.got = [lax.ppermute(self.kept, "col", self.line[0][1])]

    def land(self, token=None):
        if token is not None:
            self.kept = lax.optimization_barrier((self.kept, token))[0]
        got = self.got
        if self.order:
            bits = self.order.pop(0)
            if bits == (0,):
                dims = (2,) * len(self.left) + self.kept.shape[1:]
                self.kept, self.got = self.kept.reshape(dims), [item.reshape(dims) for item in self.got]
            if not self.order:
                self.kept = sum([item.astype(F32) for item in self.got], self.kept.astype(F32)).astype(LOW)
        else:
            ends, _ = self.line.pop(0)
            if ends is None:
                self.kept = self.kept + self.got[0]
            else:
                here = lax.axis_index("col")
                self.kept = jnp.where((here == ends[0]) | (here == ends[1]), self.got[0], self.kept)
        return got

    def turn(self, token=None):
        got = self.land(token)
        if self.done:
            return got
        self.step()
        return got + self.sent

    @property
    def done(self):
        return not self.order and not self.line


def gather_all(piece):
    row_bits = lax.axis_size("row").bit_length() - 1
    col_bits = lax.axis_size("col").bit_length() - 1
    steps = [("col", tuple(range(i, min(i + 2, col_bits)))) for i in range(0, col_bits, 2)]
    steps += [("row", tuple(range(i, min(i + 2, row_bits)))) for i in range(1, row_bits, 2)]
    for name, bits in steps + [("row", (0,))]:
        here = lax.axis_index(name)
        pieces = [piece]
        for other in range(1, 1 << len(bits)):
            mask = sum(1 << bit for i, bit in enumerate(bits) if other >> i & 1)
            pairs = [(i, i ^ mask) for i in range(lax.axis_size(name))]
            pieces.append(lax.ppermute(piece, name, pairs))
        for i, bit in enumerate(bits):
            high = ((here >> bit) & 1) == 1
            pieces = [
                jnp.where(high, pieces[place ^ (1 << i)], pieces[place]) for place in range(len(pieces))
            ]
        piece = jnp.concatenate(pieces, 0)
    return piece


def per_device(
    query_tokens, passage_tokens, query_lengths, passage_lengths, positives,
    w_query, w_key, w_value, w_attn_out, w_inner, w_outer,
    bias_query, bias_value, bias_attn_out, bias_inner, bias_outer,
    gain_one, shift_one, gain_two, shift_two,
):
    q_dev, q_len, width = query_tokens.shape
    p_dev, p_len, _ = passage_tokens.shape
    inner = w_inner.shape[1]
    rows_all = p_len
    assert q_dev * q_len == rows_all and q_dev + p_dev <= SLOTS
    blocks = 1 + p_dev
    total_rows = blocks * rows_all
    row_count = lax.axis_size("row")
    col_count = lax.axis_size("col")
    row_here = lax.axis_index("row")
    core = row_here & 1
    me = (row_here * col_count + lax.axis_index("col")).reshape(1)
    params = pltpu.CompilerParams(vmem_limit_bytes=VMEM)
    smem = pl.BlockSpec(memory_space=pltpu.SMEM)

    def line(item):
        return item

    def by_block(wide):
        return pl.BlockSpec((rows_all, wide), lambda i: (i, 0))

    def by_block_t(high):
        return pl.BlockSpec((high, rows_all), lambda i: (0, i))

    def fixed(shape):
        return pl.BlockSpec(shape, lambda i: (0,) * len(shape))

    queries_spec = pl.BlockSpec((rows_all, width), lambda i: (0, 0))
    passages_spec = pl.BlockSpec((rows_all, width), lambda i: (jnp.maximum(i - 1, 0), 0))

    lse_spec = pl.BlockSpec((1, HEADS // 2, 8, rows_all), lambda i: (i, 0, 0, 0))

    def shape(*dims, kind=LOW):
        return jax.ShapeDtypeStruct(dims, kind)

    queries = query_tokens.reshape(rows_all, width)
    passages = passage_tokens.reshape(p_dev * rows_all, width)
    square = const_spec((width, width))
    anywhere = pl.BlockSpec(memory_space=pl.ANY)
    thin = const_spec((width,))

    q, k, v, ctx_t, lse = call(
        partial(attend_kernel, (q_dev, q_len, rows_all, width)),
        (query_lengths, passage_lengths, queries, passages, w_query, w_key, w_value, bias_query, bias_value),
        [smem, smem, queries_spec, passages_spec, square, square, square, thin, thin],
        [(by_block(width), shape(total_rows, width))] * 3
        + [
            (by_block_t(width), shape(width, total_rows)),
            (lse_spec, shape(blocks, HEADS // 2, 8, rows_all, kind=F32)),
        ],
        (blocks,),
        56,
        name="attend",
        us=25,
    )

    rows_part = rows_all
    parts = blocks

    def by_part(wide):
        return pl.BlockSpec((rows_part, wide), lambda i: (i, 0))

    queries_part = pl.BlockSpec((rows_part, width), lambda i: (0, 0))
    passages_part = pl.BlockSpec((rows_part, width), lambda i: (jnp.maximum(i - 1, 0), 0))
    h1, y1, act, slope, h2, query_out, passage_out, pooled, payload = call(
        partial(dense_kernel, (q_dev, q_len, p_len, width, inner)),
        (
            query_lengths, passage_lengths, positives, queries, passages, ctx_t, w_attn_out, w_inner, w_outer,
            bias_attn_out, bias_inner, bias_outer, gain_one, shift_one, gain_two, shift_two,
        ),
        [smem, smem, smem, queries_part, passages_part, pl.BlockSpec((width, rows_part), lambda i: (0, i))]
        + [anywhere] * 3
        + [thin, const_spec((inner,))]
        + [thin] * 5,
        [
            (by_part(width), shape(total_rows, width)),
            (by_part(width), shape(total_rows, width)),
            (by_part(inner), shape(total_rows, inner)),
            (by_part(inner), shape(total_rows, inner)),
            (by_part(width), shape(total_rows, width)),
            (queries_part, shape(rows_all, width)),
            (passages_part, shape(p_dev * rows_all, width)),
            (fixed((SLOTS, width)), shape(SLOTS, width, kind=F32)),
            (fixed((SLOTS, width + 128)), shape(SLOTS, width + 128)),
        ],
        (parts,),
        56,
        name="dense",
        scratch=[
            pltpu.VMEM((width, width), LOW),
            pltpu.VMEM((width, inner), LOW),
            pltpu.VMEM((inner, width), LOW),
            pltpu.SemaphoreType.DMA((3,)),
        ],
        us=40,
    )

    gathered = gather_all(payload)
    loss, gvec = pl.pallas_call(
        partial(loss_kernel, (q_dev, p_dev, width, col_count)),
        in_specs=[smem] * 3 + [pl.BlockSpec(memory_space=pltpu.VMEM)] * 3,
        out_specs=[pl.BlockSpec(memory_space=pltpu.VMEM)] * 2,
        out_shape=[shape(8, 128, kind=F32), shape(SLOTS, width, kind=F32)],
        compiler_params=params,
        name="loss",
    )(me, query_lengths, passage_lengths, payload, gathered, pooled)

    smalls = shape(8, width, kind=F32)
    grad_f, grad_f_t, stat_two = call(
        partial(norm_two_kernel, (q_dev, q_len, rows_all, width)),
        (query_lengths, passage_lengths, gvec, h2, line(gain_two)),
        [smem, smem, fixed((SLOTS, width)), by_block(width), thin],
        [
            (by_block(width), shape(total_rows, width)),
            (by_block_t(width), shape(width, total_rows)),
            (fixed((8, width)), smalls),
        ],
        (blocks,),
        60,
        name="norm_two",
        us=9,
    )

    outer = Flow(*weight_grad(grad_f_t, act, False, row_count, core), line=True)
    outer.step()

    def dense_back(deps):
        return call(
            partial(dense_back_kernel, (rows_part, width, inner)),
            (grad_f, slope, h1, w_outer, w_inner, w_attn_out, line(gain_one)),
            [by_part(width), by_part(inner), by_part(width), anywhere, anywhere, anywhere, thin],
            [
                (by_part(inner), shape(total_rows, inner)),
                (by_part(width), shape(total_rows, width, kind=F32)),
                (by_part(width), shape(total_rows, width)),
                (by_part(width), shape(total_rows, width)),
                (fixed((8, width)), smalls),
                (fixed((8, inner)), shape(8, inner, kind=F32)),
            ],
            (parts,),
            58,
            deps,
            name="dense_back",
            scratch=[
                pltpu.VMEM((inner, width), LOW),
                pltpu.VMEM((width, inner), LOW),
                pltpu.VMEM((width, width), LOW),
                pltpu.SemaphoreType.DMA((5,)),
            ],
            us=30,
        )

    def turn(arrays, specs, deps):
        outs = [(by_block_t(width), shape(width, total_rows))]
        return call(turn_low_kernel, arrays, specs, outs, (blocks,), 56, deps, name="turn", us=3)[0]

    y1_t = turn([y1], [by_block(width)], outer.sent)
    deps = outer.turn(y1_t)
    grad_u, grad_h1, grad_attn, grad_ctx, stat_one, grad_bias_inner = dense_back(deps)
    deps = outer.turn(stat_one)
    up_flow = Flow(*weight_grad(y1_t, grad_u, True, row_count, core, deps, tile=(128, 256)))
    up_flow.step()
    deps = up_flow.sent
    x_t = turn([queries, passages], [queries_spec, passages_spec], deps)
    deps = up_flow.turn(x_t)

    head_dim = width // HEADS
    third = 4 * head_dim
    groups = [(0, 2 * third), (2 * third, third)]

    def attend_back(start, wide, deps):
        pairs = wide // (2 * head_dim)
        index = start // wide
        cols = pl.BlockSpec((rows_all, wide), lambda i: (i, index))
        return call(
            partial(attend_back_kernel, (q_dev, q_len, rows_all, head_dim)),
            (query_lengths, passage_lengths, q, k, v, ctx_t, lse, grad_ctx),
            [smem, smem]
            + [cols] * 3
            + [
                pl.BlockSpec((wide, rows_all), lambda i: (index, i)),
                pl.BlockSpec((1, pairs, 8, rows_all), lambda i: (i, index, 0, 0)),
                cols,
            ],
            [
                (by_block(3 * wide), shape(total_rows, 3 * wide)),
                (fixed((8, wide)), shape(8, wide, kind=F32)),
            ],
            (blocks,),
            56,
            deps,
            name="attend_back",
            us=12,
        )

    grad_a, stat_a = attend_back(*groups[0], deps)
    mixed = weight_grad(ctx_t, grad_attn, True, row_count, core, [stat_a], room=3 * width, tile=(768, 256))
    deps = outer.turn(mixed[0]) + up_flow.turn(mixed[0])
    mixed = weight_grad(x_t, grad_a, True, row_count, core, deps, old=mixed, room=3 * width, tile=(256, 768))
    mixed_flow = Flow(*mixed)
    mixed_flow.step()
    grad_b, stat_b = attend_back(*groups[1], mixed_flow.sent)
    deps = [stat_b, *outer.turn(stat_b), *up_flow.turn(stat_b), *mixed_flow.turn(stat_b)]

    extra = (stat_two, stat_one, grad_bias_inner, stat_a, stat_b)
    last_flow = Flow(*weight_grad(x_t, grad_b, True, row_count, core, deps, extra))
    last_flow.step()
    deps = last_flow.sent

    query_grad, passage_grad = call(
        partial(input_grad_kernel, groups),
        (grad_a, grad_b, grad_h1, w_query, w_key, w_value),
        [by_block(3 * wide) for _, wide in groups] + [by_block(width), square, square, square],
        [
            (queries_spec, shape(rows_all, width)),
            (passages_spec, shape(p_dev * rows_all, width)),
        ],
        (blocks,),
        56,
        deps,
        name="input_grad",
        us=8,
    )
    mixed_flow.turn(passage_grad)
    last_flow.turn(mixed_flow.kept)
    outer.turn(last_flow.kept)
    up_flow.turn(outer.kept)
    mixed_flow.turn(up_flow.kept)
    last_flow.turn(mixed_flow.kept)
    last_flow.turn()
    mixed_flow.turn()
    last_flow.turn(mixed_flow.kept)
    flows = [outer, up_flow, mixed_flow, last_flow]
    while not all(flow.done for flow in flows):
        for flow in flows:
            if not flow.done:
                flow.turn()
    cut = width // row_count
    turned = pl.pallas_call(
        turn_kernel,
        out_shape=shape(inner // row_count, width, kind=F32),
        compiler_params=params,
        name="turn",
    )(outer.kept)
    mixed, last = mixed_flow.kept.astype(F32), last_flow.kept.astype(F32)
    qkv = [
        jnp.concatenate(
            [mixed[:, width + i * 2 * third : width + (i + 1) * 2 * third], last[:cut, i * third : (i + 1) * third]],
            1,
        )
        for i in range(3)
    ]
    small = last[cut:]
    return (
        loss[0, 0],
        query_out.reshape(query_tokens.shape),
        passage_out.reshape(passage_tokens.shape),
        query_grad.reshape(query_tokens.shape),
        passage_grad.reshape(passage_tokens.shape),
        *qkv,
        mixed[:, :width],
        up_flow.kept.astype(F32),
        turned,
        *[small[i, :cut] for i in range(3)],
        small[8, : inner // row_count],
        *[small[i, :cut] for i in range(3, 8)],
    )


def solution(mesh):
    in_specs = (
        P(("row", "col"), None, None),
        P(("row", "col"), None, None),
        P(("row", "col")),
        P(("row", "col")),
        P(("row", "col")),
        P(),
        P(),
        P(),
        P(),
        P(),
        P(),
        P(),
        P(),
        P(),
        P(),
        P(),
        P(),
        P(),
        P(),
        P(),
    )
    out_specs = (
        P(),
        P(("row", "col"), None, None),
        P(("row", "col"), None, None),
        P(("row", "col"), None, None),
        P(("row", "col"), None, None),
        P("row", None),
        P("row", None),
        P("row", None),
        P("row", None),
        P("row", None),
        P("row", None),
        P("row"),
        P("row"),
        P("row"),
        P("row"),
        P("row"),
        P("row"),
        P("row"),
        P("row"),
        P("row"),
    )
    return jax.shard_map(
        per_device, mesh=mesh, in_specs=in_specs, out_specs=out_specs, check_vma=False
    )
```

time: 925 us -> 299 us (0.32)
  matrix products: 277 us -> 0 us
  waiting for transfers between devices: 264 us -> 45.8 us
  Pallas kernels: 0 us -> 195 us
  local copies, waits for them, and re-layouts: 163 us -> 3.15 us
  blocking collectives: 130 us -> 0 us
  other arithmetic: 64.3 us -> 12.4 us
  starting transfers between devices: 0.08 us -> 36 us
  between operations: 19.8 us -> 1.47 us
    dot_general x50 -> x0, matrix products: 262 us -> none  [the longest x13 60.4 us: with_trans(): lax.dot_general(left, right, (((1,), (1,)), ((), ())), preferred_element_...]
    pallas_call x0 -> x16, Pallas kernels: none -> 195 us  [the longest x14 189 us: call(): pl.pallas_call(kernel, grid=grid, in_specs=list(in_specs) + [pl.BlockSpec...]
    unnamed x3 -> x0, waiting for transfers between devices: 142 us -> none
    psum x1 -> x0, waiting for transfers between devices: 122 us -> none  [per_device(): summed = lax.psum(summed.astype(jnp.bfloat16), 'col').astype(jnp.float32)]
    unnamed x324 -> x10, local copies, waits for them, and re-layouts: 51.8 us -> 0.02 us
    unnamed x3 -> x0, blocking collectives: 50.1 us -> none
    psum x2 -> x0, blocking collectives: 47.3 us -> none  [the longest x1 38.5 us: per_device(): lax.psum(jnp.sum(own_losses), ('row', 'col'))]
    ppermute x0 -> x32, waiting for transfers between devices: none -> 45.8 us  [the longest x9 30.7 us: step(): self.got = [lax.ppermute(self.kept, 'col', self.line[0][1])]]
  transfers between devices with their start and end apart: 2 -> 32, of which waited for: 2 -> 15; matrix products, arithmetic and copies ran while one was open for 2% -> 3% of each run, Pallas kernels for 0% -> 31%
where the time goes in v1:
time: 299 us; the launch traced here: 293 us
  Pallas kernels  195 us (65%)
  waiting for transfers between devices  45.8 us (15%)
  starting transfers between devices  36 us (12%)
  other arithmetic  12.4 us (4%)
  local copies, waits for them, and re-layouts  3.15 us (1%)
    pallas_call x14, Pallas kernels, call(): pl.pallas_call(kernel, grid=grid, in_specs=list(in_specs) + [pl.BlockSpec...  189 us
    ppermute x9, waiting for transfers between devices, step(): self.got = [lax.ppermute(self.kept, 'col', self.line[0][1])]  30.7 us
    ppermute x16, starting transfers between devices, step(): lax.ppermute(sent, 'row', [(i, i ^ mask) for i in range(size)])  14.3 us
    ppermute x9, starting transfers between devices, step(): self.got = [lax.ppermute(self.kept, 'col', self.line[0][1])]  12.4 us
    ppermute x7, waiting for transfers between devices, gather_all(): pieces.append(lax.ppermute(piece, name, pairs))  11.8 us
    ppermute x7, starting transfers between devices, gather_all(): pieces.append(lax.ppermute(piece, name, pairs))  9.31 us
  transfers between devices with their start and end apart: 32, of which 15 were waited for; matrix products, arithmetic and copies ran while one was open for 3% of the time, Pallas kernels for 31%

profile of v1, /device:TPU:0, one launch (start us, length us, event | category | flops | bytes accessed | tf_op | source)
XLA Modules:
  0.0 293.4 jit_solution(8076862790297700663)
XLA Ops:
  0.7 20.8 %attend.1 = (bf16[1536,768]{1,0:T(8,128)(2,1)}, bf16[1536,768]{1,0:T(8,128)(2,1)}, bf16[1536,768]{1,0:T(8,128)(2,1)}, bf16[768,1536]{1,0:T(8,128)(2,1)}, f32[3,6,8,512]{3,2,1,0:T(8,128)}) custom-call(s32[4]{0:T(128)} %refs_0_.9, s32[2]{0:T(128)} %refs_1_.7, bf16[512,768]{1,0:T(8,128)(2,1)} %bitcast.69, bf16[1024,768]{1,0:T(8,128)(2,1)} %bitcast.65, ...), custom_call_target="tpu_custom_call" | custom-call | flops 287500000 | tf_op jit(solution)/shard_map/attend/pallas_call | solution.py:591
  21.5 39.3 %dense.1 = (bf16[1536,768]{1,0:T(8,128)(2,1)}, bf16[1536,768]{1,0:T(8,128)(2,1)}, bf16[1536,3072]{1,0:T(8,128)(2,1)}, bf16[1536,3072]{1,0:T(8,128)(2,1)}, bf16[1...) custom-call(s32[4]{0:T(128)} %refs_0_.9, ...), custom_call_target="tpu_custom_call" | custom-call | flops 460000000 | tf_op jit(solution)/shard_map/dense/pallas_call | solution.py:591
  60.8 3.1 %collective-permute-start.2 = (bf16[8,896]{1,0:T(8,128)(2,1)}, bf16[8,896]{1,0:T(8,128)(2,1)S(1)}, u32[]{:S(2)}, u32[]{:S(2)}) collective-permute-start(bf16[8,896]{1,0:T(8,128)(2,1)} %get-tuple-element.87.own_ref), channel_id=1, source_target_pairs={{0,1},{1,0},{2,3},{3,2},{4,5},{5,4},{6,7},{7,6},{8,9},{9,8},{10,11... | collective-permute-start | bytes 43016 | tf_op jit(solution)/shard_map/ppermute | solution.py:752
  63.9 2.6 collective-permute-start.1
  66.5 2.3 collective-permute-done.1
  68.8 3.5 %collective-permute-done = bf16[8,896]{1,0:T(8,128)(2,1)S(1)} collective-permute-done((bf16[8,896]{1,0:T(8,128)(2,1)}, bf16[8,896]{1,0:T(8,128)(2,1)S(1)}, u32[]{:S(2)}, u32[]{:S(2)}) %collective-permute-start) | collective-permute-done | bytes 14368 | tf_op jit(solution)/shard_map/ppermute | solution.py:752
  78.7 2.4 collective-permute-done.3
  83.7 2.9 %loss.1 = (f32[8,128]{1,0:T(8,128)}, f32[8,768]{1,0:T(8,128)}) custom-call(s32[1]{0:T(128)} %bitcast.me_ref, s32[4]{0:T(128)} %refs_0_.9, s32[2]{0:T(128)} %refs_1_.7, bf16[8,896]{1,0:T(8,128)(2,1)} %get-tuple-element.87.own_ref, bf16[256,896]{1,0:T(8,128)(2,1)} %pad_maximum_fusion.all_ref, f32[8,768]{1,0:T(8,128)} %get-tuple-element.88.pool_ref), custom_call_target="tpu_custom_call" | custom-call | tf_op jit(solution)/shard_map/loss/pallas_call | solution.py:866
  86.6 7.7 %norm_two.1 = (bf16[1536,768]{1,0:T(8,128)(2,1)}, bf16[768,1536]{1,0:T(8,128)(2,1)}, f32[8,768]{1,0:T(8,128)}) custom-call(s32[4]{0:T(128)} %refs_0_.9, s32[2]{0:T(128)} %refs_1_.7, f32[8,768]{1,0:T(8,128)} %get-tuple-element.92.refs_2_, bf16[1536,768]{1,0:T(8,128)(2,1)} %get-tuple-element.93.refs_3_, f32[768]{0:T(1024)} %refs_4_.5), custom_call_target="tpu_custom_call" | custom-call | flops 103500000 | tf_op jit(solution)/shard_map/norm_two/pallas_call | solution.py:591
  94.3 12.2 %weight_grad.5 = (bf16[4,768,384]{2,1,0:T(8,128)(2,1)}, bf16[4,768,384]{2,1,0:T(8,128)(2,1)}) custom-call(s32[1]{0:T(128)} %bitcast.6.refs_0_, bf16[768,1536]{1,0:T(8,128)(2,1)} %get-tuple-element.94.refs_1_, bf16[1536,3072]{1,0:T(8,128)(2,1)} %get-tuple-element.95.refs_2_), custom_call_target="tpu_custom_call" | custom-call | flops 137526192 | tf_op jit(solution)/shard_map/weight_grad/pallas_call | solution.py:591
  106.6 4.4 %turn.3.refs_1_ = bf16[768,1536]{1,0:T(8,128)(2,1)} custom-call(bf16[1536,768]{1,0:T(8,128)(2,1)} %get-tuple-element.99.refs_0_), custom_call_target="tpu_custom_call" | custom-call | flops 34500000 | tf_op jit(solution)/shard_map/turn/pallas_call | solution.py:591
  115.4 32.6 %dense_back.1 = (bf16[1536,3072]{1,0:T(8,128)(2,1)}, f32[1536,768]{1,0:T(8,128)}, bf16[1536,768]{1,0:T(8,128)(2,1)}, bf16[1536,768]{1,0:T(8,128)(2,1)}, f32[8,768]{1,0:T(8,128)}, /*index=5*/f32[8,3072]{1,0:T(8,128)}) custom-call(bf16[1536,768]{1,0:T(8,128)(2,1)} %get-tuple-element.101.refs_0_, bf16[1536,3072]{1,0:T(8,128)(2,1)} %get-tuple-element.102.refs_1_, ...), custom_call_target="tpu_custom_call" | custom-call | flops 345000000 | tf_op jit(solution)/shard_map/dense_back/pallas_call | solution.py:591
  148.3 12.2 %weight_grad.6 = (bf16[4,96,3072]{2,1,0:T(8,128)(2,1)}, bf16[4,96,3072]{2,1,0:T(8,128)(2,1)}) custom-call(s32[1]{0:T(128)} %bitcast.6.refs_0_, bf16[768,1536]{1,0:T(8,128)(2,1)} %turn.3.refs_1_, bf16[1536,3072]{1,0:T(8,128)(2,1)} %get-tuple-element.108.refs_2_), custom_call_target="tpu_custom_call" | custom-call | flops 137526192 | tf_op jit(solution)/shard_map/weight_grad/pallas_call | solution.py:591
  160.5 2.1 collective-permute-start.12
  162.6 4.9 %turn.4.refs_1_ = bf16[768,1536]{1,0:T(8,128)(2,1)} custom-call(bf16[512,768]{1,0:T(8,128)(2,1)} %bitcast.71, bf16[1024,768]{1,0:T(8,128)(2,1)} %bitcast.67), custom_call_target="tpu_custom_call" | custom-call | flops 34500000 | tf_op jit(solution)/shard_map/turn/pallas_call | solution.py:591
  172.0 15.7 %attend_back.2 = (bf16[1536,1536]{1,0:T(8,128)(2,1)}, f32[8,512]{1,0:T(8,128)}) custom-call(s32[4]{0:T(128)} %refs_0_.9, s32[2]{0:T(128)} %refs_1_.7, bf16[1536,768]{1,0:T(8,128)(2,1)} %get-tuple-element.114.refs_2_, bf16[1536,768]{1,0:T(8,128)(2,1)} %get-tuple-element.115.refs_3_, bf16[1536,768]{1,0:T(8,128)(2,1)} %get-tuple-element.116.refs_4_, ...), custom_call_target="tpu_custom_call" | custom-call | flops 138000000 | tf_op jit(solution)/shard_map/attend_back/pallas_call | solution.py:591
  187.7 5.6 %weight_grad.7 = (bf16[4,96,2304]{2,1,0:T(8,128)(2,1)}, bf16[4,96,2304]{2,1,0:T(8,128)(2,1)}) custom-call(s32[1]{0:T(128)} %bitcast.6.refs_0_, bf16[768,1536]{1,0:T(8,128)(2,1)} %get-tuple-element.86.refs_5_.refs_1_, bf16[1536,768]{1,0:T(8,128)(2,1)} %get-tuple-element.122.refs_2_), custom_call_target="tpu_custom_call" | custom-call | flops 34381548 | tf_op jit(solution)/shard_map/weight_grad/pallas_call | solution.py:591
  194.5 2.6 collective-permute-done.14
  197.4 8.0 %weight_grad.8 = (bf16[4,96,2304]{2,1,0:T(8,128)(2,1)}, bf16[4,96,2304]{2,1,0:T(8,128)(2,1)}) custom-call(s32[1]{0:T(128)} %bitcast.6.refs_0_, bf16[768,1536]{1,0:T(8,128)(2,1)} %turn.4.refs_1_, bf16[1536,1536]{1,0:T(8,128)(2,1)} %get-tuple-element.119.refs_2_.refs_0_, ...), custom_call_target="tpu_custom_call", output_to_operand_aliasing={{0}: (3, {}), {1}: (4, {})} | custom-call | flops 68763096 | tf_op jit(solution)/shard_map/weight_grad/pallas_call | solution.py:591
  206.2 9.1 %attend_back.3 = (bf16[1536,768]{1,0:T(8,128)(2,1)}, f32[8,256]{1,0:T(8,128)}) custom-call(s32[4]{0:T(128)} %refs_0_.9, s32[2]{0:T(128)} %refs_1_.7, bf16[1536,768]{1,0:T(8,128)(2,1)} %get-tuple-element.114.refs_2_, bf16[1536,768]{1,0:T(8,128)(2,1)} %get-tuple-element.115.refs_3_, bf16[1536,768]{1,0:T(8,128)(2,1)} %get-tuple-element.116.refs_4_, ...), custom_call_target="tpu_custom_call" | custom-call | flops 138000000 | tf_op jit(solution)/shard_map/attend_back/pallas_call | solution.py:591
  222.0 3.0 %collective-permute-start.24 = (bf16[96,3072]{1,0:T(8,128)(2,1)S(1)}, bf16[96,3072]{1,0:T(8,128)(2,1)S(1)}, u32[]{:S(2)}, u32[]{:S(2)}) collective-permute-start(bf16[96,3072]{1,0:T(8,128)(2,1)S(1)} %add.232), channel_id=1, source_target_pairs={{0,2},{1,3},{2,0},{3,1},{4,6},{5,7},{6,4},{7,5},{8,10},{9,11},{10,... | collective-permute-start | bytes 1769480 | tf_op jit(solution)/shard_map/ppermute | solution.py:707
  225.0 5.6 %weight_grad.9 = (bf16[4,112,768]{2,1,0:T(8,128)(2,1)}, bf16[4,112,768]{2,1,0:T(8,128)(2,1)}) custom-call(s32[1]{0:T(128)} %bitcast.6.refs_0_, bf16[768,1536]{1,0:T(8,128)(2,1)} %turn.4.refs_1_, bf16[1536,768]{1,0:T(8,128)(2,1)} %get-tuple-element.130.refs_2_.refs_1_, f32[8,768]{1,0:T(8,128)} %get-tuple-element.138.refs_3_, ...), custom_call_target="tpu_custom_call" | custom-call | flops 34381548 | tf_op jit(solution)/shard_map/weight_grad/pallas_call | solution.py:591
  230.6 11.2 %input_grad.1 = (bf16[512,768]{1,0:T(8,128)(2,1)}, bf16[1024,768]{1,0:T(8,128)(2,1)}) custom-call(bf16[1536,1536]{1,0:T(8,128)(2,1)} %get-tuple-element.119.refs_2_.refs_0_, bf16[1536,768]{1,0:T(8,128)(2,1)} %get-tuple-element.130.refs_2_.refs_1_, f32[1536,768]{1,0:T(8,128)} %get-tuple-element.131.refs_2_, bf16[768,768]{1,0:T(8,128)(2,1)} %refs_3_.2, ...), custom_call_target="tpu_custom_call" | custom-call | flops 92000000 | tf_op jit(solution)/shard_map/input_grad/pallas_call | solution.py:591
  242.0 1.6 add_convert_fusion.10
  248.7 2.1 collective-permute-done.24
  251.9 8.3 %collective-permute-done.25 = bf16[96,2304]{1,0:T(8,128)(2,1)S(1)} collective-permute-done((bf16[96,2304]{1,0:T(8,128)(2,1)S(1)}, bf16[96,2304]{1,0:T(8,128)(2,1)S(1)}, u32[]{:S(2)}, u32[]{:S(2)}) %collective-permute-start.25) | collective-permute-done | bytes 442400 | tf_op jit(solution)/shard_map/ppermute | solution.py:707
  260.5 2.3 collective-permute-start.30
  262.8 11.2 %collective-permute-done.30 = bf16[112,768]{1,0:T(8,128)(2,1)S(1)} collective-permute-done((bf16[112,768]{1,0:T(8,128)(2,1)S(1)}, bf16[112,768]{1,0:T(8,128)(2,1)S(1)}, u32[]{:S(2)}, u32[]{:S(2)}) %collective-permute-start.30) | collective-permute-done | bytes 172064 | tf_op jit(solution)/shard_map/ppermute | solution.py:707
  274.1 2.8 collective-permute-start.31
  278.1 2.3 turn.5
  280.4 5.3 %collective-permute-done.26 = bf16[96,2304]{1,0:T(8,128)(2,1)S(1)} collective-permute-done((bf16[96,2304]{1,0:T(8,128)(2,1)S(1)}, bf16[96,2304]{1,0:T(8,128)(2,1)S(1)}, u32[]{:S(2)}, u32[]{:S(2)}) %collective-permute-start.26) | collective-permute-done | bytes 442400 | tf_op jit(solution)/shard_map/ppermute | solution.py:707
  285.9 3.5 %collective-permute-done.31 = bf16[112,768]{1,0:T(8,128)(2,1)S(1)} collective-permute-done((bf16[112,768]{1,0:T(8,128)(2,1)S(1)}, bf16[112,768]{1,0:T(8,128)(2,1)S(1)}, u32[]{:S(2)}, u32[]{:S(2)}) %collective-permute-start.31) | collective-permute-done | bytes 172064 | tf_op jit(solution)/shard_map/ppermute | solution.py:707
  (90 shorter events, 38.8 us)
Async XLA Ops:
  60.8 5.7 %collective-permute-start.2 = (bf16[8,896]{1,0:T(8,128)(2,1)}, bf16[8,896]{1,0:T(8,128)(2,1)S(1)}, u32[]{:S(2)}, u32[]{:S(2)}) collective-permute-start(bf16[8,896]{1,0:T(8,128)(2,1)} %get-tuple-element.87.own_ref), channel_id=1, source_target_pairs={{0,1},{1,0},{2,3},{3,2},{4,5},{5,4},{6,7},{7,6},{8,9},{9,8},{10,11... | collective-permute-start | bytes 43016 | tf_op jit(solution)/shard_map/ppermute | solution.py:752
  63.9 4.9 %collective-permute-start.1 = (bf16[8,896]{1,0:T(8,128)(2,1)}, bf16[8,896]{1,0:T(8,128)(2,1)S(1)}, u32[]{:S(2)}, u32[]{:S(2)}) collective-permute-start(bf16[8,896]{1,0:T(8,128)(2,1)} %get-tuple-element.87.own_ref), channel_id=1, source_target_pairs={{0,2},{1,3},{2,0},{3,1},{4,6},{5,7},{6,4},{7,5},{8,10},{9,11},{10,... | collective-permute-start | bytes 43016 | tf_op jit(solution)/shard_map/ppermute | solution.py:752
  66.5 5.7 %collective-permute-start = (bf16[8,896]{1,0:T(8,128)(2,1)}, bf16[8,896]{1,0:T(8,128)(2,1)S(1)}, u32[]{:S(2)}, u32[]{:S(2)}) collective-permute-start(bf16[8,896]{1,0:T(8,128)(2,1)} %get-tuple-element.87.own_ref), channel_id=1, source_target_pairs={{0,3},{1,2},{2,1},{3,0},{4,7},{5,6},{6,5},{7,4},{8,11},{9,10},{10,... | collective-permute-start | bytes 43016 | tf_op jit(solution)/shard_map/ppermute | solution.py:752
  72.9 4.4 %collective-permute-start.5 = (bf16[32,896]{1,0:T(8,128)(2,1)S(1)}, bf16[32,896]{1,0:T(8,128)(2,1)S(1)}, u32[]{:S(2)}, u32[]{:S(2)}) collective-permute-start(bf16[32,896]{1,0:T(8,128)(2,1)S(1)} %pad_maximum_fusion.5), channel_id=1, source_target_pairs={{0,8},{4,12},{8,0},{12,4},{16,24},{20,28},{24,16},{28,20},{1,9},{5... | collective-permute-start | bytes 172040 | tf_op jit(solution)/shard_map/ppermute | solution.py:752
  74.5 4.2 %collective-permute-start.4 = (bf16[32,896]{1,0:T(8,128)(2,1)S(1)}, bf16[32,896]{1,0:T(8,128)(2,1)S(1)}, u32[]{:S(2)}, u32[]{:S(2)}) collective-permute-start(bf16[32,896]{1,0:T(8,128)(2,1)S(1)} %pad_maximum_fusion.5), channel_id=1, source_target_pairs={{0,16},{4,20},{8,24},{12,28},{16,0},{20,4},{24,8},{28,12},{1,17},{... | collective-permute-start | bytes 172040 | tf_op jit(solution)/shard_map/ppermute | solution.py:752
  76.0 5.1 %collective-permute-start.3 = (bf16[32,896]{1,0:T(8,128)(2,1)S(1)}, bf16[32,896]{1,0:T(8,128)(2,1)S(1)}, u32[]{:S(2)}, u32[]{:S(2)}) collective-permute-start(bf16[32,896]{1,0:T(8,128)(2,1)S(1)} %pad_maximum_fusion.5), channel_id=1, source_target_pairs={{0,24},{4,28},{8,16},{12,20},{16,8},{20,12},{24,0},{28,4},{1,25},{... | collective-permute-start | bytes 172040 | tf_op jit(solution)/shard_map/ppermute | solution.py:752
  81.2 1.6 collective-permute-start.6
  106.5 4.7 %collective-permute-start.7 = (bf16[4,768,384]{2,1,0:T(8,128)(2,1)}, bf16[4,768,384]{2,1,0:T(8,128)(2,1)S(1)}, u32[]{:S(2)}, u32[]{:S(2)}) collective-permute-start(bf16[4,768,384]{2,1,0:T(8,128)(2,1)} %get-tuple-element.98), channel_id=1, source_target_pairs={{0,4},{4,0},{8,12},{12,8},{16,20},{20,16},{24,28},{28,24},{1,5},{5... | collective-permute-start | bytes 7077896 | tf_op jit(solution)/shard_map/ppermute | solution.py:702
  111.8 36.2 %collective-permute-start.10 = (bf16[768,384]{1,0:T(8,128)(2,1)S(1)}, bf16[768,384]{1,0:T(8,128)(2,1)S(1)}, u32[]{:S(2)}, u32[]{:S(2)}) collective-permute-start(bf16[768,384]{1,0:T(8,128)(2,1)S(1)} %get-tuple-element.159), channel_id=1, source_target_pairs={{0,24},{4,28},{8,16},{12,20},{16,8},{20,12},{24,0},{28,4},{1,25},{... | collective-permute-start | bytes 1769480 | tf_op jit(solution)/shard_map/ppermute | solution.py:702
  112.4 35.6 %collective-permute-start.9 = (bf16[768,384]{1,0:T(8,128)(2,1)S(1)}, bf16[768,384]{1,0:T(8,128)(2,1)S(1)}, u32[]{:S(2)}, u32[]{:S(2)}) collective-permute-start(bf16[768,384]{1,0:T(8,128)(2,1)S(1)} %get-tuple-element.160), channel_id=1, source_target_pairs={{0,16},{4,20},{8,24},{12,28},{16,0},{20,4},{24,8},{28,12},{1,17},{... | collective-permute-start | bytes 1769480 | tf_op jit(solution)/shard_map/ppermute | solution.py:702
  113.9 34.1 %collective-permute-start.8 = (bf16[768,384]{1,0:T(8,128)(2,1)S(1)}, bf16[768,384]{1,0:T(8,128)(2,1)S(1)}, u32[]{:S(2)}, u32[]{:S(2)}) collective-permute-start(bf16[768,384]{1,0:T(8,128)(2,1)S(1)} %get-tuple-element.161), channel_id=1, source_target_pairs={{0,8},{4,12},{8,0},{12,4},{16,24},{20,28},{24,16},{28,20},{1,9},{5... | collective-permute-start | bytes 1769480 | tf_op jit(solution)/shard_map/ppermute | solution.py:702
  160.5 7.0 %collective-permute-start.11 = (bf16[4,96,3072]{2,1,0:T(8,128)(2,1)}, bf16[4,96,3072]{2,1,0:T(8,128)(2,1)S(1)}, u32[]{:S(2)}, u32[]{:S(2)}) collective-permute-start(bf16[4,96,3072]{2,1,0:T(8,128)(2,1)} %get-tuple-element.109), channel_id=1, source_target_pairs={{0,4},{4,0},{8,12},{12,8},{16,20},{20,16},{24,28},{28,24},{1,5},{5... | collective-permute-start | bytes 7077896 | tf_op jit(solution)/shard_map/ppermute | solution.py:702
  160.5 32.7 %collective-permute-start.12 = (bf16[768,384]{1,0:T(8,128)(2,1)S(1)}, bf16[768,384]{1,0:T(8,128)(2,1)}, u32[]{:S(2)}, u32[]{:S(2)}) collective-permute-start(bf16[768,384]{1,0:T(8,128)(2,1)S(1)} %add_convert_fusion.5), channel_id=1, source_target_pairs={{0,1},{3,2},{4,5},{7,6},{8,9},{11,10},{12,13},{15,14},{16,17},{19,... | collective-permute-start | bytes 1769480 | tf_op jit(solution)/shard_map/ppermute | solution.py:707
  168.4 26.1 %collective-permute-start.15 = (bf16[96,3072]{1,0:T(8,128)(2,1)S(1)}, bf16[96,3072]{1,0:T(8,128)(2,1)S(1)}, u32[]{:S(2)}, u32[]{:S(2)}) collective-permute-start(bf16[96,3072]{1,0:T(8,128)(2,1)S(1)} %get-tuple-element.155), channel_id=1, source_target_pairs={{0,24},{4,28},{8,16},{12,20},{16,8},{20,12},{24,0},{28,4},{1,25},{... | collective-permute-start | bytes 1769480 | tf_op jit(solution)/shard_map/ppermute | solution.py:702
  168.9 28.1 %collective-permute-start.14 = (bf16[96,3072]{1,0:T(8,128)(2,1)S(1)}, bf16[96,3072]{1,0:T(8,128)(2,1)S(1)}, u32[]{:S(2)}, u32[]{:S(2)}) collective-permute-start(bf16[96,3072]{1,0:T(8,128)(2,1)S(1)} %get-tuple-element.156), channel_id=1, source_target_pairs={{0,16},{4,20},{8,24},{12,28},{16,0},{20,4},{24,8},{28,12},{1,17},{... | collective-permute-start | bytes 1769480 | tf_op jit(solution)/shard_map/ppermute | solution.py:702
  170.5 26.6 %collective-permute-start.13 = (bf16[96,3072]{1,0:T(8,128)(2,1)S(1)}, bf16[96,3072]{1,0:T(8,128)(2,1)S(1)}, u32[]{:S(2)}, u32[]{:S(2)}) collective-permute-start(bf16[96,3072]{1,0:T(8,128)(2,1)S(1)} %get-tuple-element.157), channel_id=1, source_target_pairs={{0,8},{4,12},{8,0},{12,4},{16,24},{20,28},{24,16},{28,20},{1,9},{5... | collective-permute-start | bytes 1769480 | tf_op jit(solution)/shard_map/ppermute | solution.py:702
  205.4 10.0 %collective-permute-start.18 = (bf16[4,96,2304]{2,1,0:T(8,128)(2,1)}, bf16[4,96,2304]{2,1,0:T(8,128)(2,1)S(1)}, u32[]{:S(2)}, u32[]{:S(2)}) collective-permute-start(bf16[4,96,2304]{2,1,0:T(8,128)(2,1)} %get-tuple-element.128), channel_id=1, source_target_pairs={{0,4},{4,0},{8,12},{12,8},{16,20},{20,16},{24,28},{28,24},{1,5},{5... | collective-permute-start | bytes 5308424 | tf_op jit(solution)/shard_map/ppermute | solution.py:702
  205.4 14.8 %collective-permute-start.16 = (bf16[768,384]{1,0:T(8,128)(2,1)S(1)}, bf16[768,384]{1,0:T(8,128)(2,1)S(1)}, u32[]{:S(2)}, u32[]{:S(2)}) collective-permute-start(bf16[768,384]{1,0:T(8,128)(2,1)S(1)} %add.226), channel_id=1, source_target_pairs={{1,2},{2,1},{5,6},{6,5},{9,10},{10,9},{13,14},{14,13},{17,18},{18,... | collective-permute-start | bytes 1769480 | tf_op jit(solution)/shard_map/ppermute | solution.py:707
  206.1 15.8 %collective-permute-start.17 = (bf16[96,3072]{1,0:T(8,128)(2,1)S(1)}, bf16[96,3072]{1,0:T(8,128)(2,1)S(1)}, u32[]{:S(2)}, u32[]{:S(2)}) collective-permute-start(bf16[96,3072]{1,0:T(8,128)(2,1)S(1)} %add_convert_fusion), channel_id=1, source_target_pairs={{0,1},{1,0},{2,3},{3,2},{4,5},{5,4},{6,7},{7,6},{8,9},{9,8},{10,11... | collective-permute-start | bytes 1769480 | tf_op jit(solution)/shard_map/ppermute | solution.py:707
  216.7 25.2 %collective-permute-start.21 = (bf16[96,2304]{1,0:T(8,128)(2,1)}, bf16[96,2304]{1,0:T(8,128)(2,1)}, u32[]{:S(2)}, u32[]{:S(2)}) collective-permute-start(bf16[96,2304]{1,0:T(8,128)(2,1)} %get-tuple-element.163), channel_id=1, source_target_pairs={{0,24},{4,28},{8,16},{12,20},{16,8},{20,12},{24,0},{28,4},{1,25},{... | collective-permute-start | bytes 1327112 | tf_op jit(solution)/shard_map/ppermute | solution.py:702
  218.0 24.0 %collective-permute-start.20 = (bf16[96,2304]{1,0:T(8,128)(2,1)}, bf16[96,2304]{1,0:T(8,128)(2,1)}, u32[]{:S(2)}, u32[]{:S(2)}) collective-permute-start(bf16[96,2304]{1,0:T(8,128)(2,1)} %get-tuple-element.164), channel_id=1, source_target_pairs={{0,16},{4,20},{8,24},{12,28},{16,0},{20,4},{24,8},{28,12},{1,17},{... | collective-permute-start | bytes 1327112 | tf_op jit(solution)/shard_map/ppermute | solution.py:702
  219.5 22.5 %collective-permute-start.19 = (bf16[96,2304]{1,0:T(8,128)(2,1)S(1)}, bf16[96,2304]{1,0:T(8,128)(2,1)}, u32[]{:S(2)}, u32[]{:S(2)}) collective-permute-start(bf16[96,2304]{1,0:T(8,128)(2,1)S(1)} %get-tuple-element.165), channel_id=1, source_target_pairs={{0,8},{4,12},{8,0},{12,4},{16,24},{20,28},{24,16},{28,20},{1,9},{5... | collective-permute-start | bytes 1327112 | tf_op jit(solution)/shard_map/ppermute | solution.py:702
  220.4 23.9 %collective-permute-start.22 = (bf16[768,384]{1,0:T(8,128)(2,1)S(1)}, bf16[768,384]{1,0:T(8,128)(2,1)S(1)}, u32[]{:S(2)}, u32[]{:S(2)}) collective-permute-start(bf16[768,384]{1,0:T(8,128)(2,1)S(1)} %add.231), channel_id=1, source_target_pairs={{1,0},{2,3},{5,4},{6,7},{9,8},{10,11},{13,12},{14,15},{17,16},{18,... | collective-permute-start | bytes 1769480 | tf_op jit(solution)/shard_map/ppermute | solution.py:707
  222.0 28.8 %collective-permute-start.24 = (bf16[96,3072]{1,0:T(8,128)(2,1)S(1)}, bf16[96,3072]{1,0:T(8,128)(2,1)S(1)}, u32[]{:S(2)}, u32[]{:S(2)}) collective-permute-start(bf16[96,3072]{1,0:T(8,128)(2,1)S(1)} %add.232), channel_id=1, source_target_pairs={{0,2},{1,3},{2,0},{3,1},{4,6},{5,7},{6,4},{7,5},{8,10},{9,11},{10,... | collective-permute-start | bytes 1769480 | tf_op jit(solution)/shard_map/ppermute | solution.py:707
  241.9 2.2 collective-permute-start.23
  243.6 16.7 %collective-permute-start.25 = (bf16[96,2304]{1,0:T(8,128)(2,1)S(1)}, bf16[96,2304]{1,0:T(8,128)(2,1)S(1)}, u32[]{:S(2)}, u32[]{:S(2)}) collective-permute-start(bf16[96,2304]{1,0:T(8,128)(2,1)S(1)} %add_convert_fusion.10), channel_id=1, source_target_pairs={{0,1},{1,0},{2,3},{3,2},{4,5},{5,4},{6,7},{7,6},{8,9},{9,8},{10,11... | collective-permute-start | bytes 1327112 | tf_op jit(solution)/shard_map/ppermute | solution.py:707
  245.2 15.2 %collective-permute-start.29 = (bf16[112,768]{1,0:T(8,128)(2,1)S(1)}, bf16[112,768]{1,0:T(8,128)(2,1)S(1)}, u32[]{:S(2)}, u32[]{:S(2)}) collective-permute-start(bf16[112,768]{1,0:T(8,128)(2,1)S(1)} %get-tuple-element.167), channel_id=1, source_target_pairs={{0,24},{4,28},{8,16},{12,20},{16,8},{20,12},{24,0},{28,4},{1,25},{... | collective-permute-start | bytes 516104 | tf_op jit(solution)/shard_map/ppermute | solution.py:702
  246.5 13.9 %collective-permute-start.28 = (bf16[112,768]{1,0:T(8,128)(2,1)S(1)}, bf16[112,768]{1,0:T(8,128)(2,1)S(1)}, u32[]{:S(2)}, u32[]{:S(2)}) collective-permute-start(bf16[112,768]{1,0:T(8,128)(2,1)S(1)} %get-tuple-element.168), channel_id=1, source_target_pairs={{0,16},{4,20},{8,24},{12,28},{16,0},{20,4},{24,8},{28,12},{1,17},{... | collective-permute-start | bytes 516104 | tf_op jit(solution)/shard_map/ppermute | solution.py:702
  247.9 12.5 %collective-permute-start.27 = (bf16[112,768]{1,0:T(8,128)(2,1)S(1)}, bf16[112,768]{1,0:T(8,128)(2,1)S(1)}, u32[]{:S(2)}, u32[]{:S(2)}) collective-permute-start(bf16[112,768]{1,0:T(8,128)(2,1)S(1)} %get-tuple-element.169), channel_id=1, source_target_pairs={{0,8},{4,12},{8,0},{12,4},{16,24},{20,28},{24,16},{28,20},{1,9},{5... | collective-permute-start | bytes 516104 | tf_op jit(solution)/shard_map/ppermute | solution.py:702
  260.3 25.4 %collective-permute-start.26 = (bf16[96,2304]{1,0:T(8,128)(2,1)S(1)}, bf16[96,2304]{1,0:T(8,128)(2,1)S(1)}, u32[]{:S(2)}, u32[]{:S(2)}) collective-permute-start(bf16[96,2304]{1,0:T(8,128)(2,1)S(1)} %add.242), channel_id=1, source_target_pairs={{0,2},{1,3},{2,0},{3,1},{4,6},{5,7},{6,4},{7,5},{8,10},{9,11},{10,... | collective-permute-start | bytes 1327112 | tf_op jit(solution)/shard_map/ppermute | solution.py:707
  260.5 13.5 %collective-permute-start.30 = (bf16[112,768]{1,0:T(8,128)(2,1)S(1)}, bf16[112,768]{1,0:T(8,128)(2,1)S(1)}, u32[]{:S(2)}, u32[]{:S(2)}) collective-permute-start(bf16[112,768]{1,0:T(8,128)(2,1)S(1)} %add_convert_fusion.15), channel_id=1, source_target_pairs={{0,1},{1,0},{2,3},{3,2},{4,5},{5,4},{6,7},{7,6},{8,9},{9,8},{10,11... | collective-permute-start | bytes 516104 | tf_op jit(solution)/shard_map/ppermute | solution.py:707
  274.1 15.2 %collective-permute-start.31 = (bf16[112,768]{1,0:T(8,128)(2,1)S(1)}, bf16[112,768]{1,0:T(8,128)(2,1)S(1)}, u32[]{:S(2)}, u32[]{:S(2)}) collective-permute-start(bf16[112,768]{1,0:T(8,128)(2,1)S(1)} %add.250), channel_id=1, source_target_pairs={{0,2},{1,3},{2,0},{3,1},{4,6},{5,7},{6,4},{7,5},{8,10},{9,11},{10,... | collective-permute-start | bytes 516104 | tf_op jit(solution)/shard_map/ppermute | solution.py:707
  (5 other events, 32.1 us)

commit v2 on v1

--- a/solution.py
+++ b/solution.py
@@ -304,40 +304,67 @@
     gvec_ref[...] = (r * grad - r * r * r * inside * pooled) / length
 
 
-def norm_two_kernel(dims, qlen_ref, plen_ref, gvec_ref, h2_ref, g2_ref, gf_ref, gf_t_ref, stat_ref):
-    q_dev, q_len, rows_all, width = dims
-    block = pl.program_id(0)
-
-    @pl.when(block == 0)
+def store_shards(core_ref, result, send_ref, keep_ref, by_row=True, tails=None):
+    count = send_ref.shape[0] * 2
+    size = result.shape[0 if by_row else 1] // count
+
+    def store(even, odd):
+        for shard in range(count):
+            spot = slice(shard * size, (shard + 1) * size)
+            piece = (result[spot, :] if by_row else result[:, spot]).astype(LOW)
+            target = odd if shard % 2 else even
+            if tails is None:
+                target[shard // 2] = piece
+            else:
+                target[shard // 2, :size] = piece
+                target[shard // 2, size:] = tails[shard]
+
+    @pl.when(core_ref[0] == 0)
+    def _():
+        store(keep_ref, send_ref)
+
+    @pl.when(core_ref[0] == 1)
+    def _():
+        store(send_ref, keep_ref)
+
+
+def outer_grad_kernel(
+    dims, core_ref, qlen_ref, plen_ref, gvec_ref, h2_ref, g2_ref, act_ref,
+    gf_ref, stat_ref, send_ref, keep_ref, gf_t_ref,
+):
+    q_dev, q_len, p_len = dims
+
+    @pl.when(pl.program_id(0) == 0)
     def _():
         stat_ref[...] = jnp.zeros_like(stat_ref)
 
-    def body(part, carry):
-        rows = rows_of(part, q_len)
-        number = block * (rows_all // q_len) + part
-        slot, length, first = part_owner(number, q_dev, q_len, rows_all, qlen_ref, plen_ref)
-        in_slot = lax.broadcasted_iota(jnp.int32, (SLOTS, 1), 0) == slot
-        grad_y = jnp.sum(jnp.where(in_slot, gvec_ref[...], 0.0), 0, keepdims=True)
-        live = live_rows(first, length, q_len)
-        n2, r2 = norm_parts(h2_ref[rows, :].astype(F32))
-        g = grad_y * vec(g2_ref)
-        grad = r2 * (g - jnp.mean(g, -1, keepdims=True) - n2 * jnp.mean(g * n2, -1, keepdims=True))
-        grad = jnp.where(live, grad, 0.0)
-        low = grad.astype(LOW)
-        gf_ref[rows, :] = low
-        gf_t_ref[:, rows] = low.T
-        stat_ref[0:1, :] += grad_y * jnp.sum(jnp.where(live, n2, 0.0), 0, keepdims=True)
-        stat_ref[1:2, :] += grad_y * jnp.sum(live.astype(F32), 0, keepdims=True)
-        stat_ref[2:3, :] += jnp.sum(low.astype(F32), 0, keepdims=True)
-        return carry
-
-    lax.fori_loop(0, rows_all // q_len, body, 0)
+        def body(part, carry):
+            rows = rows_of(part, q_len)
+            slot, length, first = part_owner(part, q_dev, q_len, p_len, qlen_ref, plen_ref)
+            in_slot = lax.broadcasted_iota(jnp.int32, (SLOTS, 1), 0) == slot
+            grad_y = jnp.sum(jnp.where(in_slot, gvec_ref[...], 0.0), 0, keepdims=True)
+            live = live_rows(first, length, q_len)
+            n2, r2 = norm_parts(h2_ref[rows, :].astype(F32))
+            g = grad_y * vec(g2_ref)
+            grad = r2 * (g - jnp.mean(g, -1, keepdims=True) - n2 * jnp.mean(g * n2, -1, keepdims=True))
+            grad = jnp.where(live, grad, 0.0)
+            low = grad.astype(LOW)
+            gf_ref[rows, :] = low
+            gf_t_ref[:, rows] = low.T
+            stat_ref[0:1, :] += grad_y * jnp.sum(jnp.where(live, n2, 0.0), 0, keepdims=True)
+            stat_ref[1:2, :] += grad_y * jnp.sum(live.astype(F32), 0, keepdims=True)
+            stat_ref[2:3, :] += jnp.sum(low.astype(F32), 0, keepdims=True)
+            return carry
+
+        lax.fori_loop(0, h2_ref.shape[0] // q_len, body, 0)
+
+    store_shards(core_ref, mm(gf_t_ref[...], act_ref[...]), send_ref, keep_ref, by_row=False)
 
 
 def dense_back_kernel(
-    dims, gf_ref, dg_ref, h1_ref, wf_hbm, wi_hbm, wo_hbm, g1_ref,
-    gu_ref, gh1_ref, ga_ref, gc_ref, stat_ref, bi_ref,
-    wf_ref, wi_ref, wo_ref, sems,
+    dims, core_ref, gf_ref, dg_ref, h1_ref, ctx_t_ref, wf_hbm, wi_hbm, wo_hbm, g1_ref,
+    gu_ref, ga_ref, gc_ref, stat_ref, bi_ref, send_ref, keep_ref,
+    sum_ref, wf_ref, wi_ref, wo_ref, sems,
 ):
     rows_all, width, inner = dims
     block = pl.program_id(0)
@@ -401,16 +428,29 @@
     stat_ref[1:2, :] += jnp.sum(total, 0, keepdims=True)
     g = total * vec(g1_ref)
     grad = r1 * (g - jnp.mean(g, -1, keepdims=True) - n1 * jnp.mean(g * n1, -1, keepdims=True))
-    gh1_ref[...] = grad
     low = grad.astype(LOW)
     ga_ref[...] = low
     stat_ref[2:3, :] += jnp.sum(low.astype(F32), 0, keepdims=True)
     gc_ref[...] = mm_nt(low, wo_ref[...]).astype(LOW)
+    product = mm(ctx_t_ref[...], low)
+
+    @pl.when(block == 0)
+    def _():
+        sum_ref[...] = product
+
+    @pl.when(block > 0)
+    def _():
+        sum_ref[...] += product
+
+    @pl.when(block == pl.num_programs(0) - 1)
+    def _():
+        store_shards(core_ref, sum_ref[...], send_ref, keep_ref)
 
 
 def attend_back_kernel(
-    dims, qlen_ref, plen_ref, q_ref, k_ref, v_ref, ctx_t_ref, lse_ref, gc_ref, out_ref, stat_ref
+    dims, core_ref, qlen_ref, plen_ref, q_ref, k_ref, v_ref, ctx_t_ref, lse_ref, gc_ref, x_t_ref, *refs
 ):
+    *extra, out_ref, stat_ref, send_ref, keep_ref, sum_ref = refs
     q_dev, q_len, rows_all, head_dim = dims
     block = pl.program_id(0)
     pair_dim = 2 * head_dim
@@ -421,10 +461,10 @@
     def _():
         stat_ref[...] = jnp.zeros_like(stat_ref)
 
-    def attend(size, starts, lengths):
+    def attend(size, starts, lengths, fresh):
         lane = lax.broadcasted_iota(jnp.int32, (size, pair_dim), 1)
-        items = [(s, p, which) for s in range(len(starts)) for p in range(pairs) for which in range(2)]
-        held, raw, made = {}, {}, {}
+        items = [(s, p, which) for p in range(pairs) for s in range(len(starts)) for which in range(2)]
+        held, raw, made, grads = {}, {}, {}, {}
 
         def pair_of(s, p):
             if (s, p) not in held:
@@ -465,77 +505,69 @@
                 return
             old_v, old_k, old_q = made.pop((s, p))
             grad_q = (jnp.concatenate([old_q, add_q], 0).T * head_dim**-0.5).astype(LOW)
+            grad_k = (old_k + add_k).astype(LOW)
             grad_v = (old_v + add_v).astype(LOW)
-            out_ref[here, cols] = grad_q
-            out_ref[here, width + cols.start : width + cols.stop] = (old_k + add_k).astype(LOW)
-            out_ref[here, 2 * width + cols.start : 2 * width + cols.stop] = grad_v
+            for number, grad in enumerate((grad_q, grad_k, grad_v)):
+                out_ref[here, number * width + cols.start : number * width + cols.stop] = grad
+                grads[number, s, p] = grad
             stat_ref[0:1, cols] += jnp.sum(grad_q.astype(F32), 0, keepdims=True)
             stat_ref[1:2, cols] += jnp.sum(grad_v.astype(F32), 0, keepdims=True)
 
+            if p % 2 and s == len(starts) - 1:
+                project(p - 1)
+
+        def project(p):
+            for number in range(3):
+                rows = [
+                    jnp.concatenate([grads.pop((number, s, p)), grads.pop((number, s, p + 1))], 1)
+                    for s in range(len(starts))
+                ]
+                product = mm(x_t_ref[...], jnp.concatenate(rows, 0))
+                cols = slice(number * width + p * pair_dim, number * width + (p + 2) * pair_dim)
+                if fresh:
+                    sum_ref[:, cols] = product
+                else:
+                    sum_ref[:, cols] += product
+
         staged(len(items), compare, weigh, combine)
 
     @pl.when(block == 0)
     def _():
-        attend(q_len, [s * q_len for s in range(q_dev)], [qlen_ref[s] for s in range(q_dev)])
+        attend(q_len, [s * q_len for s in range(q_dev)], [qlen_ref[s] for s in range(q_dev)], True)
 
     @pl.when(block > 0)
     def _():
-        attend(rows_all, [0], [plen_ref[jnp.maximum(block - 1, 0)]])
-
-
-def input_grad_kernel(groups, *refs):
-    grads, (gh1_ref, wq_ref, wk_ref, wv_ref, gq_ref, gp_ref) = refs[: len(groups)], refs[len(groups) :]
-    block = pl.program_id(0)
-    total = gh1_ref[...]
-    for grad_ref, (start, wide) in zip(grads, groups):
-        for number, w_ref in enumerate((wq_ref, wk_ref, wv_ref)):
-            total = total + mm_nt(grad_ref[:, number * wide : (number + 1) * wide], w_ref[:, start : start + wide])
+        attend(rows_all, [0], [plen_ref[jnp.maximum(block - 1, 0)]], False)
+
+    @pl.when(block == pl.num_programs(0) - 1)
+    def _():
+        tails = None
+        if extra:
+            tails = small_rows([*extra, stat_ref], send_ref.shape[0] * 2, send_ref.shape[2])
+        store_shards(core_ref, sum_ref[...], send_ref, keep_ref, tails=tails)
+
+
+def input_grad_kernel(grad_ref, base_ref, wq_ref, wk_ref, wv_ref, *out_refs):
+    wide = wq_ref.shape[1]
+    total = base_ref[...].astype(F32)
+    for number, w_ref in enumerate((wq_ref, wk_ref, wv_ref)):
+        total = total + mm_nt(grad_ref[:, number * wide : (number + 1) * wide], w_ref[...])
     low = total.astype(LOW)
-
-    @pl.when(block == 0)
-    def _():
-        gq_ref[...] = low
-
-    @pl.when(block > 0)
-    def _():
-        gp_ref[...] = low
-
-
-def weight_grad_kernel(shards, by_row, tile, core_ref, left_ref, right_ref, *refs):
-    *extra, send_ref, keep_ref = refs
-    high, wide = left_ref.shape[0], right_ref.shape[1]
-    result = [
-        [
-            mm(left_ref[row : row + tile[0], :], right_ref[:, col : col + tile[1]]).astype(LOW)
-            for col in range(0, wide, tile[1])
-        ]
-        for row in range(0, high, tile[0])
-    ]
-    result = jnp.concatenate([jnp.concatenate(items, 1) for items in result], 0)
-    count = shards if by_row else send_ref.shape[0] * 2
-    size = result.shape[0 if by_row else 1] // count
-    tail = [None] * count
-    if extra:
-        tail = small_rows(extra, count, result.shape[1])
-
-    def store(even, odd):
-        for shard in range(count):
-            spot = slice(shard * size, (shard + 1) * size)
-            piece = result[spot, :] if by_row else result[:, spot]
-            target = odd if shard % 2 else even
-            if tail[shard] is None:
-                target[shard // 2] = piece
-            else:
-                target[shard // 2, :size] = piece
-                target[shard // 2, size:] = tail[shard]
-
-    @pl.when(core_ref[0] == 0)
-    def _():
-        store(keep_ref, send_ref)
-
-    @pl.when(core_ref[0] == 1)
-    def _():
-        store(send_ref, keep_ref)
+    if len(out_refs) == 1:
+        out_refs[0][...] = low
+        return
+
+    @pl.when(pl.program_id(0) == 0)
+    def _():
+        out_refs[0][...] = low
+
+    @pl.when(pl.program_id(0) > 0)
+    def _():
+        out_refs[1][...] = low
+
+
+def weight_grad_kernel(core_ref, left_ref, right_ref, send_ref, keep_ref):
+    store_shards(core_ref, mm(left_ref[...], right_ref[...]), send_ref, keep_ref)
 
 
 def small_rows(refs, count, wide):
@@ -602,61 +634,44 @@
     )(*operands, *old)
 
 
-def weight_grad(left_t, right, by_row, row_count, core, deps=(), extra=(), old=(), room=None, tile=(256, 256)):
+def weight_grad(left_t, right, row_count, core, deps, old):
     height, depth = left_t.shape
     wide = right.shape[1]
-    cut = (height if by_row else wide) // row_count
-    block = 768
-    per_block = row_count if by_row else block // cut if block % cut == 0 else 0
-    if wide % block or cut % (16 if by_row else 128) or per_block % 2:
-        whole = jnp.dot(left_t, right, preferred_element_type=F32).astype(LOW)
-        if by_row:
-            whole = whole.reshape(row_count // 2, 2, cut, wide)
-        else:
-            whole = whole.reshape(height, row_count // 2, 2, cut).transpose(1, 2, 0, 3)
-        if extra:
-
-            def rows_kernel(*refs):
-                for shard, item in enumerate(small_rows(refs[:-1], row_count, wide)):
-                    refs[-1][shard] = item
-
-            rows = pl.pallas_call(
-                rows_kernel,
-                out_shape=jax.ShapeDtypeStruct((row_count, 16, wide), LOW),
-                compiler_params=pltpu.CompilerParams(vmem_limit_bytes=VMEM),
-            )(*extra)
-            whole = jnp.concatenate([whole, rows.reshape(row_count // 2, 2, 16, wide)], 2)
-        result = [lax.dynamic_index_in_dim(whole, side, 1, keepdims=False) for side in (1 - core, core)]
-        return [jnp.concatenate([a, b], 2) for a, b in zip(old, result)] if old else result
-    if by_row:
-        rows = cut + (16 if extra else 0)
-        shape = (row_count // 2, rows, room or wide)
-        after = (room - wide) // block if old else 0
-        spec = pl.BlockSpec((row_count // 2, rows, block), lambda i: (0, 0, i + after))
-    else:
-        shape = (row_count // 2, height, cut)
-        spec = pl.BlockSpec((per_block // 2, height, cut), lambda i: (i, 0, 0))
+    block = min(wide, 768)
+    shape = old[0].shape
+    spec = pl.BlockSpec((*shape[:2], block), lambda i: (0, 0, i))
     return call(
-        partial(weight_grad_kernel, row_count, by_row, tile),
-        (core.reshape(1), left_t, right, *extra),
+        weight_grad_kernel,
+        (core, left_t, right),
         [
             pl.BlockSpec(memory_space=pltpu.SMEM),
             const_spec((height, depth)),
             pl.BlockSpec((depth, block), lambda i: (0, i)),
-        ]
-        + [const_spec(item.shape) for item in extra],
+        ],
         [(spec, jax.ShapeDtypeStruct(shape, LOW))] * 2,
         (wide // block,),
         56,
         deps,
         old,
         name="weight_grad",
-        us=height * depth * wide * 3.3e-9,
-    )
+        us=12,
+    )
+
+
+def add_kernel(*refs):
+    *terms, out_ref = refs
+    out_ref[...] = sum([ref[...].astype(F32) for ref in terms[1:]], terms[0][...].astype(F32)).astype(LOW)
+
+
+def add_all(terms):
+    shape = terms[0].shape
+    spec = pl.BlockSpec(shape, lambda i: (0,) * len(shape), pipeline_mode=pl.Buffered(1))
+    outs = [(spec, jax.ShapeDtypeStruct(shape, LOW))]
+    return call(add_kernel, terms, [spec] * len(terms), outs, (1,), 24, name="add_all", us=20_000)[0]
 
 
 class Flow:
-    def __init__(self, sent, kept, line=False):
+    def __init__(self, sent, kept, line=False, fused=False):
         bits = lax.axis_size("row").bit_length() - 1
         self.order = [(0,)] + [tuple(range(i, min(i + 2, bits))) for i in range(1, bits, 2)]
         self.left = list(range(bits - 1, 0, -1))
@@ -670,7 +685,7 @@
                 ((i, count - 1 - i), [(i + 1, i), (count - 2 - i, count - 1 - i)])
                 for i in range(half - 2, -1, -1)
             ]
-        self.sent, self.kept, self.got = [sent], kept, None
+        self.sent, self.kept, self.got, self.fused = [sent], kept, None, fused
 
     def shard(self, terms, bits, mask):
         here = lax.axis_index("row")
@@ -715,7 +730,9 @@
             if bits == (0,):
                 dims = (2,) * len(self.left) + self.kept.shape[1:]
                 self.kept, self.got = self.kept.reshape(dims), [item.reshape(dims) for item in self.got]
-            if not self.order:
+            if not self.order and self.fused:
+                self.kept = add_all([self.kept, *self.got])
+            elif not self.order:
                 self.kept = sum([item.astype(F32) for item in self.got], self.kept.astype(F32)).astype(LOW)
         else:
             ends, _ = self.line.pop(0)
@@ -775,13 +792,10 @@
     row_count = lax.axis_size("row")
     col_count = lax.axis_size("col")
     row_here = lax.axis_index("row")
-    core = row_here & 1
+    core = (row_here & 1).reshape(1)
     me = (row_here * col_count + lax.axis_index("col")).reshape(1)
     params = pltpu.CompilerParams(vmem_limit_bytes=VMEM)
     smem = pl.BlockSpec(memory_space=pltpu.SMEM)
-
-    def line(item):
-        return item
 
     def by_block(wide):
         return pl.BlockSpec((rows_all, wide), lambda i: (i, 0))
@@ -821,14 +835,14 @@
         us=25,
     )
 
-    rows_part = rows_all
-    parts = blocks
+    rows_part = rows_all // 2
+    parts = 2 * blocks
 
     def by_part(wide):
         return pl.BlockSpec((rows_part, wide), lambda i: (i, 0))
 
-    queries_part = pl.BlockSpec((rows_part, width), lambda i: (0, 0))
-    passages_part = pl.BlockSpec((rows_part, width), lambda i: (jnp.maximum(i - 1, 0), 0))
+    queries_part = pl.BlockSpec((rows_part, width), lambda i: (jnp.minimum(i, 1), 0))
+    passages_part = pl.BlockSpec((rows_part, width), lambda i: (jnp.maximum(i - 2, 0), 0))
     h1, y1, act, slope, h2, query_out, passage_out, pooled, payload = call(
         partial(dense_kernel, (q_dev, q_len, p_len, width, inner)),
         (
@@ -873,150 +887,171 @@
     )(me, query_lengths, passage_lengths, payload, gathered, pooled)
 
     smalls = shape(8, width, kind=F32)
-    grad_f, grad_f_t, stat_two = call(
-        partial(norm_two_kernel, (q_dev, q_len, rows_all, width)),
-        (query_lengths, passage_lengths, gvec, h2, line(gain_two)),
-        [smem, smem, fixed((SLOTS, width)), by_block(width), thin],
+    cut = width // row_count
+    cut_inner = inner // row_count
+    half = row_count // 2
+    step_cols = 768
+    per_step = step_cols // cut_inner
+    outer_spec = pl.BlockSpec((per_step // 2, width, cut_inner), lambda i: (i, 0, 0))
+    grad_f, stat_two, *outer_parts = call(
+        partial(outer_grad_kernel, (q_dev, q_len, p_len)),
+        (core, query_lengths, passage_lengths, gvec, h2, gain_two, act),
+        [smem, smem, smem, fixed((SLOTS, width)), const_spec((total_rows, width)), thin]
+        + [pl.BlockSpec((total_rows, step_cols), lambda i: (0, i))],
         [
+            (fixed((total_rows, width)), shape(total_rows, width)),
+            (fixed((8, width)), smalls),
+            (outer_spec, shape(half, width, cut_inner)),
+            (outer_spec, shape(half, width, cut_inner)),
+        ],
+        (inner // step_cols,),
+        56,
+        name="outer_grad",
+        scratch=[pltpu.VMEM((width, total_rows), LOW)],
+        us=16,
+    )
+    outer = Flow(*outer_parts, line=True)
+    outer.step()
+
+    def turn(arrays, specs, deps):
+        outs = [(by_block_t(width), shape(width, total_rows))]
+        return call(turn_low_kernel, arrays, specs, outs, (blocks,), 56, deps, name="turn", us=3)[0]
+
+    y1_t = turn([y1], [by_block(width)], outer.sent)
+    deps = outer.turn(y1_t)
+    attn_spec = pl.BlockSpec((half, cut, width), lambda i: (0, 0, inner // width))
+    grad_u, grad_attn, grad_ctx, stat_one, grad_bias_inner, *up_parts = call(
+        partial(dense_back_kernel, (rows_all, width, inner)),
+        (core, grad_f, slope, h1, ctx_t, w_outer, w_inner, w_attn_out, gain_one),
+        [smem, by_block(width), by_block(inner), by_block(width), by_block_t(width)]
+        + [anywhere, anywhere, anywhere, thin],
+        [
+            (by_block(inner), shape(total_rows, inner)),
             (by_block(width), shape(total_rows, width)),
-            (by_block_t(width), shape(width, total_rows)),
+            (by_block(width), shape(total_rows, width)),
             (fixed((8, width)), smalls),
+            (fixed((8, inner)), shape(8, inner, kind=F32)),
+            (attn_spec, shape(half, cut, inner + width)),
+            (attn_spec, shape(half, cut, inner + width)),
         ],
         (blocks,),
         60,
-        name="norm_two",
-        us=9,
-    )
-
-    outer = Flow(*weight_grad(grad_f_t, act, False, row_count, core), line=True)
-    outer.step()
-
-    def dense_back(deps):
-        return call(
-            partial(dense_back_kernel, (rows_part, width, inner)),
-            (grad_f, slope, h1, w_outer, w_inner, w_attn_out, line(gain_one)),
-            [by_part(width), by_part(inner), by_part(width), anywhere, anywhere, anywhere, thin],
-            [
-                (by_part(inner), shape(total_rows, inner)),
-                (by_part(width), shape(total_rows, width, kind=F32)),
-                (by_part(width), shape(total_rows, width)),
-                (by_part(width), shape(total_rows, width)),
-                (fixed((8, width)), smalls),
-                (fixed((8, inner)), shape(8, inner, kind=F32)),
-            ],
-            (parts,),
-            58,
-            deps,
-            name="dense_back",
-            scratch=[
-                pltpu.VMEM((inner, width), LOW),
-                pltpu.VMEM((width, inner), LOW),
-                pltpu.VMEM((width, width), LOW),
-                pltpu.SemaphoreType.DMA((5,)),
-            ],
-            us=30,
-        )
-
-    def turn(arrays, specs, deps):
-        outs = [(by_block_t(width), shape(width, total_rows))]
-        return call(turn_low_kernel, arrays, specs, outs, (blocks,), 56, deps, name="turn", us=3)[0]
-
-    y1_t = turn([y1], [by_block(width)], outer.sent)
-    deps = outer.turn(y1_t)
-    grad_u, grad_h1, grad_attn, grad_ctx, stat_one, grad_bias_inner = dense_back(deps)
+        deps,
+        name="dense_back",
+        scratch=[
+            pltpu.VMEM((width, width), F32),
+            pltpu.VMEM((inner, width), LOW),
+            pltpu.VMEM((width, inner), LOW),
+            pltpu.VMEM((width, width), LOW),
+            pltpu.SemaphoreType.DMA((5,)),
+        ],
+        us=30,
+    )
     deps = outer.turn(stat_one)
-    up_flow = Flow(*weight_grad(y1_t, grad_u, True, row_count, core, deps, tile=(128, 256)))
+    up_flow = Flow(*weight_grad(y1_t, grad_u, row_count, core, deps, up_parts), line=True, fused=True)
     up_flow.step()
-    deps = up_flow.sent
-    x_t = turn([queries, passages], [queries_spec, passages_spec], deps)
+    x_t = turn([queries, passages], [queries_spec, passages_spec], up_flow.sent)
     deps = up_flow.turn(x_t)
 
     head_dim = width // HEADS
     third = 4 * head_dim
     groups = [(0, 2 * third), (2 * third, third)]
 
-    def attend_back(start, wide, deps):
+    def attend_back(start, wide, deps, extra=()):
         pairs = wide // (2 * head_dim)
         index = start // wide
         cols = pl.BlockSpec((rows_all, wide), lambda i: (i, index))
+        rows = cut + (16 if extra else 0)
         return call(
             partial(attend_back_kernel, (q_dev, q_len, rows_all, head_dim)),
-            (query_lengths, passage_lengths, q, k, v, ctx_t, lse, grad_ctx),
-            [smem, smem]
+            (core, query_lengths, passage_lengths, q, k, v, ctx_t, lse, grad_ctx, x_t, *extra),
+            [smem, smem, smem]
             + [cols] * 3
             + [
                 pl.BlockSpec((wide, rows_all), lambda i: (index, i)),
                 pl.BlockSpec((1, pairs, 8, rows_all), lambda i: (i, index, 0, 0)),
                 cols,
-            ],
+                by_block_t(width),
+            ]
+            + [const_spec(item.shape) for item in extra],
             [
                 (by_block(3 * wide), shape(total_rows, 3 * wide)),
                 (fixed((8, wide)), shape(8, wide, kind=F32)),
-            ],
+            ]
+            + [(fixed((half, rows, 3 * wide)), shape(half, rows, 3 * wide))] * 2,
             (blocks,),
             56,
             deps,
             name="attend_back",
+            scratch=[pltpu.VMEM((width, 3 * wide), F32)],
             us=12,
         )
 
-    grad_a, stat_a = attend_back(*groups[0], deps)
-    mixed = weight_grad(ctx_t, grad_attn, True, row_count, core, [stat_a], room=3 * width, tile=(768, 256))
-    deps = outer.turn(mixed[0]) + up_flow.turn(mixed[0])
-    mixed = weight_grad(x_t, grad_a, True, row_count, core, deps, old=mixed, room=3 * width, tile=(256, 768))
-    mixed_flow = Flow(*mixed)
+    def input_grad(start, wide, grad, base, outs, deps):
+        index = start // wide
+        cols = pl.BlockSpec((width, wide), lambda i: (0, index), pipeline_mode=pl.Buffered(1))
+        return call(
+            input_grad_kernel,
+            (grad, base, w_query, w_key, w_value),
+            [by_block(3 * wide), by_block(width), cols, cols, cols],
+            outs,
+            (blocks,),
+            56,
+            deps,
+            name="input_grad",
+            us=6,
+        )
+
+    grad_a, stat_a, *mixed_parts = attend_back(*groups[0], deps)
+    mixed_flow = Flow(*mixed_parts)
     mixed_flow.step()
-    grad_b, stat_b = attend_back(*groups[1], mixed_flow.sent)
-    deps = [stat_b, *outer.turn(stat_b), *up_flow.turn(stat_b), *mixed_flow.turn(stat_b)]
-
-    extra = (stat_two, stat_one, grad_bias_inner, stat_a, stat_b)
-    last_flow = Flow(*weight_grad(x_t, grad_b, True, row_count, core, deps, extra))
+    deps = mixed_flow.sent + outer.turn(stat_a)
+    (part_grad,) = input_grad(
+        *groups[0], grad_a, grad_attn, [(by_block(width), shape(total_rows, width))], deps
+    )
+    deps = up_flow.turn(part_grad) + mixed_flow.turn(up_flow.kept)
+    extra = (stat_two, stat_one, grad_bias_inner, stat_a)
+    grad_b, stat_b, *last_parts = attend_back(*groups[1], deps, extra)
+    last_flow = Flow(*last_parts)
     last_flow.step()
-    deps = last_flow.sent
-
-    query_grad, passage_grad = call(
-        partial(input_grad_kernel, groups),
-        (grad_a, grad_b, grad_h1, w_query, w_key, w_value),
-        [by_block(3 * wide) for _, wide in groups] + [by_block(width), square, square, square],
+    deps = last_flow.sent + outer.turn(stat_b) + mixed_flow.turn(stat_b) + up_flow.turn(stat_b)
+    query_grad, passage_grad = input_grad(
+        *groups[1],
+        grad_b,
+        part_grad,
         [
             (queries_spec, shape(rows_all, width)),
             (passages_spec, shape(p_dev * rows_all, width)),
         ],
-        (blocks,),
-        56,
         deps,
-        name="input_grad",
-        us=8,
-    )
-    mixed_flow.turn(passage_grad)
-    last_flow.turn(mixed_flow.kept)
-    outer.turn(last_flow.kept)
-    up_flow.turn(outer.kept)
-    mixed_flow.turn(up_flow.kept)
-    last_flow.turn(mixed_flow.kept)
-    last_flow.turn()
-    mixed_flow.turn()
+    )
+    last_flow.turn(passage_grad)
+    mixed_flow.turn(last_flow.kept)
+    outer.turn(mixed_flow.kept)
+    last_flow.turn(outer.kept)
+    up_flow.turn(last_flow.kept)
+    last_flow.turn(up_flow.kept)
+    mixed_flow.turn(last_flow.kept)
     last_flow.turn(mixed_flow.kept)
     flows = [outer, up_flow, mixed_flow, last_flow]
     while not all(flow.done for flow in flows):
         for flow in flows:
             if not flow.done:
                 flow.turn()
-    cut = width // row_count
     turned = pl.pallas_call(
         turn_kernel,
-        out_shape=shape(inner // row_count, width, kind=F32),
+        out_shape=shape(cut_inner, width, kind=F32),
         compiler_params=params,
         name="turn",
     )(outer.kept)
     mixed, last = mixed_flow.kept.astype(F32), last_flow.kept.astype(F32)
     qkv = [
         jnp.concatenate(
-            [mixed[:, width + i * 2 * third : width + (i + 1) * 2 * third], last[:cut, i * third : (i + 1) * third]],
-            1,
+            [mixed[:, i * 2 * third : (i + 1) * 2 * third], last[:cut, i * third : (i + 1) * third]], 1
         )
         for i in range(3)
     ]
+    up_sum = up_flow.kept.astype(F32)
     small = last[cut:]
     return (
         loss[0, 0],
@@ -1025,8 +1060,8 @@
         query_grad.reshape(query_tokens.shape),
         passage_grad.reshape(passage_tokens.shape),
         *qkv,
-        mixed[:, :width],
-        up_flow.kept.astype(F32),
+        up_sum[:, inner:],
+        up_sum[:, :inner],
         turned,
         *[small[i, :cut] for i in range(3)],
         small[8, : inner // row_count],

time: 299 us -> 316 us (1.057)
  Pallas kernels: 195 us -> 203 us
  waiting for transfers between devices: 45.8 us -> 50.4 us
    pallas_call x14 -> x12, Pallas kernels: 189 us -> 198 us  [call(): pl.pallas_call(kernel, grid=grid, in_specs=list(in_specs) + [pl.BlockSpec...]
    convert_element_type x4, other arithmetic: 3 us -> 6.23 us  [shard(): return total.astype(LOW)]
    ppermute x9 -> x10, waiting for transfers between devices: 30.7 us -> 33.1 us  [step(): self.got = [lax.ppermute(self.kept, 'col', self.line[0][1])]]
    ppermute x9 -> x10, starting transfers between devices: 12.4 us -> 14 us  [step(): self.got = [lax.ppermute(self.kept, 'col', self.line[0][1])]]
  transfers between devices with their start and end apart: 32 -> 33, of which waited for: 15 -> 14; matrix products, arithmetic and copies ran while one was open for 3% -> 4% of each run, Pallas kernels for 31% -> 32%
where the time goes in v2:
time: 316 us; the launch traced here: 313 us
  Pallas kernels  203 us (64%)
  waiting for transfers between devices  50.4 us (16%)
  starting transfers between devices  37.6 us (12%)
  other arithmetic  15 us (5%)
  local copies, waits for them, and re-layouts  5.16 us (2%)
    pallas_call x12, Pallas kernels, call(): pl.pallas_call(kernel, grid=grid, in_specs=list(in_specs) + [pl.BlockSpec...  198 us
    ppermute x10, waiting for transfers between devices, step(): self.got = [lax.ppermute(self.kept, 'col', self.line[0][1])]  33.1 us
    ppermute x16, starting transfers between devices, step(): lax.ppermute(sent, 'row', [(i, i ^ mask) for i in range(size)])  14.2 us
    ppermute x10, starting transfers between devices, step(): self.got = [lax.ppermute(self.kept, 'col', self.line[0][1])]  14 us
    ppermute x7, waiting for transfers between devices, gather_all(): pieces.append(lax.ppermute(piece, name, pairs))  11.8 us
    ppermute x7, starting transfers between devices, gather_all(): pieces.append(lax.ppermute(piece, name, pairs))  9.31 us
  transfers between devices with their start and end apart: 33, of which 14 were waited for; matrix products, arithmetic and copies ran while one was open for 4% of the time, Pallas kernels for 32%

profile of v2, /device:TPU:0, one launch (start us, length us, event | category | flops | bytes accessed | tf_op | source)
XLA Modules:
  0.0 312.7 jit_solution(18213561622885944008)
XLA Ops:
  0.7 20.8 %attend.1 = (bf16[1536,768]{1,0:T(8,128)(2,1)}, bf16[1536,768]{1,0:T(8,128)(2,1)}, bf16[1536,768]{1,0:T(8,128)(2,1)}, bf16[768,1536]{1,0:T(8,128)(2,1)}, f32[3,6,8,512]{3,2,1,0:T(8,128)}) custom-call(s32[4]{0:T(128)} %refs_1_.9, s32[2]{0:T(128)} %refs_2_.8, bf16[512,768]{1,0:T(8,128)(2,1)} %bitcast.69, bf16[1024,768]{1,0:T(8,128)(2,1)} %bitcast.65, ...), custom_call_target="tpu_custom_call" | custom-call | flops 287500000 | tf_op jit(solution)/shard_map/attend/pallas_call | solution.py:623
  21.5 50.2 %dense.1 = (bf16[1536,768]{1,0:T(8,128)(2,1)}, bf16[1536,768]{1,0:T(8,128)(2,1)}, bf16[1536,3072]{1,0:T(8,128)(2,1)}, bf16[1536,3072]{1,0:T(8,128)(2,1)}, bf16[1...) custom-call(s32[4]{0:T(128)} %refs_1_.9, ...), custom_call_target="tpu_custom_call" | custom-call | flops 460000000 | tf_op jit(solution)/shard_map/dense/pallas_call | solution.py:623
  71.7 3.1 collective-permute-start.2
  74.8 2.6 collective-permute-start.1
  77.4 2.3 collective-permute-done.1
  79.7 3.5 %collective-permute-done = bf16[8,896]{1,0:T(8,128)(2,1)S(1)} collective-permute-done((bf16[8,896]{1,0:T(8,128)(2,1)}, bf16[8,896]{1,0:T(8,128)(2,1)S(1)}, u32[]{:S(2)}, u32[]{:S(2)}) %collective-permute-start) | collective-permute-done | bytes 14368 | tf_op jit(solution)/shard_map/ppermute | solution.py:769
  83.8 1.6 collective-permute-start.5
  89.6 2.4 collective-permute-done.3
  94.6 2.9 loss.1
  97.5 18.1 %outer_grad.1 = (bf16[1536,768]{1,0:T(8,128)(2,1)}, f32[8,768]{1,0:T(8,128)}, bf16[4,768,384]{2,1,0:T(8,128)(2,1)}, bf16[4,768,384]{2,1,0:T(8,128)(2,1)}) custom-call(s32[1]{0:T(128)} %bitcast.6.refs_0_, s32[4]{0:T(128)} %refs_1_.9, s32[2]{0:T(128)} %refs_2_.8, f32[8,768]{1,0:T(8,128)} %get-tuple-element.90.refs_3_, ...), custom_call_target="tpu_custom_call" | custom-call | flops 184000000 | tf_op jit(solution)/shard_map/outer_grad/pallas_call | solution.py:623
  115.7 4.4 %turn.3.refs_1_ = bf16[768,1536]{1,0:T(8,128)(2,1)} custom-call(bf16[1536,768]{1,0:T(8,128)(2,1)} %get-tuple-element.96.refs_0_), custom_call_target="tpu_custom_call" | custom-call | flops 34500000 | tf_op jit(solution)/shard_map/turn/pallas_call | solution.py:623
  120.4 1.6 fusion.7
  122.4 1.5 collective-permute-start.9
  125.4 38.8 %dense_back.1 = (bf16[1536,3072]{1,0:T(8,128)(2,1)}, bf16[1536,768]{1,0:T(8,128)(2,1)}, bf16[1536,768]{1,0:T(8,128)(2,1)}, f32[8,768]{1,0:T(8,128)}, f32[8,3072]...) custom-call(s32[1]{0:T(128)} %bitcast.6.refs_0_, bf16[1536,768]{1,0:T(8,128)(2,1)} %get-tuple-element.99.refs_1_, ...), custom_call_target="tpu_custom_call" | custom-call | flops 345000000 | tf_op jit(solution)/shard_map/dense_back/pallas_call | solution.py:623
  164.6 12.0 %weight_grad.1 = (bf16[4,96,3840]{2,1,0:T(8,128)(2,1)}, bf16[4,96,3840]{2,1,0:T(8,128)(2,1)}) custom-call(s32[1]{0:T(128)} %bitcast.6.refs_0_, bf16[768,1536]{1,0:T(8,128)(2,1)} %turn.3.refs_1_, bf16[1536,3072]{1,0:T(8,128)(2,1)} %get-tuple-element.105.refs_2_, ...), custom_call_target="tpu_custom_call", output_to_operand_aliasing={{0}: (3, {}), {1}: (4, {})} | custom-call | flops 138000000 | tf_op jit(solution)/shard_map/weight_grad/pallas_call | solution.py:623
  176.6 4.8 %turn.4.refs_9_ = bf16[768,1536]{1,0:T(8,128)(2,1)} custom-call(bf16[512,768]{1,0:T(8,128)(2,1)} %bitcast.71, bf16[1024,768]{1,0:T(8,128)(2,1)} %bitcast.67), custom_call_target="tpu_custom_call" | custom-call | flops 34500000 | tf_op jit(solution)/shard_map/turn/pallas_call | solution.py:623
  182.2 1.8 fusion.3
  188.7 21.8 %attend_back.2 = (bf16[1536,1536]{1,0:T(8,128)(2,1)}, f32[8,512]{1,0:T(8,128)}, bf16[4,96,1536]{2,1,0:T(8,128)(2,1)}, bf16[4,96,1536]{2,1,0:T(8,128)(2,1)}) custom-call(s32[1]{0:T(128)} %bitcast.6.refs_0_, s32[4]{0:T(128)} %refs_1_.9, s32[2]{0:T(128)} %refs_2_.8, bf16[1536,768]{1,0:T(8,128)(2,1)} %get-tuple-element.113.refs_3_, ...), custom_call_target="tpu_custom_call" | custom-call | flops 138000000 | tf_op jit(solution)/shard_map/attend_back/pallas_call | solution.py:623
  213.0 8.1 %input_grad.2.refs_1_ = bf16[1536,768]{1,0:T(8,128)(2,1)} custom-call(bf16[1536,1536]{1,0:T(8,128)(2,1)} %get-tuple-element.118.refs_0_, bf16[1536,768]{1,0:T(8,128)(2,1)} %get-tuple-element.119.refs_1_, bf16[768,768]{1,0:T(8,128)(2,1)} %refs_2_.9, bf16[768,768]{1,0:T(8,128)(2,1)} %refs_3_.3, bf16[768,768]{1,0:T(8,128)(2,1)} %refs_4_.5), custom_call_target="tpu_custom_call" | custom-call | flops 69000000 | tf_op jit(solution)/shard_map/input_grad/pallas_call | solution.py:623
  227.5 2.1 collective-permute-start.21
  229.6 12.5 %attend_back.3 = (bf16[1536,768]{1,0:T(8,128)(2,1)}, f32[8,256]{1,0:T(8,128)}, bf16[4,112,768]{2,1,0:T(8,128)(2,1)}, bf16[4,112,768]{2,1,0:T(8,128)(2,1)}) custom-call(s32[1]{0:T(128)} %bitcast.6.refs_0_, s32[4]{0:T(128)} %refs_1_.9, s32[2]{0:T(128)} %refs_2_.8, bf16[1536,768]{1,0:T(8,128)(2,1)} %get-tuple-element.113.refs_3_, ...), custom_call_target="tpu_custom_call" | custom-call | flops 138000000 | tf_op jit(solution)/shard_map/attend_back/pallas_call | solution.py:623
  245.1 3.5 %collective-permute-start.23 = (bf16[96,1536]{1,0:T(8,128)(2,1)S(1)}, bf16[96,1536]{1,0:T(8,128)(2,1)S(1)}, u32[]{:S(2)}, u32[]{:S(2)}) collective-permute-start(bf16[96,1536]{1,0:T(8,128)(2,1)S(1)} %add_convert_fusion.9), channel_id=1, source_target_pairs={{0,1},{1,0},{2,3},{3,2},{4,5},{5,4},{6,7},{7,6},{8,9},{9,8},{10,11... | collective-permute-start | bytes 884744 | tf_op jit(solution)/shard_map/ppermute | solution.py:722
  249.5 6.1 %input_grad.3 = (bf16[512,768]{1,0:T(8,128)(2,1)}, bf16[1024,768]{1,0:T(8,128)(2,1)}) custom-call(bf16[1536,768]{1,0:T(8,128)(2,1)} %get-tuple-element.130.refs_0_, bf16[1536,768]{1,0:T(8,128)(2,1)} %input_grad.2.refs_1_, bf16[768,768]{1,0:T(8,128)(2,1)} %refs_2_.9, bf16[768,768]{1,0:T(8,128)(2,1)} %refs_3_.3, bf16[768,768]{1,0:T(8,128)(2,1)} %refs_4_.5), custom_call_target="tpu_custom_call" | custom-call | flops 69000000 | tf_op jit(solution)/shard_map/input_grad/pallas_call | solution.py:623
  257.0 10.6 %collective-permute-done.23 = bf16[96,1536]{1,0:T(8,128)(2,1)S(1)} collective-permute-done((bf16[96,1536]{1,0:T(8,128)(2,1)S(1)}, bf16[96,1536]{1,0:T(8,128)(2,1)S(1)}, u32[]{:S(2)}, u32[]{:S(2)}) %collective-permute-start.23) | collective-permute-done | bytes 294944 | tf_op jit(solution)/shard_map/ppermute | solution.py:722
  271.3 1.9 broadcast_select_fusion.part_ref
  273.3 2.7 collective-permute-done.27
  276.0 1.7 collective-permute-done.26
  277.8 2.2 collective-permute-start.29
  281.2 2.3 turn.5
  283.7 2.9 collective-permute-done.29
  288.1 8.8 %collective-permute-done.31 = bf16[112,768]{1,0:T(8,128)(2,1)S(1)} collective-permute-done((bf16[112,768]{1,0:T(8,128)(2,1)S(1)}, bf16[112,768]{1,0:T(8,128)(2,1)S(1)}, u32[]{:S(2)}, u32[]{:S(2)}) %collective-permute-start.31) | collective-permute-done | bytes 172064 | tf_op jit(solution)/shard_map/ppermute | solution.py:722
  299.7 10.9 %collective-permute-done.32 = bf16[96,3840]{1,0:T(8,128)(2,1)S(1)} collective-permute-done((bf16[96,3840]{1,0:T(8,128)(2,1)S(1)}, bf16[96,3840]{1,0:T(8,128)(2,1)S(1)}, u32[]{:S(2)}, u32[]{:S(2)}) %collective-permute-start.32) | collective-permute-done | bytes 737312 | tf_op jit(solution)/shard_map/ppermute | solution.py:722
  (89 shorter events, 41.0 us)
Async XLA Ops:
  71.7 5.7 %collective-permute-start.2 = (bf16[8,896]{1,0:T(8,128)(2,1)}, bf16[8,896]{1,0:T(8,128)(2,1)S(1)}, u32[]{:S(2)}, u32[]{:S(2)}) collective-permute-start(bf16[8,896]{1,0:T(8,128)(2,1)} %get-tuple-element.85.own_ref), channel_id=1, source_target_pairs={{0,1},{1,0},{2,3},{3,2},{4,5},{5,4},{6,7},{7,6},{8,9},{9,8},{10,11... | collective-permute-start | bytes 43016 | tf_op jit(solution)/shard_map/ppermute | solution.py:769
  74.8 4.9 %collective-permute-start.1 = (bf16[8,896]{1,0:T(8,128)(2,1)}, bf16[8,896]{1,0:T(8,128)(2,1)S(1)}, u32[]{:S(2)}, u32[]{:S(2)}) collective-permute-start(bf16[8,896]{1,0:T(8,128)(2,1)} %get-tuple-element.85.own_ref), channel_id=1, source_target_pairs={{0,2},{1,3},{2,0},{3,1},{4,6},{5,7},{6,4},{7,5},{8,10},{9,11},{10,... | collective-permute-start | bytes 43016 | tf_op jit(solution)/shard_map/ppermute | solution.py:769
  77.4 5.7 %collective-permute-start = (bf16[8,896]{1,0:T(8,128)(2,1)}, bf16[8,896]{1,0:T(8,128)(2,1)S(1)}, u32[]{:S(2)}, u32[]{:S(2)}) collective-permute-start(bf16[8,896]{1,0:T(8,128)(2,1)} %get-tuple-element.85.own_ref), channel_id=1, source_target_pairs={{0,3},{1,2},{2,1},{3,0},{4,7},{5,6},{6,5},{7,4},{8,11},{9,10},{10,... | collective-permute-start | bytes 43016 | tf_op jit(solution)/shard_map/ppermute | solution.py:769
  83.8 4.4 %collective-permute-start.5 = (bf16[32,896]{1,0:T(8,128)(2,1)S(1)}, bf16[32,896]{1,0:T(8,128)(2,1)S(1)}, u32[]{:S(2)}, u32[]{:S(2)}) collective-permute-start(bf16[32,896]{1,0:T(8,128)(2,1)S(1)} %pad_maximum_fusion.5), channel_id=1, source_target_pairs={{0,8},{4,12},{8,0},{12,4},{16,24},{20,28},{24,16},{28,20},{1,9},{5... | collective-permute-start | bytes 172040 | tf_op jit(solution)/shard_map/ppermute | solution.py:769
  85.4 4.2 %collective-permute-start.4 = (bf16[32,896]{1,0:T(8,128)(2,1)S(1)}, bf16[32,896]{1,0:T(8,128)(2,1)S(1)}, u32[]{:S(2)}, u32[]{:S(2)}) collective-permute-start(bf16[32,896]{1,0:T(8,128)(2,1)S(1)} %pad_maximum_fusion.5), channel_id=1, source_target_pairs={{0,16},{4,20},{8,24},{12,28},{16,0},{20,4},{24,8},{28,12},{1,17},{... | collective-permute-start | bytes 172040 | tf_op jit(solution)/shard_map/ppermute | solution.py:769
  86.9 5.1 %collective-permute-start.3 = (bf16[32,896]{1,0:T(8,128)(2,1)S(1)}, bf16[32,896]{1,0:T(8,128)(2,1)S(1)}, u32[]{:S(2)}, u32[]{:S(2)}) collective-permute-start(bf16[32,896]{1,0:T(8,128)(2,1)S(1)} %pad_maximum_fusion.5), channel_id=1, source_target_pairs={{0,24},{4,28},{8,16},{12,20},{16,8},{20,12},{24,0},{28,4},{1,25},{... | collective-permute-start | bytes 172040 | tf_op jit(solution)/shard_map/ppermute | solution.py:769
  115.6 4.7 %collective-permute-start.7 = (bf16[4,768,384]{2,1,0:T(8,128)(2,1)}, bf16[4,768,384]{2,1,0:T(8,128)(2,1)S(1)}, u32[]{:S(2)}, u32[]{:S(2)}) collective-permute-start(bf16[4,768,384]{2,1,0:T(8,128)(2,1)} %get-tuple-element.95), channel_id=1, source_target_pairs={{0,4},{4,0},{8,12},{12,8},{16,20},{20,16},{24,28},{28,24},{1,5},{5... | collective-permute-start | bytes 7077896 | tf_op jit(solution)/shard_map/ppermute | solution.py:717
  121.9 42.3 %collective-permute-start.10 = (bf16[768,384]{1,0:T(8,128)(2,1)}, bf16[768,384]{1,0:T(8,128)(2,1)S(1)}, u32[]{:S(2)}, u32[]{:S(2)}) collective-permute-start(bf16[768,384]{1,0:T(8,128)(2,1)} %get-tuple-element.153), channel_id=1, source_target_pairs={{0,24},{4,28},{8,16},{12,20},{16,8},{20,12},{24,0},{28,4},{1,25},{... | collective-permute-start | bytes 1769480 | tf_op jit(solution)/shard_map/ppermute | solution.py:717
  122.4 41.8 %collective-permute-start.9 = (bf16[768,384]{1,0:T(8,128)(2,1)}, bf16[768,384]{1,0:T(8,128)(2,1)S(1)}, u32[]{:S(2)}, u32[]{:S(2)}) collective-permute-start(bf16[768,384]{1,0:T(8,128)(2,1)} %get-tuple-element.154), channel_id=1, source_target_pairs={{0,16},{4,20},{8,24},{12,28},{16,0},{20,4},{24,8},{28,12},{1,17},{... | collective-permute-start | bytes 1769480 | tf_op jit(solution)/shard_map/ppermute | solution.py:717
  123.9 40.3 %collective-permute-start.8 = (bf16[768,384]{1,0:T(8,128)(2,1)S(1)}, bf16[768,384]{1,0:T(8,128)(2,1)S(1)}, u32[]{:S(2)}, u32[]{:S(2)}) collective-permute-start(bf16[768,384]{1,0:T(8,128)(2,1)S(1)} %get-tuple-element.155), channel_id=1, source_target_pairs={{0,8},{4,12},{8,0},{12,4},{16,24},{20,28},{24,16},{28,20},{1,9},{5... | collective-permute-start | bytes 1769480 | tf_op jit(solution)/shard_map/ppermute | solution.py:717
  176.6 5.6 %collective-permute-start.11 = (bf16[4,96,3840]{2,1,0:T(8,128)(2,1)}, bf16[4,96,3840]{2,1,0:T(8,128)(2,1)S(1)}, u32[]{:S(2)}, u32[]{:S(2)}) collective-permute-start(bf16[4,96,3840]{2,1,0:T(8,128)(2,1)} %get-tuple-element.109), channel_id=1, source_target_pairs={{0,4},{4,0},{8,12},{12,8},{16,20},{20,16},{24,28},{28,24},{1,5},{5... | collective-permute-start | bytes 8847368 | tf_op jit(solution)/shard_map/ppermute | solution.py:717
  183.9 37.2 %collective-permute-start.14 = (bf16[96,3840]{1,0:T(8,128)(2,1)}, bf16[96,3840]{1,0:T(8,128)(2,1)S(1)}, u32[]{:S(2)}, u32[]{:S(2)}) collective-permute-start(bf16[96,3840]{1,0:T(8,128)(2,1)} %get-tuple-element.149), channel_id=1, source_target_pairs={{0,24},{4,28},{8,16},{12,20},{16,8},{20,12},{24,0},{28,4},{1,25},{... | collective-permute-start | bytes 2211848 | tf_op jit(solution)/shard_map/ppermute | solution.py:717
  184.4 36.7 %collective-permute-start.13 = (bf16[96,3840]{1,0:T(8,128)(2,1)}, bf16[96,3840]{1,0:T(8,128)(2,1)S(1)}, u32[]{:S(2)}, u32[]{:S(2)}) collective-permute-start(bf16[96,3840]{1,0:T(8,128)(2,1)} %get-tuple-element.150), channel_id=1, source_target_pairs={{0,16},{4,20},{8,24},{12,28},{16,0},{20,4},{24,8},{28,12},{1,17},{... | collective-permute-start | bytes 2211848 | tf_op jit(solution)/shard_map/ppermute | solution.py:717
  185.9 35.2 %collective-permute-start.12 = (bf16[96,3840]{1,0:T(8,128)(2,1)S(1)}, bf16[96,3840]{1,0:T(8,128)(2,1)S(1)}, u32[]{:S(2)}, u32[]{:S(2)}) collective-permute-start(bf16[96,3840]{1,0:T(8,128)(2,1)S(1)} %get-tuple-element.151), channel_id=1, source_target_pairs={{0,8},{4,12},{8,0},{12,4},{16,24},{20,28},{24,16},{28,20},{1,9},{5... | collective-permute-start | bytes 2211848 | tf_op jit(solution)/shard_map/ppermute | solution.py:717
  187.4 23.1 %collective-permute-start.15 = (bf16[768,384]{1,0:T(8,128)(2,1)S(1)}, bf16[768,384]{1,0:T(8,128)(2,1)S(1)}, u32[]{:S(2)}, u32[]{:S(2)}) collective-permute-start(bf16[768,384]{1,0:T(8,128)(2,1)S(1)} %add_convert_fusion.4), channel_id=1, source_target_pairs={{0,1},{3,2},{4,5},{7,6},{8,9},{11,10},{12,13},{15,14},{16,17},{19,... | collective-permute-start | bytes 1769480 | tf_op jit(solution)/shard_map/ppermute | solution.py:722
  211.5 30.6 %collective-permute-start.17 = (bf16[768,384]{1,0:T(8,128)(2,1)}, bf16[768,384]{1,0:T(8,128)(2,1)}, u32[]{:S(2)}, u32[]{:S(2)}) collective-permute-start(bf16[768,384]{1,0:T(8,128)(2,1)} %add.218), channel_id=1, source_target_pairs={{1,2},{2,1},{5,6},{6,5},{9,10},{10,9},{13,14},{14,13},{17,18},{18,... | collective-permute-start | bytes 1769480 | tf_op jit(solution)/shard_map/ppermute | solution.py:722
  213.0 8.5 %collective-permute-start.16 = (bf16[4,96,1536]{2,1,0:T(8,128)(2,1)}, bf16[4,96,1536]{2,1,0:T(8,128)(2,1)}, u32[]{:S(2)}, u32[]{:S(2)}) collective-permute-start(bf16[4,96,1536]{2,1,0:T(8,128)(2,1)} %get-tuple-element.120), channel_id=1, source_target_pairs={{0,4},{4,0},{8,12},{12,8},{16,20},{20,16},{24,28},{28,24},{1,5},{5... | collective-permute-start | bytes 3538952 | tf_op jit(solution)/shard_map/ppermute | solution.py:717
  223.9 19.7 %collective-permute-start.20 = (bf16[96,1536]{1,0:T(8,128)(2,1)S(1)}, bf16[96,1536]{1,0:T(8,128)(2,1)S(1)}, u32[]{:S(2)}, u32[]{:S(2)}) collective-permute-start(bf16[96,1536]{1,0:T(8,128)(2,1)S(1)} %get-tuple-element.157), channel_id=1, source_target_pairs={{0,24},{4,28},{8,16},{12,20},{16,8},{20,12},{24,0},{28,4},{1,25},{... | collective-permute-start | bytes 884744 | tf_op jit(solution)/shard_map/ppermute | solution.py:717
  224.5 20.5 %collective-permute-start.19 = (bf16[96,1536]{1,0:T(8,128)(2,1)S(1)}, bf16[96,1536]{1,0:T(8,128)(2,1)S(1)}, u32[]{:S(2)}, u32[]{:S(2)}) collective-permute-start(bf16[96,1536]{1,0:T(8,128)(2,1)S(1)} %get-tuple-element.158), channel_id=1, source_target_pairs={{0,16},{4,20},{8,24},{12,28},{16,0},{20,4},{24,8},{28,12},{1,17},{... | collective-permute-start | bytes 884744 | tf_op jit(solution)/shard_map/ppermute | solution.py:717
  226.0 18.9 %collective-permute-start.18 = (bf16[96,1536]{1,0:T(8,128)(2,1)S(1)}, bf16[96,1536]{1,0:T(8,128)(2,1)S(1)}, u32[]{:S(2)}, u32[]{:S(2)}) collective-permute-start(bf16[96,1536]{1,0:T(8,128)(2,1)S(1)} %get-tuple-element.159), channel_id=1, source_target_pairs={{0,8},{4,12},{8,0},{12,4},{16,24},{20,28},{24,16},{28,20},{1,9},{5... | collective-permute-start | bytes 884744 | tf_op jit(solution)/shard_map/ppermute | solution.py:717
  227.5 21.1 %collective-permute-start.21 = (bf16[96,3840]{1,0:T(8,128)(2,1)S(1)}, bf16[96,3840]{1,0:T(8,128)(2,1)S(1)}, u32[]{:S(2)}, u32[]{:S(2)}) collective-permute-start(bf16[96,3840]{1,0:T(8,128)(2,1)S(1)} %add_all.1), channel_id=1, source_target_pairs={{0,1},{3,2},{4,5},{7,6},{8,9},{11,10},{12,13},{15,14},{16,17},{19,... | collective-permute-start | bytes 2211848 | tf_op jit(solution)/shard_map/ppermute | solution.py:722
  242.2 13.5 %collective-permute-start.22 = (bf16[4,112,768]{2,1,0:T(8,128)(2,1)}, bf16[4,112,768]{2,1,0:T(8,128)(2,1)}, u32[]{:S(2)}, u32[]{:S(2)}) collective-permute-start(bf16[4,112,768]{2,1,0:T(8,128)(2,1)} %get-tuple-element.131), channel_id=1, source_target_pairs={{0,4},{4,0},{8,12},{12,8},{16,20},{20,16},{24,28},{28,24},{1,5},{5... | collective-permute-start | bytes 2064392 | tf_op jit(solution)/shard_map/ppermute | solution.py:717
  243.6 26.2 %collective-permute-start.24 = (bf16[768,384]{1,0:T(8,128)(2,1)S(1)}, bf16[768,384]{1,0:T(8,128)(2,1)}, u32[]{:S(2)}, u32[]{:S(2)}) collective-permute-start(bf16[768,384]{1,0:T(8,128)(2,1)S(1)} %add.222), channel_id=1, source_target_pairs={{1,0},{2,3},{5,4},{6,7},{9,8},{10,11},{13,12},{14,15},{17,16},{18,... | collective-permute-start | bytes 1769480 | tf_op jit(solution)/shard_map/ppermute | solution.py:722
  245.1 22.5 %collective-permute-start.23 = (bf16[96,1536]{1,0:T(8,128)(2,1)S(1)}, bf16[96,1536]{1,0:T(8,128)(2,1)S(1)}, u32[]{:S(2)}, u32[]{:S(2)}) collective-permute-start(bf16[96,1536]{1,0:T(8,128)(2,1)S(1)} %add_convert_fusion.9), channel_id=1, source_target_pairs={{0,1},{1,0},{2,3},{3,2},{4,5},{5,4},{6,7},{7,6},{8,9},{9,8},{10,11... | collective-permute-start | bytes 884744 | tf_op jit(solution)/shard_map/ppermute | solution.py:722
  248.8 34.7 %collective-permute-start.28 = (bf16[96,3840]{1,0:T(8,128)(2,1)S(1)}, bf16[96,3840]{1,0:T(8,128)(2,1)S(1)}, u32[]{:S(2)}, u32[]{:S(2)}) collective-permute-start(bf16[96,3840]{1,0:T(8,128)(2,1)S(1)} %add.227), channel_id=1, source_target_pairs={{1,2},{2,1},{5,6},{6,5},{9,10},{10,9},{13,14},{14,13},{17,18},{18,... | collective-permute-start | bytes 2211848 | tf_op jit(solution)/shard_map/ppermute | solution.py:722
  267.7 20.3 %collective-permute-start.30 = (bf16[96,1536]{1,0:T(8,128)(2,1)S(1)}, bf16[96,1536]{1,0:T(8,128)(2,1)S(1)}, u32[]{:S(2)}, u32[]{:S(2)}) collective-permute-start(bf16[96,1536]{1,0:T(8,128)(2,1)S(1)} %add.229), channel_id=1, source_target_pairs={{0,2},{1,3},{2,0},{3,1},{4,6},{5,7},{6,4},{7,5},{8,10},{9,11},{10,... | collective-permute-start | bytes 884744 | tf_op jit(solution)/shard_map/ppermute | solution.py:722
  267.7 8.2 %collective-permute-start.27 = (bf16[112,768]{1,0:T(8,128)(2,1)S(1)}, bf16[112,768]{1,0:T(8,128)(2,1)S(1)}, u32[]{:S(2)}, u32[]{:S(2)}) collective-permute-start(bf16[112,768]{1,0:T(8,128)(2,1)S(1)} %get-tuple-element.161), channel_id=1, source_target_pairs={{0,24},{4,28},{8,16},{12,20},{16,8},{20,12},{24,0},{28,4},{1,25},{... | collective-permute-start | bytes 516104 | tf_op jit(solution)/shard_map/ppermute | solution.py:717
  268.3 9.4 %collective-permute-start.26 = (bf16[112,768]{1,0:T(8,128)(2,1)S(1)}, bf16[112,768]{1,0:T(8,128)(2,1)S(1)}, u32[]{:S(2)}, u32[]{:S(2)}) collective-permute-start(bf16[112,768]{1,0:T(8,128)(2,1)S(1)} %get-tuple-element.162), channel_id=1, source_target_pairs={{0,16},{4,20},{8,24},{12,28},{16,0},{20,4},{24,8},{28,12},{1,17},{... | collective-permute-start | bytes 516104 | tf_op jit(solution)/shard_map/ppermute | solution.py:717
  269.8 7.9 %collective-permute-start.25 = (bf16[112,768]{1,0:T(8,128)(2,1)S(1)}, bf16[112,768]{1,0:T(8,128)(2,1)S(1)}, u32[]{:S(2)}, u32[]{:S(2)}) collective-permute-start(bf16[112,768]{1,0:T(8,128)(2,1)S(1)} %get-tuple-element.163), channel_id=1, source_target_pairs={{0,8},{4,12},{8,0},{12,4},{16,24},{20,28},{24,16},{28,20},{1,9},{5... | collective-permute-start | bytes 516104 | tf_op jit(solution)/shard_map/ppermute | solution.py:717
  277.8 8.8 %collective-permute-start.29 = (bf16[112,768]{1,0:T(8,128)(2,1)S(1)}, bf16[112,768]{1,0:T(8,128)(2,1)S(1)}, u32[]{:S(2)}, u32[]{:S(2)}) collective-permute-start(bf16[112,768]{1,0:T(8,128)(2,1)S(1)} %add_convert_fusion.14), channel_id=1, source_target_pairs={{0,1},{1,0},{2,3},{3,2},{4,5},{5,4},{6,7},{7,6},{8,9},{9,8},{10,11... | collective-permute-start | bytes 516104 | tf_op jit(solution)/shard_map/ppermute | solution.py:722
  286.6 10.3 %collective-permute-start.31 = (bf16[112,768]{1,0:T(8,128)(2,1)S(1)}, bf16[112,768]{1,0:T(8,128)(2,1)S(1)}, u32[]{:S(2)}, u32[]{:S(2)}) collective-permute-start(bf16[112,768]{1,0:T(8,128)(2,1)S(1)} %add.237), channel_id=1, source_target_pairs={{0,2},{1,3},{2,0},{3,1},{4,6},{5,7},{6,4},{7,5},{8,10},{9,11},{10,... | collective-permute-start | bytes 516104 | tf_op jit(solution)/shard_map/ppermute | solution.py:722
  286.7 23.9 %collective-permute-start.32 = (bf16[96,3840]{1,0:T(8,128)(2,1)S(1)}, bf16[96,3840]{1,0:T(8,128)(2,1)S(1)}, u32[]{:S(2)}, u32[]{:S(2)}) collective-permute-start(bf16[96,3840]{1,0:T(8,128)(2,1)S(1)} %add.236), channel_id=1, source_target_pairs={{1,0},{2,3},{5,4},{6,7},{9,8},{10,11},{13,12},{14,15},{17,16},{18,... | collective-permute-start | bytes 2211848 | tf_op jit(solution)/shard_map/ppermute | solution.py:722
  (5 other events, 19.2 us)

commit v3 on v2

--- a/solution.py
+++ b/solution.py
@@ -610,7 +610,7 @@
     return pl.BlockSpec(shape, lambda i: (0,) * len(shape), pipeline_mode=pl.Buffered(1))
 
 
-def call(body, operands, in_specs, outs, grid, room, deps=(), old=(), name=None, scratch=(), us=10):
+def call(body, operands, in_specs, outs, grid, room, deps=(), old=(), name=None, scratch=(), us=20_000):
     count, extra = len(operands), len(old)
     if deps:
         tied = min(range(count), key=lambda i: operands[i].size)
@@ -654,7 +654,6 @@
         deps,
         old,
         name="weight_grad",
-        us=12,
     )
 
 
@@ -832,7 +831,7 @@
         (blocks,),
         56,
         name="attend",
-        us=25,
+
     )
 
     rows_part = rows_all // 2
@@ -873,7 +872,7 @@
             pltpu.VMEM((inner, width), LOW),
             pltpu.SemaphoreType.DMA((3,)),
         ],
-        us=40,
+
     )
 
     gathered = gather_all(payload)
@@ -908,14 +907,13 @@
         56,
         name="outer_grad",
         scratch=[pltpu.VMEM((width, total_rows), LOW)],
-        us=16,
     )
     outer = Flow(*outer_parts, line=True)
     outer.step()
 
     def turn(arrays, specs, deps):
         outs = [(by_block_t(width), shape(width, total_rows))]
-        return call(turn_low_kernel, arrays, specs, outs, (blocks,), 56, deps, name="turn", us=3)[0]
+        return call(turn_low_kernel, arrays, specs, outs, (blocks,), 56, deps, name="turn")[0]
 
     y1_t = turn([y1], [by_block(width)], outer.sent)
     deps = outer.turn(y1_t)
@@ -945,12 +943,12 @@
             pltpu.VMEM((width, width), LOW),
             pltpu.SemaphoreType.DMA((5,)),
         ],
-        us=30,
     )
     deps = outer.turn(stat_one)
     up_flow = Flow(*weight_grad(y1_t, grad_u, row_count, core, deps, up_parts), line=True, fused=True)
     up_flow.step()
-    x_t = turn([queries, passages], [queries_spec, passages_spec], up_flow.sent)
+    deps = up_flow.sent + outer.turn(up_flow.sent[0])
+    x_t = turn([queries, passages], [queries_spec, passages_spec], deps)
     deps = up_flow.turn(x_t)
 
     head_dim = width // HEADS
@@ -984,10 +982,9 @@
             deps,
             name="attend_back",
             scratch=[pltpu.VMEM((width, 3 * wide), F32)],
-            us=12,
         )
 
-    def input_grad(start, wide, grad, base, outs, deps):
+    def input_grad(start, wide, grad, base, outs, deps, us):
         index = start // wide
         cols = pl.BlockSpec((width, wide), lambda i: (0, index), pipeline_mode=pl.Buffered(1))
         return call(
@@ -999,7 +996,7 @@
             56,
             deps,
             name="input_grad",
-            us=6,
+            us=us,
         )
 
     grad_a, stat_a, *mixed_parts = attend_back(*groups[0], deps)
@@ -1007,7 +1004,7 @@
     mixed_flow.step()
     deps = mixed_flow.sent + outer.turn(stat_a)
     (part_grad,) = input_grad(
-        *groups[0], grad_a, grad_attn, [(by_block(width), shape(total_rows, width))], deps
+        *groups[0], grad_a, grad_attn, [(by_block(width), shape(total_rows, width))], deps, 0
     )
     deps = up_flow.turn(part_grad) + mixed_flow.turn(up_flow.kept)
     extra = (stat_two, stat_one, grad_bias_inner, stat_a)
@@ -1024,13 +1021,17 @@
             (passages_spec, shape(p_dev * rows_all, width)),
         ],
         deps,
+        20_000,
     )
     last_flow.turn(passage_grad)
     mixed_flow.turn(last_flow.kept)
-    outer.turn(mixed_flow.kept)
-    last_flow.turn(outer.kept)
-    up_flow.turn(last_flow.kept)
-    last_flow.turn(up_flow.kept)
+    up_flow.turn(mixed_flow.kept)
+    outs = [(fixed((cut_inner, width)), shape(cut_inner, width, kind=F32))]
+    (turned,) = call(
+        turn_kernel, (outer.kept,), [const_spec((width, cut_inner))], outs, (1,), 56, [up_flow.kept], name="turn"
+    )
+    last_flow.turn(turned)
+    last_flow.turn()
     mixed_flow.turn(last_flow.kept)
     last_flow.turn(mixed_flow.kept)
     flows = [outer, up_flow, mixed_flow, last_flow]
@@ -1038,12 +1039,6 @@
         for flow in flows:
             if not flow.done:
                 flow.turn()
-    turned = pl.pallas_call(
-        turn_kernel,
-        out_shape=shape(cut_inner, width, kind=F32),
-        compiler_params=params,
-        name="turn",
-    )(outer.kept)
     mixed, last = mixed_flow.kept.astype(F32), last_flow.kept.astype(F32)
     qkv = [
         jnp.concatenate(

time: 316 us -> 333 us (1.054)
  other arithmetic: 15 us -> 36.4 us
  waiting for transfers between devices: 50.4 us -> 29 us
  starting transfers between devices: 37.6 us -> 53.4 us
    ppermute x10, waiting for transfers between devices: 33.1 us -> 14.5 us  [step(): self.got = [lax.ppermute(self.kept, 'col', self.line[0][1])]]
    ppermute x10, starting transfers between devices: 14 us -> 30 us  [step(): self.got = [lax.ppermute(self.kept, 'col', self.line[0][1])]]
    add x7, other arithmetic: 2.87 us -> 12.2 us  [land(): self.kept = self.kept + self.got[0]]
    convert_element_type x4, other arithmetic: 6.23 us -> 13.1 us  [shard(): return total.astype(LOW)]
    convert_element_type x3, other arithmetic: 0.54 us -> 5.71 us  [land(): sum([item.astype(F32) for item in self.got], self.kept.astype(F32))]
    pallas_call x12 -> x13, Pallas kernels: 198 us -> 202 us  [call(): pl.pallas_call(kernel, grid=grid, in_specs=list(in_specs) + [pl.BlockSpec...]
  transfers between devices with their start and end apart: 33 -> 33, of which waited for: 14 -> 12; matrix products, arithmetic and copies ran while one was open for 4% -> 9% of each run, Pallas kernels for 32% -> 34%
where the time goes in v3:
time: 333 us; the launch traced here: 329 us
  Pallas kernels  205 us (62%)
  starting transfers between devices  53.4 us (16%)
  other arithmetic  36.4 us (11%)
  waiting for transfers between devices  29 us (9%)
  local copies, waits for them, and re-layouts  4.28 us (1%)
    pallas_call x13, Pallas kernels, call(): pl.pallas_call(kernel, grid=grid, in_specs=list(in_specs) + [pl.BlockSpec...  202 us
    ppermute x10, starting transfers between devices, step(): self.got = [lax.ppermute(self.kept, 'col', self.line[0][1])]  30 us
    ppermute x10, waiting for transfers between devices, step(): self.got = [lax.ppermute(self.kept, 'col', self.line[0][1])]  14.5 us
    ppermute x16, starting transfers between devices, step(): lax.ppermute(sent, 'row', [(i, i ^ mask) for i in range(size)])  14.2 us
    convert_element_type x4, other arithmetic, shard(): return total.astype(LOW)  13.1 us
    add x7, other arithmetic, land(): self.kept = self.kept + self.got[0]  12.2 us
    ppermute x7, waiting for transfers between devices, gather_all(): pieces.append(lax.ppermute(piece, name, pairs))  11.8 us
    ppermute x7, starting transfers between devices, gather_all(): pieces.append(lax.ppermute(piece, name, pairs))  9.31 us
  transfers between devices with their start and end apart: 33, of which 12 were waited for; matrix products, arithmetic and copies ran while one was open for 9% of the time, Pallas kernels for 34%

profile of v3, /device:TPU:0, one launch (start us, length us, event | category | flops | bytes accessed | tf_op | source)
XLA Modules:
  0.0 329.0 jit_solution(1995815225853496938)
XLA Ops:
  0.7 20.9 %attend.1 = (bf16[1536,768]{1,0:T(8,128)(2,1)}, bf16[1536,768]{1,0:T(8,128)(2,1)}, bf16[1536,768]{1,0:T(8,128)(2,1)}, bf16[768,1536]{1,0:T(8,128)(2,1)}, f32[3,6,8,512]{3,2,1,0:T(8,128)}) custom-call(s32[4]{0:T(128)} %refs_1_.9, s32[2]{0:T(128)} %refs_2_.8, bf16[512,768]{1,0:T(8,128)(2,1)} %bitcast.72, bf16[1024,768]{1,0:T(8,128)(2,1)} %bitcast.69, ...), custom_call_target="tpu_custom_call" | custom-call | flops 230000001024 | tf_op jit(solution)/shard_map/attend/pallas_call | solution.py:623
  21.5 49.5 %dense.1 = (bf16[1536,768]{1,0:T(8,128)(2,1)}, bf16[1536,768]{1,0:T(8,128)(2,1)}, bf16[1536,3072]{1,0:T(8,128)(2,1)}, bf16[1536,3072]{1,0:T(8,128)(2,1)}, bf16[1...) custom-call(s32[4]{0:T(128)} %refs_1_.9, ...), custom_call_target="tpu_custom_call" | custom-call | flops 230000001024 | tf_op jit(solution)/shard_map/dense/pallas_call | solution.py:623
  71.0 3.1 collective-permute-start.2
  74.1 2.6 collective-permute-start.1
  76.7 2.3 collective-permute-done.1
  79.0 3.5 %collective-permute-done = bf16[8,896]{1,0:T(8,128)(2,1)S(1)} collective-permute-done((bf16[8,896]{1,0:T(8,128)(2,1)}, bf16[8,896]{1,0:T(8,128)(2,1)S(1)}, u32[]{:S(2)}, u32[]{:S(2)}) %collective-permute-start) | collective-permute-done | bytes 14368 | tf_op jit(solution)/shard_map/ppermute | solution.py:768
  88.9 2.4 collective-permute-done.3
  93.9 2.9 loss.1
  96.9 18.1 %outer_grad.1 = (bf16[1536,768]{1,0:T(8,128)(2,1)}, f32[8,768]{1,0:T(8,128)}, bf16[4,768,384]{2,1,0:T(8,128)(2,1)}, bf16[4,768,384]{2,1,0:T(8,128)(2,1)}) custom-call(s32[1]{0:T(128)} %bitcast.6.refs_0_, s32[4]{0:T(128)} %refs_1_.9, s32[2]{0:T(128)} %refs_2_.8, f32[8,768]{1,0:T(8,128)} %get-tuple-element.90.refs_3_, ...), custom_call_target="tpu_custom_call" | custom-call | flops 230000001024 | tf_op jit(solution)/shard_map/outer_grad/pallas_call | solution.py:623
  115.0 4.3 %turn.3.refs_1_ = bf16[768,1536]{1,0:T(8,128)(2,1)} custom-call(bf16[1536,768]{1,0:T(8,128)(2,1)} %get-tuple-element.96.refs_0_), custom_call_target="tpu_custom_call" | custom-call | flops 230000001024 | tf_op jit(solution)/shard_map/turn/pallas_call | solution.py:623
  119.8 4.1 %fusion.7 = (bf16[768,384]{1,0:T(8,128)(2,1)}, bf16[768,384]{1,0:T(8,128)(2,1)}, bf16[768,384]{1,0:T(8,128)(2,1)}, bf16[768,384]{1,0:T(8,128)(2,1)}) fusion(bf16[2,2,768,384]{3,2,1,0:T(8,128)(2,1)} %bitcast.8, s32[]{:T(128)S(6)} %select_n.213, s32[]{:T(128)S(6)} %select_n.214, bf16[2,2,768,384]{3,2,1,0:T(8,128)(2,1)} %bitcast.66, s32[]{:T(128)S(6)} %select_n.211, ...), kind=kLoop, calls=%fused_computation.17 | loop fusion | flops 4718592 | bytes 7077920 | tf_op jit(solution)/shard_map/convert_element_type | solution.py:700
  127.4 38.9 %dense_back.1 = (bf16[1536,3072]{1,0:T(8,128)(2,1)}, bf16[1536,768]{1,0:T(8,128)(2,1)}, bf16[1536,768]{1,0:T(8,128)(2,1)}, f32[8,768]{1,0:T(8,128)}, f32[8,3072]...) custom-call(s32[1]{0:T(128)} %bitcast.6.refs_0_, bf16[1536,768]{1,0:T(8,128)(2,1)} %get-tuple-element.99.refs_1_, ...), custom_call_target="tpu_custom_call" | custom-call | flops 230000001024 | tf_op jit(solution)/shard_map/dense_back/pallas_call | solution.py:623
  166.3 2.5 add_convert_fusion.4
  171.0 12.0 %weight_grad.1 = (bf16[4,96,3840]{2,1,0:T(8,128)(2,1)}, bf16[4,96,3840]{2,1,0:T(8,128)(2,1)}) custom-call(s32[1]{0:T(128)} %bitcast.6.refs_0_, bf16[768,1536]{1,0:T(8,128)(2,1)} %turn.3.refs_1_, bf16[1536,3072]{1,0:T(8,128)(2,1)} %get-tuple-element.105.refs_2_, ...), custom_call_target="tpu_custom_call", output_to_operand_aliasing={{0}: (3, {}), {1}: (4, {})} | custom-call | flops 230000001024 | tf_op jit(solution)/shard_map/weight_grad/pallas_call | solution.py:623
  183.0 2.2 add.214
  186.7 4.9 %turn.4.refs_9_ = bf16[768,1536]{1,0:T(8,128)(2,1)} custom-call(bf16[512,768]{1,0:T(8,128)(2,1)} %bitcast.74, bf16[1024,768]{1,0:T(8,128)(2,1)} %bitcast.71), custom_call_target="tpu_custom_call" | custom-call | flops 230000001024 | tf_op jit(solution)/shard_map/turn/pallas_call | solution.py:623
  191.7 4.5 %fusion.3 = (bf16[96,3840]{1,0:T(8,128)(2,1)S(1)}, bf16[96,3840]{1,0:T(8,128)(2,1)}, bf16[96,3840]{1,0:T(8,128)(2,1)}, bf16[96,3840]{1,0:T(8,128)(2,1)}) fusion(bf16[2,2,96,3840]{3,2,1,0:T(8,128)(2,1)} %bitcast.14, s32[]{:T(128)S(6)} %select_n.213, s32[]{:T(128)S(6)} %select_n.214, bf16[2,2,96,3840]{3,2,1,0:T(8,128)(2,1)} %bitcast.65, s32[]{:T(128)S(6)} %select_n.211, ...), kind=kLoop, calls=%fused_computation.12 | loop fusion | flops 5898240 | bytes 8847392 | tf_op jit(solution)/shard_map/convert_element_type | solution.py:700
  199.6 21.4 %attend_back.2 = (bf16[1536,1536]{1,0:T(8,128)(2,1)}, f32[8,512]{1,0:T(8,128)}, bf16[4,96,1536]{2,1,0:T(8,128)(2,1)}, bf16[4,96,1536]{2,1,0:T(8,128)(2,1)}) custom-call(s32[1]{0:T(128)} %bitcast.6.refs_0_, s32[4]{0:T(128)} %refs_1_.9, s32[2]{0:T(128)} %refs_2_.8, bf16[1536,768]{1,0:T(8,128)(2,1)} %get-tuple-element.114.refs_3_, ...), custom_call_target="tpu_custom_call" | custom-call | flops 230000001024 | tf_op jit(solution)/shard_map/attend_back/pallas_call | solution.py:623
  224.8 8.0 %input_grad.2.refs_1_ = bf16[1536,768]{1,0:T(8,128)(2,1)} custom-call(bf16[1536,1536]{1,0:T(8,128)(2,1)} %get-tuple-element.119.refs_0_, bf16[1536,768]{1,0:T(8,128)(2,1)} %get-tuple-element.120.refs_1_, bf16[768,768]{1,0:T(8,128)(2,1)} %refs_2_.9, bf16[768,768]{1,0:T(8,128)(2,1)} %refs_3_.3, bf16[768,768]{1,0:T(8,128)(2,1)} %refs_4_.5), custom_call_target="tpu_custom_call" | custom-call | tf_op jit(solution)/shard_map/input_grad/pallas_call | solution.py:623
  232.8 2.9 add_all.1
  235.6 6.3 %collective-permute-start.22 = (bf16[96,3840]{1,0:T(8,128)(2,1)}, bf16[96,3840]{1,0:T(8,128)(2,1)}, u32[]{:S(2)}, u32[]{:S(2)}) collective-permute-start(bf16[96,3840]{1,0:T(8,128)(2,1)} %add_all.1), channel_id=1, source_target_pairs={{0,1},{3,2},{4,5},{7,6},{8,9},{11,10},{12,13},{15,14},{16,17},{19,... | collective-permute-start | bytes 2211848 | tf_op jit(solution)/shard_map/ppermute | solution.py:721
  241.9 2.4 fusion.11
  247.8 12.5 %attend_back.3 = (bf16[1536,768]{1,0:T(8,128)(2,1)}, f32[8,256]{1,0:T(8,128)}, bf16[4,112,768]{2,1,0:T(8,128)(2,1)}, bf16[4,112,768]{2,1,0:T(8,128)(2,1)}) custom-call(s32[1]{0:T(128)} %bitcast.6.refs_0_, s32[4]{0:T(128)} %refs_1_.9, s32[2]{0:T(128)} %refs_2_.8, bf16[1536,768]{1,0:T(8,128)(2,1)} %get-tuple-element.114.refs_3_, ...), custom_call_target="tpu_custom_call" | custom-call | flops 230000001024 | tf_op jit(solution)/shard_map/attend_back/pallas_call | solution.py:623
  264.5 2.4 add.227
  268.4 6.1 %input_grad.3 = (bf16[512,768]{1,0:T(8,128)(2,1)}, bf16[1024,768]{1,0:T(8,128)(2,1)}) custom-call(bf16[1536,768]{1,0:T(8,128)(2,1)} %get-tuple-element.131.refs_0_, bf16[1536,768]{1,0:T(8,128)(2,1)} %input_grad.2.refs_1_, bf16[768,768]{1,0:T(8,128)(2,1)} %refs_2_.9, bf16[768,768]{1,0:T(8,128)(2,1)} %refs_3_.3, bf16[768,768]{1,0:T(8,128)(2,1)} %refs_4_.5), custom_call_target="tpu_custom_call" | custom-call | flops 230000001024 | tf_op jit(solution)/shard_map/input_grad/pallas_call | solution.py:623
  278.5 3.9 %collective-permute-start.30 = (bf16[96,1536]{1,0:T(8,128)(2,1)}, bf16[96,1536]{1,0:T(8,128)(2,1)}, u32[]{:S(2)}, u32[]{:S(2)}) collective-permute-start(bf16[96,1536]{1,0:T(8,128)(2,1)} %add.229), channel_id=1, source_target_pairs={{0,2},{1,3},{2,0},{3,1},{4,6},{5,7},{6,4},{7,5},{8,10},{9,11},{10,... | collective-permute-start | bytes 884744 | tf_op jit(solution)/shard_map/ppermute | solution.py:721
  285.9 2.4 add.230
  288.2 2.4 turn.5
  293.9 8.8 %collective-permute-start.29 = (bf16[112,768]{1,0:T(8,128)(2,1)S(1)}, bf16[112,768]{1,0:T(8,128)(2,1)S(1)}, u32[]{:S(2)}, u32[]{:S(2)}) collective-permute-start(bf16[112,768]{1,0:T(8,128)(2,1)S(1)} %add_convert_fusion.14), channel_id=1, source_target_pairs={{0,1},{1,0},{2,3},{3,2},{4,5},{5,4},{6,7},{7,6},{8,9},{9,8},{10,11... | collective-permute-start | bytes 516104 | tf_op jit(solution)/shard_map/ppermute | solution.py:721
  306.6 3.1 collective-permute-start.31
  310.9 5.3 %collective-permute-done.31 = bf16[112,768]{1,0:T(8,128)(2,1)S(1)} collective-permute-done((bf16[112,768]{1,0:T(8,128)(2,1)S(1)}, bf16[112,768]{1,0:T(8,128)(2,1)S(1)}, u32[]{:S(2)}, u32[]{:S(2)}) %collective-permute-start.31) | collective-permute-done | bytes 172064 | tf_op jit(solution)/shard_map/ppermute | solution.py:721
  319.0 7.8 %collective-permute-done.32 = bf16[96,3840]{1,0:T(8,128)(2,1)S(1)} collective-permute-done((bf16[96,3840]{1,0:T(8,128)(2,1)S(1)}, bf16[96,3840]{1,0:T(8,128)(2,1)S(1)}, u32[]{:S(2)}, u32[]{:S(2)}) %collective-permute-start.32) | collective-permute-done | bytes 737312 | tf_op jit(solution)/shard_map/ppermute | solution.py:721
  (93 shorter events, 53.6 us)
Async XLA Ops:
  71.0 5.7 %collective-permute-start.2 = (bf16[8,896]{1,0:T(8,128)(2,1)}, bf16[8,896]{1,0:T(8,128)(2,1)S(1)}, u32[]{:S(2)}, u32[]{:S(2)}) collective-permute-start(bf16[8,896]{1,0:T(8,128)(2,1)} %get-tuple-element.85.own_ref), channel_id=1, source_target_pairs={{0,1},{1,0},{2,3},{3,2},{4,5},{5,4},{6,7},{7,6},{8,9},{9,8},{10,11... | collective-permute-start | bytes 43016 | tf_op jit(solution)/shard_map/ppermute | solution.py:768
  74.1 4.9 %collective-permute-start.1 = (bf16[8,896]{1,0:T(8,128)(2,1)}, bf16[8,896]{1,0:T(8,128)(2,1)S(1)}, u32[]{:S(2)}, u32[]{:S(2)}) collective-permute-start(bf16[8,896]{1,0:T(8,128)(2,1)} %get-tuple-element.85.own_ref), channel_id=1, source_target_pairs={{0,2},{1,3},{2,0},{3,1},{4,6},{5,7},{6,4},{7,5},{8,10},{9,11},{10,... | collective-permute-start | bytes 43016 | tf_op jit(solution)/shard_map/ppermute | solution.py:768
  76.7 5.7 %collective-permute-start = (bf16[8,896]{1,0:T(8,128)(2,1)}, bf16[8,896]{1,0:T(8,128)(2,1)S(1)}, u32[]{:S(2)}, u32[]{:S(2)}) collective-permute-start(bf16[8,896]{1,0:T(8,128)(2,1)} %get-tuple-element.85.own_ref), channel_id=1, source_target_pairs={{0,3},{1,2},{2,1},{3,0},{4,7},{5,6},{6,5},{7,4},{8,11},{9,10},{10,... | collective-permute-start | bytes 43016 | tf_op jit(solution)/shard_map/ppermute | solution.py:768
  83.2 4.4 %collective-permute-start.5 = (bf16[32,896]{1,0:T(8,128)(2,1)S(1)}, bf16[32,896]{1,0:T(8,128)(2,1)S(1)}, u32[]{:S(2)}, u32[]{:S(2)}) collective-permute-start(bf16[32,896]{1,0:T(8,128)(2,1)S(1)} %pad_maximum_fusion.5), channel_id=1, source_target_pairs={{0,8},{4,12},{8,0},{12,4},{16,24},{20,28},{24,16},{28,20},{1,9},{5... | collective-permute-start | bytes 172040 | tf_op jit(solution)/shard_map/ppermute | solution.py:768
  84.7 4.2 %collective-permute-start.4 = (bf16[32,896]{1,0:T(8,128)(2,1)S(1)}, bf16[32,896]{1,0:T(8,128)(2,1)S(1)}, u32[]{:S(2)}, u32[]{:S(2)}) collective-permute-start(bf16[32,896]{1,0:T(8,128)(2,1)S(1)} %pad_maximum_fusion.5), channel_id=1, source_target_pairs={{0,16},{4,20},{8,24},{12,28},{16,0},{20,4},{24,8},{28,12},{1,17},{... | collective-permute-start | bytes 172040 | tf_op jit(solution)/shard_map/ppermute | solution.py:768
  86.2 5.1 %collective-permute-start.3 = (bf16[32,896]{1,0:T(8,128)(2,1)S(1)}, bf16[32,896]{1,0:T(8,128)(2,1)S(1)}, u32[]{:S(2)}, u32[]{:S(2)}) collective-permute-start(bf16[32,896]{1,0:T(8,128)(2,1)S(1)} %pad_maximum_fusion.5), channel_id=1, source_target_pairs={{0,24},{4,28},{8,16},{12,20},{16,8},{20,12},{24,0},{28,4},{1,25},{... | collective-permute-start | bytes 172040 | tf_op jit(solution)/shard_map/ppermute | solution.py:768
  114.9 4.9 %collective-permute-start.7 = (bf16[4,768,384]{2,1,0:T(8,128)(2,1)}, bf16[4,768,384]{2,1,0:T(8,128)(2,1)}, u32[]{:S(2)}, u32[]{:S(2)}) collective-permute-start(bf16[4,768,384]{2,1,0:T(8,128)(2,1)} %get-tuple-element.95), channel_id=1, source_target_pairs={{0,4},{4,0},{8,12},{12,8},{16,20},{20,16},{24,28},{28,24},{1,5},{5... | collective-permute-start | bytes 7077896 | tf_op jit(solution)/shard_map/ppermute | solution.py:716
  123.9 42.4 %collective-permute-start.10 = (bf16[768,384]{1,0:T(8,128)(2,1)}, bf16[768,384]{1,0:T(8,128)(2,1)}, u32[]{:S(2)}, u32[]{:S(2)}) collective-permute-start(bf16[768,384]{1,0:T(8,128)(2,1)} %get-tuple-element.153), channel_id=1, source_target_pairs={{0,24},{4,28},{8,16},{12,20},{16,8},{20,12},{24,0},{28,4},{1,25},{... | collective-permute-start | bytes 1769480 | tf_op jit(solution)/shard_map/ppermute | solution.py:716
  124.4 41.9 %collective-permute-start.9 = (bf16[768,384]{1,0:T(8,128)(2,1)}, bf16[768,384]{1,0:T(8,128)(2,1)}, u32[]{:S(2)}, u32[]{:S(2)}) collective-permute-start(bf16[768,384]{1,0:T(8,128)(2,1)} %get-tuple-element.154), channel_id=1, source_target_pairs={{0,16},{4,20},{8,24},{12,28},{16,0},{20,4},{24,8},{28,12},{1,17},{... | collective-permute-start | bytes 1769480 | tf_op jit(solution)/shard_map/ppermute | solution.py:716
  125.9 40.4 %collective-permute-start.8 = (bf16[768,384]{1,0:T(8,128)(2,1)}, bf16[768,384]{1,0:T(8,128)(2,1)}, u32[]{:S(2)}, u32[]{:S(2)}) collective-permute-start(bf16[768,384]{1,0:T(8,128)(2,1)} %get-tuple-element.155), channel_id=1, source_target_pairs={{0,8},{4,12},{8,0},{12,4},{16,24},{20,28},{24,16},{28,20},{1,9},{5... | collective-permute-start | bytes 1769480 | tf_op jit(solution)/shard_map/ppermute | solution.py:716
  168.9 14.2 %collective-permute-start.11 = (bf16[768,384]{1,0:T(8,128)(2,1)}, bf16[768,384]{1,0:T(8,128)(2,1)}, u32[]{:S(2)}, u32[]{:S(2)}) collective-permute-start(bf16[768,384]{1,0:T(8,128)(2,1)} %add_convert_fusion.4), channel_id=1, source_target_pairs={{0,1},{3,2},{4,5},{7,6},{8,9},{11,10},{12,13},{15,14},{16,17},{19,... | collective-permute-start | bytes 1769480 | tf_op jit(solution)/shard_map/ppermute | solution.py:721
  183.0 8.7 %collective-permute-start.12 = (bf16[4,96,3840]{2,1,0:T(8,128)(2,1)}, bf16[4,96,3840]{2,1,0:T(8,128)(2,1)}, u32[]{:S(2)}, u32[]{:S(2)}) collective-permute-start(bf16[4,96,3840]{2,1,0:T(8,128)(2,1)} %get-tuple-element.109), channel_id=1, source_target_pairs={{0,4},{4,0},{8,12},{12,8},{16,20},{20,16},{24,28},{28,24},{1,5},{5... | collective-permute-start | bytes 8847368 | tf_op jit(solution)/shard_map/ppermute | solution.py:716
  185.2 35.8 %collective-permute-start.16 = (bf16[768,384]{1,0:T(8,128)(2,1)}, bf16[768,384]{1,0:T(8,128)(2,1)}, u32[]{:S(2)}, u32[]{:S(2)}) collective-permute-start(bf16[768,384]{1,0:T(8,128)(2,1)} %add.214), channel_id=1, source_target_pairs={{1,2},{2,1},{5,6},{6,5},{9,10},{10,9},{13,14},{14,13},{17,18},{18,... | collective-permute-start | bytes 1769480 | tf_op jit(solution)/shard_map/ppermute | solution.py:721
  196.1 36.6 %collective-permute-start.15 = (bf16[96,3840]{1,0:T(8,128)(2,1)}, bf16[96,3840]{1,0:T(8,128)(2,1)}, u32[]{:S(2)}, u32[]{:S(2)}) collective-permute-start(bf16[96,3840]{1,0:T(8,128)(2,1)} %get-tuple-element.149), channel_id=1, source_target_pairs={{0,24},{4,28},{8,16},{12,20},{16,8},{20,12},{24,0},{28,4},{1,25},{... | collective-permute-start | bytes 2211848 | tf_op jit(solution)/shard_map/ppermute | solution.py:716
  196.6 36.1 %collective-permute-start.14 = (bf16[96,3840]{1,0:T(8,128)(2,1)}, bf16[96,3840]{1,0:T(8,128)(2,1)}, u32[]{:S(2)}, u32[]{:S(2)}) collective-permute-start(bf16[96,3840]{1,0:T(8,128)(2,1)} %get-tuple-element.150), channel_id=1, source_target_pairs={{0,16},{4,20},{8,24},{12,28},{16,0},{20,4},{24,8},{28,12},{1,17},{... | collective-permute-start | bytes 2211848 | tf_op jit(solution)/shard_map/ppermute | solution.py:716
  198.1 34.6 %collective-permute-start.13 = (bf16[96,3840]{1,0:T(8,128)(2,1)}, bf16[96,3840]{1,0:T(8,128)(2,1)}, u32[]{:S(2)}, u32[]{:S(2)}) collective-permute-start(bf16[96,3840]{1,0:T(8,128)(2,1)} %get-tuple-element.151), channel_id=1, source_target_pairs={{0,8},{4,12},{8,0},{12,4},{16,24},{20,28},{24,16},{28,20},{1,9},{5... | collective-permute-start | bytes 2211848 | tf_op jit(solution)/shard_map/ppermute | solution.py:716
  223.2 37.2 %collective-permute-start.18 = (bf16[768,384]{1,0:T(8,128)(2,1)}, bf16[768,384]{1,0:T(8,128)(2,1)}, u32[]{:S(2)}, u32[]{:S(2)}) collective-permute-start(bf16[768,384]{1,0:T(8,128)(2,1)} %add.219), channel_id=1, source_target_pairs={{1,0},{2,3},{5,4},{6,7},{9,8},{10,11},{13,12},{14,15},{17,16},{18,... | collective-permute-start | bytes 1769480 | tf_op jit(solution)/shard_map/ppermute | solution.py:721
  224.7 17.2 %collective-permute-start.17 = (bf16[4,96,1536]{2,1,0:T(8,128)(2,1)}, bf16[4,96,1536]{2,1,0:T(8,128)(2,1)}, u32[]{:S(2)}, u32[]{:S(2)}) collective-permute-start(bf16[4,96,1536]{2,1,0:T(8,128)(2,1)} %get-tuple-element.121), channel_id=1, source_target_pairs={{0,4},{4,0},{8,12},{12,8},{16,20},{20,16},{24,28},{28,24},{1,5},{5... | collective-permute-start | bytes 3538952 | tf_op jit(solution)/shard_map/ppermute | solution.py:716
  235.6 28.8 %collective-permute-start.22 = (bf16[96,3840]{1,0:T(8,128)(2,1)}, bf16[96,3840]{1,0:T(8,128)(2,1)}, u32[]{:S(2)}, u32[]{:S(2)}) collective-permute-start(bf16[96,3840]{1,0:T(8,128)(2,1)} %add_all.1), channel_id=1, source_target_pairs={{0,1},{3,2},{4,5},{7,6},{8,9},{11,10},{12,13},{15,14},{16,17},{19,... | collective-permute-start | bytes 2211848 | tf_op jit(solution)/shard_map/ppermute | solution.py:721
  244.3 18.1 %collective-permute-start.21 = (bf16[96,1536]{1,0:T(8,128)(2,1)}, bf16[96,1536]{1,0:T(8,128)(2,1)}, u32[]{:S(2)}, u32[]{:S(2)}) collective-permute-start(bf16[96,1536]{1,0:T(8,128)(2,1)} %get-tuple-element.157), channel_id=1, source_target_pairs={{0,24},{4,28},{8,16},{12,20},{16,8},{20,12},{24,0},{28,4},{1,25},{... | collective-permute-start | bytes 884744 | tf_op jit(solution)/shard_map/ppermute | solution.py:716
  244.8 17.6 %collective-permute-start.20 = (bf16[96,1536]{1,0:T(8,128)(2,1)}, bf16[96,1536]{1,0:T(8,128)(2,1)}, u32[]{:S(2)}, u32[]{:S(2)}) collective-permute-start(bf16[96,1536]{1,0:T(8,128)(2,1)} %get-tuple-element.158), channel_id=1, source_target_pairs={{0,16},{4,20},{8,24},{12,28},{16,0},{20,4},{24,8},{28,12},{1,17},{... | collective-permute-start | bytes 884744 | tf_op jit(solution)/shard_map/ppermute | solution.py:716
  246.3 16.1 %collective-permute-start.19 = (bf16[96,1536]{1,0:T(8,128)(2,1)}, bf16[96,1536]{1,0:T(8,128)(2,1)}, u32[]{:S(2)}, u32[]{:S(2)}) collective-permute-start(bf16[96,1536]{1,0:T(8,128)(2,1)} %get-tuple-element.159), channel_id=1, source_target_pairs={{0,8},{4,12},{8,0},{12,4},{16,24},{20,28},{24,16},{28,20},{1,9},{5... | collective-permute-start | bytes 884744 | tf_op jit(solution)/shard_map/ppermute | solution.py:716
  260.4 14.1 %collective-permute-start.23 = (bf16[4,112,768]{2,1,0:T(8,128)(2,1)}, bf16[4,112,768]{2,1,0:T(8,128)(2,1)}, u32[]{:S(2)}, u32[]{:S(2)}) collective-permute-start(bf16[4,112,768]{2,1,0:T(8,128)(2,1)} %get-tuple-element.132), channel_id=1, source_target_pairs={{0,4},{4,0},{8,12},{12,8},{16,20},{20,16},{24,28},{28,24},{1,5},{5... | collective-permute-start | bytes 2064392 | tf_op jit(solution)/shard_map/ppermute | solution.py:716
  264.5 12.1 %collective-permute-start.24 = (bf16[96,1536]{1,0:T(8,128)(2,1)}, bf16[96,1536]{1,0:T(8,128)(2,1)}, u32[]{:S(2)}, u32[]{:S(2)}) collective-permute-start(bf16[96,1536]{1,0:T(8,128)(2,1)} %add_convert_fusion.9), channel_id=1, source_target_pairs={{0,1},{1,0},{2,3},{3,2},{4,5},{5,4},{6,7},{7,6},{8,9},{9,8},{10,11... | collective-permute-start | bytes 884744 | tf_op jit(solution)/shard_map/ppermute | solution.py:721
  266.9 19.0 %collective-permute-start.25 = (bf16[96,3840]{1,0:T(8,128)(2,1)}, bf16[96,3840]{1,0:T(8,128)(2,1)}, u32[]{:S(2)}, u32[]{:S(2)}) collective-permute-start(bf16[96,3840]{1,0:T(8,128)(2,1)} %add.227), channel_id=1, source_target_pairs={{1,2},{2,1},{5,6},{6,5},{9,10},{10,9},{13,14},{14,13},{17,18},{18,... | collective-permute-start | bytes 2211848 | tf_op jit(solution)/shard_map/ppermute | solution.py:721
  278.5 31.3 %collective-permute-start.30 = (bf16[96,1536]{1,0:T(8,128)(2,1)}, bf16[96,1536]{1,0:T(8,128)(2,1)}, u32[]{:S(2)}, u32[]{:S(2)}) collective-permute-start(bf16[96,1536]{1,0:T(8,128)(2,1)} %add.229), channel_id=1, source_target_pairs={{0,2},{1,3},{2,0},{3,1},{4,6},{5,7},{6,4},{7,5},{8,10},{9,11},{10,... | collective-permute-start | bytes 884744 | tf_op jit(solution)/shard_map/ppermute | solution.py:721
  282.4 8.5 %collective-permute-start.28 = (bf16[112,768]{1,0:T(8,128)(2,1)}, bf16[112,768]{1,0:T(8,128)(2,1)}, u32[]{:S(2)}, u32[]{:S(2)}) collective-permute-start(bf16[112,768]{1,0:T(8,128)(2,1)} %get-tuple-element.161), channel_id=1, source_target_pairs={{0,24},{4,28},{8,16},{12,20},{16,8},{20,12},{24,0},{28,4},{1,25},{... | collective-permute-start | bytes 516104 | tf_op jit(solution)/shard_map/ppermute | solution.py:716
  282.8 9.9 %collective-permute-start.27 = (bf16[112,768]{1,0:T(8,128)(2,1)}, bf16[112,768]{1,0:T(8,128)(2,1)}, u32[]{:S(2)}, u32[]{:S(2)}) collective-permute-start(bf16[112,768]{1,0:T(8,128)(2,1)} %get-tuple-element.162), channel_id=1, source_target_pairs={{0,16},{4,20},{8,24},{12,28},{16,0},{20,4},{24,8},{28,12},{1,17},{... | collective-permute-start | bytes 516104 | tf_op jit(solution)/shard_map/ppermute | solution.py:716
  284.4 8.4 %collective-permute-start.26 = (bf16[112,768]{1,0:T(8,128)(2,1)}, bf16[112,768]{1,0:T(8,128)(2,1)}, u32[]{:S(2)}, u32[]{:S(2)}) collective-permute-start(bf16[112,768]{1,0:T(8,128)(2,1)} %get-tuple-element.163), channel_id=1, source_target_pairs={{0,8},{4,12},{8,0},{12,4},{16,24},{20,28},{24,16},{28,20},{1,9},{5... | collective-permute-start | bytes 516104 | tf_op jit(solution)/shard_map/ppermute | solution.py:716
  293.9 12.6 %collective-permute-start.29 = (bf16[112,768]{1,0:T(8,128)(2,1)S(1)}, bf16[112,768]{1,0:T(8,128)(2,1)S(1)}, u32[]{:S(2)}, u32[]{:S(2)}) collective-permute-start(bf16[112,768]{1,0:T(8,128)(2,1)S(1)} %add_convert_fusion.14), channel_id=1, source_target_pairs={{0,1},{1,0},{2,3},{3,2},{4,5},{5,4},{6,7},{7,6},{8,9},{9,8},{10,11... | collective-permute-start | bytes 516104 | tf_op jit(solution)/shard_map/ppermute | solution.py:721
  303.9 23.0 %collective-permute-start.32 = (bf16[96,3840]{1,0:T(8,128)(2,1)S(1)}, bf16[96,3840]{1,0:T(8,128)(2,1)S(1)}, u32[]{:S(2)}, u32[]{:S(2)}) collective-permute-start(bf16[96,3840]{1,0:T(8,128)(2,1)S(1)} %copy-done), channel_id=1, source_target_pairs={{1,0},{2,3},{5,4},{6,7},{9,8},{10,11},{13,12},{14,15},{17,16},{18,... | collective-permute-start | bytes 2211848 | tf_op jit(solution)/shard_map/ppermute | solution.py:721
  306.6 9.7 %collective-permute-start.31 = (bf16[112,768]{1,0:T(8,128)(2,1)S(1)}, bf16[112,768]{1,0:T(8,128)(2,1)S(1)}, u32[]{:S(2)}, u32[]{:S(2)}) collective-permute-start(bf16[112,768]{1,0:T(8,128)(2,1)S(1)} %add.237), channel_id=1, source_target_pairs={{0,2},{1,3},{2,0},{3,1},{4,6},{5,7},{6,4},{7,5},{8,10},{9,11},{10,... | collective-permute-start | bytes 516104 | tf_op jit(solution)/shard_map/ppermute | solution.py:721
  (7 other events, 78.1 us)

commit v4 on v3

--- a/solution.py
+++ b/solution.py
@@ -610,7 +610,7 @@
     return pl.BlockSpec(shape, lambda i: (0,) * len(shape), pipeline_mode=pl.Buffered(1))
 
 
-def call(body, operands, in_specs, outs, grid, room, deps=(), old=(), name=None, scratch=(), us=20_000):
+def call(body, operands, in_specs, outs, grid, room, deps=(), old=(), name=None, scratch=(), us=12):
     count, extra = len(operands), len(old)
     if deps:
         tied = min(range(count), key=lambda i: operands[i].size)
@@ -629,7 +629,7 @@
         scratch_shapes=scratch,
         input_output_aliases={count + i: i for i in range(extra)},
         compiler_params=pltpu.CompilerParams(vmem_limit_bytes=room * 1024 * 1024),
-        cost_estimate=pl.CostEstimate(flops=int(us * 1.15e7), bytes_accessed=0, transcendentals=0),
+        cost_estimate=pl.CostEstimate(flops=int(us * 1.15e9), bytes_accessed=0, transcendentals=0),
         name=name,
     )(*operands, *old)
 
@@ -666,7 +666,7 @@
     shape = terms[0].shape
     spec = pl.BlockSpec(shape, lambda i: (0,) * len(shape), pipeline_mode=pl.Buffered(1))
     outs = [(spec, jax.ShapeDtypeStruct(shape, LOW))]
-    return call(add_kernel, terms, [spec] * len(terms), outs, (1,), 24, name="add_all", us=20_000)[0]
+    return call(add_kernel, terms, [spec] * len(terms), outs, (1,), 24, name="add_all", us=12)[0]
 
 
 class Flow:
@@ -913,7 +913,7 @@
 
     def turn(arrays, specs, deps):
         outs = [(by_block_t(width), shape(width, total_rows))]
-        return call(turn_low_kernel, arrays, specs, outs, (blocks,), 56, deps, name="turn")[0]
+        return call(turn_low_kernel, arrays, specs, outs, (blocks,), 56, deps, name="turn", us=40)[0]
 
     y1_t = turn([y1], [by_block(width)], outer.sent)
     deps = outer.turn(y1_t)
@@ -1021,14 +1021,14 @@
             (passages_spec, shape(p_dev * rows_all, width)),
         ],
         deps,
-        20_000,
+        12,
     )
     last_flow.turn(passage_grad)
     mixed_flow.turn(last_flow.kept)
     up_flow.turn(mixed_flow.kept)
     outs = [(fixed((cut_inner, width)), shape(cut_inner, width, kind=F32))]
     (turned,) = call(
-        turn_kernel, (outer.kept,), [const_spec((width, cut_inner))], outs, (1,), 56, [up_flow.kept], name="turn"
+        turn_kernel, (outer.kept,), [const_spec((width, cut_inner))], outs, (1,), 56, [up_flow.kept], name="turn", us=40
     )
     last_flow.turn(turned)
     last_flow.turn()
@@ -1039,15 +1039,15 @@
         for flow in flows:
             if not flow.done:
                 flow.turn()
-    mixed, last = mixed_flow.kept.astype(F32), last_flow.kept.astype(F32)
+    mixed, last = mixed_flow.kept, last_flow.kept
     qkv = [
         jnp.concatenate(
             [mixed[:, i * 2 * third : (i + 1) * 2 * third], last[:cut, i * third : (i + 1) * third]], 1
-        )
+        ).astype(F32)
         for i in range(3)
     ]
-    up_sum = up_flow.kept.astype(F32)
-    small = last[cut:]
+    up_sum = up_flow.kept
+    small = last[cut:].astype(F32)
     return (
         loss[0, 0],
         query_out.reshape(query_tokens.shape),
@@ -1055,8 +1055,8 @@
         query_grad.reshape(query_tokens.shape),
         passage_grad.reshape(passage_tokens.shape),
         *qkv,
-        up_sum[:, inner:],
-        up_sum[:, :inner],
+        up_sum[:, inner:].astype(F32),
+        up_sum[:, :inner].astype(F32),
         turned,
         *[small[i, :cut] for i in range(3)],
         small[8, : inner // row_count],

time: 333 us -> 309 us (0.928)
  other arithmetic: 36.4 us -> 12.6 us
  waiting for transfers between devices: 29 us -> 38.3 us
  starting transfers between devices: 53.4 us -> 48.4 us
    convert_element_type x4, other arithmetic: 13.1 us -> 2.85 us  [shard(): return total.astype(LOW)]
    add x7 -> x8, other arithmetic: 12.2 us -> 2.03 us  [land(): self.kept = self.kept + self.got[0]]
    ppermute x10, waiting for transfers between devices: 14.5 us -> 22.2 us  [step(): self.got = [lax.ppermute(self.kept, 'col', self.line[0][1])]]
    ppermute x10, starting transfers between devices: 30 us -> 24.8 us  [step(): self.got = [lax.ppermute(self.kept, 'col', self.line[0][1])]]
    convert_element_type x3, other arithmetic: 5.71 us -> 1.6 us  [land(): sum([item.astype(F32) for item in self.got], self.kept.astype(F32))]
  transfers between devices with their start and end apart: 33 -> 33, of which waited for: 12 -> 14; matrix products, arithmetic and copies ran while one was open for 9% -> 3% of each run, Pallas kernels for 34% -> 36%
where the time goes in v4:
time: 309 us; the launch traced here: 306 us
  Pallas kernels  203 us (66%)
  starting transfers between devices  48.4 us (16%)
  waiting for transfers between devices  38.3 us (12%)
  other arithmetic  12.6 us (4%)
    pallas_call x13, Pallas kernels, call(): pl.pallas_call(kernel, grid=grid, in_specs=list(in_specs) + [pl.BlockSpec...  200 us
    ppermute x10, starting transfers between devices, step(): self.got = [lax.ppermute(self.kept, 'col', self.line[0][1])]  24.8 us
    ppermute x10, waiting for transfers between devices, step(): self.got = [lax.ppermute(self.kept, 'col', self.line[0][1])]  22.2 us
    ppermute x16, starting transfers between devices, step(): lax.ppermute(sent, 'row', [(i, i ^ mask) for i in range(size)])  14.3 us
    ppermute x7, waiting for transfers between devices, gather_all(): pieces.append(lax.ppermute(piece, name, pairs))  11.8 us
    ppermute x7, starting transfers between devices, gather_all(): pieces.append(lax.ppermute(piece, name, pairs))  9.31 us
  transfers between devices with their start and end apart: 33, of which 14 were waited for; matrix products, arithmetic and copies ran while one was open for 3% of the time, Pallas kernels for 36%

profile of v4, /device:TPU:0, one launch (start us, length us, event | category | flops | bytes accessed | tf_op | source)
XLA Modules:
  0.0 305.5 jit_solution(14621278563421228163)
XLA Ops:
  0.7 21.0 %attend.1 = (bf16[1536,768]{1,0:T(8,128)(2,1)}, bf16[1536,768]{1,0:T(8,128)(2,1)}, bf16[1536,768]{1,0:T(8,128)(2,1)}, bf16[768,1536]{1,0:T(8,128)(2,1)}, f32[3,6,8,512]{3,2,1,0:T(8,128)}) custom-call(s32[4]{0:T(128)} %refs_1_.9, s32[2]{0:T(128)} %refs_2_.8, bf16[512,768]{1,0:T(8,128)(2,1)} %bitcast.76, bf16[1024,768]{1,0:T(8,128)(2,1)} %bitcast.73, ...), custom_call_target="tpu_custom_call" | custom-call | flops 13799999488 | tf_op jit(solution)/shard_map/attend/pallas_call | solution.py:623
  21.6 49.5 %dense.1 = (bf16[1536,768]{1,0:T(8,128)(2,1)}, bf16[1536,768]{1,0:T(8,128)(2,1)}, bf16[1536,3072]{1,0:T(8,128)(2,1)}, bf16[1536,3072]{1,0:T(8,128)(2,1)}, bf16[1...) custom-call(s32[4]{0:T(128)} %refs_1_.9, ...), custom_call_target="tpu_custom_call" | custom-call | flops 13799999488 | tf_op jit(solution)/shard_map/dense/pallas_call | solution.py:623
  71.1 3.1 %collective-permute-start.2 = (bf16[8,896]{1,0:T(8,128)(2,1)}, bf16[8,896]{1,0:T(8,128)(2,1)S(1)}, u32[]{:S(2)}, u32[]{:S(2)}) collective-permute-start(bf16[8,896]{1,0:T(8,128)(2,1)} %get-tuple-element.85.own_ref), channel_id=1, source_target_pairs={{0,1},{1,0},{2,3},{3,2},{4,5},{5,4},{6,7},{7,6},{8,9},{9,8},{10,11... | collective-permute-start | bytes 43016 | tf_op jit(solution)/shard_map/ppermute | solution.py:768
  74.2 2.6 collective-permute-start.1
  76.8 2.3 collective-permute-done.1
  79.1 3.5 %collective-permute-done = bf16[8,896]{1,0:T(8,128)(2,1)S(1)} collective-permute-done((bf16[8,896]{1,0:T(8,128)(2,1)}, bf16[8,896]{1,0:T(8,128)(2,1)S(1)}, u32[]{:S(2)}, u32[]{:S(2)}) %collective-permute-start) | collective-permute-done | bytes 14368 | tf_op jit(solution)/shard_map/ppermute | solution.py:768
  83.3 1.6 collective-permute-start.5
  89.0 2.4 collective-permute-done.3
  94.0 2.9 loss.1
  96.9 18.1 %outer_grad.1 = (bf16[1536,768]{1,0:T(8,128)(2,1)}, f32[8,768]{1,0:T(8,128)}, bf16[4,768,384]{2,1,0:T(8,128)(2,1)}, bf16[4,768,384]{2,1,0:T(8,128)(2,1)}) custom-call(s32[1]{0:T(128)} %bitcast.6.refs_0_, s32[4]{0:T(128)} %refs_1_.9, s32[2]{0:T(128)} %refs_2_.8, f32[8,768]{1,0:T(8,128)} %get-tuple-element.90.refs_3_, ...), custom_call_target="tpu_custom_call" | custom-call | flops 13799999488 | tf_op jit(solution)/shard_map/outer_grad/pallas_call | solution.py:623
  115.1 4.5 %turn.3.refs_1_ = bf16[768,1536]{1,0:T(8,128)(2,1)} custom-call(bf16[1536,768]{1,0:T(8,128)(2,1)} %get-tuple-element.96.refs_0_), custom_call_target="tpu_custom_call" | custom-call | flops 46000001024 | tf_op jit(solution)/shard_map/turn/pallas_call | solution.py:623
  123.9 38.9 %dense_back.1 = (bf16[1536,3072]{1,0:T(8,128)(2,1)}, bf16[1536,768]{1,0:T(8,128)(2,1)}, bf16[1536,768]{1,0:T(8,128)(2,1)}, f32[8,768]{1,0:T(8,128)}, f32[8,3072]...) custom-call(s32[1]{0:T(128)} %bitcast.6.refs_0_, bf16[1536,768]{1,0:T(8,128)(2,1)} %get-tuple-element.99.refs_1_, ...), custom_call_target="tpu_custom_call" | custom-call | flops 13799999488 | tf_op jit(solution)/shard_map/dense_back/pallas_call | solution.py:623
  165.5 12.0 %weight_grad.1 = (bf16[4,96,3840]{2,1,0:T(8,128)(2,1)}, bf16[4,96,3840]{2,1,0:T(8,128)(2,1)}) custom-call(s32[1]{0:T(128)} %bitcast.6.refs_0_, bf16[768,1536]{1,0:T(8,128)(2,1)} %turn.3.refs_1_, bf16[1536,3072]{1,0:T(8,128)(2,1)} %get-tuple-element.105.refs_2_, ...), custom_call_target="tpu_custom_call", output_to_operand_aliasing={{0}: (3, {}), {1}: (4, {})} | custom-call | flops 13799999488 | tf_op jit(solution)/shard_map/weight_grad/pallas_call | solution.py:623
  178.0 1.5 collective-permute-start.16
  179.6 5.1 %turn.4.refs_9_ = bf16[768,1536]{1,0:T(8,128)(2,1)} custom-call(bf16[512,768]{1,0:T(8,128)(2,1)} %bitcast.78, bf16[1024,768]{1,0:T(8,128)(2,1)} %bitcast.75), custom_call_target="tpu_custom_call" | custom-call | flops 46000001024 | tf_op jit(solution)/shard_map/turn/pallas_call | solution.py:623
  184.7 1.8 fusion.3
  189.9 21.4 %attend_back.2 = (bf16[1536,1536]{1,0:T(8,128)(2,1)}, f32[8,512]{1,0:T(8,128)}, bf16[4,96,1536]{2,1,0:T(8,128)(2,1)}, bf16[4,96,1536]{2,1,0:T(8,128)(2,1)}) custom-call(s32[1]{0:T(128)} %bitcast.6.refs_0_, s32[4]{0:T(128)} %refs_1_.9, s32[2]{0:T(128)} %refs_2_.8, bf16[1536,768]{1,0:T(8,128)(2,1)} %get-tuple-element.114.refs_3_, ...), custom_call_target="tpu_custom_call" | custom-call | flops 13799999488 | tf_op jit(solution)/shard_map/attend_back/pallas_call | solution.py:623
  214.2 8.0 %input_grad.2.refs_1_ = bf16[1536,768]{1,0:T(8,128)(2,1)} custom-call(bf16[1536,1536]{1,0:T(8,128)(2,1)} %get-tuple-element.119.refs_0_, bf16[1536,768]{1,0:T(8,128)(2,1)} %get-tuple-element.120.refs_1_, bf16[768,768]{1,0:T(8,128)(2,1)} %refs_2_.9, bf16[768,768]{1,0:T(8,128)(2,1)} %refs_3_.3, bf16[768,768]{1,0:T(8,128)(2,1)} %refs_4_.5), custom_call_target="tpu_custom_call" | custom-call | tf_op jit(solution)/shard_map/input_grad/pallas_call | solution.py:623
  222.6 4.9 %collective-permute-start.22 = (bf16[96,3840]{1,0:T(8,128)(2,1)S(1)}, bf16[96,3840]{1,0:T(8,128)(2,1)S(1)}, u32[]{:S(2)}, u32[]{:S(2)}) collective-permute-start(bf16[96,3840]{1,0:T(8,128)(2,1)S(1)} %add_all.1), channel_id=1, source_target_pairs={{0,1},{3,2},{4,5},{7,6},{8,9},{11,10},{12,13},{15,14},{16,17},{19,... | collective-permute-start | bytes 2211848 | tf_op jit(solution)/shard_map/ppermute | solution.py:721
  228.4 1.5 collective-permute-start.20
  231.4 12.5 %attend_back.3 = (bf16[1536,768]{1,0:T(8,128)(2,1)}, f32[8,256]{1,0:T(8,128)}, bf16[4,112,768]{2,1,0:T(8,128)(2,1)}, bf16[4,112,768]{2,1,0:T(8,128)(2,1)}) custom-call(s32[1]{0:T(128)} %bitcast.6.refs_0_, s32[4]{0:T(128)} %refs_1_.9, s32[2]{0:T(128)} %refs_2_.8, bf16[1536,768]{1,0:T(8,128)(2,1)} %get-tuple-element.114.refs_3_, ...), custom_call_target="tpu_custom_call" | custom-call | flops 13799999488 | tf_op jit(solution)/shard_map/attend_back/pallas_call | solution.py:623
  246.1 6.1 %input_grad.3 = (bf16[512,768]{1,0:T(8,128)(2,1)}, bf16[1024,768]{1,0:T(8,128)(2,1)}) custom-call(bf16[1536,768]{1,0:T(8,128)(2,1)} %get-tuple-element.131.refs_0_, bf16[1536,768]{1,0:T(8,128)(2,1)} %input_grad.2.refs_1_, bf16[768,768]{1,0:T(8,128)(2,1)} %refs_2_.9, bf16[768,768]{1,0:T(8,128)(2,1)} %refs_3_.3, bf16[768,768]{1,0:T(8,128)(2,1)} %refs_4_.5), custom_call_target="tpu_custom_call" | custom-call | flops 13799999488 | tf_op jit(solution)/shard_map/input_grad/pallas_call | solution.py:623
  252.4 2.2 collective-permute-done.24
  254.6 2.6 collective-permute-start.30
  257.7 1.5 collective-permute-start.27
  260.9 2.3 turn.5
  263.2 2.2 collective-permute-done.28
  265.4 1.9 collective-permute-done.27
  267.4 10.1 %collective-permute-start.29 = (bf16[112,768]{1,0:T(8,128)(2,1)S(1)}, bf16[112,768]{1,0:T(8,128)(2,1)S(1)}, u32[]{:S(2)}, u32[]{:S(2)}) collective-permute-start(bf16[112,768]{1,0:T(8,128)(2,1)S(1)} %add_convert_fusion.14), channel_id=1, source_target_pairs={{0,1},{1,0},{2,3},{3,2},{4,5},{5,4},{6,7},{7,6},{8,9},{9,8},{10,11... | collective-permute-start | bytes 516104 | tf_op jit(solution)/shard_map/ppermute | solution.py:721
  280.0 4.0 %collective-permute-done.29 = bf16[112,768]{1,0:T(8,128)(2,1)S(1)} collective-permute-done((bf16[112,768]{1,0:T(8,128)(2,1)S(1)}, bf16[112,768]{1,0:T(8,128)(2,1)S(1)}, u32[]{:S(2)}, u32[]{:S(2)}) %collective-permute-start.29) | collective-permute-done | bytes 172064 | tf_op jit(solution)/shard_map/ppermute | solution.py:721
  284.9 10.1 %collective-permute-done.31 = bf16[112,768]{1,0:T(8,128)(2,1)S(1)} collective-permute-done((bf16[112,768]{1,0:T(8,128)(2,1)S(1)}, bf16[112,768]{1,0:T(8,128)(2,1)S(1)}, u32[]{:S(2)}, u32[]{:S(2)}) %collective-permute-start.31) | collective-permute-done | bytes 172064 | tf_op jit(solution)/shard_map/ppermute | solution.py:721
  297.8 5.6 %collective-permute-done.32 = bf16[96,3840]{1,0:T(8,128)(2,1)S(1)} collective-permute-done((bf16[96,3840]{1,0:T(8,128)(2,1)S(1)}, bf16[96,3840]{1,0:T(8,128)(2,1)S(1)}, u32[]{:S(2)}, u32[]{:S(2)}) %collective-permute-start.32) | collective-permute-done | bytes 737312 | tf_op jit(solution)/shard_map/ppermute | solution.py:721
  (92 shorter events, 36.8 us)
Async XLA Ops:
  71.1 5.7 %collective-permute-start.2 = (bf16[8,896]{1,0:T(8,128)(2,1)}, bf16[8,896]{1,0:T(8,128)(2,1)S(1)}, u32[]{:S(2)}, u32[]{:S(2)}) collective-permute-start(bf16[8,896]{1,0:T(8,128)(2,1)} %get-tuple-element.85.own_ref), channel_id=1, source_target_pairs={{0,1},{1,0},{2,3},{3,2},{4,5},{5,4},{6,7},{7,6},{8,9},{9,8},{10,11... | collective-permute-start | bytes 43016 | tf_op jit(solution)/shard_map/ppermute | solution.py:768
  74.2 4.9 %collective-permute-start.1 = (bf16[8,896]{1,0:T(8,128)(2,1)}, bf16[8,896]{1,0:T(8,128)(2,1)S(1)}, u32[]{:S(2)}, u32[]{:S(2)}) collective-permute-start(bf16[8,896]{1,0:T(8,128)(2,1)} %get-tuple-element.85.own_ref), channel_id=1, source_target_pairs={{0,2},{1,3},{2,0},{3,1},{4,6},{5,7},{6,4},{7,5},{8,10},{9,11},{10,... | collective-permute-start | bytes 43016 | tf_op jit(solution)/shard_map/ppermute | solution.py:768
  76.8 5.7 %collective-permute-start = (bf16[8,896]{1,0:T(8,128)(2,1)}, bf16[8,896]{1,0:T(8,128)(2,1)S(1)}, u32[]{:S(2)}, u32[]{:S(2)}) collective-permute-start(bf16[8,896]{1,0:T(8,128)(2,1)} %get-tuple-element.85.own_ref), channel_id=1, source_target_pairs={{0,3},{1,2},{2,1},{3,0},{4,7},{5,6},{6,5},{7,4},{8,11},{9,10},{10,... | collective-permute-start | bytes 43016 | tf_op jit(solution)/shard_map/ppermute | solution.py:768
  83.3 4.4 %collective-permute-start.5 = (bf16[32,896]{1,0:T(8,128)(2,1)S(1)}, bf16[32,896]{1,0:T(8,128)(2,1)S(1)}, u32[]{:S(2)}, u32[]{:S(2)}) collective-permute-start(bf16[32,896]{1,0:T(8,128)(2,1)S(1)} %pad_maximum_fusion.2), channel_id=1, source_target_pairs={{0,8},{4,12},{8,0},{12,4},{16,24},{20,28},{24,16},{28,20},{1,9},{5... | collective-permute-start | bytes 172040 | tf_op jit(solution)/shard_map/ppermute | solution.py:768
  84.8 4.2 %collective-permute-start.4 = (bf16[32,896]{1,0:T(8,128)(2,1)S(1)}, bf16[32,896]{1,0:T(8,128)(2,1)S(1)}, u32[]{:S(2)}, u32[]{:S(2)}) collective-permute-start(bf16[32,896]{1,0:T(8,128)(2,1)S(1)} %pad_maximum_fusion.2), channel_id=1, source_target_pairs={{0,16},{4,20},{8,24},{12,28},{16,0},{20,4},{24,8},{28,12},{1,17},{... | collective-permute-start | bytes 172040 | tf_op jit(solution)/shard_map/ppermute | solution.py:768
  86.3 5.1 %collective-permute-start.3 = (bf16[32,896]{1,0:T(8,128)(2,1)S(1)}, bf16[32,896]{1,0:T(8,128)(2,1)S(1)}, u32[]{:S(2)}, u32[]{:S(2)}) collective-permute-start(bf16[32,896]{1,0:T(8,128)(2,1)S(1)} %pad_maximum_fusion.2), channel_id=1, source_target_pairs={{0,24},{4,28},{8,16},{12,20},{16,8},{20,12},{24,0},{28,4},{1,25},{... | collective-permute-start | bytes 172040 | tf_op jit(solution)/shard_map/ppermute | solution.py:768
  115.0 4.7 %collective-permute-start.7 = (bf16[4,768,384]{2,1,0:T(8,128)(2,1)}, bf16[4,768,384]{2,1,0:T(8,128)(2,1)S(1)}, u32[]{:S(2)}, u32[]{:S(2)}) collective-permute-start(bf16[4,768,384]{2,1,0:T(8,128)(2,1)} %get-tuple-element.95), channel_id=1, source_target_pairs={{0,4},{4,0},{8,12},{12,8},{16,20},{20,16},{24,28},{28,24},{1,5},{5... | collective-permute-start | bytes 7077896 | tf_op jit(solution)/shard_map/ppermute | solution.py:716
  120.3 42.4 %collective-permute-start.10 = (bf16[768,384]{1,0:T(8,128)(2,1)S(1)}, bf16[768,384]{1,0:T(8,128)(2,1)S(1)}, u32[]{:S(2)}, u32[]{:S(2)}) collective-permute-start(bf16[768,384]{1,0:T(8,128)(2,1)S(1)} %get-tuple-element.153), channel_id=1, source_target_pairs={{0,24},{4,28},{8,16},{12,20},{16,8},{20,12},{24,0},{28,4},{1,25},{... | collective-permute-start | bytes 1769480 | tf_op jit(solution)/shard_map/ppermute | solution.py:716
  120.9 41.9 %collective-permute-start.9 = (bf16[768,384]{1,0:T(8,128)(2,1)S(1)}, bf16[768,384]{1,0:T(8,128)(2,1)S(1)}, u32[]{:S(2)}, u32[]{:S(2)}) collective-permute-start(bf16[768,384]{1,0:T(8,128)(2,1)S(1)} %get-tuple-element.154), channel_id=1, source_target_pairs={{0,16},{4,20},{8,24},{12,28},{16,0},{20,4},{24,8},{28,12},{1,17},{... | collective-permute-start | bytes 1769480 | tf_op jit(solution)/shard_map/ppermute | solution.py:716
  122.4 40.4 %collective-permute-start.8 = (bf16[768,384]{1,0:T(8,128)(2,1)S(1)}, bf16[768,384]{1,0:T(8,128)(2,1)}, u32[]{:S(2)}, u32[]{:S(2)}) collective-permute-start(bf16[768,384]{1,0:T(8,128)(2,1)S(1)} %get-tuple-element.155), channel_id=1, source_target_pairs={{0,8},{4,12},{8,0},{12,4},{16,24},{20,28},{24,16},{28,20},{1,9},{5... | collective-permute-start | bytes 1769480 | tf_op jit(solution)/shard_map/ppermute | solution.py:716
  164.2 13.7 %collective-permute-start.11 = (bf16[768,384]{1,0:T(8,128)(2,1)S(1)}, bf16[768,384]{1,0:T(8,128)(2,1)S(1)}, u32[]{:S(2)}, u32[]{:S(2)}) collective-permute-start(bf16[768,384]{1,0:T(8,128)(2,1)S(1)} %add_convert_fusion.4), channel_id=1, source_target_pairs={{0,1},{3,2},{4,5},{7,6},{8,9},{11,10},{12,13},{15,14},{16,17},{19,... | collective-permute-start | bytes 1769480 | tf_op jit(solution)/shard_map/ppermute | solution.py:721
  177.5 7.1 %collective-permute-start.12 = (bf16[4,96,3840]{2,1,0:T(8,128)(2,1)}, bf16[4,96,3840]{2,1,0:T(8,128)(2,1)S(1)}, u32[]{:S(2)}, u32[]{:S(2)}) collective-permute-start(bf16[4,96,3840]{2,1,0:T(8,128)(2,1)} %get-tuple-element.109), channel_id=1, source_target_pairs={{0,4},{4,0},{8,12},{12,8},{16,20},{20,16},{24,28},{28,24},{1,5},{5... | collective-permute-start | bytes 8847368 | tf_op jit(solution)/shard_map/ppermute | solution.py:716
  178.0 33.3 %collective-permute-start.16 = (bf16[768,384]{1,0:T(8,128)(2,1)S(1)}, bf16[768,384]{1,0:T(8,128)(2,1)}, u32[]{:S(2)}, u32[]{:S(2)}) collective-permute-start(bf16[768,384]{1,0:T(8,128)(2,1)S(1)} %add.214), channel_id=1, source_target_pairs={{1,2},{2,1},{5,6},{6,5},{9,10},{10,9},{13,14},{14,13},{17,18},{18,... | collective-permute-start | bytes 1769480 | tf_op jit(solution)/shard_map/ppermute | solution.py:721
  186.4 35.7 %collective-permute-start.15 = (bf16[96,3840]{1,0:T(8,128)(2,1)}, bf16[96,3840]{1,0:T(8,128)(2,1)S(1)}, u32[]{:S(2)}, u32[]{:S(2)}) collective-permute-start(bf16[96,3840]{1,0:T(8,128)(2,1)} %get-tuple-element.149), channel_id=1, source_target_pairs={{0,24},{4,28},{8,16},{12,20},{16,8},{20,12},{24,0},{28,4},{1,25},{... | collective-permute-start | bytes 2211848 | tf_op jit(solution)/shard_map/ppermute | solution.py:716
  186.9 35.3 %collective-permute-start.14 = (bf16[96,3840]{1,0:T(8,128)(2,1)}, bf16[96,3840]{1,0:T(8,128)(2,1)S(1)}, u32[]{:S(2)}, u32[]{:S(2)}) collective-permute-start(bf16[96,3840]{1,0:T(8,128)(2,1)} %get-tuple-element.150), channel_id=1, source_target_pairs={{0,16},{4,20},{8,24},{12,28},{16,0},{20,4},{24,8},{28,12},{1,17},{... | collective-permute-start | bytes 2211848 | tf_op jit(solution)/shard_map/ppermute | solution.py:716
  188.4 33.8 %collective-permute-start.13 = (bf16[96,3840]{1,0:T(8,128)(2,1)S(1)}, bf16[96,3840]{1,0:T(8,128)(2,1)S(1)}, u32[]{:S(2)}, u32[]{:S(2)}) collective-permute-start(bf16[96,3840]{1,0:T(8,128)(2,1)S(1)} %get-tuple-element.151), channel_id=1, source_target_pairs={{0,8},{4,12},{8,0},{12,4},{16,24},{20,28},{24,16},{28,20},{1,9},{5... | collective-permute-start | bytes 2211848 | tf_op jit(solution)/shard_map/ppermute | solution.py:716
  212.7 31.3 %collective-permute-start.18 = (bf16[768,384]{1,0:T(8,128)(2,1)S(1)}, bf16[768,384]{1,0:T(8,128)(2,1)S(1)}, u32[]{:S(2)}, u32[]{:S(2)}) collective-permute-start(bf16[768,384]{1,0:T(8,128)(2,1)S(1)} %add.219), channel_id=1, source_target_pairs={{1,0},{2,3},{5,4},{6,7},{9,8},{10,11},{13,12},{14,15},{17,16},{18,... | collective-permute-start | bytes 1769480 | tf_op jit(solution)/shard_map/ppermute | solution.py:721
  214.1 13.4 %collective-permute-start.17 = (bf16[4,96,1536]{2,1,0:T(8,128)(2,1)S(1)}, bf16[4,96,1536]{2,1,0:T(8,128)(2,1)S(1)}, u32[]{:S(2)}, u32[]{:S(2)}) collective-permute-start(bf16[4,96,1536]{2,1,0:T(8,128)(2,1)S(1)} %copy-done.4), channel_id=1, source_target_pairs={{0,4},{4,0},{8,12},{12,8},{16,20},{20,16},{24,28},{28,24},{1,5},{5... | collective-permute-start | bytes 3538952 | tf_op jit(solution)/shard_map/ppermute | solution.py:716
  222.6 22.6 %collective-permute-start.22 = (bf16[96,3840]{1,0:T(8,128)(2,1)S(1)}, bf16[96,3840]{1,0:T(8,128)(2,1)S(1)}, u32[]{:S(2)}, u32[]{:S(2)}) collective-permute-start(bf16[96,3840]{1,0:T(8,128)(2,1)S(1)} %add_all.1), channel_id=1, source_target_pairs={{0,1},{3,2},{4,5},{7,6},{8,9},{11,10},{12,13},{15,14},{16,17},{19,... | collective-permute-start | bytes 2211848 | tf_op jit(solution)/shard_map/ppermute | solution.py:721
  227.8 17.1 %collective-permute-start.21 = (bf16[96,1536]{1,0:T(8,128)(2,1)S(1)}, bf16[96,1536]{1,0:T(8,128)(2,1)S(1)}, u32[]{:S(2)}, u32[]{:S(2)}) collective-permute-start(bf16[96,1536]{1,0:T(8,128)(2,1)S(1)} %get-tuple-element.157), channel_id=1, source_target_pairs={{0,24},{4,28},{8,16},{12,20},{16,8},{20,12},{24,0},{28,4},{1,25},{... | collective-permute-start | bytes 884744 | tf_op jit(solution)/shard_map/ppermute | solution.py:716
  228.4 16.6 %collective-permute-start.20 = (bf16[96,1536]{1,0:T(8,128)(2,1)S(1)}, bf16[96,1536]{1,0:T(8,128)(2,1)S(1)}, u32[]{:S(2)}, u32[]{:S(2)}) collective-permute-start(bf16[96,1536]{1,0:T(8,128)(2,1)S(1)} %get-tuple-element.158), channel_id=1, source_target_pairs={{0,16},{4,20},{8,24},{12,28},{16,0},{20,4},{24,8},{28,12},{1,17},{... | collective-permute-start | bytes 884744 | tf_op jit(solution)/shard_map/ppermute | solution.py:716
  229.9 15.0 %collective-permute-start.19 = (bf16[96,1536]{1,0:T(8,128)(2,1)S(1)}, bf16[96,1536]{1,0:T(8,128)(2,1)S(1)}, u32[]{:S(2)}, u32[]{:S(2)}) collective-permute-start(bf16[96,1536]{1,0:T(8,128)(2,1)S(1)} %get-tuple-element.159), channel_id=1, source_target_pairs={{0,8},{4,12},{8,0},{12,4},{16,24},{20,28},{24,16},{28,20},{1,9},{5... | collective-permute-start | bytes 884744 | tf_op jit(solution)/shard_map/ppermute | solution.py:716
  243.9 8.3 %collective-permute-start.23 = (bf16[4,112,768]{2,1,0:T(8,128)(2,1)}, bf16[4,112,768]{2,1,0:T(8,128)(2,1)S(1)}, u32[]{:S(2)}, u32[]{:S(2)}) collective-permute-start(bf16[4,112,768]{2,1,0:T(8,128)(2,1)} %get-tuple-element.132), channel_id=1, source_target_pairs={{0,4},{4,0},{8,12},{12,8},{16,20},{20,16},{24,28},{28,24},{1,5},{5... | collective-permute-start | bytes 2064392 | tf_op jit(solution)/shard_map/ppermute | solution.py:716
  245.1 9.5 %collective-permute-start.24 = (bf16[96,1536]{1,0:T(8,128)(2,1)S(1)}, bf16[96,1536]{1,0:T(8,128)(2,1)S(1)}, u32[]{:S(2)}, u32[]{:S(2)}) collective-permute-start(bf16[96,1536]{1,0:T(8,128)(2,1)S(1)} %add_convert_fusion.9), channel_id=1, source_target_pairs={{0,1},{1,0},{2,3},{3,2},{4,5},{5,4},{6,7},{7,6},{8,9},{9,8},{10,11... | collective-permute-start | bytes 884744 | tf_op jit(solution)/shard_map/ppermute | solution.py:721
  245.4 15.4 %collective-permute-start.25 = (bf16[96,3840]{1,0:T(8,128)(2,1)S(1)}, bf16[96,3840]{1,0:T(8,128)(2,1)S(1)}, u32[]{:S(2)}, u32[]{:S(2)}) collective-permute-start(bf16[96,3840]{1,0:T(8,128)(2,1)S(1)} %add.227), channel_id=1, source_target_pairs={{1,2},{2,1},{5,6},{6,5},{9,10},{10,9},{13,14},{14,13},{17,18},{18,... | collective-permute-start | bytes 2211848 | tf_op jit(solution)/shard_map/ppermute | solution.py:721
  254.6 30.2 %collective-permute-start.30 = (bf16[96,1536]{1,0:T(8,128)(2,1)S(1)}, bf16[96,1536]{1,0:T(8,128)(2,1)S(1)}, u32[]{:S(2)}, u32[]{:S(2)}) collective-permute-start(bf16[96,1536]{1,0:T(8,128)(2,1)S(1)} %add.229), channel_id=1, source_target_pairs={{0,2},{1,3},{2,0},{3,1},{4,6},{5,7},{6,4},{7,5},{8,10},{9,11},{10,... | collective-permute-start | bytes 884744 | tf_op jit(solution)/shard_map/ppermute | solution.py:721
  257.2 8.2 %collective-permute-start.28 = (bf16[112,768]{1,0:T(8,128)(2,1)S(1)}, bf16[112,768]{1,0:T(8,128)(2,1)S(1)}, u32[]{:S(2)}, u32[]{:S(2)}) collective-permute-start(bf16[112,768]{1,0:T(8,128)(2,1)S(1)} %get-tuple-element.161), channel_id=1, source_target_pairs={{0,24},{4,28},{8,16},{12,20},{16,8},{20,12},{24,0},{28,4},{1,25},{... | collective-permute-start | bytes 516104 | tf_op jit(solution)/shard_map/ppermute | solution.py:716
  257.7 9.6 %collective-permute-start.27 = (bf16[112,768]{1,0:T(8,128)(2,1)S(1)}, bf16[112,768]{1,0:T(8,128)(2,1)S(1)}, u32[]{:S(2)}, u32[]{:S(2)}) collective-permute-start(bf16[112,768]{1,0:T(8,128)(2,1)S(1)} %get-tuple-element.162), channel_id=1, source_target_pairs={{0,16},{4,20},{8,24},{12,28},{16,0},{20,4},{24,8},{28,12},{1,17},{... | collective-permute-start | bytes 516104 | tf_op jit(solution)/shard_map/ppermute | solution.py:716
  259.2 8.1 %collective-permute-start.26 = (bf16[112,768]{1,0:T(8,128)(2,1)S(1)}, bf16[112,768]{1,0:T(8,128)(2,1)S(1)}, u32[]{:S(2)}, u32[]{:S(2)}) collective-permute-start(bf16[112,768]{1,0:T(8,128)(2,1)S(1)} %get-tuple-element.163), channel_id=1, source_target_pairs={{0,8},{4,12},{8,0},{12,4},{16,24},{20,28},{24,16},{28,20},{1,9},{5... | collective-permute-start | bytes 516104 | tf_op jit(solution)/shard_map/ppermute | solution.py:716
  267.4 16.6 %collective-permute-start.29 = (bf16[112,768]{1,0:T(8,128)(2,1)S(1)}, bf16[112,768]{1,0:T(8,128)(2,1)S(1)}, u32[]{:S(2)}, u32[]{:S(2)}) collective-permute-start(bf16[112,768]{1,0:T(8,128)(2,1)S(1)} %add_convert_fusion.14), channel_id=1, source_target_pairs={{0,1},{1,0},{2,3},{3,2},{4,5},{5,4},{6,7},{7,6},{8,9},{9,8},{10,11... | collective-permute-start | bytes 516104 | tf_op jit(solution)/shard_map/ppermute | solution.py:721
  278.7 24.7 %collective-permute-start.32 = (bf16[96,3840]{1,0:T(8,128)(2,1)S(1)}, bf16[96,3840]{1,0:T(8,128)(2,1)S(1)}, u32[]{:S(2)}, u32[]{:S(2)}) collective-permute-start(bf16[96,3840]{1,0:T(8,128)(2,1)S(1)} %add.230), channel_id=1, source_target_pairs={{1,0},{2,3},{5,4},{6,7},{9,8},{10,11},{13,12},{14,15},{17,16},{18,... | collective-permute-start | bytes 2211848 | tf_op jit(solution)/shard_map/ppermute | solution.py:721
  284.0 11.0 %collective-permute-start.31 = (bf16[112,768]{1,0:T(8,128)(2,1)S(1)}, bf16[112,768]{1,0:T(8,128)(2,1)S(1)}, u32[]{:S(2)}, u32[]{:S(2)}) collective-permute-start(bf16[112,768]{1,0:T(8,128)(2,1)S(1)} %add.237), channel_id=1, source_target_pairs={{0,2},{1,3},{2,0},{3,1},{4,6},{5,7},{6,4},{7,5},{8,10},{9,11},{10,... | collective-permute-start | bytes 516104 | tf_op jit(solution)/shard_map/ppermute | solution.py:721
  (6 other events, 25.6 us)

commit v5 on v4

--- a/solution.py
+++ b/solution.py
@@ -178,9 +178,7 @@
         copies[1].wait()
         copies[2].wait()
 
-    group = width // TILE
     raw, made = {}, {}
-    sums = [y1[:, n * TILE : (n + 1) * TILE] + vec(bf_ref, slice(n * TILE, (n + 1) * TILE)) for n in range(group)]
 
     def expand(i):
         cols = slice(i * TILE, (i + 1) * TILE)
@@ -193,16 +191,9 @@
         act_ref[:, cols] = made[i]
         dg_ref[:, cols] = slope.astype(LOW)
 
-    def contract(i):
-        first, n = i // group * group, i % group
-        left = jnp.concatenate([made[first + j] for j in range(group)], 1)
-        cols = slice(n * TILE, (n + 1) * TILE)
-        sums[n] = sums[n] + mm(left, wf_ref[first * TILE : (first + group) * TILE, cols])
-
-    late = [lambda i: None] * (group - 1)
-    staged(inner // TILE, expand, activate, *late, contract)
-
-    total = jnp.concatenate(sums, 1)
+    staged(inner // TILE, expand, activate)
+    left = jnp.concatenate([made[i] for i in range(inner // TILE)], 1)
+    total = (y1 + vec(bf_ref)) + mm(left, wf_ref[...])
     h2_ref[...] = total.astype(LOW)
     y2 = norm_parts(total)[0] * vec(g2_ref) + vec(s2_ref)
     for part in range(rows_all // q_len):
@@ -362,20 +353,15 @@
 
 
 def dense_back_kernel(
-    dims, core_ref, gf_ref, dg_ref, h1_ref, ctx_t_ref, wf_hbm, wi_hbm, wo_hbm, g1_ref,
-    gu_ref, ga_ref, gc_ref, stat_ref, bi_ref, send_ref, keep_ref,
-    sum_ref, wf_ref, wi_ref, wo_ref, sems,
+    dims, gf_ref, dg_ref, h1_ref, wf_hbm, wi_hbm, wo_hbm, g1_ref,
+    gu_ref, ga_ref, gc_ref, stat_ref, bi_ref,
+    wf_ref, wi_ref, wo_ref, sems,
 ):
-    rows_all, width, inner = dims
+    inner = dims
     block = pl.program_id(0)
-    chunk = TILE
-    group = width // chunk
     copies = [
-        fetch(wf_hbm.at[pl.ds(0, width), :], wf_ref.at[pl.ds(0, width), :], sems, 0),
-        fetch(wi_hbm.at[:, pl.ds(0, width)], wi_ref.at[:, pl.ds(0, width)], sems, 1),
-        fetch(wf_hbm.at[pl.ds(width, inner - width), :], wf_ref.at[pl.ds(width, inner - width), :], sems, 2),
-        fetch(wi_hbm.at[:, pl.ds(width, inner - width)], wi_ref.at[:, pl.ds(width, inner - width)], sems, 3),
-        fetch(wo_hbm, wo_ref, sems, 4),
+        fetch(source, target, sems, index)
+        for index, (source, target) in enumerate([(wf_hbm, wf_ref), (wi_hbm, wi_ref), (wo_hbm, wo_ref)])
     ]
 
     @pl.when(block == 0)
@@ -385,44 +371,29 @@
         stat_ref[...] = jnp.zeros_like(stat_ref)
         bi_ref[...] = jnp.zeros_like(bi_ref)
         copies[0].wait()
-        copies[1].wait()
 
     gf = gf_ref[...]
-    raw, made = {}, {}
-    sums = [gf[:, n * chunk : (n + 1) * chunk].astype(F32) for n in range(group)]
-    biases = []
+    raw, made, biases = {}, {}, []
 
     def spread(i):
-        raw[i] = mm_nt(gf, wf_ref[i * chunk : (i + 1) * chunk, :])
+        raw[i] = mm_nt(gf, wf_ref[i * TILE : (i + 1) * TILE, :])
 
     def slope(i):
-        cols = slice(i * chunk, (i + 1) * chunk)
+        cols = slice(i * TILE, (i + 1) * TILE)
         made[i] = (raw.pop(i) * dg_ref[:, cols].astype(F32)).astype(LOW)
         gu_ref[:, cols] = made[i]
         biases.append(jnp.sum(made[i].astype(F32), 0, keepdims=True))
 
-    def gather(i):
-        first, n = i // group * group, i % group
-        left = jnp.concatenate([made[first + j] for j in range(group)], 1)
-        cols = slice(n * chunk, (n + 1) * chunk)
-        sums[n] = sums[n] + mm_nt(left, wi_ref[cols, first * chunk : (first + group) * chunk])
-
-    staged(group, spread, slope)
+    staged(inner // TILE, spread, slope)
+    bi_ref[0:1, :] += jnp.concatenate(biases, 1)
+    left = jnp.concatenate([made[i] for i in range(inner // TILE)], 1)
 
     @pl.when(block == 0)
     def _():
-        for copy in copies[2:]:
+        for copy in copies[1:]:
             copy.wait()
 
-    count = inner // chunk
-    staged(
-        count,
-        lambda i: spread(i + group) if i + group < count else None,
-        lambda i: slope(i + group) if i + group < count else None,
-        gather,
-    )
-    bi_ref[0:1, :] += jnp.concatenate(biases, 1)
-    total = jnp.concatenate(sums, 1)
+    total = gf.astype(F32) + mm_nt(left, wi_ref[...])
     n1, r1 = norm_parts(h1_ref[...].astype(F32))
     stat_ref[0:1, :] += jnp.sum(total * n1, 0, keepdims=True)
     stat_ref[1:2, :] += jnp.sum(total, 0, keepdims=True)
@@ -432,19 +403,6 @@
     ga_ref[...] = low
     stat_ref[2:3, :] += jnp.sum(low.astype(F32), 0, keepdims=True)
     gc_ref[...] = mm_nt(low, wo_ref[...]).astype(LOW)
-    product = mm(ctx_t_ref[...], low)
-
-    @pl.when(block == 0)
-    def _():
-        sum_ref[...] = product
-
-    @pl.when(block > 0)
-    def _():
-        sum_ref[...] += product
-
-    @pl.when(block == pl.num_programs(0) - 1)
-    def _():
-        store_shards(core_ref, sum_ref[...], send_ref, keep_ref)
 
 
 def attend_back_kernel(
@@ -547,23 +505,21 @@
         store_shards(core_ref, sum_ref[...], send_ref, keep_ref, tails=tails)
 
 
-def input_grad_kernel(grad_ref, base_ref, wq_ref, wk_ref, wv_ref, *out_refs):
-    wide = wq_ref.shape[1]
+def input_grad_kernel(groups, *refs):
+    grads, (base_ref, wq_ref, wk_ref, wv_ref, gq_ref, gp_ref) = refs[: len(groups)], refs[len(groups) :]
     total = base_ref[...].astype(F32)
-    for number, w_ref in enumerate((wq_ref, wk_ref, wv_ref)):
-        total = total + mm_nt(grad_ref[:, number * wide : (number + 1) * wide], w_ref[...])
+    for grad_ref, (start, wide) in zip(grads, groups):
+        for number, w_ref in enumerate((wq_ref, wk_ref, wv_ref)):
+            total = total + mm_nt(grad_ref[:, number * wide : (number + 1) * wide], w_ref[:, start : start + wide])
     low = total.astype(LOW)
-    if len(out_refs) == 1:
-        out_refs[0][...] = low
-        return
 
     @pl.when(pl.program_id(0) == 0)
     def _():
-        out_refs[0][...] = low
+        gq_ref[...] = low
 
     @pl.when(pl.program_id(0) > 0)
     def _():
-        out_refs[1][...] = low
+        gp_ref[...] = low
 
 
 def weight_grad_kernel(core_ref, left_ref, right_ref, send_ref, keep_ref):
@@ -610,7 +566,7 @@
     return pl.BlockSpec(shape, lambda i: (0,) * len(shape), pipeline_mode=pl.Buffered(1))
 
 
-def call(body, operands, in_specs, outs, grid, room, deps=(), old=(), name=None, scratch=(), us=12):
+def call(body, operands, in_specs, outs, grid, room, deps=(), old=(), into=0, name=None, scratch=(), us=12):
     count, extra = len(operands), len(old)
     if deps:
         tied = min(range(count), key=lambda i: operands[i].size)
@@ -625,21 +581,21 @@
         grid=grid,
         in_specs=list(in_specs) + [pl.BlockSpec(memory_space=pl.ANY)] * extra,
         out_specs=[spec for spec, _ in outs],
-        out_shape=[kind for _, kind in outs],
+        out_shape=[jax.ShapeDtypeStruct(kind.shape, kind.dtype) for _, kind in outs],
         scratch_shapes=scratch,
-        input_output_aliases={count + i: i for i in range(extra)},
+        input_output_aliases={count + i: into + i for i in range(extra)},
         compiler_params=pltpu.CompilerParams(vmem_limit_bytes=room * 1024 * 1024),
         cost_estimate=pl.CostEstimate(flops=int(us * 1.15e9), bytes_accessed=0, transcendentals=0),
         name=name,
     )(*operands, *old)
 
 
-def weight_grad(left_t, right, row_count, core, deps, old):
+def weight_grad(left_t, right, row_count, core, deps, old=(), at=0, us=12):
     height, depth = left_t.shape
     wide = right.shape[1]
     block = min(wide, 768)
-    shape = old[0].shape
-    spec = pl.BlockSpec((*shape[:2], block), lambda i: (0, 0, i))
+    shape = old[0].shape if old else (row_count // 2, height // row_count, wide)
+    spec = pl.BlockSpec((*shape[:2], block), lambda i: (0, 0, i + at))
     return call(
         weight_grad_kernel,
         (core, left_t, right),
@@ -654,6 +610,7 @@
         deps,
         old,
         name="weight_grad",
+        us=us,
     )
 
 
@@ -834,14 +791,14 @@
 
     )
 
-    rows_part = rows_all // 2
-    parts = 2 * blocks
+    rows_part = rows_all
+    parts = blocks
 
     def by_part(wide):
         return pl.BlockSpec((rows_part, wide), lambda i: (i, 0))
 
-    queries_part = pl.BlockSpec((rows_part, width), lambda i: (jnp.minimum(i, 1), 0))
-    passages_part = pl.BlockSpec((rows_part, width), lambda i: (jnp.maximum(i - 2, 0), 0))
+    queries_part = pl.BlockSpec((rows_part, width), lambda i: (0, 0))
+    passages_part = pl.BlockSpec((rows_part, width), lambda i: (jnp.maximum(i - 1, 0), 0))
     h1, y1, act, slope, h2, query_out, passage_out, pooled, payload = call(
         partial(dense_kernel, (q_dev, q_len, p_len, width, inner)),
         (
@@ -917,45 +874,39 @@
 
     y1_t = turn([y1], [by_block(width)], outer.sent)
     deps = outer.turn(y1_t)
-    attn_spec = pl.BlockSpec((half, cut, width), lambda i: (0, 0, inner // width))
-    grad_u, grad_attn, grad_ctx, stat_one, grad_bias_inner, *up_parts = call(
-        partial(dense_back_kernel, (rows_all, width, inner)),
-        (core, grad_f, slope, h1, ctx_t, w_outer, w_inner, w_attn_out, gain_one),
-        [smem, by_block(width), by_block(inner), by_block(width), by_block_t(width)]
-        + [anywhere, anywhere, anywhere, thin],
+    head_dim = width // HEADS
+    third = 4 * head_dim
+    groups = [(0, 2 * third), (2 * third, third)]
+    grad_u, grad_attn, grad_ctx, stat_one, grad_bias_inner = call(
+        partial(dense_back_kernel, inner),
+        (grad_f, slope, h1, w_outer, w_inner, w_attn_out, gain_one),
+        [by_block(width), by_block(inner), by_block(width), anywhere, anywhere, anywhere, thin],
         [
             (by_block(inner), shape(total_rows, inner)),
             (by_block(width), shape(total_rows, width)),
             (by_block(width), shape(total_rows, width)),
             (fixed((8, width)), smalls),
             (fixed((8, inner)), shape(8, inner, kind=F32)),
-            (attn_spec, shape(half, cut, inner + width)),
-            (attn_spec, shape(half, cut, inner + width)),
         ],
         (blocks,),
         60,
         deps,
         name="dense_back",
         scratch=[
-            pltpu.VMEM((width, width), F32),
             pltpu.VMEM((inner, width), LOW),
             pltpu.VMEM((width, inner), LOW),
             pltpu.VMEM((width, width), LOW),
-            pltpu.SemaphoreType.DMA((5,)),
+            pltpu.SemaphoreType.DMA((3,)),
         ],
     )
     deps = outer.turn(stat_one)
-    up_flow = Flow(*weight_grad(y1_t, grad_u, row_count, core, deps, up_parts), line=True, fused=True)
+    up_flow = Flow(*weight_grad(y1_t, grad_u, row_count, core, deps), fused=True)
     up_flow.step()
     deps = up_flow.sent + outer.turn(up_flow.sent[0])
     x_t = turn([queries, passages], [queries_spec, passages_spec], deps)
     deps = up_flow.turn(x_t)
 
-    head_dim = width // HEADS
-    third = 4 * head_dim
-    groups = [(0, 2 * third), (2 * third, third)]
-
-    def attend_back(start, wide, deps, extra=()):
+    def attend_back(start, wide, deps, extra=(), room=None):
         pairs = wide // (2 * head_dim)
         index = start // wide
         cols = pl.BlockSpec((rows_all, wide), lambda i: (i, index))
@@ -976,52 +927,40 @@
                 (by_block(3 * wide), shape(total_rows, 3 * wide)),
                 (fixed((8, wide)), shape(8, wide, kind=F32)),
             ]
-            + [(fixed((half, rows, 3 * wide)), shape(half, rows, 3 * wide))] * 2,
+            + [(fixed((half, rows, 3 * wide)), shape(half, rows, room or 3 * wide))] * 2,
             (blocks,),
             56,
             deps,
             name="attend_back",
             scratch=[pltpu.VMEM((width, 3 * wide), F32)],
+            us=12 if room else 40,
         )
 
-    def input_grad(start, wide, grad, base, outs, deps, us):
-        index = start // wide
-        cols = pl.BlockSpec((width, wide), lambda i: (0, index), pipeline_mode=pl.Buffered(1))
-        return call(
-            input_grad_kernel,
-            (grad, base, w_query, w_key, w_value),
-            [by_block(3 * wide), by_block(width), cols, cols, cols],
-            outs,
-            (blocks,),
-            56,
-            deps,
-            name="input_grad",
-            us=us,
-        )
-
-    grad_a, stat_a, *mixed_parts = attend_back(*groups[0], deps)
+    grad_a, stat_a, *mixed_parts = attend_back(*groups[0], deps, room=6 * third + width)
+    at = 6 * third // width
+    mixed_parts = weight_grad(ctx_t, grad_attn, row_count, core, [stat_a], mixed_parts, at, us=0)
     mixed_flow = Flow(*mixed_parts)
     mixed_flow.step()
-    deps = mixed_flow.sent + outer.turn(stat_a)
-    (part_grad,) = input_grad(
-        *groups[0], grad_a, grad_attn, [(by_block(width), shape(total_rows, width))], deps, 0
-    )
-    deps = up_flow.turn(part_grad) + mixed_flow.turn(up_flow.kept)
+    token = mixed_flow.sent[0]
+    deps = mixed_flow.sent + outer.turn(token) + up_flow.turn(token)
     extra = (stat_two, stat_one, grad_bias_inner, stat_a)
     grad_b, stat_b, *last_parts = attend_back(*groups[1], deps, extra)
     last_flow = Flow(*last_parts)
     last_flow.step()
     deps = last_flow.sent + outer.turn(stat_b) + mixed_flow.turn(stat_b) + up_flow.turn(stat_b)
-    query_grad, passage_grad = input_grad(
-        *groups[1],
-        grad_b,
-        part_grad,
+    query_grad, passage_grad = call(
+        partial(input_grad_kernel, groups),
+        (grad_a, grad_b, grad_attn, w_query, w_key, w_value),
+        [by_block(3 * wide) for _, wide in groups] + [by_block(width), square, square, square],
         [
             (queries_spec, shape(rows_all, width)),
             (passages_spec, shape(p_dev * rows_all, width)),
         ],
+        (blocks,),
+        56,
         deps,
-        12,
+        name="input_grad",
+        us=40,
     )
     last_flow.turn(passage_grad)
     mixed_flow.turn(last_flow.kept)
@@ -1030,10 +969,10 @@
     (turned,) = call(
         turn_kernel, (outer.kept,), [const_spec((width, cut_inner))], outs, (1,), 56, [up_flow.kept], name="turn", us=40
     )
-    last_flow.turn(turned)
+    mixed_flow.turn(turned)
+    last_flow.turn(mixed_flow.kept)
     last_flow.turn()
     mixed_flow.turn(last_flow.kept)
-    last_flow.turn(mixed_flow.kept)
     flows = [outer, up_flow, mixed_flow, last_flow]
     while not all(flow.done for flow in flows):
         for flow in flows:
@@ -1046,7 +985,6 @@
         ).astype(F32)
         for i in range(3)
     ]
-    up_sum = up_flow.kept
     small = last[cut:].astype(F32)
     return (
         loss[0, 0],
@@ -1055,8 +993,8 @@
         query_grad.reshape(query_tokens.shape),
         passage_grad.reshape(passage_tokens.shape),
         *qkv,
-        up_sum[:, inner:].astype(F32),
-        up_sum[:, :inner].astype(F32),
+        mixed[:, 6 * third :].astype(F32),
+        up_flow.kept.astype(F32),
         turned,
         *[small[i, :cut] for i in range(3)],
         small[8, : inner // row_count],

time: 309 us -> 308 us (level)
  waiting for transfers between devices: 38.3 us -> 62.7 us
  Pallas kernels: 203 us -> 187 us
  starting transfers between devices: 48.4 us -> 38.2 us
    ppermute x10 -> x9, waiting for transfers between devices: 22.2 us -> 41.3 us  [step(): self.got = [lax.ppermute(self.kept, 'col', self.line[0][1])]]
    pallas_call x13, Pallas kernels: 200 us -> 184 us  [call(): pl.pallas_call(kernel, grid=grid, in_specs=list(in_specs) + [pl.BlockSpec...]
    ppermute x10 -> x9, starting transfers between devices: 24.8 us -> 15.8 us  [step(): self.got = [lax.ppermute(self.kept, 'col', self.line[0][1])]]
    ppermute x16, waiting for transfers between devices: 4.35 us -> 9.68 us  [step(): lax.ppermute(sent, 'row', [(i, i ^ mask) for i in range(size)])]
  transfers between devices with their start and end apart: 33 -> 32, of which waited for: 14 -> 15; matrix products, arithmetic and copies ran while one was open for 3% -> 2% of each run, Pallas kernels for 36% -> 35%
where the time goes in v5:
time: 308 us; the launch traced here: 302 us
  Pallas kernels  187 us (61%)
  waiting for transfers between devices  62.7 us (20%)
  starting transfers between devices  38.2 us (12%)
  other arithmetic  10.6 us (3%)
    pallas_call x13, Pallas kernels, call(): pl.pallas_call(kernel, grid=grid, in_specs=list(in_specs) + [pl.BlockSpec...  184 us
    ppermute x9, waiting for transfers between devices, step(): self.got = [lax.ppermute(self.kept, 'col', self.line[0][1])]  41.3 us
    ppermute x9, starting transfers between devices, step(): self.got = [lax.ppermute(self.kept, 'col', self.line[0][1])]  15.8 us
    ppermute x16, starting transfers between devices, step(): lax.ppermute(sent, 'row', [(i, i ^ mask) for i in range(size)])  13.1 us
    ppermute x7, waiting for transfers between devices, gather_all(): pieces.append(lax.ppermute(piece, name, pairs))  11.8 us
    ppermute x16, waiting for transfers between devices, step(): lax.ppermute(sent, 'row', [(i, i ^ mask) for i in range(size)])  9.68 us
    ppermute x7, starting transfers between devices, gather_all(): pieces.append(lax.ppermute(piece, name, pairs))  9.31 us
  transfers between devices with their start and end apart: 32, of which 15 were waited for; matrix products, arithmetic and copies ran while one was open for 2% of the time, Pallas kernels for 35%

profile of v5, /device:TPU:0, one launch (start us, length us, event | category | flops | bytes accessed | tf_op | source)
XLA Modules:
  0.0 302.1 jit_solution(605932826931808489)
XLA Ops:
  0.7 20.9 %attend.1 = (bf16[1536,768]{1,0:T(8,128)(2,1)}, bf16[1536,768]{1,0:T(8,128)(2,1)}, bf16[1536,768]{1,0:T(8,128)(2,1)}, bf16[768,1536]{1,0:T(8,128)(2,1)}, f32[3,6,8,512]{3,2,1,0:T(8,128)}) custom-call(s32[4]{0:T(128)} %refs_1_.9, s32[2]{0:T(128)} %refs_2_.7, bf16[512,768]{1,0:T(8,128)(2,1)} %bitcast.76, bf16[1024,768]{1,0:T(8,128)(2,1)} %bitcast.73, ...), custom_call_target="tpu_custom_call" | custom-call | flops 13799999488 | tf_op jit(solution)/shard_map/attend/pallas_call | solution.py:579
  21.5 39.0 %dense.1 = (bf16[1536,768]{1,0:T(8,128)(2,1)}, bf16[1536,768]{1,0:T(8,128)(2,1)}, bf16[1536,3072]{1,0:T(8,128)(2,1)}, bf16[1536,3072]{1,0:T(8,128)(2,1)}, bf16[1...) custom-call(s32[4]{0:T(128)} %refs_1_.9, ...), custom_call_target="tpu_custom_call" | custom-call | flops 13799999488 | tf_op jit(solution)/shard_map/dense/pallas_call | solution.py:579
  60.6 3.1 %collective-permute-start.2 = (bf16[8,896]{1,0:T(8,128)(2,1)}, bf16[8,896]{1,0:T(8,128)(2,1)S(1)}, u32[]{:S(2)}, u32[]{:S(2)}) collective-permute-start(bf16[8,896]{1,0:T(8,128)(2,1)} %get-tuple-element.84.own_ref), channel_id=1, source_target_pairs={{0,1},{1,0},{2,3},{3,2},{4,5},{5,4},{6,7},{7,6},{8,9},{9,8},{10,11... | collective-permute-start | bytes 43016 | tf_op jit(solution)/shard_map/ppermute | solution.py:725
  63.7 2.6 collective-permute-start.1
  66.3 2.3 collective-permute-done.1
  68.5 3.5 %collective-permute-done = bf16[8,896]{1,0:T(8,128)(2,1)S(1)} collective-permute-done((bf16[8,896]{1,0:T(8,128)(2,1)}, bf16[8,896]{1,0:T(8,128)(2,1)S(1)}, u32[]{:S(2)}, u32[]{:S(2)}) %collective-permute-start) | collective-permute-done | bytes 14368 | tf_op jit(solution)/shard_map/ppermute | solution.py:725
  72.7 1.6 collective-permute-start.5
  74.3 1.5 collective-permute-start.4
  78.4 2.4 collective-permute-done.3
  83.4 2.9 loss.1
  86.4 18.2 %outer_grad.1 = (bf16[1536,768]{1,0:T(8,128)(2,1)}, f32[8,768]{1,0:T(8,128)}, bf16[4,768,384]{2,1,0:T(8,128)(2,1)}, bf16[4,768,384]{2,1,0:T(8,128)(2,1)}) custom-call(s32[1]{0:T(128)} %bitcast.6.refs_0_, s32[4]{0:T(128)} %refs_1_.9, s32[2]{0:T(128)} %refs_2_.7, f32[8,768]{1,0:T(8,128)} %get-tuple-element.89.refs_3_, ...), custom_call_target="tpu_custom_call" | custom-call | flops 13799999488 | tf_op jit(solution)/shard_map/outer_grad/pallas_call | solution.py:579
  104.7 4.5 %turn.3.refs_1_ = bf16[768,1536]{1,0:T(8,128)(2,1)} custom-call(bf16[1536,768]{1,0:T(8,128)(2,1)} %get-tuple-element.95.refs_0_), custom_call_target="tpu_custom_call" | custom-call | flops 46000001024 | tf_op jit(solution)/shard_map/turn/pallas_call | solution.py:579
  110.5 1.5 collective-permute-start.9
  113.5 31.1 %dense_back.1 = (bf16[1536,3072]{1,0:T(8,128)(2,1)}, bf16[1536,768]{1,0:T(8,128)(2,1)}, bf16[1536,768]{1,0:T(8,128)(2,1)}, f32[8,768]{1,0:T(8,128)}, f32[8,3072]{1,0:T(8,128)}) custom-call(bf16[1536,768]{1,0:T(8,128)(2,1)} %get-tuple-element.97.refs_0_, bf16[1536,3072]{1,0:T(8,128)(2,1)} %get-tuple-element.98.refs_1_, ...), custom_call_target="tpu_custom_call" | custom-call | flops 13799999488 | tf_op jit(solution)/shard_map/dense_back/pallas_call | solution.py:579
  147.3 12.0 %weight_grad.2 = (bf16[4,96,3072]{2,1,0:T(8,128)(2,1)}, bf16[4,96,3072]{2,1,0:T(8,128)(2,1)}) custom-call(s32[1]{0:T(128)} %bitcast.6.refs_0_, bf16[768,1536]{1,0:T(8,128)(2,1)} %turn.3.refs_1_, bf16[1536,3072]{1,0:T(8,128)(2,1)} %get-tuple-element.104.refs_2_), custom_call_target="tpu_custom_call" | custom-call | flops 13799999488 | tf_op jit(solution)/shard_map/weight_grad/pallas_call | solution.py:579
  160.5 5.0 %turn.4.refs_9_ = bf16[768,1536]{1,0:T(8,128)(2,1)} custom-call(bf16[512,768]{1,0:T(8,128)(2,1)} %bitcast.78, bf16[1024,768]{1,0:T(8,128)(2,1)} %bitcast.75), custom_call_target="tpu_custom_call" | custom-call | flops 46000001024 | tf_op jit(solution)/shard_map/turn/pallas_call | solution.py:579
  170.0 21.7 %attend_back.2 = (bf16[1536,1536]{1,0:T(8,128)(2,1)}, f32[8,512]{1,0:T(8,128)}, bf16[4,96,2304]{2,1,0:T(8,128)(2,1)}, bf16[4,96,2304]{2,1,0:T(8,128)(2,1)}) custom-call(s32[1]{0:T(128)} %bitcast.6.refs_0_, s32[4]{0:T(128)} %refs_1_.9, s32[2]{0:T(128)} %refs_2_.7, bf16[1536,768]{1,0:T(8,128)(2,1)} %get-tuple-element.111.refs_3_, ...), custom_call_target="tpu_custom_call" | custom-call | flops 13799999488 | tf_op jit(solution)/shard_map/attend_back/pallas_call | solution.py:579
  191.7 5.6 %weight_grad.3 = (bf16[4,96,2304]{2,1,0:T(8,128)(2,1)}, bf16[4,96,2304]{2,1,0:T(8,128)(2,1)}) custom-call(s32[1]{0:T(128)} %bitcast.6.refs_0_, bf16[768,1536]{1,0:T(8,128)(2,1)} %get-tuple-element.83.refs_5_.refs_6_.refs_1_, bf16[1536,768]{1,0:T(8,128)(2,1)} %get-tuple-element.119.refs_2_, ...), custom_call_target="tpu_custom_call", output_to_operand_aliasing={{0}: (3, {}), {1}: (4, {})} | custom-call | tf_op jit(solution)/shard_map/weight_grad/pallas_call | solution.py:579
  199.1 3.8 %collective-permute-start.19 = (bf16[96,3072]{1,0:T(8,128)(2,1)S(1)}, bf16[96,3072]{1,0:T(8,128)(2,1)S(1)}, u32[]{:S(2)}, u32[]{:S(2)}) collective-permute-start(bf16[96,3072]{1,0:T(8,128)(2,1)S(1)} %add_all.1), channel_id=1, source_target_pairs={{0,1},{1,0},{2,3},{3,2},{4,5},{5,4},{6,7},{7,6},{8,9},{9,8},{10,11... | collective-permute-start | bytes 1769480 | tf_op jit(solution)/shard_map/ppermute | solution.py:678
  202.9 12.5 %attend_back.3 = (bf16[1536,768]{1,0:T(8,128)(2,1)}, f32[8,256]{1,0:T(8,128)}, bf16[4,112,768]{2,1,0:T(8,128)(2,1)}, bf16[4,112,768]{2,1,0:T(8,128)(2,1)}) custom-call(s32[1]{0:T(128)} %bitcast.6.refs_0_, s32[4]{0:T(128)} %refs_1_.9, s32[2]{0:T(128)} %refs_2_.7, bf16[1536,768]{1,0:T(8,128)(2,1)} %get-tuple-element.111.refs_3_, ...), custom_call_target="tpu_custom_call" | custom-call | flops 46000001024 | tf_op jit(solution)/shard_map/attend_back/pallas_call | solution.py:579
  217.5 11.6 %collective-permute-done.19 = bf16[96,3072]{1,0:T(8,128)(2,1)S(1)} collective-permute-done((bf16[96,3072]{1,0:T(8,128)(2,1)S(1)}, bf16[96,3072]{1,0:T(8,128)(2,1)S(1)}, u32[]{:S(2)}, u32[]{:S(2)}) %collective-permute-start.19) | collective-permute-done | bytes 589856 | tf_op jit(solution)/shard_map/ppermute | solution.py:678
  234.3 10.8 %input_grad.1 = (bf16[512,768]{1,0:T(8,128)(2,1)}, bf16[1024,768]{1,0:T(8,128)(2,1)}) custom-call(bf16[1536,1536]{1,0:T(8,128)(2,1)} %get-tuple-element.116.refs_0_, bf16[1536,768]{1,0:T(8,128)(2,1)} %get-tuple-element.128.refs_1_, bf16[1536,768]{1,0:T(8,128)(2,1)} %get-tuple-element.119.refs_2_, bf16[768,768]{1,0:T(8,128)(2,1)} %refs_3_.2, ...), custom_call_target="tpu_custom_call" | custom-call | flops 46000001024 | tf_op jit(solution)/shard_map/input_grad/pallas_call | solution.py:579
  245.8 1.5 collective-permute-start.27
  247.4 9.4 %collective-permute-done.22 = bf16[96,2304]{1,0:T(8,128)(2,1)S(1)} collective-permute-done((bf16[96,2304]{1,0:T(8,128)(2,1)S(1)}, bf16[96,2304]{1,0:T(8,128)(2,1)S(1)}, u32[]{:S(2)}, u32[]{:S(2)}) %collective-permute-start.22) | collective-permute-done | bytes 442400 | tf_op jit(solution)/shard_map/ppermute | solution.py:673
  257.0 2.5 collective-permute-start.25
  260.7 2.3 turn.5
  263.0 4.6 %collective-permute-done.25 = bf16[96,2304]{1,0:T(8,128)(2,1)S(1)} collective-permute-done((bf16[96,2304]{1,0:T(8,128)(2,1)S(1)}, bf16[96,2304]{1,0:T(8,128)(2,1)S(1)}, u32[]{:S(2)}, u32[]{:S(2)}) %collective-permute-start.25) | collective-permute-done | bytes 442400 | tf_op jit(solution)/shard_map/ppermute | solution.py:678
  267.8 2.1 collective-permute-start.29
  269.9 4.8 %collective-permute-done.29 = bf16[112,768]{1,0:T(8,128)(2,1)S(1)} collective-permute-done((bf16[112,768]{1,0:T(8,128)(2,1)S(1)}, bf16[112,768]{1,0:T(8,128)(2,1)S(1)}, u32[]{:S(2)}, u32[]{:S(2)}) %collective-permute-start.29) | collective-permute-done | bytes 172064 | tf_op jit(solution)/shard_map/ppermute | solution.py:678
  276.0 2.9 collective-permute-start.30
  278.9 12.5 %collective-permute-done.31 = bf16[112,768]{1,0:T(8,128)(2,1)S(1)} collective-permute-done((bf16[112,768]{1,0:T(8,128)(2,1)S(1)}, bf16[112,768]{1,0:T(8,128)(2,1)S(1)}, u32[]{:S(2)}, u32[]{:S(2)}) %collective-permute-start.31) | collective-permute-done | bytes 172064 | tf_op jit(solution)/shard_map/ppermute | solution.py:678
  292.7 6.5 %collective-permute-done.30 = bf16[96,2304]{1,0:T(8,128)(2,1)S(1)} collective-permute-done((bf16[96,2304]{1,0:T(8,128)(2,1)S(1)}, bf16[96,2304]{1,0:T(8,128)(2,1)S(1)}, u32[]{:S(2)}, u32[]{:S(2)}) %collective-permute-start.30) | collective-permute-done | bytes 442400 | tf_op jit(solution)/shard_map/ppermute | solution.py:678
  (86 shorter events, 33.4 us)
Async XLA Ops:
  60.6 5.7 %collective-permute-start.2 = (bf16[8,896]{1,0:T(8,128)(2,1)}, bf16[8,896]{1,0:T(8,128)(2,1)S(1)}, u32[]{:S(2)}, u32[]{:S(2)}) collective-permute-start(bf16[8,896]{1,0:T(8,128)(2,1)} %get-tuple-element.84.own_ref), channel_id=1, source_target_pairs={{0,1},{1,0},{2,3},{3,2},{4,5},{5,4},{6,7},{7,6},{8,9},{9,8},{10,11... | collective-permute-start | bytes 43016 | tf_op jit(solution)/shard_map/ppermute | solution.py:725
  63.7 4.9 %collective-permute-start.1 = (bf16[8,896]{1,0:T(8,128)(2,1)}, bf16[8,896]{1,0:T(8,128)(2,1)S(1)}, u32[]{:S(2)}, u32[]{:S(2)}) collective-permute-start(bf16[8,896]{1,0:T(8,128)(2,1)} %get-tuple-element.84.own_ref), channel_id=1, source_target_pairs={{0,2},{1,3},{2,0},{3,1},{4,6},{5,7},{6,4},{7,5},{8,10},{9,11},{10,... | collective-permute-start | bytes 43016 | tf_op jit(solution)/shard_map/ppermute | solution.py:725
  66.3 5.7 %collective-permute-start = (bf16[8,896]{1,0:T(8,128)(2,1)}, bf16[8,896]{1,0:T(8,128)(2,1)S(1)}, u32[]{:S(2)}, u32[]{:S(2)}) collective-permute-start(bf16[8,896]{1,0:T(8,128)(2,1)} %get-tuple-element.84.own_ref), channel_id=1, source_target_pairs={{0,3},{1,2},{2,1},{3,0},{4,7},{5,6},{6,5},{7,4},{8,11},{9,10},{10,... | collective-permute-start | bytes 43016 | tf_op jit(solution)/shard_map/ppermute | solution.py:725
  72.7 4.4 %collective-permute-start.5 = (bf16[32,896]{1,0:T(8,128)(2,1)S(1)}, bf16[32,896]{1,0:T(8,128)(2,1)S(1)}, u32[]{:S(2)}, u32[]{:S(2)}) collective-permute-start(bf16[32,896]{1,0:T(8,128)(2,1)S(1)} %pad_maximum_fusion.2), channel_id=1, source_target_pairs={{0,8},{4,12},{8,0},{12,4},{16,24},{20,28},{24,16},{28,20},{1,9},{5... | collective-permute-start | bytes 172040 | tf_op jit(solution)/shard_map/ppermute | solution.py:725
  74.3 4.2 %collective-permute-start.4 = (bf16[32,896]{1,0:T(8,128)(2,1)S(1)}, bf16[32,896]{1,0:T(8,128)(2,1)S(1)}, u32[]{:S(2)}, u32[]{:S(2)}) collective-permute-start(bf16[32,896]{1,0:T(8,128)(2,1)S(1)} %pad_maximum_fusion.2), channel_id=1, source_target_pairs={{0,16},{4,20},{8,24},{12,28},{16,0},{20,4},{24,8},{28,12},{1,17},{... | collective-permute-start | bytes 172040 | tf_op jit(solution)/shard_map/ppermute | solution.py:725
  75.8 5.1 %collective-permute-start.3 = (bf16[32,896]{1,0:T(8,128)(2,1)S(1)}, bf16[32,896]{1,0:T(8,128)(2,1)S(1)}, u32[]{:S(2)}, u32[]{:S(2)}) collective-permute-start(bf16[32,896]{1,0:T(8,128)(2,1)S(1)} %pad_maximum_fusion.2), channel_id=1, source_target_pairs={{0,24},{4,28},{8,16},{12,20},{16,8},{20,12},{24,0},{28,4},{1,25},{... | collective-permute-start | bytes 172040 | tf_op jit(solution)/shard_map/ppermute | solution.py:725
  81.0 1.6 collective-permute-start.6
  104.6 4.7 %collective-permute-start.7 = (bf16[4,768,384]{2,1,0:T(8,128)(2,1)}, bf16[4,768,384]{2,1,0:T(8,128)(2,1)S(1)}, u32[]{:S(2)}, u32[]{:S(2)}) collective-permute-start(bf16[4,768,384]{2,1,0:T(8,128)(2,1)} %get-tuple-element.94), channel_id=1, source_target_pairs={{0,4},{4,0},{8,12},{12,8},{16,20},{20,16},{24,28},{28,24},{1,5},{5... | collective-permute-start | bytes 7077896 | tf_op jit(solution)/shard_map/ppermute | solution.py:673
  110.0 34.6 %collective-permute-start.10 = (bf16[768,384]{1,0:T(8,128)(2,1)S(1)}, bf16[768,384]{1,0:T(8,128)(2,1)S(1)}, u32[]{:S(2)}, u32[]{:S(2)}) collective-permute-start(bf16[768,384]{1,0:T(8,128)(2,1)S(1)} %get-tuple-element.153), channel_id=1, source_target_pairs={{0,24},{4,28},{8,16},{12,20},{16,8},{20,12},{24,0},{28,4},{1,25},{... | collective-permute-start | bytes 1769480 | tf_op jit(solution)/shard_map/ppermute | solution.py:673
  110.5 34.1 %collective-permute-start.9 = (bf16[768,384]{1,0:T(8,128)(2,1)S(1)}, bf16[768,384]{1,0:T(8,128)(2,1)S(1)}, u32[]{:S(2)}, u32[]{:S(2)}) collective-permute-start(bf16[768,384]{1,0:T(8,128)(2,1)S(1)} %get-tuple-element.154), channel_id=1, source_target_pairs={{0,16},{4,20},{8,24},{12,28},{16,0},{20,4},{24,8},{28,12},{1,17},{... | collective-permute-start | bytes 1769480 | tf_op jit(solution)/shard_map/ppermute | solution.py:673
  112.0 32.6 %collective-permute-start.8 = (bf16[768,384]{1,0:T(8,128)(2,1)S(1)}, bf16[768,384]{1,0:T(8,128)(2,1)}, u32[]{:S(2)}, u32[]{:S(2)}) collective-permute-start(bf16[768,384]{1,0:T(8,128)(2,1)S(1)} %get-tuple-element.155), channel_id=1, source_target_pairs={{0,8},{4,12},{8,0},{12,4},{16,24},{20,28},{24,16},{28,20},{1,9},{5... | collective-permute-start | bytes 1769480 | tf_op jit(solution)/shard_map/ppermute | solution.py:673
  146.0 13.7 %collective-permute-start.12 = (bf16[768,384]{1,0:T(8,128)(2,1)S(1)}, bf16[768,384]{1,0:T(8,128)(2,1)S(1)}, u32[]{:S(2)}, u32[]{:S(2)}) collective-permute-start(bf16[768,384]{1,0:T(8,128)(2,1)S(1)} %add_convert_fusion.4), channel_id=1, source_target_pairs={{0,1},{3,2},{4,5},{7,6},{8,9},{11,10},{12,13},{15,14},{16,17},{19,... | collective-permute-start | bytes 1769480 | tf_op jit(solution)/shard_map/ppermute | solution.py:678
  159.3 6.2 %collective-permute-start.11 = (bf16[4,96,3072]{2,1,0:T(8,128)(2,1)}, bf16[4,96,3072]{2,1,0:T(8,128)(2,1)S(1)}, u32[]{:S(2)}, u32[]{:S(2)}) collective-permute-start(bf16[4,96,3072]{2,1,0:T(8,128)(2,1)} %get-tuple-element.105), channel_id=1, source_target_pairs={{0,4},{4,0},{8,12},{12,8},{16,20},{20,16},{24,28},{28,24},{1,5},{5... | collective-permute-start | bytes 7077896 | tf_op jit(solution)/shard_map/ppermute | solution.py:673
  159.8 37.5 %collective-permute-start.13 = (bf16[768,384]{1,0:T(8,128)(2,1)S(1)}, bf16[768,384]{1,0:T(8,128)(2,1)S(1)}, u32[]{:S(2)}, u32[]{:S(2)}) collective-permute-start(bf16[768,384]{1,0:T(8,128)(2,1)S(1)} %add.214), channel_id=1, source_target_pairs={{1,2},{2,1},{5,6},{6,5},{9,10},{10,9},{13,14},{14,13},{17,18},{18,... | collective-permute-start | bytes 1769480 | tf_op jit(solution)/shard_map/ppermute | solution.py:678
  166.4 32.4 %collective-permute-start.16 = (bf16[96,3072]{1,0:T(8,128)(2,1)S(1)}, bf16[96,3072]{1,0:T(8,128)(2,1)S(1)}, u32[]{:S(2)}, u32[]{:S(2)}) collective-permute-start(bf16[96,3072]{1,0:T(8,128)(2,1)S(1)} %get-tuple-element.149), channel_id=1, source_target_pairs={{0,24},{4,28},{8,16},{12,20},{16,8},{20,12},{24,0},{28,4},{1,25},{... | collective-permute-start | bytes 1769480 | tf_op jit(solution)/shard_map/ppermute | solution.py:673
  166.9 31.8 %collective-permute-start.15 = (bf16[96,3072]{1,0:T(8,128)(2,1)S(1)}, bf16[96,3072]{1,0:T(8,128)(2,1)S(1)}, u32[]{:S(2)}, u32[]{:S(2)}) collective-permute-start(bf16[96,3072]{1,0:T(8,128)(2,1)S(1)} %get-tuple-element.150), channel_id=1, source_target_pairs={{0,16},{4,20},{8,24},{12,28},{16,0},{20,4},{24,8},{28,12},{1,17},{... | collective-permute-start | bytes 1769480 | tf_op jit(solution)/shard_map/ppermute | solution.py:673
  168.5 30.3 %collective-permute-start.14 = (bf16[96,3072]{1,0:T(8,128)(2,1)S(1)}, bf16[96,3072]{1,0:T(8,128)(2,1)S(1)}, u32[]{:S(2)}, u32[]{:S(2)}) collective-permute-start(bf16[96,3072]{1,0:T(8,128)(2,1)S(1)} %get-tuple-element.151), channel_id=1, source_target_pairs={{0,8},{4,12},{8,0},{12,4},{16,24},{20,28},{24,16},{28,20},{1,9},{5... | collective-permute-start | bytes 1769480 | tf_op jit(solution)/shard_map/ppermute | solution.py:673
  197.3 33.0 %collective-permute-start.18 = (bf16[4,96,2304]{2,1,0:T(8,128)(2,1)}, bf16[4,96,2304]{2,1,0:T(8,128)(2,1)S(1)}, u32[]{:S(2)}, u32[]{:S(2)}) collective-permute-start(bf16[4,96,2304]{2,1,0:T(8,128)(2,1)} %get-tuple-element.122), channel_id=1, source_target_pairs={{0,4},{4,0},{8,12},{12,8},{16,20},{20,16},{24,28},{28,24},{1,5},{5... | collective-permute-start | bytes 5308424 | tf_op jit(solution)/shard_map/ppermute | solution.py:673
  197.5 19.2 %collective-permute-start.17 = (bf16[768,384]{1,0:T(8,128)(2,1)S(1)}, bf16[768,384]{1,0:T(8,128)(2,1)S(1)}, u32[]{:S(2)}, u32[]{:S(2)}) collective-permute-start(bf16[768,384]{1,0:T(8,128)(2,1)S(1)} %add.218), channel_id=1, source_target_pairs={{1,0},{2,3},{5,4},{6,7},{9,8},{10,11},{13,12},{14,15},{17,16},{18,... | collective-permute-start | bytes 1769480 | tf_op jit(solution)/shard_map/ppermute | solution.py:678
  199.1 30.0 %collective-permute-start.19 = (bf16[96,3072]{1,0:T(8,128)(2,1)S(1)}, bf16[96,3072]{1,0:T(8,128)(2,1)S(1)}, u32[]{:S(2)}, u32[]{:S(2)}) collective-permute-start(bf16[96,3072]{1,0:T(8,128)(2,1)S(1)} %add_all.1), channel_id=1, source_target_pairs={{0,1},{1,0},{2,3},{3,2},{4,5},{5,4},{6,7},{7,6},{8,9},{9,8},{10,11... | collective-permute-start | bytes 1769480 | tf_op jit(solution)/shard_map/ppermute | solution.py:678
  215.4 29.7 %collective-permute-start.20 = (bf16[4,112,768]{2,1,0:T(8,128)(2,1)}, bf16[4,112,768]{2,1,0:T(8,128)(2,1)S(1)}, u32[]{:S(2)}, u32[]{:S(2)}) collective-permute-start(bf16[4,112,768]{2,1,0:T(8,128)(2,1)} %get-tuple-element.129), channel_id=1, source_target_pairs={{0,4},{4,0},{8,12},{12,8},{16,20},{20,16},{24,28},{28,24},{1,5},{5... | collective-permute-start | bytes 2064392 | tf_op jit(solution)/shard_map/ppermute | solution.py:673
  229.2 30.3 %collective-permute-start.24 = (bf16[96,3072]{1,0:T(8,128)(2,1)S(1)}, bf16[96,3072]{1,0:T(8,128)(2,1)S(1)}, u32[]{:S(2)}, u32[]{:S(2)}) collective-permute-start(bf16[96,3072]{1,0:T(8,128)(2,1)S(1)} %add.223), channel_id=1, source_target_pairs={{0,2},{1,3},{2,0},{3,1},{4,6},{5,7},{6,4},{7,5},{8,10},{9,11},{10,... | collective-permute-start | bytes 1769480 | tf_op jit(solution)/shard_map/ppermute | solution.py:678
  230.8 15.1 %collective-permute-start.23 = (bf16[96,2304]{1,0:T(8,128)(2,1)S(1)}, bf16[96,2304]{1,0:T(8,128)(2,1)S(1)}, u32[]{:S(2)}, u32[]{:S(2)}) collective-permute-start(bf16[96,2304]{1,0:T(8,128)(2,1)S(1)} %get-tuple-element.157), channel_id=1, source_target_pairs={{0,24},{4,28},{8,16},{12,20},{16,8},{20,12},{24,0},{28,4},{1,25},{... | collective-permute-start | bytes 1327112 | tf_op jit(solution)/shard_map/ppermute | solution.py:673
  231.3 25.5 %collective-permute-start.22 = (bf16[96,2304]{1,0:T(8,128)(2,1)S(1)}, bf16[96,2304]{1,0:T(8,128)(2,1)S(1)}, u32[]{:S(2)}, u32[]{:S(2)}) collective-permute-start(bf16[96,2304]{1,0:T(8,128)(2,1)S(1)} %get-tuple-element.158), channel_id=1, source_target_pairs={{0,16},{4,20},{8,24},{12,28},{16,0},{20,4},{24,8},{28,12},{1,17},{... | collective-permute-start | bytes 1327112 | tf_op jit(solution)/shard_map/ppermute | solution.py:673
  232.8 24.0 %collective-permute-start.21 = (bf16[96,2304]{1,0:T(8,128)(2,1)S(1)}, bf16[96,2304]{1,0:T(8,128)(2,1)S(1)}, u32[]{:S(2)}, u32[]{:S(2)}) collective-permute-start(bf16[96,2304]{1,0:T(8,128)(2,1)S(1)} %get-tuple-element.159), channel_id=1, source_target_pairs={{0,8},{4,12},{8,0},{12,4},{16,24},{20,28},{24,16},{28,20},{1,9},{5... | collective-permute-start | bytes 1327112 | tf_op jit(solution)/shard_map/ppermute | solution.py:673
  245.3 22.4 %collective-permute-start.28 = (bf16[112,768]{1,0:T(8,128)(2,1)S(1)}, bf16[112,768]{1,0:T(8,128)(2,1)S(1)}, u32[]{:S(2)}, u32[]{:S(2)}) collective-permute-start(bf16[112,768]{1,0:T(8,128)(2,1)S(1)} %get-tuple-element.161), channel_id=1, source_target_pairs={{0,24},{4,28},{8,16},{12,20},{16,8},{20,12},{24,0},{28,4},{1,25},{... | collective-permute-start | bytes 516104 | tf_op jit(solution)/shard_map/ppermute | solution.py:673
  245.8 21.9 %collective-permute-start.27 = (bf16[112,768]{1,0:T(8,128)(2,1)S(1)}, bf16[112,768]{1,0:T(8,128)(2,1)S(1)}, u32[]{:S(2)}, u32[]{:S(2)}) collective-permute-start(bf16[112,768]{1,0:T(8,128)(2,1)S(1)} %get-tuple-element.162), channel_id=1, source_target_pairs={{0,16},{4,20},{8,24},{12,28},{16,0},{20,4},{24,8},{28,12},{1,17},{... | collective-permute-start | bytes 516104 | tf_op jit(solution)/shard_map/ppermute | solution.py:673
  256.8 10.9 %collective-permute-start.26 = (bf16[112,768]{1,0:T(8,128)(2,1)S(1)}, bf16[112,768]{1,0:T(8,128)(2,1)S(1)}, u32[]{:S(2)}, u32[]{:S(2)}) collective-permute-start(bf16[112,768]{1,0:T(8,128)(2,1)S(1)} %get-tuple-element.163), channel_id=1, source_target_pairs={{0,8},{4,12},{8,0},{12,4},{16,24},{20,28},{24,16},{28,20},{1,9},{5... | collective-permute-start | bytes 516104 | tf_op jit(solution)/shard_map/ppermute | solution.py:673
  257.0 10.6 %collective-permute-start.25 = (bf16[96,2304]{1,0:T(8,128)(2,1)S(1)}, bf16[96,2304]{1,0:T(8,128)(2,1)S(1)}, u32[]{:S(2)}, u32[]{:S(2)}) collective-permute-start(bf16[96,2304]{1,0:T(8,128)(2,1)S(1)} %add_convert_fusion.9), channel_id=1, source_target_pairs={{0,1},{1,0},{2,3},{3,2},{4,5},{5,4},{6,7},{7,6},{8,9},{9,8},{10,11... | collective-permute-start | bytes 1327112 | tf_op jit(solution)/shard_map/ppermute | solution.py:678
  267.8 6.9 %collective-permute-start.29 = (bf16[112,768]{1,0:T(8,128)(2,1)S(1)}, bf16[112,768]{1,0:T(8,128)(2,1)S(1)}, u32[]{:S(2)}, u32[]{:S(2)}) collective-permute-start(bf16[112,768]{1,0:T(8,128)(2,1)S(1)} %add_convert_fusion.14), channel_id=1, source_target_pairs={{0,1},{1,0},{2,3},{3,2},{4,5},{5,4},{6,7},{7,6},{8,9},{9,8},{10,11... | collective-permute-start | bytes 516104 | tf_op jit(solution)/shard_map/ppermute | solution.py:678
  274.7 16.7 %collective-permute-start.31 = (bf16[112,768]{1,0:T(8,128)(2,1)S(1)}, bf16[112,768]{1,0:T(8,128)(2,1)S(1)}, u32[]{:S(2)}, u32[]{:S(2)}) collective-permute-start(bf16[112,768]{1,0:T(8,128)(2,1)S(1)} %add.237), channel_id=1, source_target_pairs={{0,2},{1,3},{2,0},{3,1},{4,6},{5,7},{6,4},{7,5},{8,10},{9,11},{10,... | collective-permute-start | bytes 516104 | tf_op jit(solution)/shard_map/ppermute | solution.py:678
  276.0 23.2 %collective-permute-start.30 = (bf16[96,2304]{1,0:T(8,128)(2,1)S(1)}, bf16[96,2304]{1,0:T(8,128)(2,1)S(1)}, u32[]{:S(2)}, u32[]{:S(2)}) collective-permute-start(bf16[96,2304]{1,0:T(8,128)(2,1)S(1)} %add.230), channel_id=1, source_target_pairs={{0,2},{1,3},{2,0},{3,1},{4,6},{5,7},{6,4},{7,5},{8,10},{9,11},{10,... | collective-permute-start | bytes 1327112 | tf_op jit(solution)/shard_map/ppermute | solution.py:678
  (4 other events, 35.3 us)

commit v6 on v5

--- a/solution.py
+++ b/solution.py
@@ -900,7 +900,7 @@
         ],
     )
     deps = outer.turn(stat_one)
-    up_flow = Flow(*weight_grad(y1_t, grad_u, row_count, core, deps), fused=True)
+    up_flow = Flow(*weight_grad(y1_t, grad_u, row_count, core, deps), line=True, fused=True)
     up_flow.step()
     deps = up_flow.sent + outer.turn(up_flow.sent[0])
     x_t = turn([queries, passages], [queries_spec, passages_spec], deps)
@@ -939,7 +939,7 @@
     grad_a, stat_a, *mixed_parts = attend_back(*groups[0], deps, room=6 * third + width)
     at = 6 * third // width
     mixed_parts = weight_grad(ctx_t, grad_attn, row_count, core, [stat_a], mixed_parts, at, us=0)
-    mixed_flow = Flow(*mixed_parts)
+    mixed_flow = Flow(*mixed_parts, line=True)
     mixed_flow.step()
     token = mixed_flow.sent[0]
     deps = mixed_flow.sent + outer.turn(token) + up_flow.turn(token)
@@ -963,16 +963,18 @@
         us=40,
     )
     last_flow.turn(passage_grad)
-    mixed_flow.turn(last_flow.kept)
-    up_flow.turn(mixed_flow.kept)
+    up_flow.turn(last_flow.kept)
+    mixed_flow.turn(up_flow.kept)
+    last_flow.turn(mixed_flow.kept)
     outs = [(fixed((cut_inner, width)), shape(cut_inner, width, kind=F32))]
     (turned,) = call(
-        turn_kernel, (outer.kept,), [const_spec((width, cut_inner))], outs, (1,), 56, [up_flow.kept], name="turn", us=40
+        turn_kernel, (outer.kept,), [const_spec((width, cut_inner))], outs, (1,), 56, [last_flow.kept], name="turn", us=40
     )
     mixed_flow.turn(turned)
     last_flow.turn(mixed_flow.kept)
-    last_flow.turn()
-    mixed_flow.turn(last_flow.kept)
+    up_flow.turn(last_flow.kept)
+    mixed_flow.turn(up_flow.kept)
+    last_flow.turn(mixed_flow.kept)
     flows = [outer, up_flow, mixed_flow, last_flow]
     while not all(flow.done for flow in flows):
         for flow in flows:

time: 308 us -> 301 us (0.977)
  the two profiles are of different devices: /device:TPU:0 before, /device:TPU:4 now
where the time goes in v6:
time: 301 us; the launch traced here: 295 us
  Pallas kernels  187 us (62%)
  starting transfers between devices  47.2 us (16%)
  waiting for transfers between devices  46.7 us (16%)
  other arithmetic  10.8 us (4%)
    pallas_call x13, Pallas kernels, call(): pl.pallas_call(kernel, grid=grid, in_specs=list(in_specs) + [pl.BlockSpec...  184 us
    ppermute x11, waiting for transfers between devices, step(): self.got = [lax.ppermute(self.kept, 'col', self.line[0][1])]  30.5 us
    ppermute x11, starting transfers between devices, step(): self.got = [lax.ppermute(self.kept, 'col', self.line[0][1])]  25.5 us
    ppermute x16, starting transfers between devices, step(): lax.ppermute(sent, 'row', [(i, i ^ mask) for i in range(size)])  13.6 us
    ppermute x7, waiting for transfers between devices, gather_all(): pieces.append(lax.ppermute(piece, name, pairs))  10.5 us
    ppermute x7, starting transfers between devices, gather_all(): pieces.append(lax.ppermute(piece, name, pairs))  8.08 us
  transfers between devices with their start and end apart: 34, of which 13 were waited for; matrix products, arithmetic and copies ran while one was open for 2% of the time, Pallas kernels for 36%

profile of v6, /device:TPU:4, one launch (start us, length us, event | category | flops | bytes accessed | tf_op | source)
XLA Modules:
  0.0 295.2 jit_solution(11629191665349035914)
XLA Ops:
  0.7 20.9 %attend.1 = (bf16[1536,768]{1,0:T(8,128)(2,1)}, bf16[1536,768]{1,0:T(8,128)(2,1)}, bf16[1536,768]{1,0:T(8,128)(2,1)}, bf16[768,1536]{1,0:T(8,128)(2,1)}, f32[3,6,8,512]{3,2,1,0:T(8,128)}) custom-call(s32[4]{0:T(128)} %refs_1_.9, s32[2]{0:T(128)} %refs_2_.7, bf16[512,768]{1,0:T(8,128)(2,1)} %bitcast.76, bf16[1024,768]{1,0:T(8,128)(2,1)} %bitcast.73, ...), custom_call_target="tpu_custom_call" | custom-call | flops 13799999488 | tf_op jit(solution)/shard_map/attend/pallas_call | solution.py:579
  21.6 39.0 %dense.1 = (bf16[1536,768]{1,0:T(8,128)(2,1)}, bf16[1536,768]{1,0:T(8,128)(2,1)}, bf16[1536,3072]{1,0:T(8,128)(2,1)}, bf16[1536,3072]{1,0:T(8,128)(2,1)}, bf16[1...) custom-call(s32[4]{0:T(128)} %refs_1_.9, ...), custom_call_target="tpu_custom_call" | custom-call | flops 13799999488 | tf_op jit(solution)/shard_map/dense/pallas_call | solution.py:579
  60.6 1.7 collective-permute-start.2
  62.2 2.6 collective-permute-start.1
  65.0 2.2 collective-permute-done.1
  67.2 3.3 %collective-permute-done = bf16[8,896]{1,0:T(8,128)(2,1)S(1)} collective-permute-done((bf16[8,896]{1,0:T(8,128)(2,1)}, bf16[8,896]{1,0:T(8,128)(2,1)S(1)}, u32[]{:S(2)}, u32[]{:S(2)}) %collective-permute-start) | collective-permute-done | bytes 14368 | tf_op jit(solution)/shard_map/ppermute | solution.py:725
  71.3 1.6 collective-permute-start.5
  73.3 1.5 collective-permute-start.3
  81.0 2.9 loss.1
  85.1 18.2 %outer_grad.1 = (bf16[1536,768]{1,0:T(8,128)(2,1)}, f32[8,768]{1,0:T(8,128)}, bf16[4,768,384]{2,1,0:T(8,128)(2,1)}, bf16[4,768,384]{2,1,0:T(8,128)(2,1)}) custom-call(s32[1]{0:T(128)} %bitcast.6.refs_0_, s32[4]{0:T(128)} %refs_1_.9, s32[2]{0:T(128)} %refs_2_.7, f32[8,768]{1,0:T(8,128)} %get-tuple-element.92.refs_3_, ...), custom_call_target="tpu_custom_call" | custom-call | flops 13799999488 | tf_op jit(solution)/shard_map/outer_grad/pallas_call | solution.py:579
  103.4 4.5 %turn.3.refs_1_ = bf16[768,1536]{1,0:T(8,128)(2,1)} custom-call(bf16[1536,768]{1,0:T(8,128)(2,1)} %get-tuple-element.98.refs_0_), custom_call_target="tpu_custom_call" | custom-call | flops 46000001024 | tf_op jit(solution)/shard_map/turn/pallas_call | solution.py:579
  108.7 1.6 collective-permute-start.10
  112.2 31.1 %dense_back.1 = (bf16[1536,3072]{1,0:T(8,128)(2,1)}, bf16[1536,768]{1,0:T(8,128)(2,1)}, bf16[1536,768]{1,0:T(8,128)(2,1)}, f32[8,768]{1,0:T(8,128)}, f32[8,3072]{1,0:T(8,128)}) custom-call(bf16[1536,768]{1,0:T(8,128)(2,1)} %get-tuple-element.100.refs_0_, bf16[1536,3072]{1,0:T(8,128)(2,1)} %get-tuple-element.101.refs_1_, ...), custom_call_target="tpu_custom_call" | custom-call | flops 13799999488 | tf_op jit(solution)/shard_map/dense_back/pallas_call | solution.py:579
  146.0 12.0 %weight_grad.2 = (bf16[4,96,3072]{2,1,0:T(8,128)(2,1)}, bf16[4,96,3072]{2,1,0:T(8,128)(2,1)}) custom-call(s32[1]{0:T(128)} %bitcast.6.refs_0_, bf16[768,1536]{1,0:T(8,128)(2,1)} %turn.3.refs_1_, bf16[1536,3072]{1,0:T(8,128)(2,1)} %get-tuple-element.107.refs_2_), custom_call_target="tpu_custom_call" | custom-call | flops 13799999488 | tf_op jit(solution)/shard_map/weight_grad/pallas_call | solution.py:579
  159.3 4.9 %turn.4.refs_9_ = bf16[768,1536]{1,0:T(8,128)(2,1)} custom-call(bf16[512,768]{1,0:T(8,128)(2,1)} %bitcast.78, bf16[1024,768]{1,0:T(8,128)(2,1)} %bitcast.75), custom_call_target="tpu_custom_call" | custom-call | flops 46000001024 | tf_op jit(solution)/shard_map/turn/pallas_call | solution.py:579
  165.1 1.6 collective-permute-start.16
  168.6 21.8 %attend_back.2 = (bf16[1536,1536]{1,0:T(8,128)(2,1)}, f32[8,512]{1,0:T(8,128)}, bf16[4,96,2304]{2,1,0:T(8,128)(2,1)}, bf16[4,96,2304]{2,1,0:T(8,128)(2,1)}) custom-call(s32[1]{0:T(128)} %bitcast.6.refs_0_, s32[4]{0:T(128)} %refs_1_.9, s32[2]{0:T(128)} %refs_2_.7, bf16[1536,768]{1,0:T(8,128)(2,1)} %get-tuple-element.114.refs_3_, ...), custom_call_target="tpu_custom_call" | custom-call | flops 13799999488 | tf_op jit(solution)/shard_map/attend_back/pallas_call | solution.py:579
  190.5 5.6 %weight_grad.3 = (bf16[4,96,2304]{2,1,0:T(8,128)(2,1)}, bf16[4,96,2304]{2,1,0:T(8,128)(2,1)}) custom-call(s32[1]{0:T(128)} %bitcast.6.refs_0_, bf16[768,1536]{1,0:T(8,128)(2,1)} %get-tuple-element.86.refs_5_.refs_6_.refs_1_, bf16[1536,768]{1,0:T(8,128)(2,1)} %get-tuple-element.122.refs_2_, ...), custom_call_target="tpu_custom_call", output_to_operand_aliasing={{0}: (3, {}), {1}: (4, {})} | custom-call | tf_op jit(solution)/shard_map/weight_grad/pallas_call | solution.py:579
  197.9 5.7 %collective-permute-start.19 = (bf16[96,3072]{1,0:T(8,128)(2,1)S(1)}, bf16[96,3072]{1,0:T(8,128)(2,1)S(1)}, u32[]{:S(2)}, u32[]{:S(2)}) collective-permute-start(bf16[96,3072]{1,0:T(8,128)(2,1)S(1)} %add_all.1), channel_id=1, source_target_pairs={{0,1},{3,2},{4,5},{7,6},{8,9},{11,10},{12,13},{15,14},{16,17},{19,... | collective-permute-start | bytes 1769480 | tf_op jit(solution)/shard_map/ppermute | solution.py:678
  203.6 12.6 %attend_back.3 = (bf16[1536,768]{1,0:T(8,128)(2,1)}, f32[8,256]{1,0:T(8,128)}, bf16[4,112,768]{2,1,0:T(8,128)(2,1)}, bf16[4,112,768]{2,1,0:T(8,128)(2,1)}) custom-call(s32[1]{0:T(128)} %bitcast.6.refs_0_, s32[4]{0:T(128)} %refs_1_.9, s32[2]{0:T(128)} %refs_2_.7, bf16[1536,768]{1,0:T(8,128)(2,1)} %get-tuple-element.114.refs_3_, ...), custom_call_target="tpu_custom_call" | custom-call | flops 46000001024 | tf_op jit(solution)/shard_map/attend_back/pallas_call | solution.py:579
  218.8 1.6 collective-permute-start.24
  222.3 10.8 %input_grad.1 = (bf16[512,768]{1,0:T(8,128)(2,1)}, bf16[1024,768]{1,0:T(8,128)(2,1)}) custom-call(bf16[1536,1536]{1,0:T(8,128)(2,1)} %get-tuple-element.119.refs_0_, bf16[1536,768]{1,0:T(8,128)(2,1)} %get-tuple-element.131.refs_1_, bf16[1536,768]{1,0:T(8,128)(2,1)} %get-tuple-element.122.refs_2_, bf16[768,768]{1,0:T(8,128)(2,1)} %refs_3_.2, ...), custom_call_target="tpu_custom_call" | custom-call | flops 46000001024 | tf_op jit(solution)/shard_map/input_grad/pallas_call | solution.py:579
  234.7 1.6 collective-permute-start.27
  236.8 5.5 %collective-permute-done.23 = bf16[96,2304]{1,0:T(8,128)(2,1)S(1)} collective-permute-done((bf16[96,2304]{1,0:T(8,128)(2,1)S(1)}, bf16[96,2304]{1,0:T(8,128)(2,1)S(1)}, u32[]{:S(2)}, u32[]{:S(2)}) %collective-permute-start.23) | collective-permute-done | bytes 442400 | tf_op jit(solution)/shard_map/ppermute | solution.py:673
  243.1 7.2 %collective-permute-start.28 = (bf16[96,2304]{1,0:T(8,128)(2,1)S(1)}, bf16[96,2304]{1,0:T(8,128)(2,1)S(1)}, u32[]{:S(2)}, u32[]{:S(2)}) collective-permute-start(bf16[96,2304]{1,0:T(8,128)(2,1)S(1)} %add_convert_fusion.9), channel_id=1, source_target_pairs={{0,1},{3,2},{4,5},{7,6},{8,9},{11,10},{12,13},{15,14},{16,17},{19,... | collective-permute-start | bytes 1327112 | tf_op jit(solution)/shard_map/ppermute | solution.py:678
  250.4 3.4 %collective-permute-start.30 = (bf16[112,768]{1,0:T(8,128)(2,1)S(1)}, bf16[112,768]{1,0:T(8,128)(2,1)S(1)}, u32[]{:S(2)}, u32[]{:S(2)}) collective-permute-start(bf16[112,768]{1,0:T(8,128)(2,1)S(1)} %add_convert_fusion.14), channel_id=1, source_target_pairs={{0,1},{1,0},{2,3},{3,2},{4,5},{5,4},{6,7},{7,6},{8,9},{9,8},{10,11... | collective-permute-start | bytes 516104 | tf_op jit(solution)/shard_map/ppermute | solution.py:678
  253.7 2.3 turn.5
  256.0 4.8 %collective-permute-done.28 = bf16[96,2304]{1,0:T(8,128)(2,1)S(1)} collective-permute-done((bf16[96,2304]{1,0:T(8,128)(2,1)S(1)}, bf16[96,2304]{1,0:T(8,128)(2,1)S(1)}, u32[]{:S(2)}, u32[]{:S(2)}) %collective-permute-start.28) | collective-permute-done | bytes 442400 | tf_op jit(solution)/shard_map/ppermute | solution.py:678
  260.9 2.0 collective-permute-done.30
  263.0 2.0 collective-permute-start.33
  268.2 6.2 %collective-permute-done.33 = bf16[112,768]{1,0:T(8,128)(2,1)S(1)} collective-permute-done((bf16[112,768]{1,0:T(8,128)(2,1)S(1)}, bf16[112,768]{1,0:T(8,128)(2,1)S(1)}, u32[]{:S(2)}, u32[]{:S(2)}) %collective-permute-start.33) | collective-permute-done | bytes 172064 | tf_op jit(solution)/shard_map/ppermute | solution.py:678
  275.6 17.1 %collective-permute-done.32 = bf16[96,2304]{1,0:T(8,128)(2,1)S(1)} collective-permute-done((bf16[96,2304]{1,0:T(8,128)(2,1)S(1)}, bf16[96,2304]{1,0:T(8,128)(2,1)S(1)}, u32[]{:S(2)}, u32[]{:S(2)}) %collective-permute-start.32) | collective-permute-done | bytes 442400 | tf_op jit(solution)/shard_map/ppermute | solution.py:678
  (92 shorter events, 34.6 us)
Async XLA Ops:
  60.6 4.5 %collective-permute-start.2 = (bf16[8,896]{1,0:T(8,128)(2,1)}, bf16[8,896]{1,0:T(8,128)(2,1)S(1)}, u32[]{:S(2)}, u32[]{:S(2)}) collective-permute-start(bf16[8,896]{1,0:T(8,128)(2,1)} %get-tuple-element.87.own_ref), channel_id=1, source_target_pairs={{0,1},{1,0},{2,3},{3,2},{4,5},{5,4},{6,7},{7,6},{8,9},{9,8},{10,11... | collective-permute-start | bytes 43016 | tf_op jit(solution)/shard_map/ppermute | solution.py:725
  62.2 5.0 %collective-permute-start.1 = (bf16[8,896]{1,0:T(8,128)(2,1)}, bf16[8,896]{1,0:T(8,128)(2,1)S(1)}, u32[]{:S(2)}, u32[]{:S(2)}) collective-permute-start(bf16[8,896]{1,0:T(8,128)(2,1)} %get-tuple-element.87.own_ref), channel_id=1, source_target_pairs={{0,2},{1,3},{2,0},{3,1},{4,6},{5,7},{6,4},{7,5},{8,10},{9,11},{10,... | collective-permute-start | bytes 43016 | tf_op jit(solution)/shard_map/ppermute | solution.py:725
  64.8 5.7 %collective-permute-start = (bf16[8,896]{1,0:T(8,128)(2,1)}, bf16[8,896]{1,0:T(8,128)(2,1)S(1)}, u32[]{:S(2)}, u32[]{:S(2)}) collective-permute-start(bf16[8,896]{1,0:T(8,128)(2,1)} %get-tuple-element.87.own_ref), channel_id=1, source_target_pairs={{0,3},{1,2},{2,1},{3,0},{4,7},{5,6},{6,5},{7,4},{8,11},{9,10},{10,... | collective-permute-start | bytes 43016 | tf_op jit(solution)/shard_map/ppermute | solution.py:725
  71.3 4.4 %collective-permute-start.5 = (bf16[32,896]{1,0:T(8,128)(2,1)S(1)}, bf16[32,896]{1,0:T(8,128)(2,1)S(1)}, u32[]{:S(2)}, u32[]{:S(2)}) collective-permute-start(bf16[32,896]{1,0:T(8,128)(2,1)S(1)} %pad_maximum_fusion.2), channel_id=1, source_target_pairs={{0,8},{4,12},{8,0},{12,4},{16,24},{20,28},{24,16},{28,20},{1,9},{5... | collective-permute-start | bytes 172040 | tf_op jit(solution)/shard_map/ppermute | solution.py:725
  72.8 4.2 %collective-permute-start.4 = (bf16[32,896]{1,0:T(8,128)(2,1)S(1)}, bf16[32,896]{1,0:T(8,128)(2,1)S(1)}, u32[]{:S(2)}, u32[]{:S(2)}) collective-permute-start(bf16[32,896]{1,0:T(8,128)(2,1)S(1)} %pad_maximum_fusion.2), channel_id=1, source_target_pairs={{0,16},{4,20},{8,24},{12,28},{16,0},{20,4},{24,8},{28,12},{1,17},{... | collective-permute-start | bytes 172040 | tf_op jit(solution)/shard_map/ppermute | solution.py:725
  73.3 5.1 %collective-permute-start.3 = (bf16[32,896]{1,0:T(8,128)(2,1)S(1)}, bf16[32,896]{1,0:T(8,128)(2,1)S(1)}, u32[]{:S(2)}, u32[]{:S(2)}) collective-permute-start(bf16[32,896]{1,0:T(8,128)(2,1)S(1)} %pad_maximum_fusion.2), channel_id=1, source_target_pairs={{0,24},{4,28},{8,16},{12,20},{16,8},{20,12},{24,0},{28,4},{1,25},{... | collective-permute-start | bytes 172040 | tf_op jit(solution)/shard_map/ppermute | solution.py:725
  103.4 4.7 %collective-permute-start.7 = (bf16[4,768,384]{2,1,0:T(8,128)(2,1)}, bf16[4,768,384]{2,1,0:T(8,128)(2,1)S(1)}, u32[]{:S(2)}, u32[]{:S(2)}) collective-permute-start(bf16[4,768,384]{2,1,0:T(8,128)(2,1)} %get-tuple-element.97), channel_id=1, source_target_pairs={{0,4},{4,0},{8,12},{12,8},{16,20},{20,16},{24,28},{28,24},{1,5},{5... | collective-permute-start | bytes 7077896 | tf_op jit(solution)/shard_map/ppermute | solution.py:673
  108.7 34.6 %collective-permute-start.10 = (bf16[768,384]{1,0:T(8,128)(2,1)S(1)}, bf16[768,384]{1,0:T(8,128)(2,1)S(1)}, u32[]{:S(2)}, u32[]{:S(2)}) collective-permute-start(bf16[768,384]{1,0:T(8,128)(2,1)S(1)} %get-tuple-element.159), channel_id=1, source_target_pairs={{0,24},{4,28},{8,16},{12,20},{16,8},{20,12},{24,0},{28,4},{1,25},{... | collective-permute-start | bytes 1769480 | tf_op jit(solution)/shard_map/ppermute | solution.py:673
  110.2 33.1 %collective-permute-start.9 = (bf16[768,384]{1,0:T(8,128)(2,1)S(1)}, bf16[768,384]{1,0:T(8,128)(2,1)S(1)}, u32[]{:S(2)}, u32[]{:S(2)}) collective-permute-start(bf16[768,384]{1,0:T(8,128)(2,1)S(1)} %get-tuple-element.160), channel_id=1, source_target_pairs={{0,16},{4,20},{8,24},{12,28},{16,0},{20,4},{24,8},{28,12},{1,17},{... | collective-permute-start | bytes 1769480 | tf_op jit(solution)/shard_map/ppermute | solution.py:673
  110.7 32.6 %collective-permute-start.8 = (bf16[768,384]{1,0:T(8,128)(2,1)S(1)}, bf16[768,384]{1,0:T(8,128)(2,1)}, u32[]{:S(2)}, u32[]{:S(2)}) collective-permute-start(bf16[768,384]{1,0:T(8,128)(2,1)S(1)} %get-tuple-element.161), channel_id=1, source_target_pairs={{0,8},{4,12},{8,0},{12,4},{16,24},{20,28},{24,16},{28,20},{1,9},{5... | collective-permute-start | bytes 1769480 | tf_op jit(solution)/shard_map/ppermute | solution.py:673
  144.7 13.7 %collective-permute-start.12 = (bf16[768,384]{1,0:T(8,128)(2,1)S(1)}, bf16[768,384]{1,0:T(8,128)(2,1)S(1)}, u32[]{:S(2)}, u32[]{:S(2)}) collective-permute-start(bf16[768,384]{1,0:T(8,128)(2,1)S(1)} %add_convert_fusion.4), channel_id=1, source_target_pairs={{0,1},{3,2},{4,5},{7,6},{8,9},{11,10},{12,13},{15,14},{16,17},{19,... | collective-permute-start | bytes 1769480 | tf_op jit(solution)/shard_map/ppermute | solution.py:678
  158.0 6.1 %collective-permute-start.11 = (bf16[4,96,3072]{2,1,0:T(8,128)(2,1)}, bf16[4,96,3072]{2,1,0:T(8,128)(2,1)S(1)}, u32[]{:S(2)}, u32[]{:S(2)}) collective-permute-start(bf16[4,96,3072]{2,1,0:T(8,128)(2,1)} %get-tuple-element.108), channel_id=1, source_target_pairs={{0,4},{4,0},{8,12},{12,8},{16,20},{20,16},{24,28},{28,24},{1,5},{5... | collective-permute-start | bytes 7077896 | tf_op jit(solution)/shard_map/ppermute | solution.py:673
  158.6 37.5 %collective-permute-start.13 = (bf16[768,384]{1,0:T(8,128)(2,1)S(1)}, bf16[768,384]{1,0:T(8,128)(2,1)S(1)}, u32[]{:S(2)}, u32[]{:S(2)}) collective-permute-start(bf16[768,384]{1,0:T(8,128)(2,1)S(1)} %add.214), channel_id=1, source_target_pairs={{1,2},{2,1},{5,6},{6,5},{9,10},{10,9},{13,14},{14,13},{17,18},{18,... | collective-permute-start | bytes 1769480 | tf_op jit(solution)/shard_map/ppermute | solution.py:678
  165.1 32.5 %collective-permute-start.16 = (bf16[96,3072]{1,0:T(8,128)(2,1)S(1)}, bf16[96,3072]{1,0:T(8,128)(2,1)S(1)}, u32[]{:S(2)}, u32[]{:S(2)}) collective-permute-start(bf16[96,3072]{1,0:T(8,128)(2,1)S(1)} %get-tuple-element.155), channel_id=1, source_target_pairs={{0,24},{4,28},{8,16},{12,20},{16,8},{20,12},{24,0},{28,4},{1,25},{... | collective-permute-start | bytes 1769480 | tf_op jit(solution)/shard_map/ppermute | solution.py:673
  166.6 30.9 %collective-permute-start.15 = (bf16[96,3072]{1,0:T(8,128)(2,1)S(1)}, bf16[96,3072]{1,0:T(8,128)(2,1)S(1)}, u32[]{:S(2)}, u32[]{:S(2)}) collective-permute-start(bf16[96,3072]{1,0:T(8,128)(2,1)S(1)} %get-tuple-element.156), channel_id=1, source_target_pairs={{0,16},{4,20},{8,24},{12,28},{16,0},{20,4},{24,8},{28,12},{1,17},{... | collective-permute-start | bytes 1769480 | tf_op jit(solution)/shard_map/ppermute | solution.py:673
  167.2 30.4 %collective-permute-start.14 = (bf16[96,3072]{1,0:T(8,128)(2,1)S(1)}, bf16[96,3072]{1,0:T(8,128)(2,1)S(1)}, u32[]{:S(2)}, u32[]{:S(2)}) collective-permute-start(bf16[96,3072]{1,0:T(8,128)(2,1)S(1)} %get-tuple-element.157), channel_id=1, source_target_pairs={{0,8},{4,12},{8,0},{12,4},{16,24},{20,28},{24,16},{28,20},{1,9},{5... | collective-permute-start | bytes 1769480 | tf_op jit(solution)/shard_map/ppermute | solution.py:673
  196.1 22.1 %collective-permute-start.18 = (bf16[4,96,2304]{2,1,0:T(8,128)(2,1)}, bf16[4,96,2304]{2,1,0:T(8,128)(2,1)S(1)}, u32[]{:S(2)}, u32[]{:S(2)}) collective-permute-start(bf16[4,96,2304]{2,1,0:T(8,128)(2,1)} %get-tuple-element.125), channel_id=1, source_target_pairs={{0,4},{4,0},{8,12},{12,8},{16,20},{20,16},{24,28},{28,24},{1,5},{5... | collective-permute-start | bytes 5308424 | tf_op jit(solution)/shard_map/ppermute | solution.py:673
  196.3 20.2 %collective-permute-start.17 = (bf16[768,384]{1,0:T(8,128)(2,1)S(1)}, bf16[768,384]{1,0:T(8,128)(2,1)S(1)}, u32[]{:S(2)}, u32[]{:S(2)}) collective-permute-start(bf16[768,384]{1,0:T(8,128)(2,1)S(1)} %add.218), channel_id=1, source_target_pairs={{1,0},{2,3},{5,4},{6,7},{9,8},{10,11},{13,12},{14,15},{17,16},{18,... | collective-permute-start | bytes 1769480 | tf_op jit(solution)/shard_map/ppermute | solution.py:678
  197.9 19.5 %collective-permute-start.19 = (bf16[96,3072]{1,0:T(8,128)(2,1)S(1)}, bf16[96,3072]{1,0:T(8,128)(2,1)S(1)}, u32[]{:S(2)}, u32[]{:S(2)}) collective-permute-start(bf16[96,3072]{1,0:T(8,128)(2,1)S(1)} %add_all.1), channel_id=1, source_target_pairs={{0,1},{3,2},{4,5},{7,6},{8,9},{11,10},{12,13},{15,14},{16,17},{19,... | collective-permute-start | bytes 1769480 | tf_op jit(solution)/shard_map/ppermute | solution.py:678
  216.2 16.9 %collective-permute-start.20 = (bf16[4,112,768]{2,1,0:T(8,128)(2,1)}, bf16[4,112,768]{2,1,0:T(8,128)(2,1)S(1)}, u32[]{:S(2)}, u32[]{:S(2)}) collective-permute-start(bf16[4,112,768]{2,1,0:T(8,128)(2,1)} %get-tuple-element.132), channel_id=1, source_target_pairs={{0,4},{4,0},{8,12},{12,8},{16,20},{20,16},{24,28},{28,24},{1,5},{5... | collective-permute-start | bytes 2064392 | tf_op jit(solution)/shard_map/ppermute | solution.py:673
  217.5 15.7 %collective-permute-start.21 = (bf16[96,3072]{1,0:T(8,128)(2,1)S(1)}, bf16[96,3072]{1,0:T(8,128)(2,1)S(1)}, u32[]{:S(2)}, u32[]{:S(2)}) collective-permute-start(bf16[96,3072]{1,0:T(8,128)(2,1)S(1)} %add.223), channel_id=1, source_target_pairs={{1,2},{2,1},{5,6},{6,5},{9,10},{10,9},{13,14},{14,13},{17,18},{18,... | collective-permute-start | bytes 1769480 | tf_op jit(solution)/shard_map/ppermute | solution.py:678
  218.8 17.5 %collective-permute-start.24 = (bf16[96,2304]{1,0:T(8,128)(2,1)S(1)}, bf16[96,2304]{1,0:T(8,128)(2,1)S(1)}, u32[]{:S(2)}, u32[]{:S(2)}) collective-permute-start(bf16[96,2304]{1,0:T(8,128)(2,1)S(1)} %get-tuple-element.163), channel_id=1, source_target_pairs={{0,24},{4,28},{8,16},{12,20},{16,8},{20,12},{24,0},{28,4},{1,25},{... | collective-permute-start | bytes 1327112 | tf_op jit(solution)/shard_map/ppermute | solution.py:673
  220.3 22.0 %collective-permute-start.23 = (bf16[96,2304]{1,0:T(8,128)(2,1)S(1)}, bf16[96,2304]{1,0:T(8,128)(2,1)S(1)}, u32[]{:S(2)}, u32[]{:S(2)}) collective-permute-start(bf16[96,2304]{1,0:T(8,128)(2,1)S(1)} %get-tuple-element.164), channel_id=1, source_target_pairs={{0,16},{4,20},{8,24},{12,28},{16,0},{20,4},{24,8},{28,12},{1,17},{... | collective-permute-start | bytes 1327112 | tf_op jit(solution)/shard_map/ppermute | solution.py:673
  220.8 22.0 %collective-permute-start.22 = (bf16[96,2304]{1,0:T(8,128)(2,1)S(1)}, bf16[96,2304]{1,0:T(8,128)(2,1)S(1)}, u32[]{:S(2)}, u32[]{:S(2)}) collective-permute-start(bf16[96,2304]{1,0:T(8,128)(2,1)S(1)} %get-tuple-element.165), channel_id=1, source_target_pairs={{0,8},{4,12},{8,0},{12,4},{16,24},{20,28},{24,16},{28,20},{1,9},{5... | collective-permute-start | bytes 1327112 | tf_op jit(solution)/shard_map/ppermute | solution.py:673
  233.4 32.2 %collective-permute-start.29 = (bf16[96,3072]{1,0:T(8,128)(2,1)S(1)}, bf16[96,3072]{1,0:T(8,128)(2,1)S(1)}, u32[]{:S(2)}, u32[]{:S(2)}) collective-permute-start(bf16[96,3072]{1,0:T(8,128)(2,1)S(1)} %add.226), channel_id=1, source_target_pairs={{1,0},{2,3},{5,4},{6,7},{9,8},{10,11},{13,12},{14,15},{17,16},{18,... | collective-permute-start | bytes 1769480 | tf_op jit(solution)/shard_map/ppermute | solution.py:678
  234.7 15.5 %collective-permute-start.27 = (bf16[112,768]{1,0:T(8,128)(2,1)S(1)}, bf16[112,768]{1,0:T(8,128)(2,1)S(1)}, u32[]{:S(2)}, u32[]{:S(2)}) collective-permute-start(bf16[112,768]{1,0:T(8,128)(2,1)S(1)} %get-tuple-element.167), channel_id=1, source_target_pairs={{0,24},{4,28},{8,16},{12,20},{16,8},{20,12},{24,0},{28,4},{1,25},{... | collective-permute-start | bytes 516104 | tf_op jit(solution)/shard_map/ppermute | solution.py:673
  236.3 13.9 %collective-permute-start.26 = (bf16[112,768]{1,0:T(8,128)(2,1)S(1)}, bf16[112,768]{1,0:T(8,128)(2,1)S(1)}, u32[]{:S(2)}, u32[]{:S(2)}) collective-permute-start(bf16[112,768]{1,0:T(8,128)(2,1)S(1)} %get-tuple-element.168), channel_id=1, source_target_pairs={{0,16},{4,20},{8,24},{12,28},{16,0},{20,4},{24,8},{28,12},{1,17},{... | collective-permute-start | bytes 516104 | tf_op jit(solution)/shard_map/ppermute | solution.py:673
  242.3 8.0 %collective-permute-start.25 = (bf16[112,768]{1,0:T(8,128)(2,1)S(1)}, bf16[112,768]{1,0:T(8,128)(2,1)S(1)}, u32[]{:S(2)}, u32[]{:S(2)}) collective-permute-start(bf16[112,768]{1,0:T(8,128)(2,1)S(1)} %get-tuple-element.169), channel_id=1, source_target_pairs={{0,8},{4,12},{8,0},{12,4},{16,24},{20,28},{24,16},{28,20},{1,9},{5... | collective-permute-start | bytes 516104 | tf_op jit(solution)/shard_map/ppermute | solution.py:673
  243.1 17.7 %collective-permute-start.28 = (bf16[96,2304]{1,0:T(8,128)(2,1)S(1)}, bf16[96,2304]{1,0:T(8,128)(2,1)S(1)}, u32[]{:S(2)}, u32[]{:S(2)}) collective-permute-start(bf16[96,2304]{1,0:T(8,128)(2,1)S(1)} %add_convert_fusion.9), channel_id=1, source_target_pairs={{0,1},{3,2},{4,5},{7,6},{8,9},{11,10},{12,13},{15,14},{16,17},{19,... | collective-permute-start | bytes 1327112 | tf_op jit(solution)/shard_map/ppermute | solution.py:678
  250.4 12.6 %collective-permute-start.30 = (bf16[112,768]{1,0:T(8,128)(2,1)S(1)}, bf16[112,768]{1,0:T(8,128)(2,1)S(1)}, u32[]{:S(2)}, u32[]{:S(2)}) collective-permute-start(bf16[112,768]{1,0:T(8,128)(2,1)S(1)} %add_convert_fusion.14), channel_id=1, source_target_pairs={{0,1},{1,0},{2,3},{3,2},{4,5},{5,4},{6,7},{7,6},{8,9},{9,8},{10,11... | collective-permute-start | bytes 516104 | tf_op jit(solution)/shard_map/ppermute | solution.py:678
  263.0 11.4 %collective-permute-start.33 = (bf16[112,768]{1,0:T(8,128)(2,1)S(1)}, bf16[112,768]{1,0:T(8,128)(2,1)S(1)}, u32[]{:S(2)}, u32[]{:S(2)}) collective-permute-start(bf16[112,768]{1,0:T(8,128)(2,1)S(1)} %add.237), channel_id=1, source_target_pairs={{0,2},{1,3},{2,0},{3,1},{4,6},{5,7},{6,4},{7,5},{8,10},{9,11},{10,... | collective-permute-start | bytes 516104 | tf_op jit(solution)/shard_map/ppermute | solution.py:678
  266.9 25.8 %collective-permute-start.32 = (bf16[96,2304]{1,0:T(8,128)(2,1)S(1)}, bf16[96,2304]{1,0:T(8,128)(2,1)S(1)}, u32[]{:S(2)}, u32[]{:S(2)}) collective-permute-start(bf16[96,2304]{1,0:T(8,128)(2,1)S(1)} %add.238), channel_id=1, source_target_pairs={{1,0},{2,3},{5,4},{6,7},{9,8},{10,11},{13,12},{14,15},{17,16},{18,... | collective-permute-start | bytes 1327112 | tf_op jit(solution)/shard_map/ppermute | solution.py:678
  (6 other events, 25.8 us)

commit v7 on v6

--- a/solution.py
+++ b/solution.py
@@ -626,8 +626,22 @@
     return call(add_kernel, terms, [spec] * len(terms), outs, (1,), 24, name="add_all", us=12)[0]
 
 
+def masks_of(bits):
+    return [
+        sum(1 << bit for i, bit in enumerate(bits) if other >> i & 1) for other in range(1, 1 << len(bits))
+    ]
+
+
+def in_order(pieces, name, bits):
+    here = lax.axis_index(name)
+    for i, bit in enumerate(bits):
+        high = ((here >> bit) & 1) == 1
+        pieces = [jnp.where(high, pieces[place ^ (1 << i)], pieces[place]) for place in range(len(pieces))]
+    return jnp.concatenate(pieces, 0)
+
+
 class Flow:
-    def __init__(self, sent, kept, line=False, fused=False):
+    def __init__(self, sent, kept, line=False, fused=False, split=False):
         bits = lax.axis_size("row").bit_length() - 1
         self.order = [(0,)] + [tuple(range(i, min(i + 2, bits))) for i in range(1, bits, 2)]
         self.left = list(range(bits - 1, 0, -1))
@@ -641,10 +655,14 @@
                 ((i, count - 1 - i), [(i + 1, i), (count - 2 - i, count - 1 - i)])
                 for i in range(half - 2, -1, -1)
             ]
-        self.sent, self.kept, self.got, self.fused = [sent], kept, None, fused
-
-    def shard(self, terms, bits, mask):
-        here = lax.axis_index("row")
+        if split:
+            bits = count.bit_length() - 1
+            groups = [tuple(range(i, min(i + 2, bits))) for i in range(0, bits, 2)]
+            self.line = [("scatter", group) for group in groups[::-1]] + [("gather", group) for group in groups]
+        self.sent, self.kept, self.got, self.fused, self.split = [sent], kept, None, fused, split
+
+    def shard(self, terms, bits, mask, name="row"):
+        here = lax.axis_index(name)
         order = [self.left.index(bit) for bit in bits]
         total = None
         for term in terms:
@@ -659,10 +677,7 @@
     def step(self):
         if self.order:
             bits = self.order[0]
-            masks = [
-                sum(1 << bit for i, bit in enumerate(bits) if other >> i & 1)
-                for other in range(1, 1 << len(bits))
-            ]
+            masks = masks_of(bits)
             if bits != (0,):
                 terms = [self.kept, *self.got]
                 self.sent = [self.shard(terms, bits, mask) for mask in masks]
@@ -671,6 +686,26 @@
             size = lax.axis_size("row")
             self.got = [
                 lax.ppermute(sent, "row", [(i, i ^ mask) for i in range(size)])
+                for sent, mask in zip(self.sent, masks)
+            ]
+        elif self.split:
+            kind, bits = self.line[0]
+            masks = masks_of(bits)
+            size = lax.axis_size("col")
+            if kind == "scatter":
+                terms = [self.kept, *self.got]
+                if not self.left:
+                    self.left = list(range(size.bit_length() - 2, -1, -1))
+                    rows, wide = self.kept.shape
+                    dims = (2,) * len(self.left) + (rows // size, wide)
+                    terms = [term.reshape(dims) for term in terms]
+                self.sent = [self.shard(terms, bits, mask, "col") for mask in masks]
+                self.kept = self.shard(terms, bits, 0, "col")
+                self.left = [bit for bit in self.left if bit not in bits]
+            else:
+                self.sent = [self.kept] * len(masks)
+            self.got = [
+                lax.ppermute(sent, "col", [(i, i ^ mask) for i in range(size)])
                 for sent, mask in zip(self.sent, masks)
             ]
         else:
@@ -688,7 +723,13 @@
                 self.kept, self.got = self.kept.reshape(dims), [item.reshape(dims) for item in self.got]
             if not self.order and self.fused:
                 self.kept = add_all([self.kept, *self.got])
-            elif not self.order:
+            elif not self.order and not self.split:
+                self.kept = sum([item.astype(F32) for item in self.got], self.kept.astype(F32)).astype(LOW)
+        elif self.split:
+            kind, bits = self.line.pop(0)
+            if kind == "gather":
+                self.kept = in_order([self.kept, *self.got], "col", bits)
+            elif self.line[0][0] == "gather":
                 self.kept = sum([item.astype(F32) for item in self.got], self.kept.astype(F32)).astype(LOW)
         else:
             ends, _ = self.line.pop(0)
@@ -717,18 +758,9 @@
     steps = [("col", tuple(range(i, min(i + 2, col_bits)))) for i in range(0, col_bits, 2)]
     steps += [("row", tuple(range(i, min(i + 2, row_bits)))) for i in range(1, row_bits, 2)]
     for name, bits in steps + [("row", (0,))]:
-        here = lax.axis_index(name)
-        pieces = [piece]
-        for other in range(1, 1 << len(bits)):
-            mask = sum(1 << bit for i, bit in enumerate(bits) if other >> i & 1)
-            pairs = [(i, i ^ mask) for i in range(lax.axis_size(name))]
-            pieces.append(lax.ppermute(piece, name, pairs))
-        for i, bit in enumerate(bits):
-            high = ((here >> bit) & 1) == 1
-            pieces = [
-                jnp.where(high, pieces[place ^ (1 << i)], pieces[place]) for place in range(len(pieces))
-            ]
-        piece = jnp.concatenate(pieces, 0)
+        size = lax.axis_size(name)
+        got = [lax.ppermute(piece, name, [(i, i ^ mask) for i in range(size)]) for mask in masks_of(bits)]
+        piece = in_order([piece, *got], name, bits)
     return piece
 
 
@@ -865,7 +897,7 @@
         name="outer_grad",
         scratch=[pltpu.VMEM((width, total_rows), LOW)],
     )
-    outer = Flow(*outer_parts, line=True)
+    outer = Flow(*outer_parts)
     outer.step()
 
     def turn(arrays, specs, deps):
@@ -939,7 +971,7 @@
     grad_a, stat_a, *mixed_parts = attend_back(*groups[0], deps, room=6 * third + width)
     at = 6 * third // width
     mixed_parts = weight_grad(ctx_t, grad_attn, row_count, core, [stat_a], mixed_parts, at, us=0)
-    mixed_flow = Flow(*mixed_parts, line=True)
+    mixed_flow = Flow(*mixed_parts, split=True)
     mixed_flow.step()
     token = mixed_flow.sent[0]
     deps = mixed_flow.sent + outer.turn(token) + up_flow.turn(token)
@@ -947,7 +979,7 @@
     grad_b, stat_b, *last_parts = attend_back(*groups[1], deps, extra)
     last_flow = Flow(*last_parts)
     last_flow.step()
-    deps = last_flow.sent + outer.turn(stat_b) + mixed_flow.turn(stat_b) + up_flow.turn(stat_b)
+    deps = last_flow.sent + mixed_flow.turn(stat_b) + up_flow.turn(stat_b)
     query_grad, passage_grad = call(
         partial(input_grad_kernel, groups),
         (grad_a, grad_b, grad_attn, w_query, w_key, w_value),

time: 301 us -> 285 us (0.947)
  the two profiles are of different devices: /device:TPU:4 before, /device:TPU:0 now
where the time goes in v7:
time: 285 us; the launch traced here: 279 us
  Pallas kernels  187 us (66%)
  starting transfers between devices  44.6 us (16%)
  waiting for transfers between devices  33.5 us (12%)
  other arithmetic  10.7 us (4%)
    pallas_call x13, Pallas kernels, call(): pl.pallas_call(kernel, grid=grid, in_specs=list(in_specs) + [pl.BlockSpec...  184 us
    ppermute x16, starting transfers between devices, step(): lax.ppermute(sent, 'row', [(i, i ^ mask) for i in range(size)])  14.6 us
    ppermute x6, waiting for transfers between devices, step(): lax.ppermute(sent, 'col', [(i, i ^ mask) for i in range(size)])  14.2 us
    ppermute x6, starting transfers between devices, step(): lax.ppermute(sent, 'col', [(i, i ^ mask) for i in range(size)])  13.7 us
    ppermute x7, starting transfers between devices, gather_all(): lax.ppermute(piece, name, [(i, i ^ mask) for i in range(size)])  9.38 us
    ppermute x7, waiting for transfers between devices, gather_all(): lax.ppermute(piece, name, [(i, i ^ mask) for i in range(size)])  9.27 us
    ppermute x7, starting transfers between devices, step(): self.got = [lax.ppermute(self.kept, 'col', self.line[0][1])]  6.96 us
  transfers between devices with their start and end apart: 36, of which 17 were waited for; matrix products, arithmetic and copies ran while one was open for 2% of the time, Pallas kernels for 38%

profile of v7, /device:TPU:0, one launch (start us, length us, event | category | flops | bytes accessed | tf_op | source)
XLA Modules:
  0.0 279.4 jit_solution(1643804372510931775)
XLA Ops:
  0.7 20.8 %attend.1 = (bf16[1536,768]{1,0:T(8,128)(2,1)}, bf16[1536,768]{1,0:T(8,128)(2,1)}, bf16[1536,768]{1,0:T(8,128)(2,1)}, bf16[768,1536]{1,0:T(8,128)(2,1)}, f32[3,6,8,512]{3,2,1,0:T(8,128)}) custom-call(s32[4]{0:T(128)} %refs_1_.9, s32[2]{0:T(128)} %refs_2_.7, bf16[512,768]{1,0:T(8,128)(2,1)} %bitcast.92, bf16[1024,768]{1,0:T(8,128)(2,1)} %bitcast.89, ...), custom_call_target="tpu_custom_call" | custom-call | flops 13799999488 | tf_op jit(solution)/shard_map/attend/pallas_call | solution.py:579
  21.5 39.0 %dense.1 = (bf16[1536,768]{1,0:T(8,128)(2,1)}, bf16[1536,768]{1,0:T(8,128)(2,1)}, bf16[1536,3072]{1,0:T(8,128)(2,1)}, bf16[1536,3072]{1,0:T(8,128)(2,1)}, bf16[1...) custom-call(s32[4]{0:T(128)} %refs_1_.9, ...), custom_call_target="tpu_custom_call" | custom-call | flops 13799999488 | tf_op jit(solution)/shard_map/dense/pallas_call | solution.py:579
  60.5 5.1 %collective-permute-start = (bf16[8,896]{1,0:T(8,128)(2,1)}, bf16[8,896]{1,0:T(8,128)(2,1)S(1)}, u32[]{:S(2)}, u32[]{:S(2)}) collective-permute-start(bf16[8,896]{1,0:T(8,128)(2,1)} %get-tuple-element.86.own_ref), channel_id=1, source_target_pairs={{0,3},{1,2},{2,1},{3,0},{4,7},{5,6},{6,5},{7,4},{8,11},{9,10},{10,... | collective-permute-start | bytes 43016 | tf_op jit(solution)/shard_map/ppermute | solution.py:762
  67.6 2.9 %collective-permute-done.1 = bf16[8,896]{1,0:T(8,128)(2,1)S(1)} collective-permute-done((bf16[8,896]{1,0:T(8,128)(2,1)}, bf16[8,896]{1,0:T(8,128)(2,1)S(1)}, u32[]{:S(2)}, u32[]{:S(2)}) %collective-permute-start.1) | collective-permute-done | bytes 14368 | tf_op jit(solution)/shard_map/ppermute | solution.py:762
  71.2 1.6 collective-permute-start.4
  75.6 2.2 collective-permute-done.3
  81.0 2.9 %loss.1 = (f32[8,128]{1,0:T(8,128)}, f32[8,768]{1,0:T(8,128)}) custom-call(s32[1]{0:T(128)} %bitcast.me_ref, s32[4]{0:T(128)} %refs_1_.9, s32[2]{0:T(128)} %refs_2_.7, bf16[8,896]{1,0:T(8,128)(2,1)} %get-tuple-element.86.own_ref, bf16[256,896]{1,0:T(8,128)(2,1)} %pad_maximum_fusion.all_ref, f32[8,768]{1,0:T(8,128)} %get-tuple-element.87.pool_ref), custom_call_target="tpu_custom_call" | custom-call | tf_op jit(solution)/shard_map/loss/pallas_call | solution.py:868
  85.1 18.2 %outer_grad.1 = (bf16[1536,768]{1,0:T(8,128)(2,1)}, f32[8,768]{1,0:T(8,128)}, bf16[4,768,384]{2,1,0:T(8,128)(2,1)}, bf16[4,768,384]{2,1,0:T(8,128)(2,1)}) custom-call(s32[1]{0:T(128)} %bitcast.6.refs_0_, s32[4]{0:T(128)} %refs_1_.9, s32[2]{0:T(128)} %refs_2_.7, f32[8,768]{1,0:T(8,128)} %get-tuple-element.91.refs_3_, ...), custom_call_target="tpu_custom_call" | custom-call | flops 13799999488 | tf_op jit(solution)/shard_map/outer_grad/pallas_call | solution.py:579
  103.4 4.5 %turn.3.refs_1_ = bf16[768,1536]{1,0:T(8,128)(2,1)} custom-call(bf16[1536,768]{1,0:T(8,128)(2,1)} %get-tuple-element.97.refs_0_), custom_call_target="tpu_custom_call" | custom-call | flops 46000001024 | tf_op jit(solution)/shard_map/turn/pallas_call | solution.py:579
  112.2 31.1 %dense_back.1 = (bf16[1536,3072]{1,0:T(8,128)(2,1)}, bf16[1536,768]{1,0:T(8,128)(2,1)}, bf16[1536,768]{1,0:T(8,128)(2,1)}, f32[8,768]{1,0:T(8,128)}, f32[8,3072]{1,0:T(8,128)}) custom-call(bf16[1536,768]{1,0:T(8,128)(2,1)} %get-tuple-element.99.refs_0_, bf16[1536,3072]{1,0:T(8,128)(2,1)} %get-tuple-element.100.refs_1_, ...), custom_call_target="tpu_custom_call" | custom-call | flops 13799999488 | tf_op jit(solution)/shard_map/dense_back/pallas_call | solution.py:579
  144.8 12.0 %weight_grad.2 = (bf16[4,96,3072]{2,1,0:T(8,128)(2,1)}, bf16[4,96,3072]{2,1,0:T(8,128)(2,1)}) custom-call(s32[1]{0:T(128)} %bitcast.6.refs_0_, bf16[768,1536]{1,0:T(8,128)(2,1)} %turn.3.refs_1_, bf16[1536,3072]{1,0:T(8,128)(2,1)} %get-tuple-element.106.refs_2_), custom_call_target="tpu_custom_call" | custom-call | flops 13799999488 | tf_op jit(solution)/shard_map/weight_grad/pallas_call | solution.py:579
  156.8 2.6 collective-permute-done.12
  159.6 2.1 collective-permute-start.13
  161.7 4.9 %turn.4.refs_9_ = bf16[768,1536]{1,0:T(8,128)(2,1)} custom-call(bf16[512,768]{1,0:T(8,128)(2,1)} %bitcast.94, bf16[1024,768]{1,0:T(8,128)(2,1)} %bitcast.91), custom_call_target="tpu_custom_call" | custom-call | flops 46000001024 | tf_op jit(solution)/shard_map/turn/pallas_call | solution.py:579
  171.1 21.7 %attend_back.2 = (bf16[1536,1536]{1,0:T(8,128)(2,1)}, f32[8,512]{1,0:T(8,128)}, bf16[4,96,2304]{2,1,0:T(8,128)(2,1)}, bf16[4,96,2304]{2,1,0:T(8,128)(2,1)}) custom-call(s32[1]{0:T(128)} %bitcast.6.refs_0_, s32[4]{0:T(128)} %refs_1_.9, s32[2]{0:T(128)} %refs_2_.7, bf16[1536,768]{1,0:T(8,128)(2,1)} %get-tuple-element.113.refs_3_, ...), custom_call_target="tpu_custom_call" | custom-call | flops 13799999488 | tf_op jit(solution)/shard_map/attend_back/pallas_call | solution.py:579
  192.8 5.6 %weight_grad.3 = (bf16[4,96,2304]{2,1,0:T(8,128)(2,1)}, bf16[4,96,2304]{2,1,0:T(8,128)(2,1)}) custom-call(s32[1]{0:T(128)} %bitcast.6.refs_0_, bf16[768,1536]{1,0:T(8,128)(2,1)} %get-tuple-element.85.refs_5_.refs_6_.refs_1_, bf16[1536,768]{1,0:T(8,128)(2,1)} %get-tuple-element.121.refs_2_, ...), custom_call_target="tpu_custom_call", output_to_operand_aliasing={{0}: (3, {}), {1}: (4, {})} | custom-call | tf_op jit(solution)/shard_map/weight_grad/pallas_call | solution.py:579
  199.7 2.2 collective-permute-start.18
  201.9 12.5 %attend_back.3 = (bf16[1536,768]{1,0:T(8,128)(2,1)}, f32[8,256]{1,0:T(8,128)}, bf16[4,112,768]{2,1,0:T(8,128)(2,1)}, bf16[4,112,768]{2,1,0:T(8,128)(2,1)}) custom-call(s32[1]{0:T(128)} %bitcast.6.refs_0_, s32[4]{0:T(128)} %refs_1_.9, s32[2]{0:T(128)} %refs_2_.7, bf16[1536,768]{1,0:T(8,128)(2,1)} %get-tuple-element.113.refs_3_, ...), custom_call_target="tpu_custom_call" | custom-call | flops 46000001024 | tf_op jit(solution)/shard_map/attend_back/pallas_call | solution.py:579
  216.5 1.6 collective-permute-start.23
  220.0 10.8 %input_grad.1 = (bf16[512,768]{1,0:T(8,128)(2,1)}, bf16[1024,768]{1,0:T(8,128)(2,1)}) custom-call(bf16[1536,1536]{1,0:T(8,128)(2,1)} %get-tuple-element.118.refs_0_, bf16[1536,768]{1,0:T(8,128)(2,1)} %get-tuple-element.129.refs_1_, bf16[1536,768]{1,0:T(8,128)(2,1)} %get-tuple-element.121.refs_2_, bf16[768,768]{1,0:T(8,128)(2,1)} %refs_3_.2, ...), custom_call_target="tpu_custom_call" | custom-call | flops 46000001024 | tf_op jit(solution)/shard_map/input_grad/pallas_call | solution.py:579
  231.0 1.6 collective-permute-start.26
  235.0 5.0 %collective-permute-done.22 = bf16[96,2304]{1,0:T(8,128)(2,1)S(1)} collective-permute-done((bf16[96,2304]{1,0:T(8,128)(2,1)S(1)}, bf16[96,2304]{1,0:T(8,128)(2,1)S(1)}, u32[]{:S(2)}, u32[]{:S(2)}) %collective-permute-start.22) | collective-permute-done | bytes 442400 | tf_op jit(solution)/shard_map/ppermute | solution.py:688
  241.3 2.1 collective-permute-start.29
  243.6 4.2 %collective-permute-start.28 = (bf16[24,2304]{1,0:T(8,128)(2,1)S(1)}, bf16[24,2304]{1,0:T(8,128)(2,1)S(1)}, u32[]{:S(2)}, u32[]{:S(2)}) collective-permute-start(bf16[24,2304]{1,0:T(8,128)(2,1)S(1)} %get-tuple-element.166), channel_id=1, source_target_pairs={{0,2},{1,3},{2,0},{3,1},{4,6},{5,7},{6,4},{7,5},{8,10},{9,11},{10,... | collective-permute-start | bytes 331784 | tf_op jit(solution)/shard_map/ppermute | solution.py:708
  247.8 2.9 %collective-permute-start.27 = (bf16[24,2304]{1,0:T(8,128)(2,1)S(1)}, bf16[24,2304]{1,0:T(8,128)(2,1)S(1)}, u32[]{:S(2)}, u32[]{:S(2)}) collective-permute-start(bf16[24,2304]{1,0:T(8,128)(2,1)S(1)} %get-tuple-element.164), channel_id=1, source_target_pairs={{0,1},{1,0},{2,3},{3,2},{4,5},{5,4},{6,7},{7,6},{8,9},{9,8},{10,11... | collective-permute-start | bytes 331784 | tf_op jit(solution)/shard_map/ppermute | solution.py:708
  251.2 2.3 turn.5
  253.5 1.6 collective-permute-done.28
  255.1 4.6 %collective-permute-done.27 = bf16[24,2304]{1,0:T(8,128)(2,1)S(1)} collective-permute-done((bf16[24,2304]{1,0:T(8,128)(2,1)S(1)}, bf16[24,2304]{1,0:T(8,128)(2,1)S(1)}, u32[]{:S(2)}, u32[]{:S(2)}) %collective-permute-start.27) | collective-permute-done | bytes 110624 | tf_op jit(solution)/shard_map/ppermute | solution.py:708
  259.8 1.8 collective-permute-start.30
  261.6 2.6 collective-permute-start.32
  267.3 6.5 %collective-permute-done.31 = bf16[24,2304]{1,0:T(8,128)(2,1)S(1)} collective-permute-done((bf16[24,2304]{1,0:T(8,128)(2,1)S(1)}, bf16[24,2304]{1,0:T(8,128)(2,1)S(1)}, u32[]{:S(2)}, u32[]{:S(2)}) %collective-permute-start.31) | collective-permute-done | bytes 110624 | tf_op jit(solution)/shard_map/ppermute | solution.py:708
  274.6 1.5 collective-permute-done.35
  (95 shorter events, 36.5 us)
Async XLA Ops:
  60.5 7.0 %collective-permute-start = (bf16[8,896]{1,0:T(8,128)(2,1)}, bf16[8,896]{1,0:T(8,128)(2,1)S(1)}, u32[]{:S(2)}, u32[]{:S(2)}) collective-permute-start(bf16[8,896]{1,0:T(8,128)(2,1)} %get-tuple-element.86.own_ref), channel_id=1, source_target_pairs={{0,3},{1,2},{2,1},{3,0},{4,7},{5,6},{6,5},{7,4},{8,11},{9,10},{10,... | collective-permute-start | bytes 43016 | tf_op jit(solution)/shard_map/ppermute | solution.py:762
  65.6 4.8 %collective-permute-start.1 = (bf16[8,896]{1,0:T(8,128)(2,1)}, bf16[8,896]{1,0:T(8,128)(2,1)S(1)}, u32[]{:S(2)}, u32[]{:S(2)}) collective-permute-start(bf16[8,896]{1,0:T(8,128)(2,1)} %get-tuple-element.86.own_ref), channel_id=1, source_target_pairs={{0,2},{1,3},{2,0},{3,1},{4,6},{5,7},{6,4},{7,5},{8,10},{9,11},{10,... | collective-permute-start | bytes 43016 | tf_op jit(solution)/shard_map/ppermute | solution.py:762
  65.7 4.8 %collective-permute-start.2 = (bf16[8,896]{1,0:T(8,128)(2,1)}, bf16[8,896]{1,0:T(8,128)(2,1)S(1)}, u32[]{:S(2)}, u32[]{:S(2)}) collective-permute-start(bf16[8,896]{1,0:T(8,128)(2,1)} %get-tuple-element.86.own_ref), channel_id=1, source_target_pairs={{0,1},{1,0},{2,3},{3,2},{4,5},{5,4},{6,7},{7,6},{8,9},{9,8},{10,11... | collective-permute-start | bytes 43016 | tf_op jit(solution)/shard_map/ppermute | solution.py:762
  72.8 5.1 %collective-permute-start.3 = (bf16[32,896]{1,0:T(8,128)(2,1)S(1)}, bf16[32,896]{1,0:T(8,128)(2,1)S(1)}, u32[]{:S(2)}, u32[]{:S(2)}) collective-permute-start(bf16[32,896]{1,0:T(8,128)(2,1)S(1)} %pad_maximum_fusion.3), channel_id=1, source_target_pairs={{0,24},{4,28},{8,16},{12,20},{16,8},{20,12},{24,0},{28,4},{1,25},{... | collective-permute-start | bytes 172040 | tf_op jit(solution)/shard_map/ppermute | solution.py:762
  108.7 34.7 %collective-permute-start.8 = (bf16[768,384]{1,0:T(8,128)(2,1)S(1)}, bf16[768,384]{1,0:T(8,128)(2,1)S(1)}, u32[]{:S(2)}, u32[]{:S(2)}) collective-permute-start(bf16[768,384]{1,0:T(8,128)(2,1)S(1)} %get-tuple-element.159), channel_id=1, source_target_pairs={{0,8},{4,12},{8,0},{12,4},{16,24},{20,28},{24,16},{28,20},{1,9},{5... | collective-permute-start | bytes 1769480 | tf_op jit(solution)/shard_map/ppermute | solution.py:688
  109.7 33.6 %collective-permute-start.9 = (bf16[768,384]{1,0:T(8,128)(2,1)S(1)}, bf16[768,384]{1,0:T(8,128)(2,1)S(1)}, u32[]{:S(2)}, u32[]{:S(2)}) collective-permute-start(bf16[768,384]{1,0:T(8,128)(2,1)S(1)} %get-tuple-element.158), channel_id=1, source_target_pairs={{0,16},{4,20},{8,24},{12,28},{16,0},{20,4},{24,8},{28,12},{1,17},{... | collective-permute-start | bytes 1769480 | tf_op jit(solution)/shard_map/ppermute | solution.py:688
  110.9 32.5 %collective-permute-start.10 = (bf16[768,384]{1,0:T(8,128)(2,1)S(1)}, bf16[768,384]{1,0:T(8,128)(2,1)}, u32[]{:S(2)}, u32[]{:S(2)}) collective-permute-start(bf16[768,384]{1,0:T(8,128)(2,1)S(1)} %get-tuple-element.157), channel_id=1, source_target_pairs={{0,24},{4,28},{8,16},{12,20},{16,8},{20,12},{24,0},{28,4},{1,25},{... | collective-permute-start | bytes 1769480 | tf_op jit(solution)/shard_map/ppermute | solution.py:688
  144.7 14.7 %collective-permute-start.12 = (bf16[768,384]{1,0:T(8,128)(2,1)S(1)}, bf16[768,384]{1,0:T(8,128)(2,1)S(1)}, u32[]{:S(2)}, u32[]{:S(2)}) collective-permute-start(bf16[768,384]{1,0:T(8,128)(2,1)S(1)} %add_convert_fusion.4), channel_id=1, source_target_pairs={{0,1},{1,0},{2,3},{3,2},{4,5},{5,4},{6,7},{7,6},{8,9},{9,8},{10,11... | collective-permute-start | bytes 1769480 | tf_op jit(solution)/shard_map/ppermute | solution.py:713
  156.8 9.8 %collective-permute-start.11 = (bf16[4,96,3072]{2,1,0:T(8,128)(2,1)}, bf16[4,96,3072]{2,1,0:T(8,128)(2,1)S(1)}, u32[]{:S(2)}, u32[]{:S(2)}) collective-permute-start(bf16[4,96,3072]{2,1,0:T(8,128)(2,1)} %get-tuple-element.107), channel_id=1, source_target_pairs={{0,4},{4,0},{8,12},{12,8},{16,20},{20,16},{24,28},{28,24},{1,5},{5... | collective-permute-start | bytes 7077896 | tf_op jit(solution)/shard_map/ppermute | solution.py:688
  159.6 38.8 %collective-permute-start.13 = (bf16[768,384]{1,0:T(8,128)(2,1)S(1)}, bf16[768,384]{1,0:T(8,128)(2,1)S(1)}, u32[]{:S(2)}, u32[]{:S(2)}) collective-permute-start(bf16[768,384]{1,0:T(8,128)(2,1)S(1)} %add.312), channel_id=1, source_target_pairs={{0,2},{1,3},{2,0},{3,1},{4,6},{5,7},{6,4},{7,5},{8,10},{9,11},{10,... | collective-permute-start | bytes 1769480 | tf_op jit(solution)/shard_map/ppermute | solution.py:713
  167.6 31.8 %collective-permute-start.14 = (bf16[96,3072]{1,0:T(8,128)(2,1)S(1)}, bf16[96,3072]{1,0:T(8,128)(2,1)S(1)}, u32[]{:S(2)}, u32[]{:S(2)}) collective-permute-start(bf16[96,3072]{1,0:T(8,128)(2,1)S(1)} %get-tuple-element.155), channel_id=1, source_target_pairs={{0,8},{4,12},{8,0},{12,4},{16,24},{20,28},{24,16},{28,20},{1,9},{5... | collective-permute-start | bytes 1769480 | tf_op jit(solution)/shard_map/ppermute | solution.py:688
  168.6 30.8 %collective-permute-start.15 = (bf16[96,3072]{1,0:T(8,128)(2,1)S(1)}, bf16[96,3072]{1,0:T(8,128)(2,1)S(1)}, u32[]{:S(2)}, u32[]{:S(2)}) collective-permute-start(bf16[96,3072]{1,0:T(8,128)(2,1)S(1)} %get-tuple-element.154), channel_id=1, source_target_pairs={{0,16},{4,20},{8,24},{12,28},{16,0},{20,4},{24,8},{28,12},{1,17},{... | collective-permute-start | bytes 1769480 | tf_op jit(solution)/shard_map/ppermute | solution.py:688
  169.8 29.6 %collective-permute-start.16 = (bf16[96,3072]{1,0:T(8,128)(2,1)S(1)}, bf16[96,3072]{1,0:T(8,128)(2,1)S(1)}, u32[]{:S(2)}, u32[]{:S(2)}) collective-permute-start(bf16[96,3072]{1,0:T(8,128)(2,1)S(1)} %get-tuple-element.153), channel_id=1, source_target_pairs={{0,24},{4,28},{8,16},{12,20},{16,8},{20,12},{24,0},{28,4},{1,25},{... | collective-permute-start | bytes 1769480 | tf_op jit(solution)/shard_map/ppermute | solution.py:688
  198.4 17.6 %collective-permute-start.17 = (bf16[4,96,2304]{2,1,0:T(8,128)(2,1)}, bf16[4,96,2304]{2,1,0:T(8,128)(2,1)S(1)}, u32[]{:S(2)}, u32[]{:S(2)}) collective-permute-start(bf16[4,96,2304]{2,1,0:T(8,128)(2,1)} %get-tuple-element.124), channel_id=1, source_target_pairs={{0,4},{4,0},{8,12},{12,8},{16,20},{20,16},{24,28},{28,24},{1,5},{5... | collective-permute-start | bytes 5308424 | tf_op jit(solution)/shard_map/ppermute | solution.py:688
  199.7 15.4 %collective-permute-start.18 = (bf16[96,3072]{1,0:T(8,128)(2,1)S(1)}, bf16[96,3072]{1,0:T(8,128)(2,1)S(1)}, u32[]{:S(2)}, u32[]{:S(2)}) collective-permute-start(bf16[96,3072]{1,0:T(8,128)(2,1)S(1)} %add_all.1), channel_id=1, source_target_pairs={{0,1},{3,2},{4,5},{7,6},{8,9},{11,10},{12,13},{15,14},{16,17},{19,... | collective-permute-start | bytes 1769480 | tf_op jit(solution)/shard_map/ppermute | solution.py:713
  214.5 16.3 %collective-permute-start.19 = (bf16[4,112,768]{2,1,0:T(8,128)(2,1)}, bf16[4,112,768]{2,1,0:T(8,128)(2,1)S(1)}, u32[]{:S(2)}, u32[]{:S(2)}) collective-permute-start(bf16[4,112,768]{2,1,0:T(8,128)(2,1)} %get-tuple-element.130), channel_id=1, source_target_pairs={{0,4},{4,0},{8,12},{12,8},{16,20},{20,16},{24,28},{28,24},{1,5},{5... | collective-permute-start | bytes 2064392 | tf_op jit(solution)/shard_map/ppermute | solution.py:688
  215.3 17.4 %collective-permute-start.20 = (bf16[96,3072]{1,0:T(8,128)(2,1)S(1)}, bf16[96,3072]{1,0:T(8,128)(2,1)S(1)}, u32[]{:S(2)}, u32[]{:S(2)}) collective-permute-start(bf16[96,3072]{1,0:T(8,128)(2,1)S(1)} %add.320), channel_id=1, source_target_pairs={{1,2},{2,1},{5,6},{6,5},{9,10},{10,9},{13,14},{14,13},{17,18},{18,... | collective-permute-start | bytes 1769480 | tf_op jit(solution)/shard_map/ppermute | solution.py:713
  216.5 17.6 %collective-permute-start.23 = (bf16[96,2304]{1,0:T(8,128)(2,1)S(1)}, bf16[96,2304]{1,0:T(8,128)(2,1)S(1)}, u32[]{:S(2)}, u32[]{:S(2)}) collective-permute-start(bf16[96,2304]{1,0:T(8,128)(2,1)S(1)} %get-tuple-element.161), channel_id=1, source_target_pairs={{0,24},{4,28},{8,16},{12,20},{16,8},{20,12},{24,0},{28,4},{1,25},{... | collective-permute-start | bytes 1327112 | tf_op jit(solution)/shard_map/ppermute | solution.py:688
  218.1 21.9 %collective-permute-start.22 = (bf16[96,2304]{1,0:T(8,128)(2,1)S(1)}, bf16[96,2304]{1,0:T(8,128)(2,1)S(1)}, u32[]{:S(2)}, u32[]{:S(2)}) collective-permute-start(bf16[96,2304]{1,0:T(8,128)(2,1)S(1)} %get-tuple-element.162), channel_id=1, source_target_pairs={{0,16},{4,20},{8,24},{12,28},{16,0},{20,4},{24,8},{28,12},{1,17},{... | collective-permute-start | bytes 1327112 | tf_op jit(solution)/shard_map/ppermute | solution.py:688
  219.0 22.0 %collective-permute-start.21 = (bf16[96,2304]{1,0:T(8,128)(2,1)S(1)}, bf16[96,2304]{1,0:T(8,128)(2,1)S(1)}, u32[]{:S(2)}, u32[]{:S(2)}) collective-permute-start(bf16[96,2304]{1,0:T(8,128)(2,1)S(1)} %get-tuple-element.163), channel_id=1, source_target_pairs={{0,8},{4,12},{8,0},{12,4},{16,24},{20,28},{24,16},{28,20},{1,9},{5... | collective-permute-start | bytes 1327112 | tf_op jit(solution)/shard_map/ppermute | solution.py:688
  231.0 12.6 %collective-permute-start.26 = (bf16[112,768]{1,0:T(8,128)(2,1)S(1)}, bf16[112,768]{1,0:T(8,128)(2,1)S(1)}, u32[]{:S(2)}, u32[]{:S(2)}) collective-permute-start(bf16[112,768]{1,0:T(8,128)(2,1)S(1)} %get-tuple-element.169), channel_id=1, source_target_pairs={{0,24},{4,28},{8,16},{12,20},{16,8},{20,12},{24,0},{28,4},{1,25},{... | collective-permute-start | bytes 516104 | tf_op jit(solution)/shard_map/ppermute | solution.py:688
  232.8 31.8 %collective-permute-start.33 = (bf16[96,3072]{1,0:T(8,128)(2,1)S(1)}, bf16[96,3072]{1,0:T(8,128)(2,1)S(1)}, u32[]{:S(2)}, u32[]{:S(2)}) collective-permute-start(bf16[96,3072]{1,0:T(8,128)(2,1)S(1)} %add.323), channel_id=1, source_target_pairs={{1,0},{2,3},{5,4},{6,7},{9,8},{10,11},{13,12},{14,15},{17,16},{18,... | collective-permute-start | bytes 1769480 | tf_op jit(solution)/shard_map/ppermute | solution.py:713
  234.1 13.6 %collective-permute-start.25 = (bf16[112,768]{1,0:T(8,128)(2,1)S(1)}, bf16[112,768]{1,0:T(8,128)(2,1)S(1)}, u32[]{:S(2)}, u32[]{:S(2)}) collective-permute-start(bf16[112,768]{1,0:T(8,128)(2,1)S(1)} %get-tuple-element.170), channel_id=1, source_target_pairs={{0,16},{4,20},{8,24},{12,28},{16,0},{20,4},{24,8},{28,12},{1,17},{... | collective-permute-start | bytes 516104 | tf_op jit(solution)/shard_map/ppermute | solution.py:688
  240.0 10.6 %collective-permute-start.24 = (bf16[112,768]{1,0:T(8,128)(2,1)S(1)}, bf16[112,768]{1,0:T(8,128)(2,1)S(1)}, u32[]{:S(2)}, u32[]{:S(2)}) collective-permute-start(bf16[112,768]{1,0:T(8,128)(2,1)S(1)} %get-tuple-element.171), channel_id=1, source_target_pairs={{0,8},{4,12},{8,0},{12,4},{16,24},{20,28},{24,16},{28,20},{1,9},{5... | collective-permute-start | bytes 516104 | tf_op jit(solution)/shard_map/ppermute | solution.py:688
  241.3 12.3 %collective-permute-start.29 = (bf16[24,2304]{1,0:T(8,128)(2,1)S(1)}, bf16[24,2304]{1,0:T(8,128)(2,1)S(1)}, u32[]{:S(2)}, u32[]{:S(2)}) collective-permute-start(bf16[24,2304]{1,0:T(8,128)(2,1)S(1)} %get-tuple-element.165), channel_id=1, source_target_pairs={{0,3},{1,2},{2,1},{3,0},{4,7},{5,6},{6,5},{7,4},{8,11},{9,10},{10,... | collective-permute-start | bytes 331784 | tf_op jit(solution)/shard_map/ppermute | solution.py:708
  243.6 11.5 %collective-permute-start.28 = (bf16[24,2304]{1,0:T(8,128)(2,1)S(1)}, bf16[24,2304]{1,0:T(8,128)(2,1)S(1)}, u32[]{:S(2)}, u32[]{:S(2)}) collective-permute-start(bf16[24,2304]{1,0:T(8,128)(2,1)S(1)} %get-tuple-element.166), channel_id=1, source_target_pairs={{0,2},{1,3},{2,0},{3,1},{4,6},{5,7},{6,4},{7,5},{8,10},{9,11},{10,... | collective-permute-start | bytes 331784 | tf_op jit(solution)/shard_map/ppermute | solution.py:708
  247.8 12.0 %collective-permute-start.27 = (bf16[24,2304]{1,0:T(8,128)(2,1)S(1)}, bf16[24,2304]{1,0:T(8,128)(2,1)S(1)}, u32[]{:S(2)}, u32[]{:S(2)}) collective-permute-start(bf16[24,2304]{1,0:T(8,128)(2,1)S(1)} %get-tuple-element.164), channel_id=1, source_target_pairs={{0,1},{1,0},{2,3},{3,2},{4,5},{5,4},{6,7},{7,6},{8,9},{9,8},{10,11... | collective-permute-start | bytes 331784 | tf_op jit(solution)/shard_map/ppermute | solution.py:708
  250.8 13.6 %collective-permute-start.34 = (bf16[112,768]{1,0:T(8,128)(2,1)S(1)}, bf16[112,768]{1,0:T(8,128)(2,1)S(1)}, u32[]{:S(2)}, u32[]{:S(2)}) collective-permute-start(bf16[112,768]{1,0:T(8,128)(2,1)S(1)} %add_convert_fusion.13), channel_id=1, source_target_pairs={{0,1},{1,0},{2,3},{3,2},{4,5},{5,4},{6,7},{7,6},{8,9},{9,8},{10,11... | collective-permute-start | bytes 516104 | tf_op jit(solution)/shard_map/ppermute | solution.py:713
  259.8 7.5 %collective-permute-start.30 = (bf16[24,2304]{1,0:T(8,128)(2,1)S(1)}, bf16[24,2304]{1,0:T(8,128)(2,1)S(1)}, u32[]{:S(2)}, u32[]{:S(2)}) collective-permute-start(bf16[24,2304]{1,0:T(8,128)(2,1)S(1)} %add_convert_fusion.18), channel_id=1, source_target_pairs={{0,3},{1,2},{2,1},{3,0},{4,7},{5,6},{6,5},{7,4},{8,11},{9,10},{10,... | collective-permute-start | bytes 331784 | tf_op jit(solution)/shard_map/ppermute | solution.py:708
  261.6 12.1 %collective-permute-start.31 = (bf16[24,2304]{1,0:T(8,128)(2,1)S(1)}, bf16[24,2304]{1,0:T(8,128)(2,1)S(1)}, u32[]{:S(2)}, u32[]{:S(2)}) collective-permute-start(bf16[24,2304]{1,0:T(8,128)(2,1)S(1)} %add_convert_fusion.18), channel_id=1, source_target_pairs={{0,2},{1,3},{2,0},{3,1},{4,6},{5,7},{6,4},{7,5},{8,10},{9,11},{10,... | collective-permute-start | bytes 331784 | tf_op jit(solution)/shard_map/ppermute | solution.py:708
  261.6 12.1 %collective-permute-start.32 = (bf16[24,2304]{1,0:T(8,128)(2,1)S(1)}, bf16[24,2304]{1,0:T(8,128)(2,1)S(1)}, u32[]{:S(2)}, u32[]{:S(2)}) collective-permute-start(bf16[24,2304]{1,0:T(8,128)(2,1)S(1)} %add_convert_fusion.18), channel_id=1, source_target_pairs={{0,1},{1,0},{2,3},{3,2},{4,5},{5,4},{6,7},{7,6},{8,9},{9,8},{10,11... | collective-permute-start | bytes 331784 | tf_op jit(solution)/shard_map/ppermute | solution.py:708
  264.5 11.6 %collective-permute-start.35 = (bf16[112,768]{1,0:T(8,128)(2,1)S(1)}, bf16[112,768]{1,0:T(8,128)(2,1)S(1)}, u32[]{:S(2)}, u32[]{:S(2)}) collective-permute-start(bf16[112,768]{1,0:T(8,128)(2,1)S(1)} %add.358), channel_id=1, source_target_pairs={{0,2},{1,3},{2,0},{3,1},{4,6},{5,7},{6,4},{7,5},{8,10},{9,11},{10,... | collective-permute-start | bytes 516104 | tf_op jit(solution)/shard_map/ppermute | solution.py:713
  (8 other events, 36.8 us)

commit v8 on v7

--- a/solution.py
+++ b/solution.py
@@ -641,9 +641,9 @@
 
 
 class Flow:
-    def __init__(self, sent, kept, line=False, fused=False, split=False):
+    def __init__(self, sent, kept, line=False, fused=False, split=False, wide=2):
         bits = lax.axis_size("row").bit_length() - 1
-        self.order = [(0,)] + [tuple(range(i, min(i + 2, bits))) for i in range(1, bits, 2)]
+        self.order = [(0,)] + [tuple(range(i, min(i + wide, bits))) for i in range(1, bits, wide)]
         self.left = list(range(bits - 1, 0, -1))
         count = lax.axis_size("col")
         self.line = [(None, [(i, i ^ (1 << bit)) for i in range(count)]) for bit in range(count.bit_length() - 1)]
@@ -932,7 +932,7 @@
         ],
     )
     deps = outer.turn(stat_one)
-    up_flow = Flow(*weight_grad(y1_t, grad_u, row_count, core, deps), line=True, fused=True)
+    up_flow = Flow(*weight_grad(y1_t, grad_u, row_count, core, deps), fused=True)
     up_flow.step()
     deps = up_flow.sent + outer.turn(up_flow.sent[0])
     x_t = turn([queries, passages], [queries_spec, passages_spec], deps)
@@ -977,7 +977,7 @@
     deps = mixed_flow.sent + outer.turn(token) + up_flow.turn(token)
     extra = (stat_two, stat_one, grad_bias_inner, stat_a)
     grad_b, stat_b, *last_parts = attend_back(*groups[1], deps, extra)
-    last_flow = Flow(*last_parts)
+    last_flow = Flow(*last_parts, wide=1)
     last_flow.step()
     deps = last_flow.sent + mixed_flow.turn(stat_b) + up_flow.turn(stat_b)
     query_grad, passage_grad = call(
@@ -994,19 +994,18 @@
         name="input_grad",
         us=40,
     )
-    last_flow.turn(passage_grad)
-    up_flow.turn(last_flow.kept)
-    mixed_flow.turn(up_flow.kept)
+    mixed_flow.turn(passage_grad)
     last_flow.turn(mixed_flow.kept)
     outs = [(fixed((cut_inner, width)), shape(cut_inner, width, kind=F32))]
     (turned,) = call(
         turn_kernel, (outer.kept,), [const_spec((width, cut_inner))], outs, (1,), 56, [last_flow.kept], name="turn", us=40
     )
-    mixed_flow.turn(turned)
+    up_flow.turn(turned)
+    last_flow.turn(up_flow.kept)
+    mixed_flow.turn(last_flow.kept)
     last_flow.turn(mixed_flow.kept)
-    up_flow.turn(last_flow.kept)
-    mixed_flow.turn(up_flow.kept)
-    last_flow.turn(mixed_flow.kept)
+    last_flow.turn()
+    mixed_flow.turn(last_flow.kept)
     flows = [outer, up_flow, mixed_flow, last_flow]
     while not all(flow.done for flow in flows):
         for flow in flows:

time: 285 us -> 284 us (level)
  waiting for transfers between devices: 33.5 us -> 43 us
  starting transfers between devices: 44.6 us -> 35.2 us
    ppermute x16 -> x15, waiting for transfers between devices: 5.41 us -> 16.6 us  [step(): lax.ppermute(sent, 'row', [(i, i ^ mask) for i in range(size)])]
    ppermute x6, waiting for transfers between devices: 14.2 us -> 7.27 us  [step(): lax.ppermute(sent, 'col', [(i, i ^ mask) for i in range(size)])]
    ppermute x7 -> x6, waiting for transfers between devices: 4.7 us -> 9.87 us  [step(): self.got = [lax.ppermute(self.kept, 'col', self.line[0][1])]]
    ppermute x6, starting transfers between devices: 13.7 us -> 8.84 us  [step(): lax.ppermute(sent, 'col', [(i, i ^ mask) for i in range(size)])]
    ppermute x7 -> x6, starting transfers between devices: 6.96 us -> 3.99 us  [step(): self.got = [lax.ppermute(self.kept, 'col', self.line[0][1])]]
    ppermute x16 -> x15, starting transfers between devices: 14.6 us -> 13 us  [step(): lax.ppermute(sent, 'row', [(i, i ^ mask) for i in range(size)])]
  transfers between devices with their start and end apart: 36 -> 34, of which waited for: 17 -> 18; matrix products, arithmetic and copies ran while one was open for 2% -> 2% of each run, Pallas kernels for 38% -> 38%
where the time goes in v8:
time: 284 us; the launch traced here: 278 us
  Pallas kernels  187 us (66%)
  waiting for transfers between devices  43 us (15%)
  starting transfers between devices  35.2 us (12%)
  other arithmetic  9.17 us (3%)
    pallas_call x13, Pallas kernels, call(): pl.pallas_call(kernel, grid=grid, in_specs=list(in_specs) + [pl.BlockSpec...  184 us
    ppermute x15, waiting for transfers between devices, step(): lax.ppermute(sent, 'row', [(i, i ^ mask) for i in range(size)])  16.6 us
    ppermute x15, starting transfers between devices, step(): lax.ppermute(sent, 'row', [(i, i ^ mask) for i in range(size)])  13 us
    ppermute x6, waiting for transfers between devices, step(): self.got = [lax.ppermute(self.kept, 'col', self.line[0][1])]  9.87 us
    ppermute x7, starting transfers between devices, gather_all(): lax.ppermute(piece, name, [(i, i ^ mask) for i in range(size)])  9.38 us
    ppermute x7, waiting for transfers between devices, gather_all(): lax.ppermute(piece, name, [(i, i ^ mask) for i in range(size)])  9.27 us
    ppermute x6, starting transfers between devices, step(): lax.ppermute(sent, 'col', [(i, i ^ mask) for i in range(size)])  8.84 us
    ppermute x6, waiting for transfers between devices, step(): lax.ppermute(sent, 'col', [(i, i ^ mask) for i in range(size)])  7.27 us
  transfers between devices with their start and end apart: 34, of which 18 were waited for; matrix products, arithmetic and copies ran while one was open for 2% of the time, Pallas kernels for 38%

profile of v8, /device:TPU:0, one launch (start us, length us, event | category | flops | bytes accessed | tf_op | source)
XLA Modules:
  0.0 278.0 jit_solution(10002223400657856945)
XLA Ops:
  0.7 20.8 %attend.1 = (bf16[1536,768]{1,0:T(8,128)(2,1)}, bf16[1536,768]{1,0:T(8,128)(2,1)}, bf16[1536,768]{1,0:T(8,128)(2,1)}, bf16[768,1536]{1,0:T(8,128)(2,1)}, f32[3,6,8,512]{3,2,1,0:T(8,128)}) custom-call(s32[4]{0:T(128)} %refs_1_.9, s32[2]{0:T(128)} %refs_2_.7, bf16[512,768]{1,0:T(8,128)(2,1)} %bitcast.100, bf16[1024,768]{1,0:T(8,128)(2,1)} %bitcast.97, ...), custom_call_target="tpu_custom_call" | custom-call | flops 13799999488 | tf_op jit(solution)/shard_map/attend/pallas_call | solution.py:579
  21.5 39.0 %dense.1 = (bf16[1536,768]{1,0:T(8,128)(2,1)}, bf16[1536,768]{1,0:T(8,128)(2,1)}, bf16[1536,3072]{1,0:T(8,128)(2,1)}, bf16[1536,3072]{1,0:T(8,128)(2,1)}, bf16[1...) custom-call(s32[4]{0:T(128)} %refs_1_.9, ...), custom_call_target="tpu_custom_call" | custom-call | flops 13799999488 | tf_op jit(solution)/shard_map/dense/pallas_call | solution.py:579
  60.5 5.1 %collective-permute-start = (bf16[8,896]{1,0:T(8,128)(2,1)}, bf16[8,896]{1,0:T(8,128)(2,1)S(1)}, u32[]{:S(2)}, u32[]{:S(2)}) collective-permute-start(bf16[8,896]{1,0:T(8,128)(2,1)} %get-tuple-element.84.own_ref), channel_id=1, source_target_pairs={{0,3},{1,2},{2,1},{3,0},{4,7},{5,6},{6,5},{7,4},{8,11},{9,10},{10,... | collective-permute-start | bytes 43016 | tf_op jit(solution)/shard_map/ppermute | solution.py:762
  67.5 2.9 %collective-permute-done.1 = bf16[8,896]{1,0:T(8,128)(2,1)S(1)} collective-permute-done((bf16[8,896]{1,0:T(8,128)(2,1)}, bf16[8,896]{1,0:T(8,128)(2,1)S(1)}, u32[]{:S(2)}, u32[]{:S(2)}) %collective-permute-start.1) | collective-permute-done | bytes 14368 | tf_op jit(solution)/shard_map/ppermute | solution.py:762
  71.2 1.6 collective-permute-start.4
  75.6 2.2 collective-permute-done.3
  78.6 1.4 collective-permute-done.6
  81.0 2.9 %loss.1 = (f32[8,128]{1,0:T(8,128)}, f32[8,768]{1,0:T(8,128)}) custom-call(s32[1]{0:T(128)} %bitcast.me_ref, s32[4]{0:T(128)} %refs_1_.9, s32[2]{0:T(128)} %refs_2_.7, bf16[8,896]{1,0:T(8,128)(2,1)} %get-tuple-element.84.own_ref, bf16[256,896]{1,0:T(8,128)(2,1)} %pad_maximum_fusion.all_ref, f32[8,768]{1,0:T(8,128)} %get-tuple-element.85.pool_ref), custom_call_target="tpu_custom_call" | custom-call | tf_op jit(solution)/shard_map/loss/pallas_call | solution.py:868
  83.9 18.3 %outer_grad.1 = (bf16[1536,768]{1,0:T(8,128)(2,1)}, f32[8,768]{1,0:T(8,128)}, bf16[4,768,384]{2,1,0:T(8,128)(2,1)}, bf16[4,768,384]{2,1,0:T(8,128)(2,1)}) custom-call(s32[1]{0:T(128)} %bitcast.6.refs_0_, s32[4]{0:T(128)} %refs_1_.9, s32[2]{0:T(128)} %refs_2_.7, f32[8,768]{1,0:T(8,128)} %get-tuple-element.89.refs_3_, ...), custom_call_target="tpu_custom_call" | custom-call | flops 13799999488 | tf_op jit(solution)/shard_map/outer_grad/pallas_call | solution.py:579
  102.3 4.4 %turn.3.refs_1_ = bf16[768,1536]{1,0:T(8,128)(2,1)} custom-call(bf16[1536,768]{1,0:T(8,128)(2,1)} %get-tuple-element.95.refs_0_), custom_call_target="tpu_custom_call" | custom-call | flops 46000001024 | tf_op jit(solution)/shard_map/turn/pallas_call | solution.py:579
  111.1 31.1 %dense_back.1 = (bf16[1536,3072]{1,0:T(8,128)(2,1)}, bf16[1536,768]{1,0:T(8,128)(2,1)}, bf16[1536,768]{1,0:T(8,128)(2,1)}, f32[8,768]{1,0:T(8,128)}, f32[8,3072]{1,0:T(8,128)}) custom-call(bf16[1536,768]{1,0:T(8,128)(2,1)} %get-tuple-element.97.refs_0_, bf16[1536,3072]{1,0:T(8,128)(2,1)} %get-tuple-element.98.refs_1_, ...), custom_call_target="tpu_custom_call" | custom-call | flops 13799999488 | tf_op jit(solution)/shard_map/dense_back/pallas_call | solution.py:579
  143.6 12.2 %weight_grad.2 = (bf16[4,96,3072]{2,1,0:T(8,128)(2,1)}, bf16[4,96,3072]{2,1,0:T(8,128)(2,1)}) custom-call(s32[1]{0:T(128)} %bitcast.6.refs_0_, bf16[768,1536]{1,0:T(8,128)(2,1)} %turn.3.refs_1_, bf16[1536,3072]{1,0:T(8,128)(2,1)} %get-tuple-element.104.refs_2_), custom_call_target="tpu_custom_call" | custom-call | flops 13799999488 | tf_op jit(solution)/shard_map/weight_grad/pallas_call | solution.py:579
  155.9 2.3 collective-permute-done.12
  158.4 2.1 collective-permute-start.13
  160.4 4.9 %turn.4.refs_9_ = bf16[768,1536]{1,0:T(8,128)(2,1)} custom-call(bf16[512,768]{1,0:T(8,128)(2,1)} %bitcast.102, bf16[1024,768]{1,0:T(8,128)(2,1)} %bitcast.99), custom_call_target="tpu_custom_call" | custom-call | flops 46000001024 | tf_op jit(solution)/shard_map/turn/pallas_call | solution.py:579
  169.8 21.8 %attend_back.2 = (bf16[1536,1536]{1,0:T(8,128)(2,1)}, f32[8,512]{1,0:T(8,128)}, bf16[4,96,2304]{2,1,0:T(8,128)(2,1)}, bf16[4,96,2304]{2,1,0:T(8,128)(2,1)}) custom-call(s32[1]{0:T(128)} %bitcast.6.refs_0_, s32[4]{0:T(128)} %refs_1_.9, s32[2]{0:T(128)} %refs_2_.7, bf16[1536,768]{1,0:T(8,128)(2,1)} %get-tuple-element.111.refs_3_, ...), custom_call_target="tpu_custom_call" | custom-call | flops 13799999488 | tf_op jit(solution)/shard_map/attend_back/pallas_call | solution.py:579
  191.6 5.7 %weight_grad.3 = (bf16[4,96,2304]{2,1,0:T(8,128)(2,1)}, bf16[4,96,2304]{2,1,0:T(8,128)(2,1)}) custom-call(s32[1]{0:T(128)} %bitcast.6.refs_0_, bf16[768,1536]{1,0:T(8,128)(2,1)} %get-tuple-element.83.refs_5_.refs_6_.refs_1_, bf16[1536,768]{1,0:T(8,128)(2,1)} %get-tuple-element.119.refs_2_, ...), custom_call_target="tpu_custom_call", output_to_operand_aliasing={{0}: (3, {}), {1}: (4, {})} | custom-call | tf_op jit(solution)/shard_map/weight_grad/pallas_call | solution.py:579
  198.9 12.5 %attend_back.3 = (bf16[1536,768]{1,0:T(8,128)(2,1)}, f32[8,256]{1,0:T(8,128)}, bf16[4,112,768]{2,1,0:T(8,128)(2,1)}, bf16[4,112,768]{2,1,0:T(8,128)(2,1)}) custom-call(s32[1]{0:T(128)} %bitcast.6.refs_0_, s32[4]{0:T(128)} %refs_1_.9, s32[2]{0:T(128)} %refs_2_.7, bf16[1536,768]{1,0:T(8,128)(2,1)} %get-tuple-element.111.refs_3_, ...), custom_call_target="tpu_custom_call" | custom-call | flops 46000001024 | tf_op jit(solution)/shard_map/attend_back/pallas_call | solution.py:579
  211.7 2.6 collective-permute-done.18
  215.9 1.6 collective-permute-start.21
  219.5 10.7 %input_grad.1 = (bf16[512,768]{1,0:T(8,128)(2,1)}, bf16[1024,768]{1,0:T(8,128)(2,1)}) custom-call(bf16[1536,1536]{1,0:T(8,128)(2,1)} %get-tuple-element.116.refs_0_, bf16[1536,768]{1,0:T(8,128)(2,1)} %get-tuple-element.127.refs_1_, bf16[1536,768]{1,0:T(8,128)(2,1)} %get-tuple-element.119.refs_2_, bf16[768,768]{1,0:T(8,128)(2,1)} %refs_3_.2, ...), custom_call_target="tpu_custom_call" | custom-call | flops 46000001024 | tf_op jit(solution)/shard_map/input_grad/pallas_call | solution.py:579
  230.2 7.7 %collective-permute-done.20 = bf16[96,2304]{1,0:T(8,128)(2,1)S(1)} collective-permute-done((bf16[96,2304]{1,0:T(8,128)(2,1)S(1)}, bf16[96,2304]{1,0:T(8,128)(2,1)S(1)}, u32[]{:S(2)}, u32[]{:S(2)}) %collective-permute-start.20) | collective-permute-done | bytes 442400 | tf_op jit(solution)/shard_map/ppermute | solution.py:688
  238.2 1.8 collective-permute-start.27
  240.4 2.3 collective-permute-start.25
  243.8 2.3 turn.5
  247.9 4.1 %collective-permute-done.24 = bf16[2,112,768]{2,1,0:T(8,128)(2,1)S(1)} collective-permute-done((bf16[2,112,768]{2,1,0:T(8,128)(2,1)S(1)}, bf16[2,112,768]{2,1,0:T(8,128)(2,1)S(1)}, u32[]{:S(2)}, u32[]{:S(2)}) %collective-permute-start.24) | collective-permute-done | bytes 344096 | tf_op jit(solution)/shard_map/ppermute | solution.py:688
  253.1 4.4 %collective-permute-done.31 = bf16[112,768]{1,0:T(8,128)(2,1)S(1)} collective-permute-done((bf16[112,768]{1,0:T(8,128)(2,1)S(1)}, bf16[112,768]{1,0:T(8,128)(2,1)S(1)}, u32[]{:S(2)}, u32[]{:S(2)}) %collective-permute-start.31) | collective-permute-done | bytes 172064 | tf_op jit(solution)/shard_map/ppermute | solution.py:688
  257.9 2.3 collective-permute-start.28
  263.5 2.5 collective-permute-done.32
  266.2 1.8 collective-permute-done.28
  268.0 5.5 %collective-permute-done.29 = bf16[24,2304]{1,0:T(8,128)(2,1)S(1)} collective-permute-done((bf16[24,2304]{1,0:T(8,128)(2,1)S(1)}, bf16[24,2304]{1,0:T(8,128)(2,1)S(1)}, u32[]{:S(2)}, u32[]{:S(2)}) %collective-permute-start.29) | collective-permute-done | bytes 110624 | tf_op jit(solution)/shard_map/ppermute | solution.py:708
  273.5 1.8 collective-permute-done.33
  (87 shorter events, 33.9 us)
Async XLA Ops:
  60.5 7.0 %collective-permute-start = (bf16[8,896]{1,0:T(8,128)(2,1)}, bf16[8,896]{1,0:T(8,128)(2,1)S(1)}, u32[]{:S(2)}, u32[]{:S(2)}) collective-permute-start(bf16[8,896]{1,0:T(8,128)(2,1)} %get-tuple-element.84.own_ref), channel_id=1, source_target_pairs={{0,3},{1,2},{2,1},{3,0},{4,7},{5,6},{6,5},{7,4},{8,11},{9,10},{10,... | collective-permute-start | bytes 43016 | tf_op jit(solution)/shard_map/ppermute | solution.py:762
  65.6 4.8 %collective-permute-start.1 = (bf16[8,896]{1,0:T(8,128)(2,1)}, bf16[8,896]{1,0:T(8,128)(2,1)S(1)}, u32[]{:S(2)}, u32[]{:S(2)}) collective-permute-start(bf16[8,896]{1,0:T(8,128)(2,1)} %get-tuple-element.84.own_ref), channel_id=1, source_target_pairs={{0,2},{1,3},{2,0},{3,1},{4,6},{5,7},{6,4},{7,5},{8,10},{9,11},{10,... | collective-permute-start | bytes 43016 | tf_op jit(solution)/shard_map/ppermute | solution.py:762
  65.6 4.8 %collective-permute-start.2 = (bf16[8,896]{1,0:T(8,128)(2,1)}, bf16[8,896]{1,0:T(8,128)(2,1)S(1)}, u32[]{:S(2)}, u32[]{:S(2)}) collective-permute-start(bf16[8,896]{1,0:T(8,128)(2,1)} %get-tuple-element.84.own_ref), channel_id=1, source_target_pairs={{0,1},{1,0},{2,3},{3,2},{4,5},{5,4},{6,7},{7,6},{8,9},{9,8},{10,11... | collective-permute-start | bytes 43016 | tf_op jit(solution)/shard_map/ppermute | solution.py:762
  71.2 4.4 %collective-permute-start.4 = (bf16[32,896]{1,0:T(8,128)(2,1)S(1)}, bf16[32,896]{1,0:T(8,128)(2,1)S(1)}, u32[]{:S(2)}, u32[]{:S(2)}) collective-permute-start(bf16[32,896]{1,0:T(8,128)(2,1)S(1)} %pad_maximum_fusion.5), channel_id=1, source_target_pairs={{0,16},{4,20},{8,24},{12,28},{16,0},{20,4},{24,8},{28,12},{1,17},{... | collective-permute-start | bytes 172040 | tf_op jit(solution)/shard_map/ppermute | solution.py:762
  72.8 5.1 %collective-permute-start.3 = (bf16[32,896]{1,0:T(8,128)(2,1)S(1)}, bf16[32,896]{1,0:T(8,128)(2,1)S(1)}, u32[]{:S(2)}, u32[]{:S(2)}) collective-permute-start(bf16[32,896]{1,0:T(8,128)(2,1)S(1)} %pad_maximum_fusion.5), channel_id=1, source_target_pairs={{0,24},{4,28},{8,16},{12,20},{16,8},{20,12},{24,0},{28,4},{1,25},{... | collective-permute-start | bytes 172040 | tf_op jit(solution)/shard_map/ppermute | solution.py:762
  102.2 4.7 %collective-permute-start.7 = (bf16[4,768,384]{2,1,0:T(8,128)(2,1)}, bf16[4,768,384]{2,1,0:T(8,128)(2,1)S(1)}, u32[]{:S(2)}, u32[]{:S(2)}) collective-permute-start(bf16[4,768,384]{2,1,0:T(8,128)(2,1)} %get-tuple-element.94), channel_id=1, source_target_pairs={{0,4},{4,0},{8,12},{12,8},{16,20},{20,16},{24,28},{28,24},{1,5},{5... | collective-permute-start | bytes 7077896 | tf_op jit(solution)/shard_map/ppermute | solution.py:688
  107.5 34.7 %collective-permute-start.8 = (bf16[768,384]{1,0:T(8,128)(2,1)S(1)}, bf16[768,384]{1,0:T(8,128)(2,1)S(1)}, u32[]{:S(2)}, u32[]{:S(2)}) collective-permute-start(bf16[768,384]{1,0:T(8,128)(2,1)S(1)} %get-tuple-element.155), channel_id=1, source_target_pairs={{0,8},{4,12},{8,0},{12,4},{16,24},{20,28},{24,16},{28,20},{1,9},{5... | collective-permute-start | bytes 1769480 | tf_op jit(solution)/shard_map/ppermute | solution.py:688
  108.5 33.6 %collective-permute-start.9 = (bf16[768,384]{1,0:T(8,128)(2,1)S(1)}, bf16[768,384]{1,0:T(8,128)(2,1)S(1)}, u32[]{:S(2)}, u32[]{:S(2)}) collective-permute-start(bf16[768,384]{1,0:T(8,128)(2,1)S(1)} %get-tuple-element.154), channel_id=1, source_target_pairs={{0,16},{4,20},{8,24},{12,28},{16,0},{20,4},{24,8},{28,12},{1,17},{... | collective-permute-start | bytes 1769480 | tf_op jit(solution)/shard_map/ppermute | solution.py:688
  109.7 32.5 %collective-permute-start.10 = (bf16[768,384]{1,0:T(8,128)(2,1)S(1)}, bf16[768,384]{1,0:T(8,128)(2,1)}, u32[]{:S(2)}, u32[]{:S(2)}) collective-permute-start(bf16[768,384]{1,0:T(8,128)(2,1)S(1)} %get-tuple-element.153), channel_id=1, source_target_pairs={{0,24},{4,28},{8,16},{12,20},{16,8},{20,12},{24,0},{28,4},{1,25},{... | collective-permute-start | bytes 1769480 | tf_op jit(solution)/shard_map/ppermute | solution.py:688
  143.6 14.6 %collective-permute-start.12 = (bf16[768,384]{1,0:T(8,128)(2,1)S(1)}, bf16[768,384]{1,0:T(8,128)(2,1)S(1)}, u32[]{:S(2)}, u32[]{:S(2)}) collective-permute-start(bf16[768,384]{1,0:T(8,128)(2,1)S(1)} %add_convert_fusion.4), channel_id=1, source_target_pairs={{0,1},{1,0},{2,3},{3,2},{4,5},{5,4},{6,7},{7,6},{8,9},{9,8},{10,11... | collective-permute-start | bytes 1769480 | tf_op jit(solution)/shard_map/ppermute | solution.py:713
  155.9 9.4 %collective-permute-start.11 = (bf16[4,96,3072]{2,1,0:T(8,128)(2,1)}, bf16[4,96,3072]{2,1,0:T(8,128)(2,1)S(1)}, u32[]{:S(2)}, u32[]{:S(2)}) collective-permute-start(bf16[4,96,3072]{2,1,0:T(8,128)(2,1)} %get-tuple-element.105), channel_id=1, source_target_pairs={{0,4},{4,0},{8,12},{12,8},{16,20},{20,16},{24,28},{28,24},{1,5},{5... | collective-permute-start | bytes 7077896 | tf_op jit(solution)/shard_map/ppermute | solution.py:688
  158.4 38.9 %collective-permute-start.13 = (bf16[768,384]{1,0:T(8,128)(2,1)S(1)}, bf16[768,384]{1,0:T(8,128)(2,1)S(1)}, u32[]{:S(2)}, u32[]{:S(2)}) collective-permute-start(bf16[768,384]{1,0:T(8,128)(2,1)S(1)} %add.298), channel_id=1, source_target_pairs={{0,2},{1,3},{2,0},{3,1},{4,6},{5,7},{6,4},{7,5},{8,10},{9,11},{10,... | collective-permute-start | bytes 1769480 | tf_op jit(solution)/shard_map/ppermute | solution.py:713
  166.3 31.9 %collective-permute-start.14 = (bf16[96,3072]{1,0:T(8,128)(2,1)S(1)}, bf16[96,3072]{1,0:T(8,128)(2,1)S(1)}, u32[]{:S(2)}, u32[]{:S(2)}) collective-permute-start(bf16[96,3072]{1,0:T(8,128)(2,1)S(1)} %get-tuple-element.151), channel_id=1, source_target_pairs={{0,8},{4,12},{8,0},{12,4},{16,24},{20,28},{24,16},{28,20},{1,9},{5... | collective-permute-start | bytes 1769480 | tf_op jit(solution)/shard_map/ppermute | solution.py:688
  167.3 30.9 %collective-permute-start.15 = (bf16[96,3072]{1,0:T(8,128)(2,1)S(1)}, bf16[96,3072]{1,0:T(8,128)(2,1)S(1)}, u32[]{:S(2)}, u32[]{:S(2)}) collective-permute-start(bf16[96,3072]{1,0:T(8,128)(2,1)S(1)} %get-tuple-element.150), channel_id=1, source_target_pairs={{0,16},{4,20},{8,24},{12,28},{16,0},{20,4},{24,8},{28,12},{1,17},{... | collective-permute-start | bytes 1769480 | tf_op jit(solution)/shard_map/ppermute | solution.py:688
  168.5 29.7 %collective-permute-start.16 = (bf16[96,3072]{1,0:T(8,128)(2,1)S(1)}, bf16[96,3072]{1,0:T(8,128)(2,1)S(1)}, u32[]{:S(2)}, u32[]{:S(2)}) collective-permute-start(bf16[96,3072]{1,0:T(8,128)(2,1)S(1)} %get-tuple-element.149), channel_id=1, source_target_pairs={{0,24},{4,28},{8,16},{12,20},{16,8},{20,12},{24,0},{28,4},{1,25},{... | collective-permute-start | bytes 1769480 | tf_op jit(solution)/shard_map/ppermute | solution.py:688
  197.2 18.2 %collective-permute-start.17 = (bf16[4,96,2304]{2,1,0:T(8,128)(2,1)}, bf16[4,96,2304]{2,1,0:T(8,128)(2,1)S(1)}, u32[]{:S(2)}, u32[]{:S(2)}) collective-permute-start(bf16[4,96,2304]{2,1,0:T(8,128)(2,1)} %get-tuple-element.122), channel_id=1, source_target_pairs={{0,4},{4,0},{8,12},{12,8},{16,20},{20,16},{24,28},{28,24},{1,5},{5... | collective-permute-start | bytes 5308424 | tf_op jit(solution)/shard_map/ppermute | solution.py:688
  198.5 15.8 %collective-permute-start.18 = (bf16[96,3072]{1,0:T(8,128)(2,1)S(1)}, bf16[96,3072]{1,0:T(8,128)(2,1)S(1)}, u32[]{:S(2)}, u32[]{:S(2)}) collective-permute-start(bf16[96,3072]{1,0:T(8,128)(2,1)S(1)} %add_all.1), channel_id=1, source_target_pairs={{0,1},{1,0},{2,3},{3,2},{4,5},{5,4},{6,7},{7,6},{8,9},{9,8},{10,11... | collective-permute-start | bytes 1769480 | tf_op jit(solution)/shard_map/ppermute | solution.py:713
  211.4 31.3 %collective-permute-start.22 = (bf16[4,112,768]{2,1,0:T(8,128)(2,1)}, bf16[4,112,768]{2,1,0:T(8,128)(2,1)S(1)}, u32[]{:S(2)}, u32[]{:S(2)}) collective-permute-start(bf16[4,112,768]{2,1,0:T(8,128)(2,1)} %get-tuple-element.128), channel_id=1, source_target_pairs={{0,4},{4,0},{8,12},{12,8},{16,20},{20,16},{24,28},{28,24},{1,5},{5... | collective-permute-start | bytes 2064392 | tf_op jit(solution)/shard_map/ppermute | solution.py:688
  214.5 32.3 %collective-permute-start.23 = (bf16[96,3072]{1,0:T(8,128)(2,1)S(1)}, bf16[96,3072]{1,0:T(8,128)(2,1)S(1)}, u32[]{:S(2)}, u32[]{:S(2)}) collective-permute-start(bf16[96,3072]{1,0:T(8,128)(2,1)S(1)} %add.306), channel_id=1, source_target_pairs={{0,2},{1,3},{2,0},{3,1},{4,6},{5,7},{6,4},{7,5},{8,10},{9,11},{10,... | collective-permute-start | bytes 1769480 | tf_op jit(solution)/shard_map/ppermute | solution.py:713
  215.9 14.3 %collective-permute-start.21 = (bf16[96,2304]{1,0:T(8,128)(2,1)S(1)}, bf16[96,2304]{1,0:T(8,128)(2,1)S(1)}, u32[]{:S(2)}, u32[]{:S(2)}) collective-permute-start(bf16[96,2304]{1,0:T(8,128)(2,1)S(1)} %get-tuple-element.157), channel_id=1, source_target_pairs={{0,24},{4,28},{8,16},{12,20},{16,8},{20,12},{24,0},{28,4},{1,25},{... | collective-permute-start | bytes 1327112 | tf_op jit(solution)/shard_map/ppermute | solution.py:688
  217.6 20.3 %collective-permute-start.20 = (bf16[96,2304]{1,0:T(8,128)(2,1)S(1)}, bf16[96,2304]{1,0:T(8,128)(2,1)S(1)}, u32[]{:S(2)}, u32[]{:S(2)}) collective-permute-start(bf16[96,2304]{1,0:T(8,128)(2,1)S(1)} %get-tuple-element.158), channel_id=1, source_target_pairs={{0,16},{4,20},{8,24},{12,28},{16,0},{20,4},{24,8},{28,12},{1,17},{... | collective-permute-start | bytes 1327112 | tf_op jit(solution)/shard_map/ppermute | solution.py:688
  218.4 19.6 %collective-permute-start.19 = (bf16[96,2304]{1,0:T(8,128)(2,1)S(1)}, bf16[96,2304]{1,0:T(8,128)(2,1)S(1)}, u32[]{:S(2)}, u32[]{:S(2)}) collective-permute-start(bf16[96,2304]{1,0:T(8,128)(2,1)S(1)} %get-tuple-element.159), channel_id=1, source_target_pairs={{0,8},{4,12},{8,0},{12,4},{16,24},{20,28},{24,16},{28,20},{1,9},{5... | collective-permute-start | bytes 1327112 | tf_op jit(solution)/shard_map/ppermute | solution.py:688
  238.2 14.8 %collective-permute-start.27 = (bf16[24,2304]{1,0:T(8,128)(2,1)S(1)}, bf16[24,2304]{1,0:T(8,128)(2,1)S(1)}, u32[]{:S(2)}, u32[]{:S(2)}) collective-permute-start(bf16[24,2304]{1,0:T(8,128)(2,1)S(1)} %get-tuple-element.161), channel_id=1, source_target_pairs={{0,3},{1,2},{2,1},{3,0},{4,7},{5,6},{6,5},{7,4},{8,11},{9,10},{10,... | collective-permute-start | bytes 331784 | tf_op jit(solution)/shard_map/ppermute | solution.py:708
  240.0 13.0 %collective-permute-start.26 = (bf16[24,2304]{1,0:T(8,128)(2,1)S(1)}, bf16[24,2304]{1,0:T(8,128)(2,1)S(1)}, u32[]{:S(2)}, u32[]{:S(2)}) collective-permute-start(bf16[24,2304]{1,0:T(8,128)(2,1)S(1)} %get-tuple-element.162), channel_id=1, source_target_pairs={{0,2},{1,3},{2,0},{3,1},{4,6},{5,7},{6,4},{7,5},{8,10},{9,11},{10,... | collective-permute-start | bytes 331784 | tf_op jit(solution)/shard_map/ppermute | solution.py:708
  240.4 12.7 %collective-permute-start.25 = (bf16[24,2304]{1,0:T(8,128)(2,1)S(1)}, bf16[24,2304]{1,0:T(8,128)(2,1)S(1)}, u32[]{:S(2)}, u32[]{:S(2)}) collective-permute-start(bf16[24,2304]{1,0:T(8,128)(2,1)S(1)} %get-tuple-element.163), channel_id=1, source_target_pairs={{0,1},{1,0},{2,3},{3,2},{4,5},{5,4},{6,7},{7,6},{8,9},{9,8},{10,11... | collective-permute-start | bytes 331784 | tf_op jit(solution)/shard_map/ppermute | solution.py:708
  242.9 9.1 %collective-permute-start.24 = (bf16[2,112,768]{2,1,0:T(8,128)(2,1)S(1)}, bf16[2,112,768]{2,1,0:T(8,128)(2,1)S(1)}, u32[]{:S(2)}, u32[]{:S(2)}) collective-permute-start(bf16[2,112,768]{2,1,0:T(8,128)(2,1)S(1)} %get-tuple-element.165), channel_id=1, source_target_pairs={{0,8},{4,12},{8,0},{12,4},{16,24},{20,28},{24,16},{28,20},{1,9},{5... | collective-permute-start | bytes 1032200 | tf_op jit(solution)/shard_map/ppermute | solution.py:688
  252.1 5.5 %collective-permute-start.31 = (bf16[112,768]{1,0:T(8,128)(2,1)S(1)}, bf16[112,768]{1,0:T(8,128)(2,1)S(1)}, u32[]{:S(2)}, u32[]{:S(2)}) collective-permute-start(bf16[112,768]{1,0:T(8,128)(2,1)S(1)} %get-tuple-element.166), channel_id=1, source_target_pairs={{0,16},{4,20},{8,24},{12,28},{16,0},{20,4},{24,8},{28,12},{1,17},{... | collective-permute-start | bytes 516104 | tf_op jit(solution)/shard_map/ppermute | solution.py:688
  257.6 8.4 %collective-permute-start.32 = (bf16[112,768]{1,0:T(8,128)(2,1)S(1)}, bf16[112,768]{1,0:T(8,128)(2,1)S(1)}, u32[]{:S(2)}, u32[]{:S(2)}) collective-permute-start(bf16[112,768]{1,0:T(8,128)(2,1)S(1)} %add_convert_fusion.15), channel_id=1, source_target_pairs={{0,1},{1,0},{2,3},{3,2},{4,5},{5,4},{6,7},{7,6},{8,9},{9,8},{10,11... | collective-permute-start | bytes 516104 | tf_op jit(solution)/shard_map/ppermute | solution.py:713
  257.9 10.1 %collective-permute-start.28 = (bf16[24,2304]{1,0:T(8,128)(2,1)S(1)}, bf16[24,2304]{1,0:T(8,128)(2,1)S(1)}, u32[]{:S(2)}, u32[]{:S(2)}) collective-permute-start(bf16[24,2304]{1,0:T(8,128)(2,1)S(1)} %add_convert_fusion.18), channel_id=1, source_target_pairs={{0,3},{1,2},{2,1},{3,0},{4,7},{5,6},{6,5},{7,4},{8,11},{9,10},{10,... | collective-permute-start | bytes 331784 | tf_op jit(solution)/shard_map/ppermute | solution.py:708
  260.2 13.2 %collective-permute-start.29 = (bf16[24,2304]{1,0:T(8,128)(2,1)S(1)}, bf16[24,2304]{1,0:T(8,128)(2,1)S(1)}, u32[]{:S(2)}, u32[]{:S(2)}) collective-permute-start(bf16[24,2304]{1,0:T(8,128)(2,1)S(1)} %add_convert_fusion.18), channel_id=1, source_target_pairs={{0,2},{1,3},{2,0},{3,1},{4,6},{5,7},{6,4},{7,5},{8,10},{9,11},{10,... | collective-permute-start | bytes 331784 | tf_op jit(solution)/shard_map/ppermute | solution.py:708
  261.1 12.3 %collective-permute-start.30 = (bf16[24,2304]{1,0:T(8,128)(2,1)S(1)}, bf16[24,2304]{1,0:T(8,128)(2,1)S(1)}, u32[]{:S(2)}, u32[]{:S(2)}) collective-permute-start(bf16[24,2304]{1,0:T(8,128)(2,1)S(1)} %add_convert_fusion.18), channel_id=1, source_target_pairs={{0,1},{1,0},{2,3},{3,2},{4,5},{5,4},{6,7},{7,6},{8,9},{9,8},{10,11... | collective-permute-start | bytes 331784 | tf_op jit(solution)/shard_map/ppermute | solution.py:708
  266.1 9.3 %collective-permute-start.33 = (bf16[112,768]{1,0:T(8,128)(2,1)S(1)}, bf16[112,768]{1,0:T(8,128)(2,1)S(1)}, u32[]{:S(2)}, u32[]{:S(2)}) collective-permute-start(bf16[112,768]{1,0:T(8,128)(2,1)S(1)} %add.342), channel_id=1, source_target_pairs={{0,2},{1,3},{2,0},{3,1},{4,6},{5,7},{6,4},{7,5},{8,10},{9,11},{10,... | collective-permute-start | bytes 516104 | tf_op jit(solution)/shard_map/ppermute | solution.py:713
  (6 other events, 31.9 us)

commit v9 on v8

--- a/solution.py
+++ b/solution.py
@@ -994,17 +994,17 @@
         name="input_grad",
         us=40,
     )
-    mixed_flow.turn(passage_grad)
-    last_flow.turn(mixed_flow.kept)
+    last_flow.turn(passage_grad)
+    mixed_flow.turn(last_flow.kept)
     outs = [(fixed((cut_inner, width)), shape(cut_inner, width, kind=F32))]
     (turned,) = call(
-        turn_kernel, (outer.kept,), [const_spec((width, cut_inner))], outs, (1,), 56, [last_flow.kept], name="turn", us=40
-    )
-    up_flow.turn(turned)
+        turn_kernel, (outer.kept,), [const_spec((width, cut_inner))], outs, (1,), 56, [mixed_flow.kept], name="turn", us=40
+    )
+    last_flow.turn(turned)
+    up_flow.turn(last_flow.kept)
     last_flow.turn(up_flow.kept)
     mixed_flow.turn(last_flow.kept)
     last_flow.turn(mixed_flow.kept)
-    last_flow.turn()
     mixed_flow.turn(last_flow.kept)
     flows = [outer, up_flow, mixed_flow, last_flow]
     while not all(flow.done for flow in flows):

time: 284 us -> 280 us (0.986)
  waiting for transfers between devices: 43 us -> 39.9 us
    ppermute x15, waiting for transfers between devices: 16.6 us -> 12.1 us  [step(): lax.ppermute(sent, 'row', [(i, i ^ mask) for i in range(size)])]
  transfers between devices with their start and end apart: 34 -> 34, of which waited for: 18 -> 16; matrix products, arithmetic and copies ran while one was open for 2% -> 2% of each run, Pallas kernels for 38% -> 39%
where the time goes in v9:
time: 280 us; the launch traced here: 274 us
  Pallas kernels  187 us (67%)
  waiting for transfers between devices  39.9 us (14%)
  starting transfers between devices  34.6 us (12%)
  other arithmetic  9.18 us (3%)
    pallas_call x13, Pallas kernels, call(): pl.pallas_call(kernel, grid=grid, in_specs=list(in_specs) + [pl.BlockSpec...  184 us
    ppermute x15, starting transfers between devices, step(): lax.ppermute(sent, 'row', [(i, i ^ mask) for i in range(size)])  12.7 us
    ppermute x6, waiting for transfers between devices, step(): self.got = [lax.ppermute(self.kept, 'col', self.line[0][1])]  12.2 us
    ppermute x15, waiting for transfers between devices, step(): lax.ppermute(sent, 'row', [(i, i ^ mask) for i in range(size)])  12.1 us
    ppermute x7, starting transfers between devices, gather_all(): lax.ppermute(piece, name, [(i, i ^ mask) for i in range(size)])  9.38 us
    ppermute x7, waiting for transfers between devices, gather_all(): lax.ppermute(piece, name, [(i, i ^ mask) for i in range(size)])  9.27 us
    ppermute x6, starting transfers between devices, step(): lax.ppermute(sent, 'col', [(i, i ^ mask) for i in range(size)])  8.91 us
    ppermute x6, waiting for transfers between devices, step(): lax.ppermute(sent, 'col', [(i, i ^ mask) for i in range(size)])  6.3 us
  transfers between devices with their start and end apart: 34, of which 16 were waited for; matrix products, arithmetic and copies ran while one was open for 2% of the time, Pallas kernels for 39%

profile of v9, /device:TPU:0, one launch (start us, length us, event | category | flops | bytes accessed | tf_op | source)
XLA Modules:
  0.0 274.4 jit_solution(7285482002374694386)
XLA Ops:
  0.7 20.8 %attend.1 = (bf16[1536,768]{1,0:T(8,128)(2,1)}, bf16[1536,768]{1,0:T(8,128)(2,1)}, bf16[1536,768]{1,0:T(8,128)(2,1)}, bf16[768,1536]{1,0:T(8,128)(2,1)}, f32[3,6,8,512]{3,2,1,0:T(8,128)}) custom-call(s32[4]{0:T(128)} %refs_1_.9, s32[2]{0:T(128)} %refs_2_.7, bf16[512,768]{1,0:T(8,128)(2,1)} %bitcast.100, bf16[1024,768]{1,0:T(8,128)(2,1)} %bitcast.97, ...), custom_call_target="tpu_custom_call" | custom-call | flops 13799999488 | tf_op jit(solution)/shard_map/attend/pallas_call | solution.py:579
  21.5 39.0 %dense.1 = (bf16[1536,768]{1,0:T(8,128)(2,1)}, bf16[1536,768]{1,0:T(8,128)(2,1)}, bf16[1536,3072]{1,0:T(8,128)(2,1)}, bf16[1536,3072]{1,0:T(8,128)(2,1)}, bf16[1...) custom-call(s32[4]{0:T(128)} %refs_1_.9, ...), custom_call_target="tpu_custom_call" | custom-call | flops 13799999488 | tf_op jit(solution)/shard_map/dense/pallas_call | solution.py:579
  60.5 5.1 %collective-permute-start = (bf16[8,896]{1,0:T(8,128)(2,1)}, bf16[8,896]{1,0:T(8,128)(2,1)S(1)}, u32[]{:S(2)}, u32[]{:S(2)}) collective-permute-start(bf16[8,896]{1,0:T(8,128)(2,1)} %get-tuple-element.85.own_ref), channel_id=1, source_target_pairs={{0,3},{1,2},{2,1},{3,0},{4,7},{5,6},{6,5},{7,4},{8,11},{9,10},{10,... | collective-permute-start | bytes 43016 | tf_op jit(solution)/shard_map/ppermute | solution.py:762
  67.5 2.9 %collective-permute-done.1 = bf16[8,896]{1,0:T(8,128)(2,1)S(1)} collective-permute-done((bf16[8,896]{1,0:T(8,128)(2,1)}, bf16[8,896]{1,0:T(8,128)(2,1)S(1)}, u32[]{:S(2)}, u32[]{:S(2)}) %collective-permute-start.1) | collective-permute-done | bytes 14368 | tf_op jit(solution)/shard_map/ppermute | solution.py:762
  71.2 1.6 collective-permute-start.4
  72.8 1.4 collective-permute-start.3
  75.6 2.2 collective-permute-done.3
  78.6 1.4 collective-permute-done.6
  81.0 2.9 %loss.1 = (f32[8,128]{1,0:T(8,128)}, f32[8,768]{1,0:T(8,128)}) custom-call(s32[1]{0:T(128)} %bitcast.me_ref, s32[4]{0:T(128)} %refs_1_.9, s32[2]{0:T(128)} %refs_2_.7, bf16[8,896]{1,0:T(8,128)(2,1)} %get-tuple-element.85.own_ref, bf16[256,896]{1,0:T(8,128)(2,1)} %pad_maximum_fusion.all_ref, f32[8,768]{1,0:T(8,128)} %get-tuple-element.86.pool_ref), custom_call_target="tpu_custom_call" | custom-call | tf_op jit(solution)/shard_map/loss/pallas_call | solution.py:868
  83.9 18.3 %outer_grad.1 = (bf16[1536,768]{1,0:T(8,128)(2,1)}, f32[8,768]{1,0:T(8,128)}, bf16[4,768,384]{2,1,0:T(8,128)(2,1)}, bf16[4,768,384]{2,1,0:T(8,128)(2,1)}) custom-call(s32[1]{0:T(128)} %bitcast.6.refs_0_, s32[4]{0:T(128)} %refs_1_.9, s32[2]{0:T(128)} %refs_2_.7, f32[8,768]{1,0:T(8,128)} %get-tuple-element.90.refs_3_, ...), custom_call_target="tpu_custom_call" | custom-call | flops 13799999488 | tf_op jit(solution)/shard_map/outer_grad/pallas_call | solution.py:579
  102.3 4.4 %turn.3.refs_1_ = bf16[768,1536]{1,0:T(8,128)(2,1)} custom-call(bf16[1536,768]{1,0:T(8,128)(2,1)} %get-tuple-element.96.refs_0_), custom_call_target="tpu_custom_call" | custom-call | flops 46000001024 | tf_op jit(solution)/shard_map/turn/pallas_call | solution.py:579
  111.1 31.1 %dense_back.1 = (bf16[1536,3072]{1,0:T(8,128)(2,1)}, bf16[1536,768]{1,0:T(8,128)(2,1)}, bf16[1536,768]{1,0:T(8,128)(2,1)}, f32[8,768]{1,0:T(8,128)}, f32[8,3072]{1,0:T(8,128)}) custom-call(bf16[1536,768]{1,0:T(8,128)(2,1)} %get-tuple-element.98.refs_0_, bf16[1536,3072]{1,0:T(8,128)(2,1)} %get-tuple-element.99.refs_1_, ...), custom_call_target="tpu_custom_call" | custom-call | flops 13799999488 | tf_op jit(solution)/shard_map/dense_back/pallas_call | solution.py:579
  143.6 12.2 %weight_grad.2 = (bf16[4,96,3072]{2,1,0:T(8,128)(2,1)}, bf16[4,96,3072]{2,1,0:T(8,128)(2,1)}) custom-call(s32[1]{0:T(128)} %bitcast.6.refs_0_, bf16[768,1536]{1,0:T(8,128)(2,1)} %turn.3.refs_1_, bf16[1536,3072]{1,0:T(8,128)(2,1)} %get-tuple-element.105.refs_2_), custom_call_target="tpu_custom_call" | custom-call | flops 13799999488 | tf_op jit(solution)/shard_map/weight_grad/pallas_call | solution.py:579
  155.9 2.3 collective-permute-done.12
  158.4 2.1 collective-permute-start.13
  160.4 4.9 %turn.4.refs_9_ = bf16[768,1536]{1,0:T(8,128)(2,1)} custom-call(bf16[512,768]{1,0:T(8,128)(2,1)} %bitcast.102, bf16[1024,768]{1,0:T(8,128)(2,1)} %bitcast.99), custom_call_target="tpu_custom_call" | custom-call | flops 46000001024 | tf_op jit(solution)/shard_map/turn/pallas_call | solution.py:579
  169.8 21.8 %attend_back.2 = (bf16[1536,1536]{1,0:T(8,128)(2,1)}, f32[8,512]{1,0:T(8,128)}, bf16[4,96,2304]{2,1,0:T(8,128)(2,1)}, bf16[4,96,2304]{2,1,0:T(8,128)(2,1)}) custom-call(s32[1]{0:T(128)} %bitcast.6.refs_0_, s32[4]{0:T(128)} %refs_1_.9, s32[2]{0:T(128)} %refs_2_.7, bf16[1536,768]{1,0:T(8,128)(2,1)} %get-tuple-element.112.refs_3_, ...), custom_call_target="tpu_custom_call" | custom-call | flops 13799999488 | tf_op jit(solution)/shard_map/attend_back/pallas_call | solution.py:579
  191.6 5.7 %weight_grad.3 = (bf16[4,96,2304]{2,1,0:T(8,128)(2,1)}, bf16[4,96,2304]{2,1,0:T(8,128)(2,1)}) custom-call(s32[1]{0:T(128)} %bitcast.6.refs_0_, bf16[768,1536]{1,0:T(8,128)(2,1)} %get-tuple-element.84.refs_5_.refs_6_.refs_1_, bf16[1536,768]{1,0:T(8,128)(2,1)} %get-tuple-element.120.refs_2_, ...), custom_call_target="tpu_custom_call", output_to_operand_aliasing={{0}: (3, {}), {1}: (4, {})} | custom-call | tf_op jit(solution)/shard_map/weight_grad/pallas_call | solution.py:579
  198.9 12.5 %attend_back.3 = (bf16[1536,768]{1,0:T(8,128)(2,1)}, f32[8,256]{1,0:T(8,128)}, bf16[4,112,768]{2,1,0:T(8,128)(2,1)}, bf16[4,112,768]{2,1,0:T(8,128)(2,1)}) custom-call(s32[1]{0:T(128)} %bitcast.6.refs_0_, s32[4]{0:T(128)} %refs_1_.9, s32[2]{0:T(128)} %refs_2_.7, bf16[1536,768]{1,0:T(8,128)(2,1)} %get-tuple-element.112.refs_3_, ...), custom_call_target="tpu_custom_call" | custom-call | flops 46000001024 | tf_op jit(solution)/shard_map/attend_back/pallas_call | solution.py:579
  211.7 2.6 collective-permute-done.18
  215.9 1.6 collective-permute-start.22
  219.5 10.8 %input_grad.1 = (bf16[512,768]{1,0:T(8,128)(2,1)}, bf16[1024,768]{1,0:T(8,128)(2,1)}) custom-call(bf16[1536,1536]{1,0:T(8,128)(2,1)} %get-tuple-element.117.refs_0_, bf16[1536,768]{1,0:T(8,128)(2,1)} %get-tuple-element.128.refs_1_, bf16[1536,768]{1,0:T(8,128)(2,1)} %get-tuple-element.120.refs_2_, bf16[768,768]{1,0:T(8,128)(2,1)} %refs_3_.2, ...), custom_call_target="tpu_custom_call" | custom-call | flops 46000001024 | tf_op jit(solution)/shard_map/input_grad/pallas_call | solution.py:579
  231.5 6.4 %collective-permute-done.21 = bf16[96,2304]{1,0:T(8,128)(2,1)S(1)} collective-permute-done((bf16[96,2304]{1,0:T(8,128)(2,1)S(1)}, bf16[96,2304]{1,0:T(8,128)(2,1)S(1)}, u32[]{:S(2)}, u32[]{:S(2)}) %collective-permute-start.21) | collective-permute-done | bytes 442400 | tf_op jit(solution)/shard_map/ppermute | solution.py:688
  237.9 1.7 collective-permute-done.20
  239.8 1.8 collective-permute-start.28
  241.9 2.3 collective-permute-start.26
  244.2 2.3 turn.5
  248.3 3.8 %collective-permute-done.25 = bf16[112,768]{1,0:T(8,128)(2,1)S(1)} collective-permute-done((bf16[112,768]{1,0:T(8,128)(2,1)S(1)}, bf16[112,768]{1,0:T(8,128)(2,1)S(1)}, u32[]{:S(2)}, u32[]{:S(2)}) %collective-permute-start.25) | collective-permute-done | bytes 172064 | tf_op jit(solution)/shard_map/ppermute | solution.py:688
  252.4 2.5 collective-permute-start.29
  258.0 4.9 %collective-permute-done.32 = bf16[112,768]{1,0:T(8,128)(2,1)S(1)} collective-permute-done((bf16[112,768]{1,0:T(8,128)(2,1)S(1)}, bf16[112,768]{1,0:T(8,128)(2,1)S(1)}, u32[]{:S(2)}, u32[]{:S(2)}) %collective-permute-start.32) | collective-permute-done | bytes 172064 | tf_op jit(solution)/shard_map/ppermute | solution.py:713
  263.0 6.2 %collective-permute-done.30 = bf16[24,2304]{1,0:T(8,128)(2,1)S(1)} collective-permute-done((bf16[24,2304]{1,0:T(8,128)(2,1)S(1)}, bf16[24,2304]{1,0:T(8,128)(2,1)S(1)}, u32[]{:S(2)}, u32[]{:S(2)}) %collective-permute-start.30) | collective-permute-done | bytes 110624 | tf_op jit(solution)/shard_map/ppermute | solution.py:708
  269.3 2.4 collective-permute-done.33
  (87 shorter events, 31.0 us)
Async XLA Ops:
  60.5 7.0 %collective-permute-start = (bf16[8,896]{1,0:T(8,128)(2,1)}, bf16[8,896]{1,0:T(8,128)(2,1)S(1)}, u32[]{:S(2)}, u32[]{:S(2)}) collective-permute-start(bf16[8,896]{1,0:T(8,128)(2,1)} %get-tuple-element.85.own_ref), channel_id=1, source_target_pairs={{0,3},{1,2},{2,1},{3,0},{4,7},{5,6},{6,5},{7,4},{8,11},{9,10},{10,... | collective-permute-start | bytes 43016 | tf_op jit(solution)/shard_map/ppermute | solution.py:762
  65.6 4.8 %collective-permute-start.1 = (bf16[8,896]{1,0:T(8,128)(2,1)}, bf16[8,896]{1,0:T(8,128)(2,1)S(1)}, u32[]{:S(2)}, u32[]{:S(2)}) collective-permute-start(bf16[8,896]{1,0:T(8,128)(2,1)} %get-tuple-element.85.own_ref), channel_id=1, source_target_pairs={{0,2},{1,3},{2,0},{3,1},{4,6},{5,7},{6,4},{7,5},{8,10},{9,11},{10,... | collective-permute-start | bytes 43016 | tf_op jit(solution)/shard_map/ppermute | solution.py:762
  65.6 4.8 %collective-permute-start.2 = (bf16[8,896]{1,0:T(8,128)(2,1)}, bf16[8,896]{1,0:T(8,128)(2,1)S(1)}, u32[]{:S(2)}, u32[]{:S(2)}) collective-permute-start(bf16[8,896]{1,0:T(8,128)(2,1)} %get-tuple-element.85.own_ref), channel_id=1, source_target_pairs={{0,1},{1,0},{2,3},{3,2},{4,5},{5,4},{6,7},{7,6},{8,9},{9,8},{10,11... | collective-permute-start | bytes 43016 | tf_op jit(solution)/shard_map/ppermute | solution.py:762
  71.2 4.4 %collective-permute-start.4 = (bf16[32,896]{1,0:T(8,128)(2,1)S(1)}, bf16[32,896]{1,0:T(8,128)(2,1)S(1)}, u32[]{:S(2)}, u32[]{:S(2)}) collective-permute-start(bf16[32,896]{1,0:T(8,128)(2,1)S(1)} %pad_maximum_fusion.5), channel_id=1, source_target_pairs={{0,16},{4,20},{8,24},{12,28},{16,0},{20,4},{24,8},{28,12},{1,17},{... | collective-permute-start | bytes 172040 | tf_op jit(solution)/shard_map/ppermute | solution.py:762
  72.8 5.1 %collective-permute-start.3 = (bf16[32,896]{1,0:T(8,128)(2,1)S(1)}, bf16[32,896]{1,0:T(8,128)(2,1)S(1)}, u32[]{:S(2)}, u32[]{:S(2)}) collective-permute-start(bf16[32,896]{1,0:T(8,128)(2,1)S(1)} %pad_maximum_fusion.5), channel_id=1, source_target_pairs={{0,24},{4,28},{8,16},{12,20},{16,8},{20,12},{24,0},{28,4},{1,25},{... | collective-permute-start | bytes 172040 | tf_op jit(solution)/shard_map/ppermute | solution.py:762
  102.2 4.7 %collective-permute-start.7 = (bf16[4,768,384]{2,1,0:T(8,128)(2,1)}, bf16[4,768,384]{2,1,0:T(8,128)(2,1)S(1)}, u32[]{:S(2)}, u32[]{:S(2)}) collective-permute-start(bf16[4,768,384]{2,1,0:T(8,128)(2,1)} %get-tuple-element.95), channel_id=1, source_target_pairs={{0,4},{4,0},{8,12},{12,8},{16,20},{20,16},{24,28},{28,24},{1,5},{5... | collective-permute-start | bytes 7077896 | tf_op jit(solution)/shard_map/ppermute | solution.py:688
  107.5 34.7 %collective-permute-start.8 = (bf16[768,384]{1,0:T(8,128)(2,1)S(1)}, bf16[768,384]{1,0:T(8,128)(2,1)S(1)}, u32[]{:S(2)}, u32[]{:S(2)}) collective-permute-start(bf16[768,384]{1,0:T(8,128)(2,1)S(1)} %get-tuple-element.157), channel_id=1, source_target_pairs={{0,8},{4,12},{8,0},{12,4},{16,24},{20,28},{24,16},{28,20},{1,9},{5... | collective-permute-start | bytes 1769480 | tf_op jit(solution)/shard_map/ppermute | solution.py:688
  108.5 33.6 %collective-permute-start.9 = (bf16[768,384]{1,0:T(8,128)(2,1)S(1)}, bf16[768,384]{1,0:T(8,128)(2,1)S(1)}, u32[]{:S(2)}, u32[]{:S(2)}) collective-permute-start(bf16[768,384]{1,0:T(8,128)(2,1)S(1)} %get-tuple-element.156), channel_id=1, source_target_pairs={{0,16},{4,20},{8,24},{12,28},{16,0},{20,4},{24,8},{28,12},{1,17},{... | collective-permute-start | bytes 1769480 | tf_op jit(solution)/shard_map/ppermute | solution.py:688
  109.7 32.5 %collective-permute-start.10 = (bf16[768,384]{1,0:T(8,128)(2,1)S(1)}, bf16[768,384]{1,0:T(8,128)(2,1)}, u32[]{:S(2)}, u32[]{:S(2)}) collective-permute-start(bf16[768,384]{1,0:T(8,128)(2,1)S(1)} %get-tuple-element.155), channel_id=1, source_target_pairs={{0,24},{4,28},{8,16},{12,20},{16,8},{20,12},{24,0},{28,4},{1,25},{... | collective-permute-start | bytes 1769480 | tf_op jit(solution)/shard_map/ppermute | solution.py:688
  143.6 14.6 %collective-permute-start.12 = (bf16[768,384]{1,0:T(8,128)(2,1)S(1)}, bf16[768,384]{1,0:T(8,128)(2,1)S(1)}, u32[]{:S(2)}, u32[]{:S(2)}) collective-permute-start(bf16[768,384]{1,0:T(8,128)(2,1)S(1)} %add_convert_fusion.4), channel_id=1, source_target_pairs={{0,1},{1,0},{2,3},{3,2},{4,5},{5,4},{6,7},{7,6},{8,9},{9,8},{10,11... | collective-permute-start | bytes 1769480 | tf_op jit(solution)/shard_map/ppermute | solution.py:713
  155.9 9.4 %collective-permute-start.11 = (bf16[4,96,3072]{2,1,0:T(8,128)(2,1)}, bf16[4,96,3072]{2,1,0:T(8,128)(2,1)S(1)}, u32[]{:S(2)}, u32[]{:S(2)}) collective-permute-start(bf16[4,96,3072]{2,1,0:T(8,128)(2,1)} %get-tuple-element.106), channel_id=1, source_target_pairs={{0,4},{4,0},{8,12},{12,8},{16,20},{20,16},{24,28},{28,24},{1,5},{5... | collective-permute-start | bytes 7077896 | tf_op jit(solution)/shard_map/ppermute | solution.py:688
  158.4 38.9 %collective-permute-start.13 = (bf16[768,384]{1,0:T(8,128)(2,1)S(1)}, bf16[768,384]{1,0:T(8,128)(2,1)S(1)}, u32[]{:S(2)}, u32[]{:S(2)}) collective-permute-start(bf16[768,384]{1,0:T(8,128)(2,1)S(1)} %add.298), channel_id=1, source_target_pairs={{0,2},{1,3},{2,0},{3,1},{4,6},{5,7},{6,4},{7,5},{8,10},{9,11},{10,... | collective-permute-start | bytes 1769480 | tf_op jit(solution)/shard_map/ppermute | solution.py:713
  166.3 31.9 %collective-permute-start.14 = (bf16[96,3072]{1,0:T(8,128)(2,1)S(1)}, bf16[96,3072]{1,0:T(8,128)(2,1)S(1)}, u32[]{:S(2)}, u32[]{:S(2)}) collective-permute-start(bf16[96,3072]{1,0:T(8,128)(2,1)S(1)} %get-tuple-element.153), channel_id=1, source_target_pairs={{0,8},{4,12},{8,0},{12,4},{16,24},{20,28},{24,16},{28,20},{1,9},{5... | collective-permute-start | bytes 1769480 | tf_op jit(solution)/shard_map/ppermute | solution.py:688
  167.3 30.9 %collective-permute-start.15 = (bf16[96,3072]{1,0:T(8,128)(2,1)S(1)}, bf16[96,3072]{1,0:T(8,128)(2,1)S(1)}, u32[]{:S(2)}, u32[]{:S(2)}) collective-permute-start(bf16[96,3072]{1,0:T(8,128)(2,1)S(1)} %get-tuple-element.152), channel_id=1, source_target_pairs={{0,16},{4,20},{8,24},{12,28},{16,0},{20,4},{24,8},{28,12},{1,17},{... | collective-permute-start | bytes 1769480 | tf_op jit(solution)/shard_map/ppermute | solution.py:688
  168.5 29.7 %collective-permute-start.16 = (bf16[96,3072]{1,0:T(8,128)(2,1)S(1)}, bf16[96,3072]{1,0:T(8,128)(2,1)S(1)}, u32[]{:S(2)}, u32[]{:S(2)}) collective-permute-start(bf16[96,3072]{1,0:T(8,128)(2,1)S(1)} %get-tuple-element.151), channel_id=1, source_target_pairs={{0,24},{4,28},{8,16},{12,20},{16,8},{20,12},{24,0},{28,4},{1,25},{... | collective-permute-start | bytes 1769480 | tf_op jit(solution)/shard_map/ppermute | solution.py:688
  197.2 18.2 %collective-permute-start.17 = (bf16[4,96,2304]{2,1,0:T(8,128)(2,1)}, bf16[4,96,2304]{2,1,0:T(8,128)(2,1)S(1)}, u32[]{:S(2)}, u32[]{:S(2)}) collective-permute-start(bf16[4,96,2304]{2,1,0:T(8,128)(2,1)} %get-tuple-element.123), channel_id=1, source_target_pairs={{0,4},{4,0},{8,12},{12,8},{16,20},{20,16},{24,28},{28,24},{1,5},{5... | collective-permute-start | bytes 5308424 | tf_op jit(solution)/shard_map/ppermute | solution.py:688
  198.5 15.8 %collective-permute-start.18 = (bf16[96,3072]{1,0:T(8,128)(2,1)S(1)}, bf16[96,3072]{1,0:T(8,128)(2,1)S(1)}, u32[]{:S(2)}, u32[]{:S(2)}) collective-permute-start(bf16[96,3072]{1,0:T(8,128)(2,1)S(1)} %add_all.1), channel_id=1, source_target_pairs={{0,1},{1,0},{2,3},{3,2},{4,5},{5,4},{6,7},{7,6},{8,9},{9,8},{10,11... | collective-permute-start | bytes 1769480 | tf_op jit(solution)/shard_map/ppermute | solution.py:713
  211.4 18.8 %collective-permute-start.19 = (bf16[4,112,768]{2,1,0:T(8,128)(2,1)}, bf16[4,112,768]{2,1,0:T(8,128)(2,1)S(1)}, u32[]{:S(2)}, u32[]{:S(2)}) collective-permute-start(bf16[4,112,768]{2,1,0:T(8,128)(2,1)} %get-tuple-element.129), channel_id=1, source_target_pairs={{0,4},{4,0},{8,12},{12,8},{16,20},{20,16},{24,28},{28,24},{1,5},{5... | collective-permute-start | bytes 2064392 | tf_op jit(solution)/shard_map/ppermute | solution.py:688
  214.5 32.8 %collective-permute-start.24 = (bf16[96,3072]{1,0:T(8,128)(2,1)S(1)}, bf16[96,3072]{1,0:T(8,128)(2,1)S(1)}, u32[]{:S(2)}, u32[]{:S(2)}) collective-permute-start(bf16[96,3072]{1,0:T(8,128)(2,1)S(1)} %add.306), channel_id=1, source_target_pairs={{0,2},{1,3},{2,0},{3,1},{4,6},{5,7},{6,4},{7,5},{8,10},{9,11},{10,... | collective-permute-start | bytes 1769480 | tf_op jit(solution)/shard_map/ppermute | solution.py:713
  215.9 15.5 %collective-permute-start.22 = (bf16[96,2304]{1,0:T(8,128)(2,1)S(1)}, bf16[96,2304]{1,0:T(8,128)(2,1)S(1)}, u32[]{:S(2)}, u32[]{:S(2)}) collective-permute-start(bf16[96,2304]{1,0:T(8,128)(2,1)S(1)} %get-tuple-element.159), channel_id=1, source_target_pairs={{0,24},{4,28},{8,16},{12,20},{16,8},{20,12},{24,0},{28,4},{1,25},{... | collective-permute-start | bytes 1327112 | tf_op jit(solution)/shard_map/ppermute | solution.py:688
  217.6 20.3 %collective-permute-start.21 = (bf16[96,2304]{1,0:T(8,128)(2,1)S(1)}, bf16[96,2304]{1,0:T(8,128)(2,1)S(1)}, u32[]{:S(2)}, u32[]{:S(2)}) collective-permute-start(bf16[96,2304]{1,0:T(8,128)(2,1)S(1)} %get-tuple-element.160), channel_id=1, source_target_pairs={{0,16},{4,20},{8,24},{12,28},{16,0},{20,4},{24,8},{28,12},{1,17},{... | collective-permute-start | bytes 1327112 | tf_op jit(solution)/shard_map/ppermute | solution.py:688
  218.4 21.1 %collective-permute-start.20 = (bf16[96,2304]{1,0:T(8,128)(2,1)S(1)}, bf16[96,2304]{1,0:T(8,128)(2,1)S(1)}, u32[]{:S(2)}, u32[]{:S(2)}) collective-permute-start(bf16[96,2304]{1,0:T(8,128)(2,1)S(1)} %get-tuple-element.161), channel_id=1, source_target_pairs={{0,8},{4,12},{8,0},{12,4},{16,24},{20,28},{24,16},{28,20},{1,9},{5... | collective-permute-start | bytes 1327112 | tf_op jit(solution)/shard_map/ppermute | solution.py:688
  230.4 16.1 %collective-permute-start.23 = (bf16[2,112,768]{2,1,0:T(8,128)(2,1)S(1)}, bf16[2,112,768]{2,1,0:T(8,128)(2,1)S(1)}, u32[]{:S(2)}, u32[]{:S(2)}) collective-permute-start(bf16[2,112,768]{2,1,0:T(8,128)(2,1)S(1)} %get-tuple-element.166), channel_id=1, source_target_pairs={{0,8},{4,12},{8,0},{12,4},{16,24},{20,28},{24,16},{28,20},{1,9},{5... | collective-permute-start | bytes 1032200 | tf_op jit(solution)/shard_map/ppermute | solution.py:688
  239.8 12.5 %collective-permute-start.28 = (bf16[24,2304]{1,0:T(8,128)(2,1)S(1)}, bf16[24,2304]{1,0:T(8,128)(2,1)S(1)}, u32[]{:S(2)}, u32[]{:S(2)}) collective-permute-start(bf16[24,2304]{1,0:T(8,128)(2,1)S(1)} %get-tuple-element.163), channel_id=1, source_target_pairs={{0,3},{1,2},{2,1},{3,0},{4,7},{5,6},{6,5},{7,4},{8,11},{9,10},{10,... | collective-permute-start | bytes 331784 | tf_op jit(solution)/shard_map/ppermute | solution.py:708
  241.6 10.8 %collective-permute-start.27 = (bf16[24,2304]{1,0:T(8,128)(2,1)S(1)}, bf16[24,2304]{1,0:T(8,128)(2,1)S(1)}, u32[]{:S(2)}, u32[]{:S(2)}) collective-permute-start(bf16[24,2304]{1,0:T(8,128)(2,1)S(1)} %get-tuple-element.164), channel_id=1, source_target_pairs={{0,2},{1,3},{2,0},{3,1},{4,6},{5,7},{6,4},{7,5},{8,10},{9,11},{10,... | collective-permute-start | bytes 331784 | tf_op jit(solution)/shard_map/ppermute | solution.py:708
  241.9 10.4 %collective-permute-start.26 = (bf16[24,2304]{1,0:T(8,128)(2,1)S(1)}, bf16[24,2304]{1,0:T(8,128)(2,1)S(1)}, u32[]{:S(2)}, u32[]{:S(2)}) collective-permute-start(bf16[24,2304]{1,0:T(8,128)(2,1)S(1)} %get-tuple-element.165), channel_id=1, source_target_pairs={{0,1},{1,0},{2,3},{3,2},{4,5},{5,4},{6,7},{7,6},{8,9},{9,8},{10,11... | collective-permute-start | bytes 331784 | tf_op jit(solution)/shard_map/ppermute | solution.py:708
  246.6 5.5 %collective-permute-start.25 = (bf16[112,768]{1,0:T(8,128)(2,1)S(1)}, bf16[112,768]{1,0:T(8,128)(2,1)S(1)}, u32[]{:S(2)}, u32[]{:S(2)}) collective-permute-start(bf16[112,768]{1,0:T(8,128)(2,1)S(1)} %get-tuple-element.169), channel_id=1, source_target_pairs={{0,16},{4,20},{8,24},{12,28},{16,0},{20,4},{24,8},{28,12},{1,17},{... | collective-permute-start | bytes 516104 | tf_op jit(solution)/shard_map/ppermute | solution.py:688
  252.1 10.8 %collective-permute-start.32 = (bf16[112,768]{1,0:T(8,128)(2,1)S(1)}, bf16[112,768]{1,0:T(8,128)(2,1)S(1)}, u32[]{:S(2)}, u32[]{:S(2)}) collective-permute-start(bf16[112,768]{1,0:T(8,128)(2,1)S(1)} %add_convert_fusion.15), channel_id=1, source_target_pairs={{0,1},{1,0},{2,3},{3,2},{4,5},{5,4},{6,7},{7,6},{8,9},{9,8},{10,11... | collective-permute-start | bytes 516104 | tf_op jit(solution)/shard_map/ppermute | solution.py:713
  252.4 10.6 %collective-permute-start.29 = (bf16[24,2304]{1,0:T(8,128)(2,1)S(1)}, bf16[24,2304]{1,0:T(8,128)(2,1)S(1)}, u32[]{:S(2)}, u32[]{:S(2)}) collective-permute-start(bf16[24,2304]{1,0:T(8,128)(2,1)S(1)} %add_convert_fusion.18), channel_id=1, source_target_pairs={{0,3},{1,2},{2,1},{3,0},{4,7},{5,6},{6,5},{7,4},{8,11},{9,10},{10,... | collective-permute-start | bytes 331784 | tf_op jit(solution)/shard_map/ppermute | solution.py:708
  254.9 14.3 %collective-permute-start.30 = (bf16[24,2304]{1,0:T(8,128)(2,1)S(1)}, bf16[24,2304]{1,0:T(8,128)(2,1)S(1)}, u32[]{:S(2)}, u32[]{:S(2)}) collective-permute-start(bf16[24,2304]{1,0:T(8,128)(2,1)S(1)} %add_convert_fusion.18), channel_id=1, source_target_pairs={{0,2},{1,3},{2,0},{3,1},{4,6},{5,7},{6,4},{7,5},{8,10},{9,11},{10,... | collective-permute-start | bytes 331784 | tf_op jit(solution)/shard_map/ppermute | solution.py:708
  255.8 13.4 %collective-permute-start.31 = (bf16[24,2304]{1,0:T(8,128)(2,1)S(1)}, bf16[24,2304]{1,0:T(8,128)(2,1)S(1)}, u32[]{:S(2)}, u32[]{:S(2)}) collective-permute-start(bf16[24,2304]{1,0:T(8,128)(2,1)S(1)} %add_convert_fusion.18), channel_id=1, source_target_pairs={{0,1},{1,0},{2,3},{3,2},{4,5},{5,4},{6,7},{7,6},{8,9},{9,8},{10,11... | collective-permute-start | bytes 331784 | tf_op jit(solution)/shard_map/ppermute | solution.py:708
  263.0 8.7 %collective-permute-start.33 = (bf16[112,768]{1,0:T(8,128)(2,1)S(1)}, bf16[112,768]{1,0:T(8,128)(2,1)S(1)}, u32[]{:S(2)}, u32[]{:S(2)}) collective-permute-start(bf16[112,768]{1,0:T(8,128)(2,1)S(1)} %add.342), channel_id=1, source_target_pairs={{0,2},{1,3},{2,0},{3,1},{4,6},{5,7},{6,4},{7,5},{8,10},{9,11},{10,... | collective-permute-start | bytes 516104 | tf_op jit(solution)/shard_map/ppermute | solution.py:713
  (6 other events, 30.1 us)

commit v10 on v9

--- a/solution.py
+++ b/solution.py
@@ -1003,9 +1003,9 @@
     last_flow.turn(turned)
     up_flow.turn(last_flow.kept)
     last_flow.turn(up_flow.kept)
+    last_flow.turn()
     mixed_flow.turn(last_flow.kept)
-    last_flow.turn(mixed_flow.kept)
-    mixed_flow.turn(last_flow.kept)
+    mixed_flow.turn()
     flows = [outer, up_flow, mixed_flow, last_flow]
     while not all(flow.done for flow in flows):
         for flow in flows:

time: 280 us -> 288 us (1.029)
  waiting for transfers between devices: 39.9 us -> 47.6 us
    ppermute x6, waiting for transfers between devices: 6.3 us -> 10 us  [step(): lax.ppermute(sent, 'col', [(i, i ^ mask) for i in range(size)])]
    ppermute x15, waiting for transfers between devices: 12.1 us -> 15.4 us  [step(): lax.ppermute(sent, 'row', [(i, i ^ mask) for i in range(size)])]
  transfers between devices with their start and end apart: 34 -> 34, of which waited for: 16 -> 19; matrix products, arithmetic and copies ran while one was open for 2% -> 2% of each run, Pallas kernels for 39% -> 38%
where the time goes in v10:
time: 288 us; the launch traced here: 282 us
  Pallas kernels  187 us (65%)
  waiting for transfers between devices  47.6 us (17%)
  starting transfers between devices  34.8 us (12%)
  other arithmetic  9.18 us (3%)
    pallas_call x13, Pallas kernels, call(): pl.pallas_call(kernel, grid=grid, in_specs=list(in_specs) + [pl.BlockSpec...  184 us
    ppermute x15, waiting for transfers between devices, step(): lax.ppermute(sent, 'row', [(i, i ^ mask) for i in range(size)])  15.4 us
    ppermute x6, waiting for transfers between devices, step(): self.got = [lax.ppermute(self.kept, 'col', self.line[0][1])]  12.9 us
    ppermute x15, starting transfers between devices, step(): lax.ppermute(sent, 'row', [(i, i ^ mask) for i in range(size)])  12.7 us
    ppermute x6, waiting for transfers between devices, step(): lax.ppermute(sent, 'col', [(i, i ^ mask) for i in range(size)])  10 us
    ppermute x7, starting transfers between devices, gather_all(): lax.ppermute(piece, name, [(i, i ^ mask) for i in range(size)])  9.38 us
    ppermute x7, waiting for transfers between devices, gather_all(): lax.ppermute(piece, name, [(i, i ^ mask) for i in range(size)])  9.27 us
    ppermute x6, starting transfers between devices, step(): lax.ppermute(sent, 'col', [(i, i ^ mask) for i in range(size)])  8.84 us
  transfers between devices with their start and end apart: 34, of which 19 were waited for; matrix products, arithmetic and copies ran while one was open for 2% of the time, Pallas kernels for 38%

profile of v10, /device:TPU:0, one launch (start us, length us, event | category | flops | bytes accessed | tf_op | source)
XLA Modules:
  0.0 282.3 jit_solution(9529353909583436055)
XLA Ops:
  0.7 20.8 %attend.1 = (bf16[1536,768]{1,0:T(8,128)(2,1)}, bf16[1536,768]{1,0:T(8,128)(2,1)}, bf16[1536,768]{1,0:T(8,128)(2,1)}, bf16[768,1536]{1,0:T(8,128)(2,1)}, f32[3,6,8,512]{3,2,1,0:T(8,128)}) custom-call(s32[4]{0:T(128)} %refs_1_.9, s32[2]{0:T(128)} %refs_2_.7, bf16[512,768]{1,0:T(8,128)(2,1)} %bitcast.100, bf16[1024,768]{1,0:T(8,128)(2,1)} %bitcast.97, ...), custom_call_target="tpu_custom_call" | custom-call | flops 13799999488 | tf_op jit(solution)/shard_map/attend/pallas_call | solution.py:579
  21.5 39.0 %dense.1 = (bf16[1536,768]{1,0:T(8,128)(2,1)}, bf16[1536,768]{1,0:T(8,128)(2,1)}, bf16[1536,3072]{1,0:T(8,128)(2,1)}, bf16[1536,3072]{1,0:T(8,128)(2,1)}, bf16[1...) custom-call(s32[4]{0:T(128)} %refs_1_.9, ...), custom_call_target="tpu_custom_call" | custom-call | flops 13799999488 | tf_op jit(solution)/shard_map/dense/pallas_call | solution.py:579
  60.5 5.1 %collective-permute-start = (bf16[8,896]{1,0:T(8,128)(2,1)}, bf16[8,896]{1,0:T(8,128)(2,1)S(1)}, u32[]{:S(2)}, u32[]{:S(2)}) collective-permute-start(bf16[8,896]{1,0:T(8,128)(2,1)} %get-tuple-element.83.own_ref), channel_id=1, source_target_pairs={{0,3},{1,2},{2,1},{3,0},{4,7},{5,6},{6,5},{7,4},{8,11},{9,10},{10,... | collective-permute-start | bytes 43016 | tf_op jit(solution)/shard_map/ppermute | solution.py:762
  67.5 2.9 %collective-permute-done.1 = bf16[8,896]{1,0:T(8,128)(2,1)S(1)} collective-permute-done((bf16[8,896]{1,0:T(8,128)(2,1)}, bf16[8,896]{1,0:T(8,128)(2,1)S(1)}, u32[]{:S(2)}, u32[]{:S(2)}) %collective-permute-start.1) | collective-permute-done | bytes 14368 | tf_op jit(solution)/shard_map/ppermute | solution.py:762
  71.2 1.6 collective-permute-start.4
  75.6 2.2 collective-permute-done.3
  81.0 2.9 %loss.1 = (f32[8,128]{1,0:T(8,128)}, f32[8,768]{1,0:T(8,128)}) custom-call(s32[1]{0:T(128)} %bitcast.me_ref, s32[4]{0:T(128)} %refs_1_.9, s32[2]{0:T(128)} %refs_2_.7, bf16[8,896]{1,0:T(8,128)(2,1)} %get-tuple-element.83.own_ref, bf16[256,896]{1,0:T(8,128)(2,1)} %pad_maximum_fusion.all_ref, f32[8,768]{1,0:T(8,128)} %get-tuple-element.84.pool_ref), custom_call_target="tpu_custom_call" | custom-call | tf_op jit(solution)/shard_map/loss/pallas_call | solution.py:868
  83.9 18.3 %outer_grad.1 = (bf16[1536,768]{1,0:T(8,128)(2,1)}, f32[8,768]{1,0:T(8,128)}, bf16[4,768,384]{2,1,0:T(8,128)(2,1)}, bf16[4,768,384]{2,1,0:T(8,128)(2,1)}) custom-call(s32[1]{0:T(128)} %bitcast.6.refs_0_, s32[4]{0:T(128)} %refs_1_.9, s32[2]{0:T(128)} %refs_2_.7, f32[8,768]{1,0:T(8,128)} %get-tuple-element.88.refs_3_, ...), custom_call_target="tpu_custom_call" | custom-call | flops 13799999488 | tf_op jit(solution)/shard_map/outer_grad/pallas_call | solution.py:579
  102.3 4.4 %turn.3.refs_1_ = bf16[768,1536]{1,0:T(8,128)(2,1)} custom-call(bf16[1536,768]{1,0:T(8,128)(2,1)} %get-tuple-element.94.refs_0_), custom_call_target="tpu_custom_call" | custom-call | flops 46000001024 | tf_op jit(solution)/shard_map/turn/pallas_call | solution.py:579
  111.1 31.1 %dense_back.1 = (bf16[1536,3072]{1,0:T(8,128)(2,1)}, bf16[1536,768]{1,0:T(8,128)(2,1)}, bf16[1536,768]{1,0:T(8,128)(2,1)}, f32[8,768]{1,0:T(8,128)}, f32[8,3072]{1,0:T(8,128)}) custom-call(bf16[1536,768]{1,0:T(8,128)(2,1)} %get-tuple-element.96.refs_0_, bf16[1536,3072]{1,0:T(8,128)(2,1)} %get-tuple-element.97.refs_1_, ...), custom_call_target="tpu_custom_call" | custom-call | flops 13799999488 | tf_op jit(solution)/shard_map/dense_back/pallas_call | solution.py:579
  143.6 12.2 %weight_grad.2 = (bf16[4,96,3072]{2,1,0:T(8,128)(2,1)}, bf16[4,96,3072]{2,1,0:T(8,128)(2,1)}) custom-call(s32[1]{0:T(128)} %bitcast.6.refs_0_, bf16[768,1536]{1,0:T(8,128)(2,1)} %turn.3.refs_1_, bf16[1536,3072]{1,0:T(8,128)(2,1)} %get-tuple-element.103.refs_2_), custom_call_target="tpu_custom_call" | custom-call | flops 13799999488 | tf_op jit(solution)/shard_map/weight_grad/pallas_call | solution.py:579
  155.9 2.3 collective-permute-done.12
  158.4 2.1 collective-permute-start.13
  160.4 4.9 %turn.4.refs_9_ = bf16[768,1536]{1,0:T(8,128)(2,1)} custom-call(bf16[512,768]{1,0:T(8,128)(2,1)} %bitcast.102, bf16[1024,768]{1,0:T(8,128)(2,1)} %bitcast.99), custom_call_target="tpu_custom_call" | custom-call | flops 46000001024 | tf_op jit(solution)/shard_map/turn/pallas_call | solution.py:579
  169.8 21.8 %attend_back.2 = (bf16[1536,1536]{1,0:T(8,128)(2,1)}, f32[8,512]{1,0:T(8,128)}, bf16[4,96,2304]{2,1,0:T(8,128)(2,1)}, bf16[4,96,2304]{2,1,0:T(8,128)(2,1)}) custom-call(s32[1]{0:T(128)} %bitcast.6.refs_0_, s32[4]{0:T(128)} %refs_1_.9, s32[2]{0:T(128)} %refs_2_.7, bf16[1536,768]{1,0:T(8,128)(2,1)} %get-tuple-element.110.refs_3_, ...), custom_call_target="tpu_custom_call" | custom-call | flops 13799999488 | tf_op jit(solution)/shard_map/attend_back/pallas_call | solution.py:579
  191.6 5.7 %weight_grad.3 = (bf16[4,96,2304]{2,1,0:T(8,128)(2,1)}, bf16[4,96,2304]{2,1,0:T(8,128)(2,1)}) custom-call(s32[1]{0:T(128)} %bitcast.6.refs_0_, bf16[768,1536]{1,0:T(8,128)(2,1)} %get-tuple-element.82.refs_5_.refs_6_.refs_1_, bf16[1536,768]{1,0:T(8,128)(2,1)} %get-tuple-element.118.refs_2_, ...), custom_call_target="tpu_custom_call", output_to_operand_aliasing={{0}: (3, {}), {1}: (4, {})} | custom-call | tf_op jit(solution)/shard_map/weight_grad/pallas_call | solution.py:579
  198.9 12.5 %attend_back.3 = (bf16[1536,768]{1,0:T(8,128)(2,1)}, f32[8,256]{1,0:T(8,128)}, bf16[4,112,768]{2,1,0:T(8,128)(2,1)}, bf16[4,112,768]{2,1,0:T(8,128)(2,1)}) custom-call(s32[1]{0:T(128)} %bitcast.6.refs_0_, s32[4]{0:T(128)} %refs_1_.9, s32[2]{0:T(128)} %refs_2_.7, bf16[1536,768]{1,0:T(8,128)(2,1)} %get-tuple-element.110.refs_3_, ...), custom_call_target="tpu_custom_call" | custom-call | flops 46000001024 | tf_op jit(solution)/shard_map/attend_back/pallas_call | solution.py:579
  211.7 2.6 collective-permute-done.18
  215.9 1.6 collective-permute-start.22
  219.5 10.8 %input_grad.1 = (bf16[512,768]{1,0:T(8,128)(2,1)}, bf16[1024,768]{1,0:T(8,128)(2,1)}) custom-call(bf16[1536,1536]{1,0:T(8,128)(2,1)} %get-tuple-element.115.refs_0_, bf16[1536,768]{1,0:T(8,128)(2,1)} %get-tuple-element.126.refs_1_, bf16[1536,768]{1,0:T(8,128)(2,1)} %get-tuple-element.118.refs_2_, bf16[768,768]{1,0:T(8,128)(2,1)} %refs_3_.2, ...), custom_call_target="tpu_custom_call" | custom-call | flops 46000001024 | tf_op jit(solution)/shard_map/input_grad/pallas_call | solution.py:579
  231.5 6.4 %collective-permute-done.21 = bf16[96,2304]{1,0:T(8,128)(2,1)S(1)} collective-permute-done((bf16[96,2304]{1,0:T(8,128)(2,1)S(1)}, bf16[96,2304]{1,0:T(8,128)(2,1)S(1)}, u32[]{:S(2)}, u32[]{:S(2)}) %collective-permute-start.21) | collective-permute-done | bytes 442400 | tf_op jit(solution)/shard_map/ppermute | solution.py:688
  237.9 1.7 collective-permute-done.20
  239.8 2.3 turn.5
  242.1 3.3 %collective-permute-done.23 = bf16[2,112,768]{2,1,0:T(8,128)(2,1)S(1)} collective-permute-done((bf16[2,112,768]{2,1,0:T(8,128)(2,1)S(1)}, bf16[2,112,768]{2,1,0:T(8,128)(2,1)S(1)}, u32[]{:S(2)}, u32[]{:S(2)}) %collective-permute-start.23) | collective-permute-done | bytes 344096 | tf_op jit(solution)/shard_map/ppermute | solution.py:688
  247.1 3.8 %collective-permute-done.25 = bf16[112,768]{1,0:T(8,128)(2,1)S(1)} collective-permute-done((bf16[112,768]{1,0:T(8,128)(2,1)S(1)}, bf16[112,768]{1,0:T(8,128)(2,1)S(1)}, u32[]{:S(2)}, u32[]{:S(2)}) %collective-permute-start.25) | collective-permute-done | bytes 172064 | tf_op jit(solution)/shard_map/ppermute | solution.py:688
  251.3 3.2 %collective-permute-start.29 = (bf16[24,2304]{1,0:T(8,128)(2,1)S(1)}, bf16[24,2304]{1,0:T(8,128)(2,1)S(1)}, u32[]{:S(2)}, u32[]{:S(2)}) collective-permute-start(bf16[24,2304]{1,0:T(8,128)(2,1)S(1)} %get-tuple-element.159), channel_id=1, source_target_pairs={{0,3},{1,2},{2,1},{3,0},{4,7},{5,6},{6,5},{7,4},{8,11},{9,10},{10,... | collective-permute-start | bytes 331784 | tf_op jit(solution)/shard_map/ppermute | solution.py:708
  255.7 5.6 %collective-permute-done.26 = bf16[112,768]{1,0:T(8,128)(2,1)S(1)} collective-permute-done((bf16[112,768]{1,0:T(8,128)(2,1)S(1)}, bf16[112,768]{1,0:T(8,128)(2,1)S(1)}, u32[]{:S(2)}, u32[]{:S(2)}) %collective-permute-start.26) | collective-permute-done | bytes 172064 | tf_op jit(solution)/shard_map/ppermute | solution.py:713
  263.0 1.7 collective-permute-start.30
  264.8 2.6 collective-permute-start.32
  268.8 2.0 collective-permute-done.30
  270.7 6.5 %collective-permute-done.31 = bf16[24,2304]{1,0:T(8,128)(2,1)S(1)} collective-permute-done((bf16[24,2304]{1,0:T(8,128)(2,1)S(1)}, bf16[24,2304]{1,0:T(8,128)(2,1)S(1)}, u32[]{:S(2)}, u32[]{:S(2)}) %collective-permute-start.31) | collective-permute-done | bytes 110624 | tf_op jit(solution)/shard_map/ppermute | solution.py:708
  277.3 2.4 collective-permute-done.33
  (87 shorter events, 34.7 us)
Async XLA Ops:
  60.5 7.0 %collective-permute-start = (bf16[8,896]{1,0:T(8,128)(2,1)}, bf16[8,896]{1,0:T(8,128)(2,1)S(1)}, u32[]{:S(2)}, u32[]{:S(2)}) collective-permute-start(bf16[8,896]{1,0:T(8,128)(2,1)} %get-tuple-element.83.own_ref), channel_id=1, source_target_pairs={{0,3},{1,2},{2,1},{3,0},{4,7},{5,6},{6,5},{7,4},{8,11},{9,10},{10,... | collective-permute-start | bytes 43016 | tf_op jit(solution)/shard_map/ppermute | solution.py:762
  65.6 4.8 %collective-permute-start.1 = (bf16[8,896]{1,0:T(8,128)(2,1)}, bf16[8,896]{1,0:T(8,128)(2,1)S(1)}, u32[]{:S(2)}, u32[]{:S(2)}) collective-permute-start(bf16[8,896]{1,0:T(8,128)(2,1)} %get-tuple-element.83.own_ref), channel_id=1, source_target_pairs={{0,2},{1,3},{2,0},{3,1},{4,6},{5,7},{6,4},{7,5},{8,10},{9,11},{10,... | collective-permute-start | bytes 43016 | tf_op jit(solution)/shard_map/ppermute | solution.py:762
  65.6 4.8 %collective-permute-start.2 = (bf16[8,896]{1,0:T(8,128)(2,1)}, bf16[8,896]{1,0:T(8,128)(2,1)S(1)}, u32[]{:S(2)}, u32[]{:S(2)}) collective-permute-start(bf16[8,896]{1,0:T(8,128)(2,1)} %get-tuple-element.83.own_ref), channel_id=1, source_target_pairs={{0,1},{1,0},{2,3},{3,2},{4,5},{5,4},{6,7},{7,6},{8,9},{9,8},{10,11... | collective-permute-start | bytes 43016 | tf_op jit(solution)/shard_map/ppermute | solution.py:762
  71.2 4.4 %collective-permute-start.4 = (bf16[32,896]{1,0:T(8,128)(2,1)S(1)}, bf16[32,896]{1,0:T(8,128)(2,1)S(1)}, u32[]{:S(2)}, u32[]{:S(2)}) collective-permute-start(bf16[32,896]{1,0:T(8,128)(2,1)S(1)} %pad_maximum_fusion.5), channel_id=1, source_target_pairs={{0,16},{4,20},{8,24},{12,28},{16,0},{20,4},{24,8},{28,12},{1,17},{... | collective-permute-start | bytes 172040 | tf_op jit(solution)/shard_map/ppermute | solution.py:762
  72.8 5.1 %collective-permute-start.3 = (bf16[32,896]{1,0:T(8,128)(2,1)S(1)}, bf16[32,896]{1,0:T(8,128)(2,1)S(1)}, u32[]{:S(2)}, u32[]{:S(2)}) collective-permute-start(bf16[32,896]{1,0:T(8,128)(2,1)S(1)} %pad_maximum_fusion.5), channel_id=1, source_target_pairs={{0,24},{4,28},{8,16},{12,20},{16,8},{20,12},{24,0},{28,4},{1,25},{... | collective-permute-start | bytes 172040 | tf_op jit(solution)/shard_map/ppermute | solution.py:762
  102.2 4.7 %collective-permute-start.7 = (bf16[4,768,384]{2,1,0:T(8,128)(2,1)}, bf16[4,768,384]{2,1,0:T(8,128)(2,1)S(1)}, u32[]{:S(2)}, u32[]{:S(2)}) collective-permute-start(bf16[4,768,384]{2,1,0:T(8,128)(2,1)} %get-tuple-element.93), channel_id=1, source_target_pairs={{0,4},{4,0},{8,12},{12,8},{16,20},{20,16},{24,28},{28,24},{1,5},{5... | collective-permute-start | bytes 7077896 | tf_op jit(solution)/shard_map/ppermute | solution.py:688
  107.5 34.7 %collective-permute-start.8 = (bf16[768,384]{1,0:T(8,128)(2,1)S(1)}, bf16[768,384]{1,0:T(8,128)(2,1)S(1)}, u32[]{:S(2)}, u32[]{:S(2)}) collective-permute-start(bf16[768,384]{1,0:T(8,128)(2,1)S(1)} %get-tuple-element.153), channel_id=1, source_target_pairs={{0,8},{4,12},{8,0},{12,4},{16,24},{20,28},{24,16},{28,20},{1,9},{5... | collective-permute-start | bytes 1769480 | tf_op jit(solution)/shard_map/ppermute | solution.py:688
  108.5 33.6 %collective-permute-start.9 = (bf16[768,384]{1,0:T(8,128)(2,1)S(1)}, bf16[768,384]{1,0:T(8,128)(2,1)S(1)}, u32[]{:S(2)}, u32[]{:S(2)}) collective-permute-start(bf16[768,384]{1,0:T(8,128)(2,1)S(1)} %get-tuple-element.152), channel_id=1, source_target_pairs={{0,16},{4,20},{8,24},{12,28},{16,0},{20,4},{24,8},{28,12},{1,17},{... | collective-permute-start | bytes 1769480 | tf_op jit(solution)/shard_map/ppermute | solution.py:688
  109.7 32.5 %collective-permute-start.10 = (bf16[768,384]{1,0:T(8,128)(2,1)S(1)}, bf16[768,384]{1,0:T(8,128)(2,1)}, u32[]{:S(2)}, u32[]{:S(2)}) collective-permute-start(bf16[768,384]{1,0:T(8,128)(2,1)S(1)} %get-tuple-element.151), channel_id=1, source_target_pairs={{0,24},{4,28},{8,16},{12,20},{16,8},{20,12},{24,0},{28,4},{1,25},{... | collective-permute-start | bytes 1769480 | tf_op jit(solution)/shard_map/ppermute | solution.py:688
  143.6 14.6 %collective-permute-start.12 = (bf16[768,384]{1,0:T(8,128)(2,1)S(1)}, bf16[768,384]{1,0:T(8,128)(2,1)S(1)}, u32[]{:S(2)}, u32[]{:S(2)}) collective-permute-start(bf16[768,384]{1,0:T(8,128)(2,1)S(1)} %add_convert_fusion.4), channel_id=1, source_target_pairs={{0,1},{1,0},{2,3},{3,2},{4,5},{5,4},{6,7},{7,6},{8,9},{9,8},{10,11... | collective-permute-start | bytes 1769480 | tf_op jit(solution)/shard_map/ppermute | solution.py:713
  155.9 9.4 %collective-permute-start.11 = (bf16[4,96,3072]{2,1,0:T(8,128)(2,1)}, bf16[4,96,3072]{2,1,0:T(8,128)(2,1)S(1)}, u32[]{:S(2)}, u32[]{:S(2)}) collective-permute-start(bf16[4,96,3072]{2,1,0:T(8,128)(2,1)} %get-tuple-element.104), channel_id=1, source_target_pairs={{0,4},{4,0},{8,12},{12,8},{16,20},{20,16},{24,28},{28,24},{1,5},{5... | collective-permute-start | bytes 7077896 | tf_op jit(solution)/shard_map/ppermute | solution.py:688
  158.4 38.9 %collective-permute-start.13 = (bf16[768,384]{1,0:T(8,128)(2,1)S(1)}, bf16[768,384]{1,0:T(8,128)(2,1)S(1)}, u32[]{:S(2)}, u32[]{:S(2)}) collective-permute-start(bf16[768,384]{1,0:T(8,128)(2,1)S(1)} %add.298), channel_id=1, source_target_pairs={{0,2},{1,3},{2,0},{3,1},{4,6},{5,7},{6,4},{7,5},{8,10},{9,11},{10,... | collective-permute-start | bytes 1769480 | tf_op jit(solution)/shard_map/ppermute | solution.py:713
  166.3 31.9 %collective-permute-start.14 = (bf16[96,3072]{1,0:T(8,128)(2,1)S(1)}, bf16[96,3072]{1,0:T(8,128)(2,1)S(1)}, u32[]{:S(2)}, u32[]{:S(2)}) collective-permute-start(bf16[96,3072]{1,0:T(8,128)(2,1)S(1)} %get-tuple-element.149), channel_id=1, source_target_pairs={{0,8},{4,12},{8,0},{12,4},{16,24},{20,28},{24,16},{28,20},{1,9},{5... | collective-permute-start | bytes 1769480 | tf_op jit(solution)/shard_map/ppermute | solution.py:688
  167.3 30.9 %collective-permute-start.15 = (bf16[96,3072]{1,0:T(8,128)(2,1)S(1)}, bf16[96,3072]{1,0:T(8,128)(2,1)S(1)}, u32[]{:S(2)}, u32[]{:S(2)}) collective-permute-start(bf16[96,3072]{1,0:T(8,128)(2,1)S(1)} %get-tuple-element.148), channel_id=1, source_target_pairs={{0,16},{4,20},{8,24},{12,28},{16,0},{20,4},{24,8},{28,12},{1,17},{... | collective-permute-start | bytes 1769480 | tf_op jit(solution)/shard_map/ppermute | solution.py:688
  168.5 29.7 %collective-permute-start.16 = (bf16[96,3072]{1,0:T(8,128)(2,1)S(1)}, bf16[96,3072]{1,0:T(8,128)(2,1)S(1)}, u32[]{:S(2)}, u32[]{:S(2)}) collective-permute-start(bf16[96,3072]{1,0:T(8,128)(2,1)S(1)} %get-tuple-element.147), channel_id=1, source_target_pairs={{0,24},{4,28},{8,16},{12,20},{16,8},{20,12},{24,0},{28,4},{1,25},{... | collective-permute-start | bytes 1769480 | tf_op jit(solution)/shard_map/ppermute | solution.py:688
  197.2 18.2 %collective-permute-start.17 = (bf16[4,96,2304]{2,1,0:T(8,128)(2,1)}, bf16[4,96,2304]{2,1,0:T(8,128)(2,1)S(1)}, u32[]{:S(2)}, u32[]{:S(2)}) collective-permute-start(bf16[4,96,2304]{2,1,0:T(8,128)(2,1)} %get-tuple-element.121), channel_id=1, source_target_pairs={{0,4},{4,0},{8,12},{12,8},{16,20},{20,16},{24,28},{28,24},{1,5},{5... | collective-permute-start | bytes 5308424 | tf_op jit(solution)/shard_map/ppermute | solution.py:688
  198.5 15.8 %collective-permute-start.18 = (bf16[96,3072]{1,0:T(8,128)(2,1)S(1)}, bf16[96,3072]{1,0:T(8,128)(2,1)S(1)}, u32[]{:S(2)}, u32[]{:S(2)}) collective-permute-start(bf16[96,3072]{1,0:T(8,128)(2,1)S(1)} %add_all.1), channel_id=1, source_target_pairs={{0,1},{1,0},{2,3},{3,2},{4,5},{5,4},{6,7},{7,6},{8,9},{9,8},{10,11... | collective-permute-start | bytes 1769480 | tf_op jit(solution)/shard_map/ppermute | solution.py:713
  211.4 18.8 %collective-permute-start.19 = (bf16[4,112,768]{2,1,0:T(8,128)(2,1)}, bf16[4,112,768]{2,1,0:T(8,128)(2,1)S(1)}, u32[]{:S(2)}, u32[]{:S(2)}) collective-permute-start(bf16[4,112,768]{2,1,0:T(8,128)(2,1)} %get-tuple-element.127), channel_id=1, source_target_pairs={{0,4},{4,0},{8,12},{12,8},{16,20},{20,16},{24,28},{28,24},{1,5},{5... | collective-permute-start | bytes 2064392 | tf_op jit(solution)/shard_map/ppermute | solution.py:688
  214.5 31.5 %collective-permute-start.24 = (bf16[96,3072]{1,0:T(8,128)(2,1)S(1)}, bf16[96,3072]{1,0:T(8,128)(2,1)S(1)}, u32[]{:S(2)}, u32[]{:S(2)}) collective-permute-start(bf16[96,3072]{1,0:T(8,128)(2,1)S(1)} %add.306), channel_id=1, source_target_pairs={{0,2},{1,3},{2,0},{3,1},{4,6},{5,7},{6,4},{7,5},{8,10},{9,11},{10,... | collective-permute-start | bytes 1769480 | tf_op jit(solution)/shard_map/ppermute | solution.py:713
  215.9 15.5 %collective-permute-start.22 = (bf16[96,2304]{1,0:T(8,128)(2,1)S(1)}, bf16[96,2304]{1,0:T(8,128)(2,1)S(1)}, u32[]{:S(2)}, u32[]{:S(2)}) collective-permute-start(bf16[96,2304]{1,0:T(8,128)(2,1)S(1)} %get-tuple-element.155), channel_id=1, source_target_pairs={{0,24},{4,28},{8,16},{12,20},{16,8},{20,12},{24,0},{28,4},{1,25},{... | collective-permute-start | bytes 1327112 | tf_op jit(solution)/shard_map/ppermute | solution.py:688
  217.6 20.3 %collective-permute-start.21 = (bf16[96,2304]{1,0:T(8,128)(2,1)S(1)}, bf16[96,2304]{1,0:T(8,128)(2,1)S(1)}, u32[]{:S(2)}, u32[]{:S(2)}) collective-permute-start(bf16[96,2304]{1,0:T(8,128)(2,1)S(1)} %get-tuple-element.156), channel_id=1, source_target_pairs={{0,16},{4,20},{8,24},{12,28},{16,0},{20,4},{24,8},{28,12},{1,17},{... | collective-permute-start | bytes 1327112 | tf_op jit(solution)/shard_map/ppermute | solution.py:688
  218.4 21.1 %collective-permute-start.20 = (bf16[96,2304]{1,0:T(8,128)(2,1)S(1)}, bf16[96,2304]{1,0:T(8,128)(2,1)S(1)}, u32[]{:S(2)}, u32[]{:S(2)}) collective-permute-start(bf16[96,2304]{1,0:T(8,128)(2,1)S(1)} %get-tuple-element.157), channel_id=1, source_target_pairs={{0,8},{4,12},{8,0},{12,4},{16,24},{20,28},{24,16},{28,20},{1,9},{5... | collective-permute-start | bytes 1327112 | tf_op jit(solution)/shard_map/ppermute | solution.py:688
  230.4 14.9 %collective-permute-start.23 = (bf16[2,112,768]{2,1,0:T(8,128)(2,1)S(1)}, bf16[2,112,768]{2,1,0:T(8,128)(2,1)S(1)}, u32[]{:S(2)}, u32[]{:S(2)}) collective-permute-start(bf16[2,112,768]{2,1,0:T(8,128)(2,1)S(1)} %get-tuple-element.162), channel_id=1, source_target_pairs={{0,8},{4,12},{8,0},{12,4},{16,24},{20,28},{24,16},{28,20},{1,9},{5... | collective-permute-start | bytes 1032200 | tf_op jit(solution)/shard_map/ppermute | solution.py:688
  245.4 5.5 %collective-permute-start.25 = (bf16[112,768]{1,0:T(8,128)(2,1)S(1)}, bf16[112,768]{1,0:T(8,128)(2,1)S(1)}, u32[]{:S(2)}, u32[]{:S(2)}) collective-permute-start(bf16[112,768]{1,0:T(8,128)(2,1)S(1)} %get-tuple-element.165), channel_id=1, source_target_pairs={{0,16},{4,20},{8,24},{12,28},{16,0},{20,4},{24,8},{28,12},{1,17},{... | collective-permute-start | bytes 516104 | tf_op jit(solution)/shard_map/ppermute | solution.py:688
  251.0 10.3 %collective-permute-start.26 = (bf16[112,768]{1,0:T(8,128)(2,1)S(1)}, bf16[112,768]{1,0:T(8,128)(2,1)S(1)}, u32[]{:S(2)}, u32[]{:S(2)}) collective-permute-start(bf16[112,768]{1,0:T(8,128)(2,1)S(1)} %add_convert_fusion.15), channel_id=1, source_target_pairs={{0,1},{1,0},{2,3},{3,2},{4,5},{5,4},{6,7},{7,6},{8,9},{9,8},{10,11... | collective-permute-start | bytes 516104 | tf_op jit(solution)/shard_map/ppermute | solution.py:713
  251.3 10.0 %collective-permute-start.29 = (bf16[24,2304]{1,0:T(8,128)(2,1)S(1)}, bf16[24,2304]{1,0:T(8,128)(2,1)S(1)}, u32[]{:S(2)}, u32[]{:S(2)}) collective-permute-start(bf16[24,2304]{1,0:T(8,128)(2,1)S(1)} %get-tuple-element.159), channel_id=1, source_target_pairs={{0,3},{1,2},{2,1},{3,0},{4,7},{5,6},{6,5},{7,4},{8,11},{9,10},{10,... | collective-permute-start | bytes 331784 | tf_op jit(solution)/shard_map/ppermute | solution.py:708
  254.5 8.3 %collective-permute-start.28 = (bf16[24,2304]{1,0:T(8,128)(2,1)S(1)}, bf16[24,2304]{1,0:T(8,128)(2,1)S(1)}, u32[]{:S(2)}, u32[]{:S(2)}) collective-permute-start(bf16[24,2304]{1,0:T(8,128)(2,1)S(1)} %get-tuple-element.160), channel_id=1, source_target_pairs={{0,2},{1,3},{2,0},{3,1},{4,6},{5,7},{6,4},{7,5},{8,10},{9,11},{10,... | collective-permute-start | bytes 331784 | tf_op jit(solution)/shard_map/ppermute | solution.py:708
  254.5 8.4 %collective-permute-start.27 = (bf16[24,2304]{1,0:T(8,128)(2,1)S(1)}, bf16[24,2304]{1,0:T(8,128)(2,1)S(1)}, u32[]{:S(2)}, u32[]{:S(2)}) collective-permute-start(bf16[24,2304]{1,0:T(8,128)(2,1)S(1)} %get-tuple-element.161), channel_id=1, source_target_pairs={{0,1},{1,0},{2,3},{3,2},{4,5},{5,4},{6,7},{7,6},{8,9},{9,8},{10,11... | collective-permute-start | bytes 331784 | tf_op jit(solution)/shard_map/ppermute | solution.py:708
  263.0 7.7 %collective-permute-start.30 = (bf16[24,2304]{1,0:T(8,128)(2,1)S(1)}, bf16[24,2304]{1,0:T(8,128)(2,1)S(1)}, u32[]{:S(2)}, u32[]{:S(2)}) collective-permute-start(bf16[24,2304]{1,0:T(8,128)(2,1)S(1)} %add_convert_fusion.18), channel_id=1, source_target_pairs={{0,3},{1,2},{2,1},{3,0},{4,7},{5,6},{6,5},{7,4},{8,11},{9,10},{10,... | collective-permute-start | bytes 331784 | tf_op jit(solution)/shard_map/ppermute | solution.py:708
  264.7 12.5 %collective-permute-start.31 = (bf16[24,2304]{1,0:T(8,128)(2,1)S(1)}, bf16[24,2304]{1,0:T(8,128)(2,1)S(1)}, u32[]{:S(2)}, u32[]{:S(2)}) collective-permute-start(bf16[24,2304]{1,0:T(8,128)(2,1)S(1)} %add_convert_fusion.18), channel_id=1, source_target_pairs={{0,2},{1,3},{2,0},{3,1},{4,6},{5,7},{6,4},{7,5},{8,10},{9,11},{10,... | collective-permute-start | bytes 331784 | tf_op jit(solution)/shard_map/ppermute | solution.py:708
  264.8 12.4 %collective-permute-start.32 = (bf16[24,2304]{1,0:T(8,128)(2,1)S(1)}, bf16[24,2304]{1,0:T(8,128)(2,1)S(1)}, u32[]{:S(2)}, u32[]{:S(2)}) collective-permute-start(bf16[24,2304]{1,0:T(8,128)(2,1)S(1)} %add_convert_fusion.18), channel_id=1, source_target_pairs={{0,1},{1,0},{2,3},{3,2},{4,5},{5,4},{6,7},{7,6},{8,9},{9,8},{10,11... | collective-permute-start | bytes 331784 | tf_op jit(solution)/shard_map/ppermute | solution.py:708
  268.6 11.0 %collective-permute-start.33 = (bf16[112,768]{1,0:T(8,128)(2,1)S(1)}, bf16[112,768]{1,0:T(8,128)(2,1)S(1)}, u32[]{:S(2)}, u32[]{:S(2)}) collective-permute-start(bf16[112,768]{1,0:T(8,128)(2,1)S(1)} %add.321), channel_id=1, source_target_pairs={{0,2},{1,3},{2,0},{3,1},{4,6},{5,7},{6,4},{7,5},{8,10},{9,11},{10,... | collective-permute-start | bytes 516104 | tf_op jit(solution)/shard_map/ppermute | solution.py:713
  (6 other events, 30.1 us)
